TPU v7x, 32 devices: a whole 2x2x4 slice. The times are simulated.
32 devices in a mesh: fsdp: 2 (over y), tensor: 16 (over z, x, core).
Axes of the slice: x: 2, y: 2, z: 4, core: 2. Of those that a mesh axis runs over, the one named last changes fastest.
Arguments:
- tokens: bfloat16 [256, 8192], P('fsdp', 'tensor'), may hold values from -6 to 6
- in_values: bfloat16 [8192, 3, 8192], P('fsdp', None, 'tensor'), may hold values from -0.09375 to 0.09375
- in_scales: bfloat16 [64, 3, 8192], P('fsdp', None, 'tensor'), may hold values from 0.5 to 2
- filters: float32 [512, 128], P('tensor'), may hold values from -0.6 to 0.6
- out_weight: bfloat16 [8192, 8192], P('tensor', 'fsdp'), may hold values from -0.0625 to 0.0625
- cotangent: bfloat16 [256, 8192], P('fsdp', 'tensor'), may hold values from -15 to 15
Outputs:
- input_grad: bfloat16 [256, 8192], P('fsdp', 'tensor')
- filter_grad: float32 [512, 128], P('tensor')
All inputs are finite; a program needn't handle non-finite values.
Results may differ from a plain program's by a relative error of at most 0.012.
Values may be sent and summed in bfloat16 or wider, within the bound.
No kernel may reach another device: no remote copies, remote signals or barrier semaphores. Data moves between devices by JAX's collectives and lax.ppermute only.
A program may use at most 192 MiB of HBM per device.

v0:
```python
import jax
import jax.numpy as jnp
from jax import lax
from jax.sharding import PartitionSpec as P

BLOCK = 128


def passed_along(array, axis, by):
    length = lax.axis_size(axis)
    pairs = [(i, i + by) for i in range(length) if 0 <= i + by < length]
    return lax.ppermute(array, axis, pairs)


def dequantize(values, scales):
    blocks = scales.shape[0]
    channels = values.shape[2]
    scaled = (
        values.astype(jnp.float32).reshape(blocks, BLOCK, 3, channels)
        * scales.astype(jnp.float32)[:, None]
    )
    return scaled.reshape(blocks * BLOCK, 3 * channels).astype(jnp.bfloat16)


def apply_taps(filt, extended, rows, per_group, causal):
    taps = filt.shape[1]
    repeated = jnp.repeat(filt, per_group, axis=0)

    def one_step(lag_index, total):
        lag_value = jnp.asarray(lag_index).astype(jnp.int32)
        offset = taps - 1 - lag_value if causal else lag_value
        slab = lax.dynamic_slice_in_dim(extended, offset, rows, 0)
        column = lax.dynamic_slice_in_dim(repeated, lag_value, 1, 1)[:, 0]
        return total + column[None, :] * slab

    return lax.fori_loop(0, taps, one_step, jnp.zeros((rows, repeated.shape[0]), jnp.float32))


def filter_terms(grad_rows, extended, groups_here, per_group, taps):
    rows = grad_rows.shape[0]
    ext_rows = extended.shape[0]
    corr = jnp.einsum(
        "tgj,ugj->gtu",
        grad_rows.reshape(rows, groups_here, per_group),
        extended.reshape(ext_rows, groups_here, per_group),
        precision=lax.Precision.HIGHEST,
    )
    flat = jnp.concatenate(
        [corr.reshape(groups_here, rows * ext_rows), jnp.zeros((groups_here, rows), jnp.float32)], 1
    )
    diagonal = flat.reshape(groups_here, rows, ext_rows + 1)[:, :, :taps]
    return jnp.sum(diagonal, axis=1)[:, ::-1]


def fetch_out(out_weight):
    return lax.all_gather(out_weight, "fsdp", axis=1, tiled=True)


def on_device(tokens, in_values, in_scales, filters, out_weight, cotangent):
    rows = tokens.shape[0]
    channels = tokens.shape[1]
    groups_here, taps = filters.shape
    per_group = channels // groups_here
    whole = lax.all_gather(tokens, "tensor", axis=1, tiled=True)
    values, scales = (
        lax.all_gather(in_values, "fsdp", axis=0, tiled=True),
        lax.all_gather(in_scales, "fsdp", axis=0, tiled=True),
    )
    weight = dequantize(values, scales)
    proj = (
        jnp.dot(whole, weight, preferred_element_type=jnp.float32)
        .astype(jnp.bfloat16)
        .reshape(rows, 3, channels)
    )
    query = proj[:, 0].astype(jnp.float32)
    key_part = proj[:, 1].astype(jnp.float32)
    value_part = proj[:, 2].astype(jnp.float32)
    product = key_part * value_part
    earlier = passed_along(product[rows - (taps - 1) :].astype(jnp.bfloat16), "fsdp", 1).astype(
        jnp.float32
    )
    extended = jnp.concatenate([earlier, product], 0)
    conv = apply_taps(filters, extended, rows, per_group, True)
    out_full = fetch_out(out_weight)
    cot_whole = lax.all_gather(cotangent, "tensor", axis=1, tiled=True)
    grad_z = lax.dot_general(
        cot_whole, out_full, (((1,), (1,)), ((), ())), preferred_element_type=jnp.float32
    )
    grad_query = grad_z * conv
    grad_conv = grad_z * query
    following = passed_along(grad_conv[: taps - 1].astype(jnp.bfloat16), "fsdp", -1).astype(
        jnp.float32
    )
    grad_ext = jnp.concatenate([grad_conv, following], 0)
    grad_product = apply_taps(filters, grad_ext, rows, per_group, False)
    grad_proj = jnp.stack([grad_query, grad_product * value_part, grad_product * key_part], axis=1)
    grad_proj = grad_proj.astype(jnp.bfloat16).reshape(rows, 3 * channels)
    summed = lax.psum_scatter(
        lax.dot_general(
            weight, grad_proj, (((1,), (1,)), ((), ())), preferred_element_type=jnp.float32
        ),
        "tensor",
        scatter_dimension=0,
        tiled=True,
    )
    input_grad = summed.T.astype(jnp.bfloat16)
    local_filter = filter_terms(grad_conv, extended, groups_here, per_group, taps) / rows
    filter_grad = lax.psum(local_filter, "fsdp")
    return (input_grad, filter_grad)


def solution(mesh):
    placed = (
        P("fsdp", "tensor"),
        P("fsdp", None, "tensor"),
        P("fsdp", None, "tensor"),
        P("tensor", None),
        P("tensor", "fsdp"),
        P("fsdp", "tensor"),
    )
    return jax.shard_map(
        on_device,
        mesh=mesh,
        in_specs=placed,
        out_specs=(P("fsdp", "tensor"), P("tensor", None)),
        check_vma=False,
    )
```

profile of v0, /device:TPU:0, one launch (start us, length us, event | category | flops | bytes accessed | tf_op | source)
XLA Modules:
  0.0 723.2 jit_solution(154292737714200289)
XLA Ops:
  7.2 16.9 %copy.21 = bf16[4096,3,512]{0,2,1:T(8,128)(2,1)} copy(bf16[4096,3,512]{2,0,1:T(8,128)(2,1)} %param.11) | data formatting | bytes 25165824 | tf_op args[1]
  24.2 0.7 all-gather.11.cloned.1.call-update
  25.0 0.7 all-gather.7.cloned.1.call-update
  25.7 0.5 all-gather.9.cloned.1.call-update
  26.3 6.4 all_gather.16
  32.8 0.1 copy.25
  32.9 0.2 copy.22
  33.1 287.7 %all-gather.5.cloned.1.call-done = bf16[8192,3,512]{0,2,1:T(8,128)(2,1)} async-done(((bf16[4096,3,512]{0,2,1:T(8,128)(2,1)}), bf16[8192,3,512]{0,2,1:T(8,128)(2,1)}) %all-gather.5.cloned.1.call-update) | async-done | bytes 25165840 | tf_op jit(solution)/shard_map/all_gather | solution.py:66
  320.8 16.7 %mul.88 = f32[64,128,3,512]{1,0,3,2:T(8,128)} broadcast(f32[64,3,512]{0,2,1:T(8,128)S(1)} %copy.22), dimensions={0,2,3} | broadcast | bytes 50724864 | tf_op jit(solution)/shard_map/mul | solution.py:19
  337.4 43.8 %fusion = bf16[8192,1536]{0,1:T(8,128)(2,1)} fusion(f32[192,8,64,128]{3,2,1,0:T(8,128)} %bitcast.55, bf16[8192,3,512]{0,2,1:T(8,128)(2,1)} %all-gather.5.cloned.1.call-done), kind=kLoop, calls=%fused_computation.5 | loop fusion | flops 37748736 | bytes 100663296 | tf_op jit(solution)/shard_map/convert_element_type | solution.py:22
  381.2 12.2 %convolution_convert_fusion = bf16[1536,128]{1,0:T(8,128)(2,1)S(1)} fusion(bf16[8192,1536]{0,1:T(8,128)(2,1)} %fusion, bf16[128,8192]{1,0:T(8,128)(2,1)} %all-gather.11.cloned.1.call-done), kind=kOutput, calls=%fused_computation.10 | convolution fusion | flops 3221422080 | bytes 27656192 | tf_op jit(solution)/shard_map/dot_general | solution.py:71
  393.4 0.1 copy.34
  393.8 2.2 collective-permute-start
  396.0 10.5 %all-gather.7.cloned.1.call-done = bf16[128,8192]{1,0:T(8,128)(2,1)} async-done(((bf16[128,512]{1,0:T(8,128)(2,1)}), bf16[128,8192]{1,0:T(8,128)(2,1)}) %all-gather.7.cloned.1.call-update) | async-done | bytes 2097168 | tf_op jit(solution)/shard_map/all_gather | solution.py:85
  406.5 104.4 %all-gather.9.cloned.1.call-done = bf16[512,8192]{1,0:T(8,128)(2,1)} async-done(((bf16[512,4096]{1,0:T(8,128)(2,1)}), bf16[512,8192]{1,0:T(8,128)(2,1)}) %all-gather.9.cloned.1.call-update) | async-done | bytes 8388624 | tf_op jit(solution)/shard_map/all_gather | solution.py:56
  510.8 6.9 fusion.16
  518.0 20.3 %while.30 = (s32[]{:T(128)}, f32[128,512]{1,0:T(8,128)S(1)}, f32[512,128]{0,1:T(8,128)S(1)}, f32[255,512]{1,0:T(8,128)S(1)}, s32[]{:T(128)}, /*index=5*/s32[]{:T(128)}, s32[]{:T(128)}, s32[]{:T(128)}) while((s32[]{:T(128)}, f32[128,512]{1,0:T(8,128)S(1)}, f32[512,128]{0,1:T(8,128)S(1)}, f32[255,512]{1,0:T(8,128)S(1)}, s32[]{:T(128)}, ...), condition=%wide.region_1.0_spmd.clone, body=%wide.region_0.0_spmd.clone.sunk | while | flops 196615 | bytes 792733 | solution.py:36
  538.4 1.5 collective-permute-start.1
  539.9 53.6 %mul.89 = f32[8192,3,512]{0,2,1:T(8,128)} reshape(f32[64,128,3,512]{1,0,3,2:T(8,128)} %mul.88) | data formatting | bytes 100663296 | tf_op jit(solution)/shard_map/mul | solution.py:19
  593.5 19.6 %while.31 = (s32[]{:T(128)}, f32[128,512]{1,0:T(8,128)S(1)}, f32[512,128]{0,1:T(8,128)S(1)}, f32[255,512]{1,0:T(8,128)S(1)}, s32[]{:T(128)}, /*index=5*/s32[]{:T(128)}) while((s32[]{:T(128)}, f32[128,512]{1,0:T(8,128)S(1)}, f32[512,128]{0,1:T(8,128)S(1)}, f32[255,512]{1,0:T(8,128)S(1)}, s32[]{:T(128)}, /*index=5*/s32[]{:T(128)}) %tuple.96), condition=%wide.region_3.0_spmd.clone, body=%wide.region_2.0_spmd.clone.sunk | while | flops 196611 | bytes 792671 | solution.py:36
  613.2 27.1 %fusion.3 = f32[8192,128]{1,0:T(8,128)} fusion(f32[8192,3,512]{0,2,1:T(8,128)} %mul.89, bf16[8192,3,512]{0,2,1:T(8,128)(2,1)} %all-gather.5.cloned.1.call-done, bf16[128,1,512]{2,0,1:T(8,128)(2,1)S(1)} %get-tuple-element.259, bf16[128,1,512]{2,0,1:T(8,128)(2,1)S(1)} %get-tuple-element.258, bf16[128,1,512]{2,0,1:T(8,128)(2,1)S(1)} %get-tuple-element.256), kind=kOutput, calls=%fused_computation.9 | convolution fusion | flops 3259367424 | bytes 80084992 | tf_op jit(solution)/shard_map/dot_general | solution.py:99
  640.3 0.1 copy.29
  640.5 0.2 copy.30
  640.7 5.1 fusion.17
  645.7 5.2 reshape.48
  651.0 2.7 concatenate.11
  653.6 1.3 copy.37
  654.9 0.2 slice_reduce_fusion
  655.2 10.0 %psum.7 = f32[32,128]{1,0:T(8,128)} all-reduce(f32[32,128]{1,0:T(8,128)S(1)} %broadcast_multiply_fusion), channel_id=1, replica_groups=mesh['fsdp'=2,'tensor'=16] {'fsdp'}, use_global_device_ids=true, to_apply=%region_6.0 | all-reduce | flops 4096 | bytes 32768 | tf_op jit(solution)/shard_map/psum | solution.py:108
  665.2 49.8 %reduce-scatter.2.cloned.1.call-done = f32[512,128]{1,0:T(8,128)} async-done(((f32[8192,128]{1,0:T(8,128)}), f32[512,128]{1,0:T(8,128)}) %reduce-scatter.2.cloned.1.call-update) | async-done | bytes 262160 | tf_op jit(solution)/shard_map/reduce_scatter | solution.py:98
  714.9 1.0 convert_bitcast_fusion
  715.9 0.8 copy.31
  (543 shorter events, 32.7 us)
Async XLA Ops:
  7.2 313.6 %all-gather.5.cloned.1.call-start = ((), (), s32[]{:S(2)}) async-start(), calls=%async_computation.1 | async-start | bytes 37748736 | tf_op jit(solution)/shard_map/all_gather | solution.py:66
  24.2 2.1 copy-start
  24.2 8.6 %copy-start.1 = (f32[32,128]{1,0:T(8,128)S(1)}, f32[32,128]{1,0:T(8,128)}, u32[]{:S(2)}) copy-start(f32[32,128]{1,0:T(8,128)} %param.13) | copy-start | bytes 49156
  24.2 357.0 %all-gather.11.cloned.1.call-start = ((), (), s32[]{:S(2)}) async-start(), calls=%async_computation.4 | async-start | bytes 2228224 | tf_op jit(solution)/shard_map/all_gather | solution.py:64
  24.9 381.5 %all-gather.7.cloned.1.call-start = ((), (), s32[]{:S(2)}) async-start(), calls=%async_computation.2 | async-start | bytes 2228224 | tf_op jit(solution)/shard_map/all_gather | solution.py:85
  25.7 485.2 %all-gather.9.cloned.1.call-start = ((), (), s32[]{:S(2)}) async-start(), calls=%async_computation.3 | async-start | bytes 12582912 | tf_op jit(solution)/shard_map/all_gather | solution.py:56
  26.3 688.7 %reduce-scatter.2.cloned.1.call-start = ((), (), s32[]{:S(2)}) async-start(), calls=%async_computation.5 | async-start | bytes 4456448 | tf_op jit(solution)/shard_map/reduce_scatter | solution.py:98
  393.8 124.1 %collective-permute-start = (bf16[127,512]{1,0:T(8,128)(2,1)S(1)}, bf16[127,512]{1,0:T(8,128)(2,1)S(1)}, u32[]{:S(2)}, u32[]{:S(2)}) collective-permute-start(bf16[127,512]{1,0:T(8,128)(2,1)S(1)} %slice.36), channel_id=1, source_target_pairs={{0,16},{1,17},{2,18},{3,19},{4,20},{5,21},{6,22},{7,23},{8,24},{9,... | collective-permute-start | bytes 390152 | tf_op jit(solution)/shard_map/ppermute | solution.py:12
  538.4 55.1 %collective-permute-start.1 = (bf16[127,512]{1,0:T(8,128)(2,1)S(1)}, bf16[127,512]{1,0:T(8,128)(2,1)S(1)}, u32[]{:S(2)}, u32[]{:S(2)}) collective-permute-start(bf16[127,512]{1,0:T(8,128)(2,1)S(1)} %slice.35), channel_id=1, source_target_pairs={{16,0},{17,1},{18,2},{19,3},{20,4},{21,5},{22,6},{23,7},{24,8},{25... | collective-permute-start | bytes 390152 | tf_op jit(solution)/shard_map/ppermute | solution.py:12
Sparse Core Ops, SparseCore 0:
  24.3 296.4 all-gather.4
  322.9 41.1 all-gather.10
  366.3 40.1 all-gather.6
  407.9 102.9 all-gather.8
  640.5 74.4 reduce-scatter.1
where the time goes:
time: 725 us; the launch traced here: 723 us
  waiting for transfers between devices  454 us (63%)
  local copies, waits for them, and re-layouts  101 us (14%)
  other arithmetic  74.4 us (10%)
  matrix products  51.3 us (7%)
  blocking collectives  16.4 us (2%)
  between operations  14 us (2%)
  loops' own time  8.08 us (1%)
    all_gather x1, waiting for transfers between devices, on_device(): lax.all_gather(in_values, 'fsdp', axis=0, tiled=True)  288 us
    all_gather x1, waiting for transfers between devices, fetch_out(): return lax.all_gather(out_weight, 'fsdp', axis=1, tiled=True)  104 us
    mul x2, local copies, waits for them, and re-layouts, dequantize(): values.astype(jnp.float32).reshape(blocks, BLOCK, 3, channels)  70.3 us
    reduce_scatter x1, waiting for transfers between devices, on_device(): lax.psum_scatter(lax.dot_general(weight, grad_proj, (((1,), (1,)), ((), (...  49.8 us
    convert_element_type x1, other arithmetic, dequantize(): return scaled.reshape(blocks * BLOCK, 3 * channels).astype(jnp.bfloat16)  43.8 us
    add x256, other arithmetic, one_step(): return total + column[None, :] * slab  29.2 us
    dot_general x1, matrix products, on_device(): lax.dot_general(weight, grad_proj, (((1,), (1,)), ((), ())), preferred_el...  27.1 us
    unnamed x11, local copies, waits for them, and re-layouts  19.5 us
  transfers between devices with their start and end apart: 7, of which 4 were waited for; matrix products, arithmetic and copies ran while one was open for 21% of the time, Pallas kernels for 0%

commit v1 on v0

v1 whole, which is shorter than its diff:
```python
import functools

import jax
import jax.numpy as jnp
from jax import lax
from jax.experimental import pallas as pl
from jax.experimental.pallas import tpu as pltpu
from jax.sharding import PartitionSpec as P

BLOCK = 128
TOK_DEV = 128
BF16 = jnp.bfloat16
F32 = jnp.float32
MIB = 1 << 20


def cost(flops, read):
    return pl.CostEstimate(flops=int(flops), bytes_accessed=int(read), transcendentals=0)


def params(mib):
    return pltpu.CompilerParams(vmem_limit_bytes=mib * MIB)


def dequantized(v_ref, s_ref, part):
    blocks = s_ref.shape[2]
    rows = []
    for b in range(blocks):
        scale = s_ref[part, 0, b : b + 1, :].astype(F32)
        values = v_ref[part, b * BLOCK : (b + 1) * BLOCK, :].astype(F32)
        rows.append((values * scale).astype(BF16))
    return jnp.concatenate(rows, 0) if blocks > 1 else rows[0]


def piece_into(step, refs, held):
    for r, ref in enumerate(refs):

        @pl.when(step == r)
        def _(ref=ref):
            held[...] = ref[...]


def proj_kernel(pieces, runs, place_ref, *refs):
    xs, (v_ref, s_ref, out_ref, held, total) = refs[:pieces], refs[pieces:]
    step = pl.program_id(0)
    piece_into(step, xs, held)
    channels = v_ref.shape[2]
    x = held[...]
    for j in range(3):
        cols = slice(j * channels, (j + 1) * channels)
        term = jnp.dot(x, dequantized(v_ref, s_ref, j), preferred_element_type=F32)

        @pl.when(step == 0)
        def _(term=term, cols=cols):
            total[:, cols] = term

        @pl.when(step > 0)
        def _(term=term, cols=cols):
            total[:, cols] += term

    @pl.when(step == pieces - 1)
    def _():
        run = x.shape[0] // runs
        for h in range(runs):
            at = pl.ds(pl.multiple_of(place_ref[pieces + h], BLOCK), run)
            for j in range(3):
                cols = slice(j * channels, (j + 1) * channels)
                out_ref[j, :, at] = total[h * run : (h + 1) * run, cols].T.astype(BF16)


def proj_partial(xs, place, runs, values, scales):
    pieces = len(xs)
    tokens, rows = xs[0].shape
    channels = values.shape[2]
    blocks = rows // BLOCK
    return pl.pallas_call(
        functools.partial(proj_kernel, pieces, runs),
        grid_spec=pltpu.PrefetchScalarGridSpec(
            num_scalar_prefetch=1,
            grid=(pieces,),
            in_specs=[pl.BlockSpec((tokens, rows), lambda i, p: (0, 0))] * pieces
            + [
                pl.BlockSpec((3, rows, channels), lambda i, p: (0, p[i], 0)),
                pl.BlockSpec((3, 1, blocks, channels), lambda i, p: (0, p[i], 0, 0)),
            ],
            out_specs=pl.BlockSpec((3, channels, tokens), lambda i, p: (0, 0, 0)),
            scratch_shapes=[
                pltpu.VMEM((tokens, rows), BF16),
                pltpu.VMEM((tokens, 3 * channels), F32),
            ],
        ),
        out_shape=jax.ShapeDtypeStruct((3, channels, tokens), BF16),
        compiler_params=params(32),
        cost_estimate=cost(
            2 * tokens * pieces * rows * 3 * channels, 2 * pieces * rows * (3 * channels + tokens)
        ),
        name="proj_partial",
    )(place, *xs, values, scales)


def grad_z_kernel(pieces, runs, place_ref, *refs):
    xs, (w_ref, out_ref, held, total) = refs[:pieces], refs[pieces:]
    step = pl.program_id(0)
    piece_into(step, xs, held)
    term = lax.dot_general(
        w_ref[...], held[...], (((1,), (1,)), ((), ())), preferred_element_type=F32
    )

    @pl.when(step == 0)
    def _():
        total[...] = term

    @pl.when(step > 0)
    def _():
        total[...] += term

    @pl.when(step == pieces - 1)
    def _():
        run = total.shape[1] // runs
        for h in range(runs):
            at = pl.ds(pl.multiple_of(place_ref[pieces + h], BLOCK), run)
            out_ref[:, at] = total[:, h * run : (h + 1) * run].astype(BF16)


def grad_z_partial(xs, place, runs, out_weight):
    pieces = len(xs)
    tokens, rows = xs[0].shape
    channels = out_weight.shape[0]
    return pl.pallas_call(
        functools.partial(grad_z_kernel, pieces, runs),
        grid_spec=pltpu.PrefetchScalarGridSpec(
            num_scalar_prefetch=1,
            grid=(pieces,),
            in_specs=[pl.BlockSpec((tokens, rows), lambda i, p: (0, 0))] * pieces
            + [pl.BlockSpec((channels, rows), lambda i, p: (0, p[i]))],
            out_specs=pl.BlockSpec((channels, tokens), lambda i, p: (0, 0)),
            scratch_shapes=[
                pltpu.VMEM((tokens, rows), BF16),
                pltpu.VMEM((channels, tokens), F32),
            ],
        ),
        out_shape=jax.ShapeDtypeStruct((channels, tokens), BF16),
        compiler_params=params(32),
        cost_estimate=cost(
            2 * tokens * pieces * rows * channels, 2 * pieces * rows * (channels + tokens)
        ),
        name="grad_z_partial",
    )(place, *xs, out_weight)


def iotas():
    shape = (BLOCK, BLOCK)
    return lax.broadcasted_iota(jnp.int32, shape, 0), lax.broadcasted_iota(jnp.int32, shape, 1)


def sheared(array):
    return pltpu.roll(array, 0, 1, stride=1, stride_axis=0)


def toeplitz_kernel(taps_ref, back_ref, past_ref, next_ref):
    row, lane = iotas()
    for g in range(taps_ref.shape[0]):
        ahead = sheared(jnp.broadcast_to(taps_ref[g : g + 1, :], (BLOCK, BLOCK)))
        behind = sheared(jnp.broadcast_to(back_ref[g : g + 1, :], (BLOCK, BLOCK)))
        past_ref[g, :BLOCK] = jnp.where(lane < row, ahead, 0.0).astype(BF16)
        past_ref[g, BLOCK:] = jnp.where(lane >= row, ahead, 0.0).astype(BF16)
        next_ref[g, :BLOCK] = jnp.where(lane <= row, behind, 0.0).astype(BF16)
        next_ref[g, BLOCK:] = jnp.where(lane > row, behind, 0.0).astype(BF16)


def toeplitz(filters):
    groups, taps = filters.shape
    back = jnp.roll(filters[:, ::-1], 1, axis=1)
    step = min(8, groups)
    shape = jax.ShapeDtypeStruct((groups, 2 * BLOCK, taps), BF16)
    return pl.pallas_call(
        toeplitz_kernel,
        grid=(groups // step,),
        in_specs=[pl.BlockSpec((step, taps), lambda i: (i, 0))] * 2,
        out_specs=[pl.BlockSpec((step, 2 * BLOCK, taps), lambda i: (i, 0, 0))] * 2,
        out_shape=[shape, shape],
        cost_estimate=cost(groups * taps * 2000, groups * taps * 1024),
        name="toeplitz",
    )(filters, back)


def block_of(array, i):
    blocks = array.shape[1] // BLOCK
    if 0 <= i < blocks:
        return array[:, i * BLOCK : (i + 1) * BLOCK]
    return jnp.zeros((array.shape[0], BLOCK), array.dtype)


def paired(array, by):
    blocks = array.shape[1] // BLOCK
    low, high = min(by, 0), max(by, 0)
    return jnp.concatenate(
        [
            jnp.concatenate([block_of(array, i + low), block_of(array, i + high)], 1)
            for i in range(blocks)
        ],
        0,
    )


def unstacked(array, blocks):
    rows = array.shape[0] // blocks
    return jnp.concatenate([array[i * rows : (i + 1) * rows] for i in range(blocks)], 1)


def conv_kernel(parts, groups, *refs):
    partials, (past_ref, proj_ref, prod_ref, conv_ref) = refs[:parts], refs[parts:]
    proj = partials[0][...].astype(F32)
    for ref in partials[1:]:
        proj = proj + ref[...].astype(F32)
    proj = proj.astype(BF16)
    proj_ref[...] = proj
    product = (proj[1].astype(F32) * proj[2].astype(F32)).astype(BF16)
    prod_ref[...] = product
    channels, tokens = product.shape
    per = channels // groups
    for g in range(groups):
        rows = slice(g * per, (g + 1) * per)
        result = jnp.dot(paired(product[rows], -1), past_ref[g], preferred_element_type=F32)
        conv_ref[rows] = unstacked(result, tokens // BLOCK)


def conv_forward(partials, past):
    _, channels, tokens = partials[0].shape
    groups = past.shape[0]
    steps = max(1, groups // 8)
    chunk = channels // steps
    parts = len(partials)
    three = pl.BlockSpec((3, chunk, tokens), lambda i: (0, i, 0))
    one = pl.BlockSpec((chunk, tokens), lambda i: (i, 0))
    return pl.pallas_call(
        functools.partial(conv_kernel, parts, groups // steps),
        grid=(steps,),
        in_specs=[three] * parts
        + [pl.BlockSpec((groups // steps,) + past.shape[1:], lambda i: (i, 0, 0))],
        out_specs=[three, one, one],
        out_shape=[
            jax.ShapeDtypeStruct((3, channels, tokens), BF16),
            jax.ShapeDtypeStruct((channels, tokens), BF16),
            jax.ShapeDtypeStruct((channels, tokens), F32),
        ],
        compiler_params=params(32),
        cost_estimate=cost(4 * channels * tokens * BLOCK * 8, channels * tokens * 24),
        name="conv_forward",
    )(*partials, past)


def conv_back_kernel(parts, groups, *refs):
    partials, (proj_ref, conv_ref, next_ref, out_ref, grad_ref) = refs[:parts], refs[parts:]
    grad_z = partials[0][...].astype(F32)
    for ref in partials[1:]:
        grad_z = grad_z + ref[...].astype(F32)
    out_ref[0] = (grad_z * conv_ref[...]).astype(BF16)
    grad = (grad_z * proj_ref[0].astype(F32)).astype(BF16)
    grad_ref[...] = grad
    channels, tokens = grad.shape
    per = channels // groups
    for g in range(groups):
        rows = slice(g * per, (g + 1) * per)
        result = jnp.dot(paired(grad[rows], 1), next_ref[g], preferred_element_type=F32)
        result = unstacked(result, tokens // BLOCK)
        out_ref[1, rows] = (result * proj_ref[2, rows].astype(F32)).astype(BF16)
        out_ref[2, rows] = (result * proj_ref[1, rows].astype(F32)).astype(BF16)


def conv_backward(partials, proj, conv, after):
    channels, tokens = conv.shape
    groups = after.shape[0]
    steps = max(1, groups // 8)
    chunk = channels // steps
    parts = len(partials)
    three = pl.BlockSpec((3, chunk, tokens), lambda i: (0, i, 0))
    one = pl.BlockSpec((chunk, tokens), lambda i: (i, 0))
    return pl.pallas_call(
        functools.partial(conv_back_kernel, parts, groups // steps),
        grid=(steps,),
        in_specs=[one] * parts
        + [
            three,
            one,
            pl.BlockSpec((groups // steps,) + after.shape[1:], lambda i: (i, 0, 0)),
        ],
        out_specs=[three, one],
        out_shape=[
            jax.ShapeDtypeStruct((3, channels, tokens), BF16),
            jax.ShapeDtypeStruct((channels, tokens), BF16),
        ],
        compiler_params=params(32),
        cost_estimate=cost(4 * channels * tokens * BLOCK * 8, channels * tokens * 24),
        name="conv_backward",
    )(*partials, proj, conv, after)


def taps_kernel(groups, prod_ref, grad_ref, out_ref):
    row, lane = iotas()
    flip = (row + lane == BLOCK - 1).astype(F32).astype(BF16)
    channels, tokens = prod_ref.shape
    per = channels // groups
    blocks = tokens // BLOCK
    for g in range(groups):
        rows = slice(g * per, (g + 1) * per)
        earlier = paired(prod_ref[rows, :], -1)
        grad = grad_ref[rows, :]
        later = jnp.concatenate([block_of(grad, i) for i in range(blocks)], 0)
        later = jnp.dot(later, flip, preferred_element_type=F32).astype(BF16)
        both = lax.dot_general(
            earlier, later, (((0,), (0,)), ((), ())), preferred_element_type=F32
        )
        folded = jnp.where(row + lane <= BLOCK - 1, both[BLOCK:], both[:BLOCK])
        out_ref[g : g + 1, :] = jnp.sum(sheared(folded), axis=0, keepdims=True)


def taps_gradient(product, grad, groups):
    channels, tokens = product.shape
    steps = max(1, groups // 8)
    chunk = channels // steps
    one = pl.BlockSpec((chunk, tokens), lambda i: (i, 0))
    backwards = pl.pallas_call(
        functools.partial(taps_kernel, groups // steps),
        grid=(steps,),
        in_specs=[one, one],
        out_specs=pl.BlockSpec((groups // steps, BLOCK), lambda i: (i, 0)),
        out_shape=jax.ShapeDtypeStruct((groups, BLOCK), F32),
        compiler_params=params(32),
        cost_estimate=cost(4 * channels * tokens * BLOCK * 8, channels * tokens * 24),
        name="taps_gradient",
    )(product, grad)
    return backwards[:, ::-1] / TOK_DEV


def input_kernel(place_ref, v_ref, s_ref, g_ref, out_ref):
    total = None
    for j in range(3):
        term = jnp.dot(dequantized(v_ref, s_ref, j), g_ref[j], preferred_element_type=F32)
        total = term if total is None else total + term
    out_ref[0] = total.astype(BF16)


def input_partial(place, pieces, rows, values, scales, grad_proj):
    _, channels, tokens = grad_proj.shape
    blocks = rows // BLOCK
    return pl.pallas_call(
        input_kernel,
        grid_spec=pltpu.PrefetchScalarGridSpec(
            num_scalar_prefetch=1,
            grid=(pieces,),
            in_specs=[
                pl.BlockSpec((3, rows, channels), lambda i, p: (0, p[i], 0)),
                pl.BlockSpec((3, 1, blocks, channels), lambda i, p: (0, p[i], 0, 0)),
                pl.BlockSpec((3, channels, tokens), lambda i, p: (0, 0, 0)),
            ],
            out_specs=pl.BlockSpec((1, rows, tokens), lambda i, p: (i, 0, 0)),
        ),
        out_shape=jax.ShapeDtypeStruct((pieces, rows, tokens), BF16),
        compiler_params=params(32),
        cost_estimate=cost(
            2 * tokens * pieces * rows * 3 * channels, 2 * pieces * rows * (3 * channels + tokens)
        ),
        name="input_partial",
    )(place, values, scales, grad_proj)


def across(array, mask):
    return lax.ppermute(array, "tensor", [(i, i ^ mask) for i in range(16)])


def other_row(array):
    return lax.ppermute(array, "fsdp", [(0, 1), (1, 0)])


Z1, Z0, X, CORE = 8, 4, 2, 1
MINE = (0, X, Z0, X + Z0)


def gathered(array, home):
    far = across(array, Z1)
    keep = jnp.where(home, array, far)
    send = jnp.where(home, far, array)
    own = jnp.concatenate([keep, other_row(send)], 0)
    same = [own] + [across(own, mask) for mask in MINE[1:]]
    return same + [across(piece, CORE) for piece in same]


def scattered(same, others, home, y):
    got = across(others, CORE)
    summed = [(same[i].astype(F32) + got[i].astype(F32)).astype(BF16) for i in range(4)]
    total = summed[0].astype(F32)
    for piece, mask in zip(summed[1:], MINE[1:]):
        total = total + across(piece, mask).astype(F32)
    total = total.astype(BF16)
    first, second = total[:, :TOK_DEV], total[:, TOK_DEV:]
    keep = jnp.where(y == 0, first, second)
    far = other_row(jnp.where(y == 0, second, first))
    stay = jnp.where(home, keep, far)
    leave = jnp.where(home, far, keep)
    return (stay.astype(F32) + across(leave, Z1).astype(F32)).astype(BF16).T


def on_small_slice(tokens, values, scales, filters, out_weight, cotangent):
    rows = tokens.shape[1]
    k = lax.axis_index("tensor")
    y = lax.axis_index("fsdp")
    home = (k // Z1) == y
    low = k % Z1
    order = MINE + tuple(mask + CORE for mask in MINE)
    slices = [low ^ mask for mask in order]
    place = jnp.stack(slices + [y * TOK_DEV, (1 - y) * TOK_DEV]).astype(jnp.int32)
    past, after = toeplitz(filters)
    xs = gathered(tokens, home)
    cots = gathered(cotangent, home)
    proj_part = proj_partial(xs, place, 2, values, scales)
    proj, product, conv = conv_forward([proj_part, other_row(proj_part)], past)
    z_part = grad_z_partial(cots, place, 2, out_weight)
    grad_proj, grad = conv_backward([z_part, other_row(z_part)], proj, conv, after)
    others = input_partial(place[4:8], 4, rows, values, scales, grad_proj)
    same = input_partial(place[:4], 4, rows, values, scales, grad_proj)
    input_grad = scattered(same, others, home, y)
    return input_grad, taps_gradient(product, grad, filters.shape[0])


def on_any_slice(tokens, values, scales, filters, out_weight, cotangent):
    count = lax.axis_size("fsdp")
    rows = values.shape[1]
    piece = min(rows, 512)
    pieces = rows // piece
    place = jnp.arange(pieces + 1, dtype=jnp.int32) * (jnp.arange(pieces + 1) < pieces)

    def gather(array):
        whole = lax.all_gather(array, "tensor", axis=1, tiled=True)
        mine = lax.all_to_all(whole, "fsdp", 1, 0, tiled=True)
        return [mine[:, i * piece : (i + 1) * piece] for i in range(pieces)]

    def shares(array):
        every = lax.all_gather(array, "fsdp", axis=0)
        return [every[i] for i in range(count)]

    past, after = toeplitz(filters)
    proj_part = proj_partial(gather(tokens), place, 1, values, scales)
    proj, product, conv = conv_forward(shares(proj_part), past)
    z_part = grad_z_partial(gather(cotangent), place, 1, out_weight)
    grad_proj, grad = conv_backward(shares(z_part), proj, conv, after)
    partial = input_partial(place[:pieces], pieces, piece, values, scales, grad_proj)
    partial = partial.reshape(rows, partial.shape[2]).astype(F32)
    partial = lax.all_to_all(partial, "fsdp", 1, 0, tiled=True)
    summed = lax.psum_scatter(partial, "tensor", scatter_dimension=0, tiled=True)
    return summed.T.astype(BF16), taps_gradient(product, grad, filters.shape[0])


def on_device(tokens, in_values, in_scales, filters, out_weight, cotangent):
    values = jnp.transpose(in_values, (1, 0, 2))
    small = lax.axis_size("fsdp") == 2 and lax.axis_size("tensor") == 16
    piece = tokens.shape[1] if small else min(values.shape[1], 512)
    scales = jnp.transpose(in_scales, (1, 0, 2))
    scales = scales.reshape(3, -1, piece // BLOCK, scales.shape[2])
    inner = on_small_slice if small else on_any_slice
    return inner(tokens, values, scales, filters, out_weight, cotangent)


def solution(mesh):
    placed = (
        P("fsdp", "tensor"),
        P("fsdp", None, "tensor"),
        P("fsdp", None, "tensor"),
        P("tensor", None),
        P("tensor", "fsdp"),
        P("fsdp", "tensor"),
    )
    return jax.shard_map(
        on_device,
        mesh=mesh,
        in_specs=placed,
        out_specs=(P("fsdp", "tensor"), P("tensor", None)),
        check_vma=False,
    )
```

time: 725 us -> 129 us (0.18)
  waiting for transfers between devices: 454 us -> 46.2 us
  local copies, waits for them, and re-layouts: 101 us -> 15 us
  other arithmetic: 74.4 us -> 4.9 us
  matrix products: 51.3 us -> 0 us
  Pallas kernels: 0 us -> 32.9 us
  starting transfers between devices: 3.88 us -> 29.1 us
  blocking collectives: 16.4 us -> 0 us
  between operations: 14 us -> 0.79 us
  loops' own time: 8.08 us -> 0 us
    all_gather x4 -> x0, waiting for transfers between devices: 403 us -> none  [the longest x1 288 us: on_device(): lax.all_gather(in_values, 'fsdp', axis=0, tiled=True)]
    mul x3 -> x0, local copies, waits for them, and re-layouts: 70.4 us -> none  [the longest x2 70.3 us: dequantize(): values.astype(jnp.float32).reshape(blocks, BLOCK, 3, channels)]
    dot_general x4 -> x0, matrix products: 51.3 us -> none  [the longest x1 27.1 us: on_device(): lax.dot_general(weight, grad_proj, (((1,), (1,)), ((), ())), preferred_el...]
    reduce_scatter x1 -> x0, waiting for transfers between devices: 49.8 us -> none  [on_device(): lax.psum_scatter(lax.dot_general(weight, grad_proj, (((1,), (1,)), ((), (...]
    ppermute x2 -> x26, waiting for transfers between devices: 0.01 us -> 46.2 us  [the longest x21 35.8 us: across(): return lax.ppermute(array, 'tensor', [(i, i ^ mask) for i in range(16)])]
    convert_element_type x4 -> x2, other arithmetic: 44.8 us -> 1.45 us  [the longest x1 1.27 us: scattered(): total = total.astype(BF16)]
    pallas_call x0 -> x8, Pallas kernels: none -> 32.9 us  [the longest x1 11 us: proj_partial(): pl.pallas_call(functools.partial(proj_kernel, pieces, runs), grid_spec=pl...]
    add x256 -> x0, other arithmetic: 29.2 us -> none  [one_step(): return total + column[None, :] * slab]
  transfers between devices with their start and end apart: 7 -> 26, of which waited for: 4 -> 16; matrix products, arithmetic and copies ran while one was open for 21% -> 3% of each run, Pallas kernels for 0% -> 22%
where the time goes in v1:
time: 129 us
  waiting for transfers between devices  46.2 us (36%)
  Pallas kernels  32.9 us (26%)
  starting transfers between devices  29.1 us (23%)
  local copies, waits for them, and re-layouts  15 us (12%)
  other arithmetic  4.9 us (4%)
    ppermute x21, waiting for transfers between devices, across(): return lax.ppermute(array, 'tensor', [(i, i ^ mask) for i in range(16)])  35.8 us
    ppermute x21, starting transfers between devices, across(): return lax.ppermute(array, 'tensor', [(i, i ^ mask) for i in range(16)])  22.1 us
    unnamed x13, local copies, waits for them, and re-layouts  13.8 us
    pallas_call x1, Pallas kernels, proj_partial(): pl.pallas_call(functools.partial(proj_kernel, pieces, runs), grid_spec=pl...  11 us
    ppermute x5, waiting for transfers between devices, other_row(): return lax.ppermute(array, 'fsdp', [(0, 1), (1, 0)])  10.4 us
    ppermute x5, starting transfers between devices, other_row(): return lax.ppermute(array, 'fsdp', [(0, 1), (1, 0)])  6.96 us
    pallas_call x2, Pallas kernels, input_partial(): pl.pallas_call(input_kernel, grid_spec=pltpu.PrefetchScalarGridSpec(num_s...  6.87 us
    pallas_call x1, Pallas kernels, grad_z_partial(): pl.pallas_call(functools.partial(grad_z_kernel, pieces, runs), grid_spec=...  5.41 us
  transfers between devices with their start and end apart: 26, of which 16 were waited for; matrix products, arithmetic and copies ran while one was open for 3% of the time, Pallas kernels for 22%

profile of v1, /device:TPU:0, one launch (start us, length us, event | category | flops | bytes accessed | tf_op | source)
XLA Modules:
  0.0 128.9 jit_solution(5966219337052531199)
XLA Ops:
  0.6 4.1 %collective-permute-start.10 = (bf16[128,512]{1,0:T(8,128)(2,1)}, bf16[128,512]{1,0:T(8,128)(2,1)S(1)}, u32[]{:S(2)}, u32[]{:S(2)}) collective-permute-start(bf16[128,512]{1,0:T(8,128)(2,1)} %param.6), channel_id=1, source_target_pairs={{0,8},{1,9},{2,10},{3,11},{4,12},{5,13},{6,14},{7,15},{8,0},{9,1},... | collective-permute-start | bytes 393224 | tf_op jit(solution)/shard_map/ppermute | solution.py:369
  4.7 6.5 %collective-permute-done.10 = bf16[128,512]{1,0:T(8,128)(2,1)S(1)} collective-permute-done((bf16[128,512]{1,0:T(8,128)(2,1)}, bf16[128,512]{1,0:T(8,128)(2,1)S(1)}, u32[]{:S(2)}, u32[]{:S(2)}) %collective-permute-start.10) | collective-permute-done | bytes 131104 | tf_op jit(solution)/shard_map/ppermute | solution.py:369
  12.2 1.6 %collective-permute-start.11 = (bf16[128,512]{1,0:T(8,128)(2,1)S(1)}, bf16[128,512]{1,0:T(8,128)(2,1)S(1)}, u32[]{:S(2)}, u32[]{:S(2)}) collective-permute-start(bf16[128,512]{1,0:T(8,128)(2,1)S(1)} %get-tuple-element.22), channel_id=1, source_target_pairs={{0,16},{16,0},{1,17},{17,1},{2,18},{18,2},{3,19},{19,3},{4,20},{20... | collective-permute-start | bytes 393224 | tf_op jit(solution)/shard_map/ppermute | solution.py:373
  13.8 3.4 %collective-permute-done.11 = bf16[128,512]{1,0:T(8,128)(2,1)S(1)} collective-permute-done((bf16[128,512]{1,0:T(8,128)(2,1)S(1)}, bf16[128,512]{1,0:T(8,128)(2,1)S(1)}, u32[]{:S(2)}, u32[]{:S(2)}) %collective-permute-start.11) | collective-permute-done | bytes 131104 | tf_op jit(solution)/shard_map/ppermute | solution.py:373
  17.2 1.6 %collective-permute-start.12 = (bf16[256,512]{1,0:T(8,128)(2,1)S(1)}, bf16[256,512]{1,0:T(8,128)(2,1)S(1)}, u32[]{:S(2)}, u32[]{:S(2)}) collective-permute-start(bf16[256,512]{1,0:T(8,128)(2,1)S(1)} %pad_maximum_fusion.1.refs_0_), channel_id=1, source_target_pairs={{0,2},{1,3},{2,0},{3,1},{4,6},{5,7},{6,4},{7,5},{8,10},{9,11},{10,... | collective-permute-start | bytes 786440 | tf_op jit(solution)/shard_map/ppermute | solution.py:369
  20.8 2.6 %collective-permute-start = (bf16[128,512]{1,0:T(8,128)(2,1)}, bf16[128,512]{1,0:T(8,128)(2,1)S(1)}, u32[]{:S(2)}, u32[]{:S(2)}) collective-permute-start(bf16[128,512]{1,0:T(8,128)(2,1)} %param.11), channel_id=1, source_target_pairs={{0,8},{1,9},{2,10},{3,11},{4,12},{5,13},{6,14},{7,15},{8,0},{9,1},... | collective-permute-start | bytes 393224 | tf_op jit(solution)/shard_map/ppermute | solution.py:369
  24.3 6.6 %collective-permute-done.13.refs_2_ = bf16[256,512]{1,0:T(8,128)(2,1)S(1)} collective-permute-done((bf16[256,512]{1,0:T(8,128)(2,1)S(1)}, bf16[256,512]{1,0:T(8,128)(2,1)S(1)}, u32[]{:S(2)}, u32[]{:S(2)}) %collective-permute-start.13) | collective-permute-done | bytes 262176 | tf_op jit(solution)/shard_map/ppermute | solution.py:369
  30.9 2.9 %collective-permute-done.14.refs_3_ = bf16[256,512]{1,0:T(8,128)(2,1)S(1)} collective-permute-done((bf16[256,512]{1,0:T(8,128)(2,1)S(1)}, bf16[256,512]{1,0:T(8,128)(2,1)S(1)}, u32[]{:S(2)}, u32[]{:S(2)}) %collective-permute-start.14) | collective-permute-done | bytes 262176 | tf_op jit(solution)/shard_map/ppermute | solution.py:369
  34.8 1.6 %collective-permute-start.1 = (bf16[128,512]{1,0:T(8,128)(2,1)S(1)}, bf16[128,512]{1,0:T(8,128)(2,1)S(1)}, u32[]{:S(2)}, u32[]{:S(2)}) collective-permute-start(bf16[128,512]{1,0:T(8,128)(2,1)S(1)} %get-tuple-element.24), channel_id=1, source_target_pairs={{0,16},{16,0},{1,17},{17,1},{2,18},{18,2},{3,19},{19,3},{4,20},{20... | collective-permute-start | bytes 393224 | tf_op jit(solution)/shard_map/ppermute | solution.py:373
  37.4 3.4 %collective-permute-done.1 = bf16[128,512]{1,0:T(8,128)(2,1)S(1)} collective-permute-done((bf16[128,512]{1,0:T(8,128)(2,1)S(1)}, bf16[128,512]{1,0:T(8,128)(2,1)S(1)}, u32[]{:S(2)}, u32[]{:S(2)}) %collective-permute-start.1) | collective-permute-done | bytes 131104 | tf_op jit(solution)/shard_map/ppermute | solution.py:373
  40.8 1.6 %collective-permute-start.2 = (bf16[256,512]{1,0:T(8,128)(2,1)S(1)}, bf16[256,512]{1,0:T(8,128)(2,1)S(1)}, u32[]{:S(2)}, u32[]{:S(2)}) collective-permute-start(bf16[256,512]{1,0:T(8,128)(2,1)S(1)} %pad_maximum_fusion.refs_0_), channel_id=1, source_target_pairs={{0,2},{1,3},{2,0},{3,1},{4,6},{5,7},{6,4},{7,5},{8,10},{9,11},{10,... | collective-permute-start | bytes 786440 | tf_op jit(solution)/shard_map/ppermute | solution.py:369
  42.3 1.4 %collective-permute-start.3 = (bf16[256,512]{1,0:T(8,128)(2,1)S(1)}, bf16[256,512]{1,0:T(8,128)(2,1)}, u32[]{:S(2)}, u32[]{:S(2)}) collective-permute-start(bf16[256,512]{1,0:T(8,128)(2,1)S(1)} %pad_maximum_fusion.refs_0_), channel_id=1, source_target_pairs={{0,4},{1,5},{2,6},{3,7},{4,0},{5,1},{6,2},{7,3},{8,12},{9,13},{10,... | collective-permute-start | bytes 786440 | tf_op jit(solution)/shard_map/ppermute | solution.py:369
  44.7 4.6 %copy-done = bf16[4096,3,512]{2,0,1:T(8,128)(2,1)S(1)} copy-done((bf16[4096,3,512]{2,0,1:T(8,128)(2,1)S(1)}, bf16[4096,3,512]{2,0,1:T(8,128)(2,1)}, u32[]{:S(2)}) %copy-start) | copy-done | bytes 12582936
  49.3 11.0 %proj_partial.1.refs_0_ = bf16[3,512,256]{2,1,0:T(8,128)(2,1)S(1)} custom-call(s32[10]{0:T(128)S(1)} %stack.48.place_ref, bf16[256,512]{1,0:T(8,128)(2,1)S(1)} %pad_maximum_fusion.1.refs_0_, bf16[256,512]{1,0:T(8,128)(2,1)S(1)} %collective-permute-done.12.refs_1_, bf16[256,512]{1,0:T(8,128)(2,1)S(1)} %collective-permute-done.13.refs_2_, ...), custom_call_target="tpu_custom_call" | custom-call | flops 3221225472 | bytes 14680064 | tf_op jit(solution)/shard_map/proj_partial/pallas_call | solution.py:76
  60.3 1.6 %collective-permute-start.19 = (bf16[3,512,256]{2,1,0:T(8,128)(2,1)S(1)}, bf16[3,512,256]{2,1,0:T(8,128)(2,1)S(1)}, u32[]{:S(2)}, u32[]{:S(2)}) collective-permute-start(bf16[3,512,256]{2,1,0:T(8,128)(2,1)S(1)} %proj_partial.1.refs_0_), channel_id=1, source_target_pairs={{0,16},{16,0},{1,17},{17,1},{2,18},{18,2},{3,19},{19,3},{4,20},{20... | collective-permute-start | bytes 2359304 | tf_op jit(solution)/shard_map/ppermute | solution.py:373
  64.8 2.2 %copy-done.2 = bf16[512,4096]{1,0:T(8,128)(2,1)S(1)} copy-done((bf16[512,4096]{1,0:T(8,128)(2,1)S(1)}, bf16[512,4096]{1,0:T(8,128)(2,1)}, u32[]{:S(2)}) %copy-start.2) | copy-done | bytes 4194328
  67.0 5.4 %grad_z_partial.1.refs_0_ = bf16[512,256]{1,0:T(8,128)(2,1)S(1)} custom-call(s32[10]{0:T(128)S(1)} %stack.48.place_ref, bf16[256,512]{1,0:T(8,128)(2,1)S(1)} %pad_maximum_fusion.refs_0_, bf16[256,512]{1,0:T(8,128)(2,1)S(1)} %collective-permute-done.2.refs_1_, bf16[256,512]{1,0:T(8,128)(2,1)} %collective-permute-done.3.refs_2_, ...), custom_call_target="tpu_custom_call" | custom-call | flops 1073741824 | bytes 6291456 | tf_op jit(solution)/shard_map/grad_z_partial/pallas_call | solution.py:129
  73.6 3.9 %toeplitz.1 = (bf16[32,256,128]{2,1,0:T(8,128)(2,1)}, bf16[32,256,128]{2,1,0:T(8,128)(2,1)}) custom-call(f32[32,128]{1,0:T(8,128)} %taps_ref.1, f32[32,128]{1,0:T(8,128)} %pad_maximum_fusion.2.back_ref), custom_call_target="tpu_custom_call" | custom-call | flops 8192000 | bytes 4194304 | tf_op jit(solution)/shard_map/toeplitz/pallas_call | solution.py:176
  77.7 3.2 %collective-permute-done.19.refs_1_ = bf16[3,512,256]{2,1,0:T(8,128)(2,1)S(1)} collective-permute-done((bf16[3,512,256]{2,1,0:T(8,128)(2,1)S(1)}, bf16[3,512,256]{2,1,0:T(8,128)(2,1)S(1)}, u32[]{:S(2)}, u32[]{:S(2)}) %collective-permute-start.19) | collective-permute-done | bytes 786464 | tf_op jit(solution)/shard_map/ppermute | solution.py:373
  80.9 1.6 %copy-done.3 = bf16[32,256,128]{2,1,0:T(8,128)(2,1)S(1)} copy-done((bf16[32,256,128]{2,1,0:T(8,128)(2,1)S(1)}, bf16[32,256,128]{2,1,0:T(8,128)(2,1)}, u32[]{:S(2)}) %copy-start.3) | copy-done | bytes 2097176
  85.0 4.6 %copy-done.1 = bf16[4096,3,512]{2,0,1:T(8,128)(2,1)S(1)} copy-done((bf16[4096,3,512]{2,0,1:T(8,128)(2,1)S(1)}, bf16[4096,3,512]{2,0,1:T(8,128)(2,1)}, u32[]{:S(2)}) %copy-start.1) | copy-done | bytes 12582936
  89.6 3.4 %input_partial.3 = bf16[4,512,256]{2,1,0:T(8,128)(2,1)S(1)} custom-call(s32[4]{0:T(128)S(1)} %pad_add_fusion.1.place_ref, bf16[3,4096,512]{2,1,0:T(8,128)(2,1)S(1)} %bitcast.27, bf16[3,8,4,512]{3,2,1,0:T(4,128)(2,1)S(1)} %reshape.25.refs_9_.s_ref, bf16[3,512,256]{2,1,0:T(8,128)(2,1)S(1)} %get-tuple-element.13.g_ref), custom_call_target="tpu_custom_call" | custom-call | flops 1610612736 | bytes 7340032 | tf_op jit(solution)/shard_map/input_partial/pallas_call | solution.py:347
  93.2 3.4 %input_partial.2 = bf16[4,512,256]{2,1,0:T(8,128)(2,1)S(1)} custom-call(s32[4]{0:T(128)S(1)} %pad_add_fusion.place_ref, bf16[3,4096,512]{2,1,0:T(8,128)(2,1)S(1)} %bitcast.28, bf16[3,8,4,512]{3,2,1,0:T(4,128)(2,1)S(1)} %reshape.25.refs_9_.s_ref, bf16[3,512,256]{2,1,0:T(8,128)(2,1)S(1)} %get-tuple-element.13.g_ref), custom_call_target="tpu_custom_call" | custom-call | flops 1610612736 | bytes 7340032 | tf_op jit(solution)/shard_map/input_partial/pallas_call | solution.py:347
  96.9 1.4 %collective-permute-start.21 = (bf16[512,256]{1,0:T(8,128)(2,1)S(1)}, bf16[512,256]{1,0:T(8,128)(2,1)}, u32[]{:S(2)}, u32[]{:S(2)}) collective-permute-start(bf16[512,256]{1,0:T(8,128)(2,1)S(1)} %get-tuple-element.18), channel_id=1, source_target_pairs={{0,2},{1,3},{2,0},{3,1},{4,6},{5,7},{6,4},{7,5},{8,10},{9,11},{10,... | collective-permute-start | bytes 786440 | tf_op jit(solution)/shard_map/ppermute | solution.py:369
  98.7 1.8 %collective-permute-start.23 = (bf16[512,256]{1,0:T(8,128)(2,1)S(1)}, bf16[512,256]{1,0:T(8,128)(2,1)}, u32[]{:S(2)}, u32[]{:S(2)}) collective-permute-start(bf16[512,256]{1,0:T(8,128)(2,1)S(1)} %get-tuple-element.19), channel_id=1, source_target_pairs={{0,6},{1,7},{2,4},{3,5},{4,2},{5,3},{6,0},{7,1},{8,14},{9,15},{10,... | collective-permute-start | bytes 786440 | tf_op jit(solution)/shard_map/ppermute | solution.py:369
  100.4 5.3 %collective-permute-done.21 = bf16[512,256]{1,0:T(8,128)(2,1)} collective-permute-done((bf16[512,256]{1,0:T(8,128)(2,1)S(1)}, bf16[512,256]{1,0:T(8,128)(2,1)}, u32[]{:S(2)}, u32[]{:S(2)}) %collective-permute-start.21) | collective-permute-done | bytes 262176 | tf_op jit(solution)/shard_map/ppermute | solution.py:369
  105.7 1.8 %collective-permute-done.22 = bf16[512,256]{1,0:T(8,128)(2,1)} collective-permute-done((bf16[512,256]{1,0:T(8,128)(2,1)S(1)}, bf16[512,256]{1,0:T(8,128)(2,1)}, u32[]{:S(2)}, u32[]{:S(2)}) %collective-permute-start.22) | collective-permute-done | bytes 262176 | tf_op jit(solution)/shard_map/ppermute | solution.py:369
  107.5 5.0 %collective-permute-done.23 = bf16[512,256]{1,0:T(8,128)(2,1)} collective-permute-done((bf16[512,256]{1,0:T(8,128)(2,1)S(1)}, bf16[512,256]{1,0:T(8,128)(2,1)}, u32[]{:S(2)}, u32[]{:S(2)}) %collective-permute-start.23) | collective-permute-done | bytes 262176 | tf_op jit(solution)/shard_map/ppermute | solution.py:369
  113.8 1.6 %collective-permute-start.24 = (bf16[512,128]{1,0:T(8,128)(2,1)S(1)}, bf16[512,128]{1,0:T(8,128)(2,1)S(1)}, u32[]{:S(2)}, u32[]{:S(2)}) collective-permute-start(bf16[512,128]{1,0:T(8,128)(2,1)S(1)} %broadcast_select_fusion.4), channel_id=1, source_target_pairs={{0,16},{16,0},{1,17},{17,1},{2,18},{18,2},{3,19},{19,3},{4,20},{20... | collective-permute-start | bytes 393224 | tf_op jit(solution)/shard_map/ppermute | solution.py:373
  115.4 3.6 %taps_gradient.1 = f32[32,128]{1,0:T(8,128)S(1)} custom-call(bf16[512,256]{1,0:T(8,128)(2,1)S(1)} %get-tuple-element.14.prod_ref, bf16[512,256]{1,0:T(8,128)(2,1)S(1)} %get-tuple-element.15.grad_ref), custom_call_target="tpu_custom_call" | custom-call | flops 536870912 | bytes 3145728 | tf_op jit(solution)/shard_map/taps_gradient/pallas_call | solution.py:323
  119.2 3.3 %collective-permute-start.25 = (bf16[512,128]{1,0:T(8,128)(2,1)S(1)}, bf16[512,128]{1,0:T(8,128)(2,1)S(1)}, u32[]{:S(2)}, u32[]{:S(2)}) collective-permute-start(bf16[512,128]{1,0:T(8,128)(2,1)S(1)} %broadcast_select_fusion.6), channel_id=1, source_target_pairs={{0,8},{1,9},{2,10},{3,11},{4,12},{5,13},{6,14},{7,15},{8,0},{9,1},... | collective-permute-start | bytes 393224 | tf_op jit(solution)/shard_map/ppermute | solution.py:369
  123.1 5.0 %collective-permute-done.25 = bf16[512,128]{1,0:T(8,128)(2,1)S(1)} collective-permute-done((bf16[512,128]{1,0:T(8,128)(2,1)S(1)}, bf16[512,128]{1,0:T(8,128)(2,1)S(1)}, u32[]{:S(2)}, u32[]{:S(2)}) %collective-permute-start.25) | collective-permute-done | bytes 131104 | tf_op jit(solution)/shard_map/ppermute | solution.py:369
  (59 shorter events, 17.1 us)
Async XLA Ops:
  0.6 10.6 %collective-permute-start.10 = (bf16[128,512]{1,0:T(8,128)(2,1)}, bf16[128,512]{1,0:T(8,128)(2,1)S(1)}, u32[]{:S(2)}, u32[]{:S(2)}) collective-permute-start(bf16[128,512]{1,0:T(8,128)(2,1)} %param.6), channel_id=1, source_target_pairs={{0,8},{1,9},{2,10},{3,11},{4,12},{5,13},{6,14},{7,15},{8,0},{9,1},... | collective-permute-start | bytes 393224 | tf_op jit(solution)/shard_map/ppermute | solution.py:369
  12.2 5.0 %collective-permute-start.11 = (bf16[128,512]{1,0:T(8,128)(2,1)S(1)}, bf16[128,512]{1,0:T(8,128)(2,1)S(1)}, u32[]{:S(2)}, u32[]{:S(2)}) collective-permute-start(bf16[128,512]{1,0:T(8,128)(2,1)S(1)} %get-tuple-element.22), channel_id=1, source_target_pairs={{0,16},{16,0},{1,17},{17,1},{2,18},{18,2},{3,19},{19,3},{4,20},{20... | collective-permute-start | bytes 393224 | tf_op jit(solution)/shard_map/ppermute | solution.py:373
  17.2 7.1 %collective-permute-start.12 = (bf16[256,512]{1,0:T(8,128)(2,1)S(1)}, bf16[256,512]{1,0:T(8,128)(2,1)S(1)}, u32[]{:S(2)}, u32[]{:S(2)}) collective-permute-start(bf16[256,512]{1,0:T(8,128)(2,1)S(1)} %pad_maximum_fusion.1.refs_0_), channel_id=1, source_target_pairs={{0,2},{1,3},{2,0},{3,1},{4,6},{5,7},{6,4},{7,5},{8,10},{9,11},{10,... | collective-permute-start | bytes 786440 | tf_op jit(solution)/shard_map/ppermute | solution.py:369
  18.8 12.1 %collective-permute-start.13 = (bf16[256,512]{1,0:T(8,128)(2,1)S(1)}, bf16[256,512]{1,0:T(8,128)(2,1)S(1)}, u32[]{:S(2)}, u32[]{:S(2)}) collective-permute-start(bf16[256,512]{1,0:T(8,128)(2,1)S(1)} %pad_maximum_fusion.1.refs_0_), channel_id=1, source_target_pairs={{0,4},{1,5},{2,6},{3,7},{4,0},{5,1},{6,2},{7,3},{8,12},{9,13},{10,... | collective-permute-start | bytes 786440 | tf_op jit(solution)/shard_map/ppermute | solution.py:369
  20.1 13.8 %collective-permute-start.14 = (bf16[256,512]{1,0:T(8,128)(2,1)S(1)}, bf16[256,512]{1,0:T(8,128)(2,1)S(1)}, u32[]{:S(2)}, u32[]{:S(2)}) collective-permute-start(bf16[256,512]{1,0:T(8,128)(2,1)S(1)} %pad_maximum_fusion.1.refs_0_), channel_id=1, source_target_pairs={{0,6},{1,7},{2,4},{3,5},{4,2},{5,3},{6,0},{7,1},{8,14},{9,15},{10,... | collective-permute-start | bytes 786440 | tf_op jit(solution)/shard_map/ppermute | solution.py:369
  20.8 13.0 %collective-permute-start = (bf16[128,512]{1,0:T(8,128)(2,1)}, bf16[128,512]{1,0:T(8,128)(2,1)S(1)}, u32[]{:S(2)}, u32[]{:S(2)}) collective-permute-start(bf16[128,512]{1,0:T(8,128)(2,1)} %param.11), channel_id=1, source_target_pairs={{0,8},{1,9},{2,10},{3,11},{4,12},{5,13},{6,14},{7,15},{8,0},{9,1},... | collective-permute-start | bytes 393224 | tf_op jit(solution)/shard_map/ppermute | solution.py:369
  23.3 19.0 %collective-permute-start.15 = (bf16[256,512]{1,0:T(8,128)(2,1)S(1)}, bf16[256,512]{1,0:T(8,128)(2,1)S(1)}, u32[]{:S(2)}, u32[]{:S(2)}) collective-permute-start(bf16[256,512]{1,0:T(8,128)(2,1)S(1)} %pad_maximum_fusion.1.refs_0_), channel_id=1, source_target_pairs={{0,1},{1,0},{2,3},{3,2},{4,5},{5,4},{6,7},{7,6},{8,9},{9,8},{10,11... | collective-permute-start | bytes 786440 | tf_op jit(solution)/shard_map/ppermute | solution.py:369
  24.3 19.4 %collective-permute-start.16 = (bf16[256,512]{1,0:T(8,128)(2,1)S(1)}, bf16[256,512]{1,0:T(8,128)(2,1)S(1)}, u32[]{:S(2)}, u32[]{:S(2)}) collective-permute-start(bf16[256,512]{1,0:T(8,128)(2,1)S(1)} %collective-permute-done.12.refs_1_), channel_id=1, source_target_pairs={{0,1},{1,0},{2,3},{3,2},{4,5},{5,4},{6,7},{7,6},{8,9},{9,8},{10,11... | collective-permute-start | bytes 786440 | tf_op jit(solution)/shard_map/ppermute | solution.py:369
  30.9 13.8 %collective-permute-start.17 = (bf16[256,512]{1,0:T(8,128)(2,1)S(1)}, bf16[256,512]{1,0:T(8,128)(2,1)S(1)}, u32[]{:S(2)}, u32[]{:S(2)}) collective-permute-start(bf16[256,512]{1,0:T(8,128)(2,1)S(1)} %collective-permute-done.13.refs_2_), channel_id=1, source_target_pairs={{0,1},{1,0},{2,3},{3,2},{4,5},{5,4},{6,7},{7,6},{8,9},{9,8},{10,11... | collective-permute-start | bytes 786440 | tf_op jit(solution)/shard_map/ppermute | solution.py:369
  33.8 10.9 %collective-permute-start.18 = (bf16[256,512]{1,0:T(8,128)(2,1)S(1)}, bf16[256,512]{1,0:T(8,128)(2,1)S(1)}, u32[]{:S(2)}, u32[]{:S(2)}) collective-permute-start(bf16[256,512]{1,0:T(8,128)(2,1)S(1)} %collective-permute-done.14.refs_3_), channel_id=1, source_target_pairs={{0,1},{1,0},{2,3},{3,2},{4,5},{5,4},{6,7},{7,6},{8,9},{9,8},{10,11... | collective-permute-start | bytes 786440 | tf_op jit(solution)/shard_map/ppermute | solution.py:369
  34.8 6.0 %collective-permute-start.1 = (bf16[128,512]{1,0:T(8,128)(2,1)S(1)}, bf16[128,512]{1,0:T(8,128)(2,1)S(1)}, u32[]{:S(2)}, u32[]{:S(2)}) collective-permute-start(bf16[128,512]{1,0:T(8,128)(2,1)S(1)} %get-tuple-element.24), channel_id=1, source_target_pairs={{0,16},{16,0},{1,17},{17,1},{2,18},{18,2},{3,19},{19,3},{4,20},{20... | collective-permute-start | bytes 393224 | tf_op jit(solution)/shard_map/ppermute | solution.py:373
  40.8 21.2 %collective-permute-start.2 = (bf16[256,512]{1,0:T(8,128)(2,1)S(1)}, bf16[256,512]{1,0:T(8,128)(2,1)S(1)}, u32[]{:S(2)}, u32[]{:S(2)}) collective-permute-start(bf16[256,512]{1,0:T(8,128)(2,1)S(1)} %pad_maximum_fusion.refs_0_), channel_id=1, source_target_pairs={{0,2},{1,3},{2,0},{3,1},{4,6},{5,7},{6,4},{7,5},{8,10},{9,11},{10,... | collective-permute-start | bytes 786440 | tf_op jit(solution)/shard_map/ppermute | solution.py:369
  42.3 20.1 %collective-permute-start.3 = (bf16[256,512]{1,0:T(8,128)(2,1)S(1)}, bf16[256,512]{1,0:T(8,128)(2,1)}, u32[]{:S(2)}, u32[]{:S(2)}) collective-permute-start(bf16[256,512]{1,0:T(8,128)(2,1)S(1)} %pad_maximum_fusion.refs_0_), channel_id=1, source_target_pairs={{0,4},{1,5},{2,6},{3,7},{4,0},{5,1},{6,2},{7,3},{8,12},{9,13},{10,... | collective-permute-start | bytes 786440 | tf_op jit(solution)/shard_map/ppermute | solution.py:369
  43.7 18.8 %collective-permute-start.4 = (bf16[256,512]{1,0:T(8,128)(2,1)S(1)}, bf16[256,512]{1,0:T(8,128)(2,1)}, u32[]{:S(2)}, u32[]{:S(2)}) collective-permute-start(bf16[256,512]{1,0:T(8,128)(2,1)S(1)} %pad_maximum_fusion.refs_0_), channel_id=1, source_target_pairs={{0,6},{1,7},{2,4},{3,5},{4,2},{5,3},{6,0},{7,1},{8,14},{9,15},{10,... | collective-permute-start | bytes 786440 | tf_op jit(solution)/shard_map/ppermute | solution.py:369
  44.7 4.6 %copy-start = (bf16[4096,3,512]{2,0,1:T(8,128)(2,1)S(1)}, bf16[4096,3,512]{2,0,1:T(8,128)(2,1)}, u32[]{:S(2)}) copy-start(bf16[4096,3,512]{2,0,1:T(8,128)(2,1)} %param.7) | copy-start | bytes 37748740
  49.3 13.6 %copy-start.5 = (f32[32,128]{1,0:T(8,128)S(1)}, f32[32,128]{1,0:T(8,128)}, u32[]{:S(2)}) copy-start(f32[32,128]{1,0:T(8,128)} %taps_ref.1) | copy-start | bytes 49156
  60.3 20.5 %collective-permute-start.19 = (bf16[3,512,256]{2,1,0:T(8,128)(2,1)S(1)}, bf16[3,512,256]{2,1,0:T(8,128)(2,1)S(1)}, u32[]{:S(2)}, u32[]{:S(2)}) collective-permute-start(bf16[3,512,256]{2,1,0:T(8,128)(2,1)S(1)} %proj_partial.1.refs_0_), channel_id=1, source_target_pairs={{0,16},{16,0},{1,17},{17,1},{2,18},{18,2},{3,19},{19,3},{4,20},{20... | collective-permute-start | bytes 2359304 | tf_op jit(solution)/shard_map/ppermute | solution.py:373
  61.9 1.5 %collective-permute-start.5 = (bf16[256,512]{1,0:T(8,128)(2,1)S(1)}, bf16[256,512]{1,0:T(8,128)(2,1)S(1)}, u32[]{:S(2)}, u32[]{:S(2)}) collective-permute-start(bf16[256,512]{1,0:T(8,128)(2,1)S(1)} %pad_maximum_fusion.refs_0_), channel_id=1, source_target_pairs={{0,1},{1,0},{2,3},{3,2},{4,5},{5,4},{6,7},{7,6},{8,9},{9,8},{10,11... | collective-permute-start | bytes 786440 | tf_op jit(solution)/shard_map/ppermute | solution.py:369
  61.9 1.9 %collective-permute-start.6 = (bf16[256,512]{1,0:T(8,128)(2,1)S(1)}, bf16[256,512]{1,0:T(8,128)(2,1)S(1)}, u32[]{:S(2)}, u32[]{:S(2)}) collective-permute-start(bf16[256,512]{1,0:T(8,128)(2,1)S(1)} %collective-permute-done.2.refs_1_), channel_id=1, source_target_pairs={{0,1},{1,0},{2,3},{3,2},{4,5},{5,4},{6,7},{7,6},{8,9},{9,8},{10,11... | collective-permute-start | bytes 786440 | tf_op jit(solution)/shard_map/ppermute | solution.py:369
  62.4 2.0 %collective-permute-start.7 = (bf16[256,512]{1,0:T(8,128)(2,1)}, bf16[256,512]{1,0:T(8,128)(2,1)S(1)}, u32[]{:S(2)}, u32[]{:S(2)}) collective-permute-start(bf16[256,512]{1,0:T(8,128)(2,1)} %collective-permute-done.3.refs_2_), channel_id=1, source_target_pairs={{0,1},{1,0},{2,3},{3,2},{4,5},{5,4},{6,7},{7,6},{8,9},{9,8},{10,11... | collective-permute-start | bytes 786440 | tf_op jit(solution)/shard_map/ppermute | solution.py:369
  62.5 2.3 %collective-permute-start.8 = (bf16[256,512]{1,0:T(8,128)(2,1)}, bf16[256,512]{1,0:T(8,128)(2,1)S(1)}, u32[]{:S(2)}, u32[]{:S(2)}) collective-permute-start(bf16[256,512]{1,0:T(8,128)(2,1)} %collective-permute-done.4.refs_3_), channel_id=1, source_target_pairs={{0,1},{1,0},{2,3},{3,2},{4,5},{5,4},{6,7},{7,6},{8,9},{9,8},{10,11... | collective-permute-start | bytes 786440 | tf_op jit(solution)/shard_map/ppermute | solution.py:369
  64.8 2.2 %copy-start.2 = (bf16[512,4096]{1,0:T(8,128)(2,1)S(1)}, bf16[512,4096]{1,0:T(8,128)(2,1)}, u32[]{:S(2)}) copy-start(bf16[512,4096]{1,0:T(8,128)(2,1)} %refs_8_.1) | copy-start | bytes 12582916
  72.4 11.6 %collective-permute-start.9 = (bf16[512,256]{1,0:T(8,128)(2,1)S(1)}, bf16[512,256]{1,0:T(8,128)(2,1)S(1)}, u32[]{:S(2)}, u32[]{:S(2)}) collective-permute-start(bf16[512,256]{1,0:T(8,128)(2,1)S(1)} %grad_z_partial.1.refs_0_), channel_id=1, source_target_pairs={{0,16},{16,0},{1,17},{17,1},{2,18},{18,2},{3,19},{19,3},{4,20},{20... | collective-permute-start | bytes 786440 | tf_op jit(solution)/shard_map/ppermute | solution.py:373
  80.9 1.6 %copy-start.3 = (bf16[32,256,128]{2,1,0:T(8,128)(2,1)S(1)}, bf16[32,256,128]{2,1,0:T(8,128)(2,1)}, u32[]{:S(2)}) copy-start(bf16[32,256,128]{2,1,0:T(8,128)(2,1)} %get-tuple-element.9.refs_2_) | copy-start | bytes 6291460
  82.5 1.6 %copy-start.4 = (bf16[32,256,128]{2,1,0:T(8,128)(2,1)S(1)}, bf16[32,256,128]{2,1,0:T(8,128)(2,1)}, u32[]{:S(2)}) copy-start(bf16[32,256,128]{2,1,0:T(8,128)(2,1)} %get-tuple-element.12.refs_4_) | copy-start | bytes 6291460
  85.0 4.6 %copy-start.1 = (bf16[4096,3,512]{2,0,1:T(8,128)(2,1)S(1)}, bf16[4096,3,512]{2,0,1:T(8,128)(2,1)}, u32[]{:S(2)}) copy-start(bf16[4096,3,512]{2,0,1:T(8,128)(2,1)} %param.7) | copy-start | bytes 37748740
  93.1 3.6 %collective-permute-start.20 = (bf16[4,512,256]{2,1,0:T(8,128)(2,1)S(1)}, bf16[4,512,256]{2,1,0:T(8,128)(2,1)S(1)}, u32[]{:S(2)}, u32[]{:S(2)}) collective-permute-start(bf16[4,512,256]{2,1,0:T(8,128)(2,1)S(1)} %input_partial.3), channel_id=1, source_target_pairs={{0,1},{1,0},{2,3},{3,2},{4,5},{5,4},{6,7},{7,6},{8,9},{9,8},{10,11... | collective-permute-start | bytes 3145736 | tf_op jit(solution)/shard_map/ppermute | solution.py:369
  96.9 8.9 %collective-permute-start.21 = (bf16[512,256]{1,0:T(8,128)(2,1)S(1)}, bf16[512,256]{1,0:T(8,128)(2,1)}, u32[]{:S(2)}, u32[]{:S(2)}) collective-permute-start(bf16[512,256]{1,0:T(8,128)(2,1)S(1)} %get-tuple-element.18), channel_id=1, source_target_pairs={{0,2},{1,3},{2,0},{3,1},{4,6},{5,7},{6,4},{7,5},{8,10},{9,11},{10,... | collective-permute-start | bytes 786440 | tf_op jit(solution)/shard_map/ppermute | solution.py:369
  98.3 9.2 %collective-permute-start.22 = (bf16[512,256]{1,0:T(8,128)(2,1)S(1)}, bf16[512,256]{1,0:T(8,128)(2,1)}, u32[]{:S(2)}, u32[]{:S(2)}) collective-permute-start(bf16[512,256]{1,0:T(8,128)(2,1)S(1)} %get-tuple-element.20), channel_id=1, source_target_pairs={{0,4},{1,5},{2,6},{3,7},{4,0},{5,1},{6,2},{7,3},{8,12},{9,13},{10,... | collective-permute-start | bytes 786440 | tf_op jit(solution)/shard_map/ppermute | solution.py:369
  98.7 13.9 %collective-permute-start.23 = (bf16[512,256]{1,0:T(8,128)(2,1)S(1)}, bf16[512,256]{1,0:T(8,128)(2,1)}, u32[]{:S(2)}, u32[]{:S(2)}) collective-permute-start(bf16[512,256]{1,0:T(8,128)(2,1)S(1)} %get-tuple-element.19), channel_id=1, source_target_pairs={{0,6},{1,7},{2,4},{3,5},{4,2},{5,3},{6,0},{7,1},{8,14},{9,15},{10,... | collective-permute-start | bytes 786440 | tf_op jit(solution)/shard_map/ppermute | solution.py:369
  113.8 5.3 %collective-permute-start.24 = (bf16[512,128]{1,0:T(8,128)(2,1)S(1)}, bf16[512,128]{1,0:T(8,128)(2,1)S(1)}, u32[]{:S(2)}, u32[]{:S(2)}) collective-permute-start(bf16[512,128]{1,0:T(8,128)(2,1)S(1)} %broadcast_select_fusion.4), channel_id=1, source_target_pairs={{0,16},{16,0},{1,17},{17,1},{2,18},{18,2},{3,19},{19,3},{4,20},{20... | collective-permute-start | bytes 393224 | tf_op jit(solution)/shard_map/ppermute | solution.py:373
  119.2 8.9 %collective-permute-start.25 = (bf16[512,128]{1,0:T(8,128)(2,1)S(1)}, bf16[512,128]{1,0:T(8,128)(2,1)S(1)}, u32[]{:S(2)}, u32[]{:S(2)}) collective-permute-start(bf16[512,128]{1,0:T(8,128)(2,1)S(1)} %broadcast_select_fusion.6), channel_id=1, source_target_pairs={{0,8},{1,9},{2,10},{3,11},{4,12},{5,13},{6,14},{7,15},{8,0},{9,1},... | collective-permute-start | bytes 393224 | tf_op jit(solution)/shard_map/ppermute | solution.py:369

commit v2 on v1

v2 whole, which is shorter than its diff:
```python
import functools

import jax
import jax.numpy as jnp
from jax import lax
from jax.experimental import pallas as pl
from jax.experimental.pallas import tpu as pltpu
from jax.sharding import PartitionSpec as P

BLOCK = 128
TOK_DEV = 128
BF16 = jnp.bfloat16
F32 = jnp.float32
MIB = 1 << 20


def cost(flops, read):
    return pl.CostEstimate(flops=int(flops) >> 12, bytes_accessed=int(read) >> 12, transcendentals=0)


def params(mib):
    return pltpu.CompilerParams(vmem_limit_bytes=mib * MIB)


def in_hbm(array):
    return pltpu.with_memory_space_constraint(array, pltpu.HBM)


VMEM_SPEC = pl.BlockSpec(memory_space=pltpu.VMEM)
SMEM_SPEC = pl.BlockSpec(memory_space=pltpu.SMEM)
LATER_SPEC = pl.BlockSpec(memory_space=pl.ANY)


def copy_kernel(in_ref, *refs):
    refs[-1][...] = in_ref[...]


def copied(array, *earlier):
    return pl.pallas_call(
        copy_kernel,
        in_specs=[VMEM_SPEC] + [LATER_SPEC] * len(earlier),
        out_specs=VMEM_SPEC,
        out_shape=jax.ShapeDtypeStruct(array.shape, array.dtype),
        compiler_params=params(8),
        cost_estimate=cost(0, 4 * array.size),
        name="copied",
    )(array, *earlier)


def at_home():
    return lax.axis_index("tensor") // Z1 == lax.axis_index("fsdp")


def stack_kernel(first_ref, second_ref, out_ref, sems):
    run = first_ref.shape[0]
    copies = [
        pltpu.make_async_copy(ref, out_ref.at[pl.ds(n * run, run), :], sems.at[n])
        for n, ref in enumerate((first_ref, second_ref))
    ]
    for copy in copies:
        copy.start()
    for copy in copies:
        copy.wait()


def stacked(first, second):
    shape = (2 * first.shape[0], first.shape[1])
    return pl.pallas_call(
        stack_kernel,
        in_specs=[LATER_SPEC] * 2,
        out_specs=VMEM_SPEC,
        out_shape=pltpu.VMEM(shape, first.dtype),
        scratch_shapes=[pltpu.SemaphoreType.DMA((2,))],
        compiler_params=params(8),
        cost_estimate=cost(0, 8 * first.size),
        name="stacked",
    )(in_hbm(first), in_hbm(second))


def own_kernel(both_ref, turned_ref, crossed_ref, *out_refs):
    run = both_ref.shape[0] // 2
    home = at_home()
    for n, out_ref in enumerate(out_refs):
        at = slice(n * run, (n + 1) * run)

        @pl.when(home)
        def _(out_ref=out_ref, at=at):
            out_ref[:run] = both_ref[at]
            out_ref[run:] = turned_ref[at]

        @pl.when(jnp.logical_not(home))
        def _(out_ref=out_ref, at=at):
            out_ref[:run] = turned_ref[at]
            out_ref[run:] = crossed_ref[at]


def own_slices(both, turned, crossed):
    out = jax.ShapeDtypeStruct(both.shape, both.dtype)
    return pl.pallas_call(
        own_kernel,
        in_specs=[VMEM_SPEC] * 3,
        out_specs=[VMEM_SPEC] * 2,
        out_shape=[out, out],
        compiler_params=params(8),
        cost_estimate=cost(0, 10 * both.size),
        name="own_slices",
    )(both, turned, crossed)


def in_vmem(array):
    return pltpu.with_memory_space_constraint(array, pltpu.VMEM)


AHEAD = 3


def prepare_kernel(v_ref, s_ref, ow_ref, *refs):
    weights, (ow_out, done_ref, held, ins, in_sems, ow_sem) = refs[-9:-6], refs[-6:]
    piece = ins.shape[2]
    pieces = v_ref.shape[1] // piece

    def rows(i):
        return pl.ds(pl.multiple_of(i * piece, BLOCK), piece)

    def fetch(i, j):
        slot = lax.rem(i, AHEAD)
        return pltpu.make_async_copy(
            v_ref.at[j, rows(i), :], ins.at[slot, j], in_sems.at[slot, j]
        )

    for i in range(min(AHEAD, pieces)):
        for j in range(3):
            fetch(i, j).start()
    whole = pltpu.make_async_copy(ow_ref, ow_out, ow_sem)
    whole.start()
    held[...] = s_ref[...].astype(F32)
    done_ref[...] = jnp.zeros(done_ref.shape, F32)

    def one(i, carry):
        for j in range(3):
            fetch(i, j).wait()
            for b in range(piece // BLOCK):
                scale = held[j, pl.ds(i * (piece // BLOCK) + b, 1), :]
                at = pl.ds(pl.multiple_of(i * piece + b * BLOCK, BLOCK), BLOCK)
                values = ins[lax.rem(i, AHEAD), j, b * BLOCK : (b + 1) * BLOCK, :]
                weights[j][at, :] = (values.astype(F32) * scale).astype(BF16)

            @pl.when(i + AHEAD < pieces)
            def _(j=j):
                fetch(i + AHEAD, j).start()

        return carry

    lax.fori_loop(0, pieces, one, 0)
    whole.wait()


def prepared(values, scales, out_weight, *earlier):
    _, rows, channels = values.shape
    piece = min(rows, 512)
    *weights, out_held, ready = pl.pallas_call(
        prepare_kernel,
        in_specs=[LATER_SPEC, VMEM_SPEC, LATER_SPEC] + [LATER_SPEC] * len(earlier),
        out_specs=[VMEM_SPEC] * 5,
        out_shape=[pltpu.VMEM((rows, channels), BF16)] * 3
        + [pltpu.VMEM(out_weight.shape, BF16), jax.ShapeDtypeStruct((8, 128), F32)],
        scratch_shapes=[
            pltpu.VMEM(scales.shape, F32),
            pltpu.VMEM((AHEAD, 3, piece, channels), BF16),
            pltpu.SemaphoreType.DMA((AHEAD, 3)),
            pltpu.SemaphoreType.DMA,
        ],
        compiler_params=params(16),
        cost_estimate=cost(values.size * 4, 4 * values.size),
        name="prepare",
    )(in_hbm(values), scales, in_hbm(out_weight), *earlier)
    return weights, out_held, ready


Z1, Z0, X, CORE = 8, 4, 2, 1
MINE = (0, X, Z0, X + Z0)
OTHERS = tuple(mask + CORE for mask in MINE)


def slices_of(masks):
    low = lax.rem(lax.axis_index("tensor"), Z1)
    return [low ^ mask for mask in masks]


def run_starts(runs, run):
    if runs == 1:
        return [0]
    y = lax.axis_index("fsdp")
    return [pl.multiple_of(y * run, BLOCK), pl.multiple_of((1 - y) * run, BLOCK)]


def piece_rows(masks, n, rows):
    if masks is None:
        return pl.ds(n * rows, rows)
    return pl.ds(pl.multiple_of(slices_of(masks)[n] * rows, BLOCK), rows)


def assembled(masks, refs, held):
    for n, ref in enumerate(refs):
        held[:, piece_rows(masks, n, ref.shape[1])] = ref[...]


def proj_part(runs, held_ref, w_ref, out_ref):
    run = held_ref.shape[0] // runs
    total = jnp.dot(held_ref[...], w_ref[...], preferred_element_type=F32)
    for h, start in enumerate(run_starts(runs, run)):
        out_ref[:, pl.ds(start, run)] = total[h * run : (h + 1) * run].T.astype(BF16)


def first_proj_kernel(masks, runs, *refs):
    xs, (key_ref, value_ref, key_out, value_out, held_ref) = refs[:-5], refs[-5:]
    assembled(masks, xs, held_ref)
    proj_part(runs, held_ref, key_ref, key_out)
    proj_part(runs, held_ref, value_ref, value_out)


def more_proj_kernel(runs, held_ref, w_ref, out_ref):
    proj_part(runs, held_ref, w_ref, out_ref)


def proj_partial(xs, masks, runs, weights):
    tokens = xs[0].shape[0]
    depth, channels = weights[0].shape
    flops = 2 * tokens * depth * channels
    weights = [in_vmem(weight) for weight in weights]
    part = jax.ShapeDtypeStruct((channels, tokens), BF16)
    *keys, held = pl.pallas_call(
        functools.partial(first_proj_kernel, masks, runs),
        in_specs=[VMEM_SPEC] * (len(xs) + 2),
        out_specs=[VMEM_SPEC] * 3,
        out_shape=[part, part, pltpu.VMEM((tokens, depth), BF16)],
        compiler_params=params(16),
        cost_estimate=cost(2 * flops, 4 * depth * channels),
        name="proj_keys_values",
    )(*xs, *weights[1:])
    others = pl.pallas_call(
        functools.partial(more_proj_kernel, runs),
        in_specs=[VMEM_SPEC] * 2,
        out_specs=VMEM_SPEC,
        out_shape=part,
        compiler_params=params(16),
        cost_estimate=cost(flops, 2 * depth * channels),
        name="proj_queries",
    )(held, weights[0])
    return keys, others


def grad_z_kernel(masks, runs, *refs):
    xs, (w_ref, out_ref, held) = refs[:-3], refs[-3:]
    assembled(masks, xs, held)
    total = lax.dot_general(
        w_ref[...], held[...], (((1,), (1,)), ((), ())), preferred_element_type=F32
    )
    run = total.shape[1] // runs
    for h, start in enumerate(run_starts(runs, run)):
        out_ref[:, pl.ds(start, run)] = total[:, h * run : (h + 1) * run].astype(BF16)


def grad_z_partial(xs, masks, runs, out_weight):
    tokens = xs[0].shape[0]
    channels, depth = out_weight.shape
    return pl.pallas_call(
        functools.partial(grad_z_kernel, masks, runs),
        in_specs=[VMEM_SPEC] * (len(xs) + 1),
        out_specs=VMEM_SPEC,
        out_shape=jax.ShapeDtypeStruct((channels, tokens), BF16),
        scratch_shapes=[pltpu.VMEM((tokens, depth), BF16)],
        compiler_params=params(16),
        cost_estimate=cost(2 * tokens * depth * channels, 2 * depth * channels),
        name="grad_z_partial",
    )(*xs, in_vmem(out_weight))


def iotas():
    shape = (BLOCK, BLOCK)
    return lax.broadcasted_iota(jnp.int32, shape, 0), lax.broadcasted_iota(jnp.int32, shape, 1)


def sheared(array):
    return pltpu.roll(array, 0, 1, stride=1, stride_axis=0)


def toeplitz_kernel(taps_ref, *refs):
    past_ref, next_ref = refs[-2:]
    row, lane = iotas()
    for g in range(taps_ref.shape[0]):
        ahead = sheared(jnp.broadcast_to(taps_ref[g : g + 1, :], (BLOCK, BLOCK)))
        behind = ahead.T
        past_ref[g, :BLOCK] = jnp.where(lane < row, ahead, 0.0).astype(BF16)
        past_ref[g, BLOCK:] = jnp.where(lane >= row, ahead, 0.0).astype(BF16)
        next_ref[g, :BLOCK] = jnp.where(lane <= row, behind, 0.0).astype(BF16)
        next_ref[g, BLOCK:] = jnp.where(lane > row, behind, 0.0).astype(BF16)


def toeplitz(filters, *earlier):
    groups, taps = filters.shape
    step = min(8, groups)
    shape = pltpu.VMEM((groups, 2 * BLOCK, taps), BF16)
    return pl.pallas_call(
        toeplitz_kernel,
        grid=(groups // step,),
        in_specs=[pl.BlockSpec((step, taps), lambda i: (i, 0))]
        + [LATER_SPEC] * len(earlier),
        out_specs=[pl.BlockSpec((step, 2 * BLOCK, taps), lambda i: (i, 0, 0))] * 2,
        out_shape=[shape, shape],
        compiler_params=params(16),
        cost_estimate=cost(groups * taps * 2000, groups * taps * 1024),
        name="toeplitz",
    )(filters, *earlier)


def block_of(array, i):
    blocks = array.shape[1] // BLOCK
    if 0 <= i < blocks:
        return array[:, i * BLOCK : (i + 1) * BLOCK]
    return jnp.zeros((array.shape[0], BLOCK), array.dtype)


def paired(array, by):
    blocks = array.shape[1] // BLOCK
    low, high = min(by, 0), max(by, 0)
    return jnp.concatenate(
        [
            jnp.concatenate([block_of(array, i + low), block_of(array, i + high)], 1)
            for i in range(blocks)
        ],
        0,
    )


def unstacked(array, blocks):
    rows = array.shape[0] // blocks
    return jnp.concatenate([array[i * rows : (i + 1) * rows] for i in range(blocks)], 1)


def summed(refs):
    total = refs[0][...].astype(F32)
    for ref in refs[1:]:
        total = total + ref[...].astype(F32)
    return total.astype(BF16)


def conv_kernel(parts, groups, *refs):
    keys, values, queries = (refs[n * parts : (n + 1) * parts] for n in range(3))
    past_ref, proj_ref, prod_ref, conv_ref = refs[3 * parts :]
    key, value = summed(keys), summed(values)
    proj_ref[0] = summed(queries)
    proj_ref[1] = key
    proj_ref[2] = value
    product = (key.astype(F32) * value.astype(F32)).astype(BF16)
    prod_ref[...] = product
    channels, tokens = product.shape
    per = channels // groups
    for g in range(groups):
        rows = slice(g * per, (g + 1) * per)
        result = jnp.dot(paired(product[rows], -1), past_ref[g], preferred_element_type=F32)
        conv_ref[rows] = unstacked(result, tokens // BLOCK)


def conv_forward(keys, values, queries, past):
    channels, tokens = keys[0].shape
    groups = past.shape[0]
    steps = max(1, groups // 8)
    chunk = channels // steps
    parts = len(keys)
    one = pl.BlockSpec((chunk, tokens), lambda i: (i, 0))
    return pl.pallas_call(
        functools.partial(conv_kernel, parts, groups // steps),
        grid=(steps,),
        in_specs=[one] * (3 * parts)
        + [pl.BlockSpec((groups // steps,) + past.shape[1:], lambda i: (i, 0, 0))],
        out_specs=[pl.BlockSpec((3, chunk, tokens), lambda i: (0, i, 0)), one, one],
        out_shape=[
            jax.ShapeDtypeStruct((3, channels, tokens), BF16),
            jax.ShapeDtypeStruct((channels, tokens), BF16),
            jax.ShapeDtypeStruct((channels, tokens), F32),
        ],
        compiler_params=params(16),
        cost_estimate=cost(4 * channels * tokens * BLOCK * 8, channels * tokens * 24),
        name="conv_forward",
    )(*keys, *values, *queries, past)


def conv_back_kernel(parts, groups, *refs):
    partials, (proj_ref, conv_ref, next_ref, out_ref, grad_ref) = refs[:parts], refs[parts:]
    grad_z = partials[0][...].astype(F32)
    for ref in partials[1:]:
        grad_z = grad_z + ref[...].astype(F32)
    out_ref[0] = (grad_z * conv_ref[...]).astype(BF16)
    grad = (grad_z * proj_ref[0].astype(F32)).astype(BF16)
    grad_ref[...] = grad
    channels, tokens = grad.shape
    per = channels // groups
    for g in range(groups):
        rows = slice(g * per, (g + 1) * per)
        result = jnp.dot(paired(grad[rows], 1), next_ref[g], preferred_element_type=F32)
        result = unstacked(result, tokens // BLOCK)
        out_ref[1, rows] = (result * proj_ref[2, rows].astype(F32)).astype(BF16)
        out_ref[2, rows] = (result * proj_ref[1, rows].astype(F32)).astype(BF16)


def conv_backward(partials, proj, conv, after):
    channels, tokens = conv.shape
    groups = after.shape[0]
    steps = max(1, groups // 8)
    chunk = channels // steps
    parts = len(partials)
    three = pl.BlockSpec((3, chunk, tokens), lambda i: (0, i, 0))
    one = pl.BlockSpec((chunk, tokens), lambda i: (i, 0))
    return pl.pallas_call(
        functools.partial(conv_back_kernel, parts, groups // steps),
        grid=(steps,),
        in_specs=[one] * parts
        + [
            three,
            one,
            pl.BlockSpec((groups // steps,) + after.shape[1:], lambda i: (i, 0, 0)),
        ],
        out_specs=[three, one],
        out_shape=[
            jax.ShapeDtypeStruct((3, channels, tokens), BF16),
            jax.ShapeDtypeStruct((channels, tokens), BF16),
        ],
        compiler_params=params(16),
        cost_estimate=cost(4 * channels * tokens * BLOCK * 8, channels * tokens * 24),
        name="conv_backward",
    )(*partials, proj, conv, after)


def taps_kernel(groups, prod_ref, grad_ref, out_ref):
    row, lane = iotas()
    flip = (row + lane == BLOCK - 1).astype(F32).astype(BF16)
    channels, tokens = prod_ref.shape
    per = channels // groups
    blocks = tokens // BLOCK
    for g in range(groups):
        rows = slice(g * per, (g + 1) * per)
        product, grad = prod_ref[rows, :], grad_ref[rows, :]
        turned = jnp.dot(
            jnp.concatenate([block_of(product, i) for i in range(blocks)], 0),
            flip,
            preferred_element_type=F32,
        )
        earlier = paired(unstacked(turned.astype(BF16), blocks), -1)
        later = jnp.concatenate([block_of(grad, i) for i in range(blocks)], 0)
        both = lax.dot_general(
            earlier, later, (((0,), (0,)), ((), ())), preferred_element_type=F32
        )
        folded = jnp.where(row + lane >= BLOCK - 1, both[BLOCK:], both[:BLOCK])
        out_ref[g : g + 1, :] = jnp.sum(sheared(folded), axis=0, keepdims=True)
    out_ref[...] = pltpu.roll(out_ref[...], 1, 1) / TOK_DEV


def taps_gradient(product, grad, groups):
    channels, tokens = product.shape
    steps = max(1, groups // 8)
    chunk = channels // steps
    one = pl.BlockSpec((chunk, tokens), lambda i: (i, 0))
    return pl.pallas_call(
        functools.partial(taps_kernel, groups // steps),
        grid=(steps,),
        in_specs=[one, one],
        out_specs=pl.BlockSpec((groups // steps, BLOCK), lambda i: (i, 0)),
        out_shape=jax.ShapeDtypeStruct((groups, BLOCK), F32),
        compiler_params=params(16),
        cost_estimate=cost(4 * channels * tokens * BLOCK * 8, channels * tokens * 24),
        name="taps_gradient",
    )(product, grad)


def input_kernel(masks, *refs):
    w_refs, (g_ref, out_ref) = refs[:3], refs[3:]
    pieces, rows, _ = out_ref.shape
    for i in range(pieces):
        at = piece_rows(masks, i, rows)
        w = jnp.concatenate([ref[at, :] for ref in w_refs], 1)
        out_ref[i] = jnp.dot(w, g_ref[...], preferred_element_type=F32).astype(BF16)


def input_partial(masks, pieces, rows, weights, grad_proj):
    _, channels, tokens = grad_proj.shape
    return pl.pallas_call(
        functools.partial(input_kernel, masks),
        in_specs=[VMEM_SPEC] * 4,
        out_specs=VMEM_SPEC,
        out_shape=jax.ShapeDtypeStruct((pieces, rows, tokens), BF16),
        compiler_params=params(16),
        cost_estimate=cost(
            2 * tokens * pieces * rows * 3 * channels, 2 * pieces * rows * (3 * channels + tokens)
        ),
        name="input_partial",
    )(*[in_vmem(weight) for weight in weights], grad_proj.reshape(3 * channels, tokens))


def across(array, mask):
    return lax.ppermute(array, "tensor", [(i, i ^ mask) for i in range(16)])


def other_row(array):
    return lax.ppermute(array, "fsdp", [(0, 1), (1, 0)])


def in_square(array, turn):
    pairs = []
    for i in range(32):
        y, k = divmod(i, 16)
        target = turn(y, k // Z1)
        if target is not None:
            pairs.append((i, target[0] * 16 + target[1] * Z1 + k % Z1))
    return lax.ppermute(array, ("fsdp", "tensor"), pairs)


def from_turn(y, z1):
    return (y, 1 - z1) if y == z1 else (1 - y, z1)


def over_diagonal(y, z1):
    return None if y == z1 else (1 - y, 1 - z1)


def first_stage(array):
    return in_square(array, from_turn), in_square(array, over_diagonal)


def second_stage(own):
    return [own] + [across(own, mask) for mask in MINE[1:]]


def both_cores(same):
    return same + [across(piece, CORE) for piece in same]


def split_kernel(same_ref, got_ref, *out_refs):
    pieces = same_ref.shape[0]
    y = lax.axis_index("fsdp")
    leave = pl.ds(pl.multiple_of((1 - y) * TOK_DEV, BLOCK), TOK_DEV)
    stay = pl.ds(pl.multiple_of(y * TOK_DEV, BLOCK), TOK_DEV)
    for n in range(pieces):
        for at, out_ref in ((leave, out_refs[n]), (stay, out_refs[pieces + n])):
            total = same_ref[n, :, at].astype(F32) + got_ref[n, :, at].astype(F32)
            out_ref[...] = total.astype(BF16)


def split(same, got):
    pieces, rows, _ = same.shape
    out = jax.ShapeDtypeStruct((rows, TOK_DEV), BF16)
    halves = pl.pallas_call(
        split_kernel,
        in_specs=[VMEM_SPEC] * 2,
        out_specs=[VMEM_SPEC] * (2 * pieces),
        out_shape=[out] * (2 * pieces),
        compiler_params=params(8),
        cost_estimate=cost(0, 6 * same.size),
        name="split",
    )(same, got)
    return halves[:pieces], halves[pieces:]


def sum_kernel(*refs):
    total = refs[0][...].astype(F32)
    for ref in refs[1:-1]:
        total = total + ref[...].astype(F32)
    refs[-1][...] = total.astype(BF16)


def total_of(pieces):
    return pl.pallas_call(
        sum_kernel,
        in_specs=[VMEM_SPEC] * len(pieces),
        out_specs=VMEM_SPEC,
        out_shape=jax.ShapeDtypeStruct(pieces[0].shape, BF16),
        compiler_params=params(8),
        cost_estimate=cost(0, 8 * pieces[0].size),
        name="total",
    )(*pieces)


def sides_kernel(near_ref, far_ref, keep_ref, send_ref):
    home = at_home()

    @pl.when(home)
    def _():
        keep_ref[...] = near_ref[...]
        send_ref[...] = far_ref[...]

    @pl.when(jnp.logical_not(home))
    def _():
        keep_ref[...] = far_ref[...]
        send_ref[...] = near_ref[...]


def sides(near, far):
    out = jax.ShapeDtypeStruct(near.shape, BF16)
    return pl.pallas_call(
        sides_kernel,
        in_specs=[VMEM_SPEC] * 2,
        out_specs=[VMEM_SPEC] * 2,
        out_shape=[out] * 2,
        compiler_params=params(8),
        cost_estimate=cost(0, 8 * near.size),
        name="sides",
    )(near, far)


def last_kernel(keep_ref, got_ref, out_ref):
    total = keep_ref[...].astype(F32) + got_ref[...].astype(F32)
    out_ref[...] = total.T.astype(BF16)


def last_sum(keep, got):
    return pl.pallas_call(
        last_kernel,
        in_specs=[VMEM_SPEC] * 2,
        out_specs=VMEM_SPEC,
        out_shape=jax.ShapeDtypeStruct(keep.shape[::-1], BF16),
        compiler_params=params(8),
        cost_estimate=cost(0, 6 * keep.size),
        name="last_sum",
    )(keep, got)


def moved(pieces):
    return [pieces[0]] + [across(piece, mask) for piece, mask in zip(pieces[1:], MINE[1:])]


def scattered(same, others):
    leave, stay = split(same, across(others, CORE))
    leave, stay = moved(leave), moved(stay)
    far = other_row(total_of(leave))
    keep, send = sides(total_of(stay), far)
    return last_sum(keep, across(send, Z1))


def on_small_slice(tokens, values, scales, filters, out_weight, cotangent):
    rows = tokens.shape[1]
    both = stacked(tokens, cotangent)
    token_own, cot_own = own_slices(both, *first_stage(both))
    token_same = second_stage(token_own)
    weights, out_held, ready = prepared(values, scales, out_weight, token_own)
    past, later = toeplitz(filters, token_own)
    cot_own = copied(cot_own, ready, past, *token_same[1:])
    cot_same = second_stage(cot_own)
    keys, queries = proj_partial(both_cores(token_same), MINE + OTHERS, 2, weights)
    proj, product, conv = conv_forward(
        *[[part, other_row(part)] for part in (*keys, queries)], past
    )
    z_part = grad_z_partial(both_cores(cot_same), MINE + OTHERS, 2, out_held)
    grad_proj, grad = conv_backward([z_part, other_row(z_part)], proj, conv, later)
    others = input_partial(OTHERS, 4, rows, weights, grad_proj)
    same = input_partial(MINE, 4, rows, weights, grad_proj)
    return scattered(same, others), taps_gradient(product, grad, filters.shape[0])


def on_any_slice(tokens, values, scales, filters, out_weight, cotangent):
    count = lax.axis_size("fsdp")
    rows = values.shape[1]
    piece = min(rows, 512)
    pieces = rows // piece

    def gather(array):
        whole = lax.all_gather(array, "tensor", axis=1, tiled=True)
        mine = lax.all_to_all(whole, "fsdp", 1, 0, tiled=True)
        return [mine[:, i * piece : (i + 1) * piece] for i in range(pieces)]

    def shares(array):
        every = lax.all_gather(array, "fsdp", axis=0)
        return [every[i] for i in range(count)]

    weights, out_held, _ = prepared(values, scales, out_weight)
    past, later = toeplitz(filters)
    keys, queries = proj_partial(gather(tokens), None, 1, weights)
    proj, product, conv = conv_forward(*[shares(part) for part in (*keys, queries)], past)
    z_part = grad_z_partial(gather(cotangent), None, 1, out_held)
    grad_proj, grad = conv_backward(shares(z_part), proj, conv, later)
    partial = input_partial(None, pieces, piece, weights, grad_proj)
    partial = partial.reshape(rows, partial.shape[2]).astype(F32)
    partial = lax.all_to_all(partial, "fsdp", 1, 0, tiled=True)
    total = lax.psum_scatter(partial, "tensor", scatter_dimension=0, tiled=True)
    return total.T.astype(BF16), taps_gradient(product, grad, filters.shape[0])


def on_device(tokens, in_values, in_scales, filters, out_weight, cotangent):
    values = jnp.transpose(in_values, (1, 0, 2))
    scales = jnp.transpose(in_scales, (1, 0, 2))
    small = lax.axis_size("fsdp") == 2 and lax.axis_size("tensor") == 16
    inner = on_small_slice if small else on_any_slice
    return inner(tokens, values, scales, filters, out_weight, cotangent)


def solution(mesh):
    placed = (
        P("fsdp", "tensor"),
        P("fsdp", None, "tensor"),
        P("fsdp", None, "tensor"),
        P("tensor", None),
        P("tensor", "fsdp"),
        P("fsdp", "tensor"),
    )
    return jax.shard_map(
        on_device,
        mesh=mesh,
        in_specs=placed,
        out_specs=(P("fsdp", "tensor"), P("tensor", None)),
        check_vma=False,
    )
```

time: 129 us -> 110 us (0.85)
  local copies, waits for them, and re-layouts: 15 us -> 1.6 us
  starting transfers between devices: 29.1 us -> 37.4 us
  Pallas kernels: 32.9 us -> 25.7 us
  other arithmetic: 4.9 us -> 0 us
  waiting for transfers between devices: 46.2 us -> 44.5 us
    ppermute x21 -> x22, waiting for transfers between devices: 35.8 us -> 21.4 us  [across(): return lax.ppermute(array, 'tensor', [(i, i ^ mask) for i in range(16)])]
    unnamed x13 -> x4, local copies, waits for them, and re-layouts: 13.8 us -> 1.6 us
    ppermute x5, waiting for transfers between devices: 10.4 us -> 18.1 us  [other_row(): return lax.ppermute(array, 'fsdp', [(0, 1), (1, 0)])]
    pallas_call x4 -> x14, Pallas kernels: 23.3 us -> 17.5 us  [the longest x1 6.18 us: prepared(): pl.pallas_call(prepare_kernel, in_specs=[LATER_SPEC, VMEM_SPEC, LATER_SPE...]
    ppermute x0 -> x2, waiting for transfers between devices: none -> 4.94 us  [in_square(): return lax.ppermute(array, ('fsdp', 'tensor'), pairs)]
    ppermute x0 -> x2, starting transfers between devices: none -> 4.75 us  [in_square(): return lax.ppermute(array, ('fsdp', 'tensor'), pairs)]
    ppermute x21 -> x22, starting transfers between devices: 22.1 us -> 26.2 us  [across(): return lax.ppermute(array, 'tensor', [(i, i ^ mask) for i in range(16)])]
    pallas_call x1, Pallas kernels: 3.94 us -> 1.03 us  [toeplitz(): pl.pallas_call(toeplitz_kernel, grid=(groups // step,), in_specs=[pl.Bloc...]
  transfers between devices with their start and end apart: 26 -> 29, of which waited for: 16 -> 15; matrix products, arithmetic and copies ran while one was open for 3% -> 0% of each run, Pallas kernels for 22% -> 19%
where the time goes in v2:
time: 110 us
  waiting for transfers between devices  44.5 us (40%)
  starting transfers between devices  37.4 us (34%)
  Pallas kernels  25.7 us (23%)
  local copies, waits for them, and re-layouts  1.6 us (1%)
    ppermute x22, starting transfers between devices, across(): return lax.ppermute(array, 'tensor', [(i, i ^ mask) for i in range(16)])  26.2 us
    ppermute x22, waiting for transfers between devices, across(): return lax.ppermute(array, 'tensor', [(i, i ^ mask) for i in range(16)])  21.4 us
    ppermute x5, waiting for transfers between devices, other_row(): return lax.ppermute(array, 'fsdp', [(0, 1), (1, 0)])  18.1 us
    ppermute x5, starting transfers between devices, other_row(): return lax.ppermute(array, 'fsdp', [(0, 1), (1, 0)])  6.39 us
    pallas_call x1, Pallas kernels, prepared(): pl.pallas_call(prepare_kernel, in_specs=[LATER_SPEC, VMEM_SPEC, LATER_SPE...  6.18 us
    pallas_call x1, Pallas kernels, taps_gradient(): pl.pallas_call(functools.partial(taps_kernel, groups // steps), grid=(ste...  5.31 us
    ppermute x2, waiting for transfers between devices, in_square(): return lax.ppermute(array, ('fsdp', 'tensor'), pairs)  4.94 us
    ppermute x2, starting transfers between devices, in_square(): return lax.ppermute(array, ('fsdp', 'tensor'), pairs)  4.75 us
  transfers between devices with their start and end apart: 29, of which 15 were waited for; matrix products, arithmetic and copies ran while one was open for 0% of the time, Pallas kernels for 19%

profile of v2, /device:TPU:0, one launch (start us, length us, event | category | flops | bytes accessed | tf_op | source)
XLA Modules:
  0.0 110.0 jit_solution(7244983979195152010)
XLA Ops:
  1.6 4.1 %collective-permute-start = (bf16[256,512]{1,0:T(8,128)(2,1)S(1)}, bf16[256,512]{1,0:T(8,128)(2,1)S(1)}, u32[]{:S(2)}, u32[]{:S(2)}) collective-permute-start(bf16[256,512]{1,0:T(8,128)(2,1)S(1)} %stacked.1.both_ref), channel_id=1, source_target_pairs={{0,8},{1,9},{2,10},{3,11},{4,12},{5,13},{6,14},{7,15},{8,24},{9,25... | collective-permute-start | bytes 786440 | tf_op jit(solution)/shard_map/ppermute | solution.py:515
  6.4 4.9 %collective-permute-done.turned_ref = bf16[256,512]{1,0:T(8,128)(2,1)S(1)} collective-permute-done((bf16[256,512]{1,0:T(8,128)(2,1)S(1)}, bf16[256,512]{1,0:T(8,128)(2,1)S(1)}, u32[]{:S(2)}, u32[]{:S(2)}) %collective-permute-start) | collective-permute-done | bytes 262176 | tf_op jit(solution)/shard_map/ppermute | solution.py:515
  11.4 1.6 %collective-permute-start.2 = (bf16[256,512]{1,0:T(8,128)(2,1)S(1)}, bf16[256,512]{1,0:T(8,128)(2,1)S(1)}, u32[]{:S(2)}, u32[]{:S(2)}) collective-permute-start(bf16[256,512]{1,0:T(8,128)(2,1)S(1)} %get-tuple-element.29.refs_0_), channel_id=1, source_target_pairs={{0,2},{1,3},{2,0},{3,1},{4,6},{5,7},{6,4},{7,5},{8,10},{9,11},{10,... | collective-permute-start | bytes 786440 | tf_op jit(solution)/shard_map/ppermute | solution.py:501
  12.9 7.0 %collective-permute-start.3 = (bf16[256,512]{1,0:T(8,128)(2,1)S(1)}, bf16[256,512]{1,0:T(8,128)(2,1)S(1)}, u32[]{:S(2)}, u32[]{:S(2)}) collective-permute-start(bf16[256,512]{1,0:T(8,128)(2,1)S(1)} %get-tuple-element.29.refs_0_), channel_id=1, source_target_pairs={{0,4},{1,5},{2,6},{3,7},{4,0},{5,1},{6,2},{7,3},{8,12},{9,13},{10,... | collective-permute-start | bytes 786440 | tf_op jit(solution)/shard_map/ppermute | solution.py:501
  22.6 6.2 %prepare.1 = (bf16[4096,512]{1,0:T(8,128)(2,1)S(1)}, bf16[4096,512]{1,0:T(8,128)(2,1)S(1)}, bf16[4096,512]{1,0:T(8,128)(2,1)S(1)}, bf16[512,4096]{1,0:T(8,128)(2,1)S(1)}, f32[8,128]{1,0:T(8,128)S(1)}) custom-call(bf16[3,4096,512]{2,1,0:T(8,128)(2,1)} %bitcast.6, bf16[3,32,512]{2,1,0:T(8,128)(2,1)S(1)} %bitcast.5, bf16[512,4096]{1,0:T(8,128)(2,1)} %ow_ref.1, ...), custom_call_target="tpu_custom_call" | custom-call | flops 6144 | bytes 6144 | tf_op jit(solution)/shard_map/prepare/pallas_call | solution.py:161
  28.8 4.1 %collective-permute-done.4.refs_4_.refs_3_ = bf16[256,512]{1,0:T(8,128)(2,1)S(1)} collective-permute-done((bf16[256,512]{1,0:T(8,128)(2,1)S(1)}, bf16[256,512]{1,0:T(8,128)(2,1)S(1)}, u32[]{:S(2)}, u32[]{:S(2)}) %collective-permute-start.4) | collective-permute-done | bytes 262176 | tf_op jit(solution)/shard_map/ppermute | solution.py:501
  33.5 1.5 %collective-permute-start.6 = (bf16[256,512]{1,0:T(8,128)(2,1)S(1)}, bf16[256,512]{1,0:T(8,128)(2,1)S(1)}, u32[]{:S(2)}, u32[]{:S(2)}) collective-permute-start(bf16[256,512]{1,0:T(8,128)(2,1)S(1)} %copied.1.refs_0_), channel_id=1, source_target_pairs={{0,4},{1,5},{2,6},{3,7},{4,0},{5,1},{6,2},{7,3},{8,12},{9,13},{10,... | collective-permute-start | bytes 786440 | tf_op jit(solution)/shard_map/ppermute | solution.py:501
  35.1 1.4 %collective-permute-start.7 = (bf16[256,512]{1,0:T(8,128)(2,1)S(1)}, bf16[256,512]{1,0:T(8,128)(2,1)S(1)}, u32[]{:S(2)}, u32[]{:S(2)}) collective-permute-start(bf16[256,512]{1,0:T(8,128)(2,1)S(1)} %copied.1.refs_0_), channel_id=1, source_target_pairs={{0,6},{1,7},{2,4},{3,5},{4,2},{5,3},{6,0},{7,1},{8,14},{9,15},{10,... | collective-permute-start | bytes 786440 | tf_op jit(solution)/shard_map/ppermute | solution.py:501
  37.0 4.3 %collective-permute-done.5.refs_1_ = bf16[256,512]{1,0:T(8,128)(2,1)S(1)} collective-permute-done((bf16[256,512]{1,0:T(8,128)(2,1)S(1)}, bf16[256,512]{1,0:T(8,128)(2,1)S(1)}, u32[]{:S(2)}, u32[]{:S(2)}) %collective-permute-start.5) | collective-permute-done | bytes 262176 | tf_op jit(solution)/shard_map/ppermute | solution.py:501
  41.3 1.5 %collective-permute-done.6.refs_2_ = bf16[256,512]{1,0:T(8,128)(2,1)S(1)} collective-permute-done((bf16[256,512]{1,0:T(8,128)(2,1)S(1)}, bf16[256,512]{1,0:T(8,128)(2,1)S(1)}, u32[]{:S(2)}, u32[]{:S(2)}) %collective-permute-start.6) | collective-permute-done | bytes 262176 | tf_op jit(solution)/shard_map/ppermute | solution.py:501
  42.8 5.3 %collective-permute-done.7.refs_3_ = bf16[256,512]{1,0:T(8,128)(2,1)S(1)} collective-permute-done((bf16[256,512]{1,0:T(8,128)(2,1)S(1)}, bf16[256,512]{1,0:T(8,128)(2,1)S(1)}, u32[]{:S(2)}, u32[]{:S(2)}) %collective-permute-start.7) | collective-permute-done | bytes 262176 | tf_op jit(solution)/shard_map/ppermute | solution.py:501
  48.6 2.7 %proj_keys_values.1 = (bf16[512,256]{1,0:T(8,128)(2,1)S(1)}, bf16[512,256]{1,0:T(8,128)(2,1)S(1)}, bf16[256,4096]{1,0:T(8,128)(2,1)S(1)}) custom-call(bf16[256,512]{1,0:T(8,128)(2,1)S(1)} %get-tuple-element.29.refs_0_, bf16[256,512]{1,0:T(8,128)(2,1)S(1)} %collective-permute-done.2.refs_2_.refs_1_, ...), custom_call_target="tpu_custom_call" | custom-call | flops 524288 | bytes 2048 | tf_op jit(solution)/shard_map/proj_keys_values/pallas_call | solution.py:232
  51.3 2.4 %collective-permute-start.17 = (bf16[512,256]{1,0:T(8,128)(2,1)S(1)}, bf16[512,256]{1,0:T(8,128)(2,1)S(1)}, u32[]{:S(2)}, u32[]{:S(2)}) collective-permute-start(bf16[512,256]{1,0:T(8,128)(2,1)S(1)} %get-tuple-element.37.refs_0_), channel_id=1, source_target_pairs={{0,16},{16,0},{1,17},{17,1},{2,18},{18,2},{3,19},{19,3},{4,20},{20... | collective-permute-start | bytes 786440 | tf_op jit(solution)/shard_map/ppermute | solution.py:505
  53.7 1.4 %proj_queries.1.refs_4_ = bf16[512,256]{1,0:T(8,128)(2,1)S(1)} custom-call(bf16[256,4096]{1,0:T(8,128)(2,1)S(1)} %get-tuple-element.39.held_ref, bf16[4096,512]{1,0:T(8,128)(2,1)S(1)} %get-tuple-element.30.w_ref.refs_0_), custom_call_target="tpu_custom_call" | custom-call | flops 262144 | bytes 1024 | tf_op jit(solution)/shard_map/proj_queries/pallas_call | solution.py:241
  55.2 2.0 %collective-permute-start.19 = (bf16[512,256]{1,0:T(8,128)(2,1)S(1)}, bf16[512,256]{1,0:T(8,128)(2,1)S(1)}, u32[]{:S(2)}, u32[]{:S(2)}) collective-permute-start(bf16[512,256]{1,0:T(8,128)(2,1)S(1)} %proj_queries.1.refs_4_), channel_id=1, source_target_pairs={{0,16},{16,0},{1,17},{17,1},{2,18},{18,2},{3,19},{19,3},{4,20},{20... | collective-permute-start | bytes 786440 | tf_op jit(solution)/shard_map/ppermute | solution.py:505
  57.2 1.5 %grad_z_partial.1.refs_0_ = bf16[512,256]{1,0:T(8,128)(2,1)S(1)} custom-call(bf16[256,512]{1,0:T(8,128)(2,1)S(1)} %copied.1.refs_0_, bf16[256,512]{1,0:T(8,128)(2,1)S(1)} %collective-permute-done.5.refs_1_, bf16[256,512]{1,0:T(8,128)(2,1)S(1)} %collective-permute-done.6.refs_2_, bf16[256,512]{1,0:T(8,128)(2,1)S(1)} %collective-permute-done.7.refs_3_, ...), custom_call_target="tpu_custom_call" | custom-call | flops 262144 | bytes 1024 | tf_op jit(solution)/shard_map/grad_z_partial/pallas_call | solution.py:267
  58.8 2.0 %collective-permute-done.17.refs_1_ = bf16[512,256]{1,0:T(8,128)(2,1)S(1)} collective-permute-done((bf16[512,256]{1,0:T(8,128)(2,1)S(1)}, bf16[512,256]{1,0:T(8,128)(2,1)S(1)}, u32[]{:S(2)}, u32[]{:S(2)}) %collective-permute-start.17) | collective-permute-done | bytes 262176 | tf_op jit(solution)/shard_map/ppermute | solution.py:505
  60.8 5.6 %collective-permute-done.18.refs_3_ = bf16[512,256]{1,0:T(8,128)(2,1)S(1)} collective-permute-done((bf16[512,256]{1,0:T(8,128)(2,1)S(1)}, bf16[512,256]{1,0:T(8,128)(2,1)S(1)}, u32[]{:S(2)}, u32[]{:S(2)}) %collective-permute-start.18) | collective-permute-done | bytes 262176 | tf_op jit(solution)/shard_map/ppermute | solution.py:505
  66.5 5.6 %collective-permute-done.19.refs_5_ = bf16[512,256]{1,0:T(8,128)(2,1)S(1)} collective-permute-done((bf16[512,256]{1,0:T(8,128)(2,1)S(1)}, bf16[512,256]{1,0:T(8,128)(2,1)S(1)}, u32[]{:S(2)}, u32[]{:S(2)}) %collective-permute-start.19) | collective-permute-done | bytes 262176 | tf_op jit(solution)/shard_map/ppermute | solution.py:505
  73.0 4.5 %collective-permute-done.12.refs_1_ = bf16[512,256]{1,0:T(8,128)(2,1)S(1)} collective-permute-done((bf16[512,256]{1,0:T(8,128)(2,1)S(1)}, bf16[512,256]{1,0:T(8,128)(2,1)S(1)}, u32[]{:S(2)}, u32[]{:S(2)}) %collective-permute-start.12) | collective-permute-done | bytes 262176 | tf_op jit(solution)/shard_map/ppermute | solution.py:505
  78.4 1.8 %input_partial.3 = bf16[4,512,256]{2,1,0:T(8,128)(2,1)S(1)} custom-call(bf16[4096,512]{1,0:T(8,128)(2,1)S(1)} %get-tuple-element.30.w_ref.refs_0_, bf16[4096,512]{1,0:T(8,128)(2,1)S(1)} %get-tuple-element.31.refs_8_.refs_1_, bf16[4096,512]{1,0:T(8,128)(2,1)S(1)} %get-tuple-element.32.refs_9_.refs_2_, bf16[1536,256]{1,0:T(8,128)(2,1)S(1)} %bitcast.3), custom_call_target="tpu_custom_call" | custom-call | flops 393216 | bytes 1792 | tf_op jit(solution)/shard_map/input_partial/pallas_call | solution.py:487
  80.3 1.8 %input_partial.2.same_ref = bf16[4,512,256]{2,1,0:T(8,128)(2,1)S(1)} custom-call(bf16[4096,512]{1,0:T(8,128)(2,1)S(1)} %get-tuple-element.30.w_ref.refs_0_, bf16[4096,512]{1,0:T(8,128)(2,1)S(1)} %get-tuple-element.31.refs_8_.refs_1_, bf16[4096,512]{1,0:T(8,128)(2,1)S(1)} %get-tuple-element.32.refs_9_.refs_2_, bf16[1536,256]{1,0:T(8,128)(2,1)S(1)} %bitcast.4), custom_call_target="tpu_custom_call" | custom-call | flops 393216 | bytes 1792 | tf_op jit(solution)/shard_map/input_partial/pallas_call | solution.py:487
  83.2 1.6 %collective-permute-start.24 = (bf16[512,128]{1,0:T(8,128)(2,1)S(1)}, bf16[512,128]{1,0:T(8,128)(2,1)S(1)}, u32[]{:S(2)}, u32[]{:S(2)}) collective-permute-start(bf16[512,128]{1,0:T(8,128)(2,1)S(1)} %get-tuple-element.49), channel_id=1, source_target_pairs={{0,2},{1,3},{2,0},{3,1},{4,6},{5,7},{6,4},{7,5},{8,10},{9,11},{10,... | collective-permute-start | bytes 393224 | tf_op jit(solution)/shard_map/ppermute | solution.py:501
  84.8 1.6 %collective-permute-start.25 = (bf16[512,128]{1,0:T(8,128)(2,1)S(1)}, bf16[512,128]{1,0:T(8,128)(2,1)S(1)}, u32[]{:S(2)}, u32[]{:S(2)}) collective-permute-start(bf16[512,128]{1,0:T(8,128)(2,1)S(1)} %get-tuple-element.50), channel_id=1, source_target_pairs={{0,4},{1,5},{2,6},{3,7},{4,0},{5,1},{6,2},{7,3},{8,12},{9,13},{10,... | collective-permute-start | bytes 393224 | tf_op jit(solution)/shard_map/ppermute | solution.py:501
  86.8 1.6 %collective-permute-start.21 = (bf16[512,128]{1,0:T(8,128)(2,1)S(1)}, bf16[512,128]{1,0:T(8,128)(2,1)S(1)}, u32[]{:S(2)}, u32[]{:S(2)}) collective-permute-start(bf16[512,128]{1,0:T(8,128)(2,1)S(1)} %get-tuple-element.45), channel_id=1, source_target_pairs={{0,2},{1,3},{2,0},{3,1},{4,6},{5,7},{6,4},{7,5},{8,10},{9,11},{10,... | collective-permute-start | bytes 393224 | tf_op jit(solution)/shard_map/ppermute | solution.py:501
  88.3 1.6 %collective-permute-start.22 = (bf16[512,128]{1,0:T(8,128)(2,1)S(1)}, bf16[512,128]{1,0:T(8,128)(2,1)S(1)}, u32[]{:S(2)}, u32[]{:S(2)}) collective-permute-start(bf16[512,128]{1,0:T(8,128)(2,1)S(1)} %get-tuple-element.46), channel_id=1, source_target_pairs={{0,4},{1,5},{2,6},{3,7},{4,0},{5,1},{6,2},{7,3},{8,12},{9,13},{10,... | collective-permute-start | bytes 393224 | tf_op jit(solution)/shard_map/ppermute | solution.py:501
  90.0 1.6 %collective-permute-start.23 = (bf16[512,128]{1,0:T(8,128)(2,1)S(1)}, bf16[512,128]{1,0:T(8,128)(2,1)S(1)}, u32[]{:S(2)}, u32[]{:S(2)}) collective-permute-start(bf16[512,128]{1,0:T(8,128)(2,1)S(1)} %get-tuple-element.47), channel_id=1, source_target_pairs={{0,6},{1,7},{2,4},{3,5},{4,2},{5,3},{6,0},{7,1},{8,14},{9,15},{10,... | collective-permute-start | bytes 393224 | tf_op jit(solution)/shard_map/ppermute | solution.py:501
  91.6 2.3 %collective-permute-done.26.refs_3_ = bf16[512,128]{1,0:T(8,128)(2,1)S(1)} collective-permute-done((bf16[512,128]{1,0:T(8,128)(2,1)S(1)}, bf16[512,128]{1,0:T(8,128)(2,1)S(1)}, u32[]{:S(2)}, u32[]{:S(2)}) %collective-permute-start.26) | collective-permute-done | bytes 131104 | tf_op jit(solution)/shard_map/ppermute | solution.py:501
  93.9 1.8 %collective-permute-start.27 = (bf16[512,128]{1,0:T(8,128)(2,1)S(1)}, bf16[512,128]{1,0:T(8,128)(2,1)S(1)}, u32[]{:S(2)}, u32[]{:S(2)}) collective-permute-start(bf16[512,128]{1,0:T(8,128)(2,1)S(1)} %total.3), channel_id=1, source_target_pairs={{0,16},{16,0},{1,17},{17,1},{2,18},{18,2},{3,19},{19,3},{4,20},{20... | collective-permute-start | bytes 393224 | tf_op jit(solution)/shard_map/ppermute | solution.py:505
  96.8 1.6 %collective-permute-done.23.refs_3_ = bf16[512,128]{1,0:T(8,128)(2,1)S(1)} collective-permute-done((bf16[512,128]{1,0:T(8,128)(2,1)S(1)}, bf16[512,128]{1,0:T(8,128)(2,1)S(1)}, u32[]{:S(2)}, u32[]{:S(2)}) %collective-permute-start.23) | collective-permute-done | bytes 131104 | tf_op jit(solution)/shard_map/ppermute | solution.py:501
  99.0 4.5 %collective-permute-start.28 = (bf16[512,128]{1,0:T(8,128)(2,1)S(1)}, bf16[512,128]{1,0:T(8,128)(2,1)S(1)}, u32[]{:S(2)}, u32[]{:S(2)}) collective-permute-start(bf16[512,128]{1,0:T(8,128)(2,1)S(1)} %get-tuple-element.53), channel_id=1, source_target_pairs={{0,8},{1,9},{2,10},{3,11},{4,12},{5,13},{6,14},{7,15},{8,0},{9,1},... | collective-permute-start | bytes 393224 | tf_op jit(solution)/shard_map/ppermute | solution.py:501
  103.5 5.3 %taps_gradient.1 = f32[32,128]{1,0:T(8,128)} custom-call(bf16[512,256]{1,0:T(8,128)(2,1)S(1)} %get-tuple-element.54.prod_ref, bf16[512,256]{1,0:T(8,128)(2,1)S(1)} %get-tuple-element.55.grad_ref), custom_call_target="tpu_custom_call" | custom-call | flops 131072 | bytes 768 | tf_op jit(solution)/shard_map/taps_gradient/pallas_call | solution.py:464
  (48 shorter events, 12.5 us)
Async XLA Ops:
  1.6 9.7 %collective-permute-start = (bf16[256,512]{1,0:T(8,128)(2,1)S(1)}, bf16[256,512]{1,0:T(8,128)(2,1)S(1)}, u32[]{:S(2)}, u32[]{:S(2)}) collective-permute-start(bf16[256,512]{1,0:T(8,128)(2,1)S(1)} %stacked.1.both_ref), channel_id=1, source_target_pairs={{0,8},{1,9},{2,10},{3,11},{4,12},{5,13},{6,14},{7,15},{8,24},{9,25... | collective-permute-start | bytes 786440 | tf_op jit(solution)/shard_map/ppermute | solution.py:515
  5.7 5.6 %collective-permute-start.1 = (bf16[256,512]{1,0:T(8,128)(2,1)S(1)}, bf16[256,512]{1,0:T(8,128)(2,1)S(1)}, u32[]{:S(2)}, u32[]{:S(2)}) collective-permute-start(bf16[256,512]{1,0:T(8,128)(2,1)S(1)} %stacked.1.both_ref), channel_id=1, source_target_pairs={{8,16},{9,17},{10,18},{11,19},{12,20},{13,21},{14,22},{15,23},{16,... | collective-permute-start | bytes 786440 | tf_op jit(solution)/shard_map/ppermute | solution.py:515
  11.4 17.5 %collective-permute-start.2 = (bf16[256,512]{1,0:T(8,128)(2,1)S(1)}, bf16[256,512]{1,0:T(8,128)(2,1)S(1)}, u32[]{:S(2)}, u32[]{:S(2)}) collective-permute-start(bf16[256,512]{1,0:T(8,128)(2,1)S(1)} %get-tuple-element.29.refs_0_), channel_id=1, source_target_pairs={{0,2},{1,3},{2,0},{3,1},{4,6},{5,7},{6,4},{7,5},{8,10},{9,11},{10,... | collective-permute-start | bytes 786440 | tf_op jit(solution)/shard_map/ppermute | solution.py:501
  12.9 15.9 %collective-permute-start.3 = (bf16[256,512]{1,0:T(8,128)(2,1)S(1)}, bf16[256,512]{1,0:T(8,128)(2,1)S(1)}, u32[]{:S(2)}, u32[]{:S(2)}) collective-permute-start(bf16[256,512]{1,0:T(8,128)(2,1)S(1)} %get-tuple-element.29.refs_0_), channel_id=1, source_target_pairs={{0,4},{1,5},{2,6},{3,7},{4,0},{5,1},{6,2},{7,3},{8,12},{9,13},{10,... | collective-permute-start | bytes 786440 | tf_op jit(solution)/shard_map/ppermute | solution.py:501
  20.0 13.0 %collective-permute-start.4 = (bf16[256,512]{1,0:T(8,128)(2,1)S(1)}, bf16[256,512]{1,0:T(8,128)(2,1)S(1)}, u32[]{:S(2)}, u32[]{:S(2)}) collective-permute-start(bf16[256,512]{1,0:T(8,128)(2,1)S(1)} %get-tuple-element.29.refs_0_), channel_id=1, source_target_pairs={{0,6},{1,7},{2,4},{3,5},{4,2},{5,3},{6,0},{7,1},{8,14},{9,15},{10,... | collective-permute-start | bytes 786440 | tf_op jit(solution)/shard_map/ppermute | solution.py:501
  20.0 16.5 %collective-permute-start.13 = (bf16[256,512]{1,0:T(8,128)(2,1)S(1)}, bf16[256,512]{1,0:T(8,128)(2,1)S(1)}, u32[]{:S(2)}, u32[]{:S(2)}) collective-permute-start(bf16[256,512]{1,0:T(8,128)(2,1)S(1)} %get-tuple-element.29.refs_0_), channel_id=1, source_target_pairs={{0,1},{1,0},{2,3},{3,2},{4,5},{5,4},{6,7},{7,6},{8,9},{9,8},{10,11... | collective-permute-start | bytes 786440 | tf_op jit(solution)/shard_map/ppermute | solution.py:501
  20.0 0.7 copy-start.1
  21.7 0.9 copy-start
  32.9 8.4 %collective-permute-start.5 = (bf16[256,512]{1,0:T(8,128)(2,1)S(1)}, bf16[256,512]{1,0:T(8,128)(2,1)S(1)}, u32[]{:S(2)}, u32[]{:S(2)}) collective-permute-start(bf16[256,512]{1,0:T(8,128)(2,1)S(1)} %copied.1.refs_0_), channel_id=1, source_target_pairs={{0,2},{1,3},{2,0},{3,1},{4,6},{5,7},{6,4},{7,5},{8,10},{9,11},{10,... | collective-permute-start | bytes 786440 | tf_op jit(solution)/shard_map/ppermute | solution.py:501
  33.5 9.2 %collective-permute-start.6 = (bf16[256,512]{1,0:T(8,128)(2,1)S(1)}, bf16[256,512]{1,0:T(8,128)(2,1)S(1)}, u32[]{:S(2)}, u32[]{:S(2)}) collective-permute-start(bf16[256,512]{1,0:T(8,128)(2,1)S(1)} %copied.1.refs_0_), channel_id=1, source_target_pairs={{0,4},{1,5},{2,6},{3,7},{4,0},{5,1},{6,2},{7,3},{8,12},{9,13},{10,... | collective-permute-start | bytes 786440 | tf_op jit(solution)/shard_map/ppermute | solution.py:501
  35.1 13.0 %collective-permute-start.7 = (bf16[256,512]{1,0:T(8,128)(2,1)S(1)}, bf16[256,512]{1,0:T(8,128)(2,1)S(1)}, u32[]{:S(2)}, u32[]{:S(2)}) collective-permute-start(bf16[256,512]{1,0:T(8,128)(2,1)S(1)} %copied.1.refs_0_), channel_id=1, source_target_pairs={{0,6},{1,7},{2,4},{3,5},{4,2},{5,3},{6,0},{7,1},{8,14},{9,15},{10,... | collective-permute-start | bytes 786440 | tf_op jit(solution)/shard_map/ppermute | solution.py:501
  36.5 11.6 %collective-permute-start.14 = (bf16[256,512]{1,0:T(8,128)(2,1)S(1)}, bf16[256,512]{1,0:T(8,128)(2,1)S(1)}, u32[]{:S(2)}, u32[]{:S(2)}) collective-permute-start(bf16[256,512]{1,0:T(8,128)(2,1)S(1)} %collective-permute-done.2.refs_2_.refs_1_), channel_id=1, source_target_pairs={{0,1},{1,0},{2,3},{3,2},{4,5},{5,4},{6,7},{7,6},{8,9},{9,8},{10,11... | collective-permute-start | bytes 786440 | tf_op jit(solution)/shard_map/ppermute | solution.py:501
  36.5 12.1 %collective-permute-start.15 = (bf16[256,512]{1,0:T(8,128)(2,1)S(1)}, bf16[256,512]{1,0:T(8,128)(2,1)S(1)}, u32[]{:S(2)}, u32[]{:S(2)}) collective-permute-start(bf16[256,512]{1,0:T(8,128)(2,1)S(1)} %collective-permute-done.3.refs_3_.refs_2_), channel_id=1, source_target_pairs={{0,1},{1,0},{2,3},{3,2},{4,5},{5,4},{6,7},{7,6},{8,9},{9,8},{10,11... | collective-permute-start | bytes 786440 | tf_op jit(solution)/shard_map/ppermute | solution.py:501
  41.3 7.3 %collective-permute-start.16 = (bf16[256,512]{1,0:T(8,128)(2,1)S(1)}, bf16[256,512]{1,0:T(8,128)(2,1)S(1)}, u32[]{:S(2)}, u32[]{:S(2)}) collective-permute-start(bf16[256,512]{1,0:T(8,128)(2,1)S(1)} %collective-permute-done.4.refs_4_.refs_3_), channel_id=1, source_target_pairs={{0,1},{1,0},{2,3},{3,2},{4,5},{5,4},{6,7},{7,6},{8,9},{9,8},{10,11... | collective-permute-start | bytes 786440 | tf_op jit(solution)/shard_map/ppermute | solution.py:501
  42.8 12.3 %collective-permute-start.8 = (bf16[256,512]{1,0:T(8,128)(2,1)S(1)}, bf16[256,512]{1,0:T(8,128)(2,1)S(1)}, u32[]{:S(2)}, u32[]{:S(2)}) collective-permute-start(bf16[256,512]{1,0:T(8,128)(2,1)S(1)} %copied.1.refs_0_), channel_id=1, source_target_pairs={{0,1},{1,0},{2,3},{3,2},{4,5},{5,4},{6,7},{7,6},{8,9},{9,8},{10,11... | collective-permute-start | bytes 786440 | tf_op jit(solution)/shard_map/ppermute | solution.py:501
  48.0 7.1 %collective-permute-start.9 = (bf16[256,512]{1,0:T(8,128)(2,1)S(1)}, bf16[256,512]{1,0:T(8,128)(2,1)S(1)}, u32[]{:S(2)}, u32[]{:S(2)}) collective-permute-start(bf16[256,512]{1,0:T(8,128)(2,1)S(1)} %collective-permute-done.5.refs_1_), channel_id=1, source_target_pairs={{0,1},{1,0},{2,3},{3,2},{4,5},{5,4},{6,7},{7,6},{8,9},{9,8},{10,11... | collective-permute-start | bytes 786440 | tf_op jit(solution)/shard_map/ppermute | solution.py:501
  48.1 9.1 %collective-permute-start.10 = (bf16[256,512]{1,0:T(8,128)(2,1)S(1)}, bf16[256,512]{1,0:T(8,128)(2,1)S(1)}, u32[]{:S(2)}, u32[]{:S(2)}) collective-permute-start(bf16[256,512]{1,0:T(8,128)(2,1)S(1)} %collective-permute-done.6.refs_2_), channel_id=1, source_target_pairs={{0,1},{1,0},{2,3},{3,2},{4,5},{5,4},{6,7},{7,6},{8,9},{9,8},{10,11... | collective-permute-start | bytes 786440 | tf_op jit(solution)/shard_map/ppermute | solution.py:501
  48.6 8.6 %collective-permute-start.11 = (bf16[256,512]{1,0:T(8,128)(2,1)S(1)}, bf16[256,512]{1,0:T(8,128)(2,1)S(1)}, u32[]{:S(2)}, u32[]{:S(2)}) collective-permute-start(bf16[256,512]{1,0:T(8,128)(2,1)S(1)} %collective-permute-done.7.refs_3_), channel_id=1, source_target_pairs={{0,1},{1,0},{2,3},{3,2},{4,5},{5,4},{6,7},{7,6},{8,9},{9,8},{10,11... | collective-permute-start | bytes 786440 | tf_op jit(solution)/shard_map/ppermute | solution.py:501
  51.3 9.5 %collective-permute-start.17 = (bf16[512,256]{1,0:T(8,128)(2,1)S(1)}, bf16[512,256]{1,0:T(8,128)(2,1)S(1)}, u32[]{:S(2)}, u32[]{:S(2)}) collective-permute-start(bf16[512,256]{1,0:T(8,128)(2,1)S(1)} %get-tuple-element.37.refs_0_), channel_id=1, source_target_pairs={{0,16},{16,0},{1,17},{17,1},{2,18},{18,2},{3,19},{19,3},{4,20},{20... | collective-permute-start | bytes 786440 | tf_op jit(solution)/shard_map/ppermute | solution.py:505
  55.1 11.4 %collective-permute-start.18 = (bf16[512,256]{1,0:T(8,128)(2,1)S(1)}, bf16[512,256]{1,0:T(8,128)(2,1)S(1)}, u32[]{:S(2)}, u32[]{:S(2)}) collective-permute-start(bf16[512,256]{1,0:T(8,128)(2,1)S(1)} %get-tuple-element.38.refs_2_), channel_id=1, source_target_pairs={{0,16},{16,0},{1,17},{17,1},{2,18},{18,2},{3,19},{19,3},{4,20},{20... | collective-permute-start | bytes 786440 | tf_op jit(solution)/shard_map/ppermute | solution.py:505
  55.2 16.9 %collective-permute-start.19 = (bf16[512,256]{1,0:T(8,128)(2,1)S(1)}, bf16[512,256]{1,0:T(8,128)(2,1)S(1)}, u32[]{:S(2)}, u32[]{:S(2)}) collective-permute-start(bf16[512,256]{1,0:T(8,128)(2,1)S(1)} %proj_queries.1.refs_4_), channel_id=1, source_target_pairs={{0,16},{16,0},{1,17},{17,1},{2,18},{18,2},{3,19},{19,3},{4,20},{20... | collective-permute-start | bytes 786440 | tf_op jit(solution)/shard_map/ppermute | solution.py:505
  58.7 18.8 %collective-permute-start.12 = (bf16[512,256]{1,0:T(8,128)(2,1)S(1)}, bf16[512,256]{1,0:T(8,128)(2,1)S(1)}, u32[]{:S(2)}, u32[]{:S(2)}) collective-permute-start(bf16[512,256]{1,0:T(8,128)(2,1)S(1)} %grad_z_partial.1.refs_0_), channel_id=1, source_target_pairs={{0,16},{16,0},{1,17},{17,1},{2,18},{18,2},{3,19},{19,3},{4,20},{20... | collective-permute-start | bytes 786440 | tf_op jit(solution)/shard_map/ppermute | solution.py:505
  80.2 2.7 %collective-permute-start.20 = (bf16[4,512,256]{2,1,0:T(8,128)(2,1)S(1)}, bf16[4,512,256]{2,1,0:T(8,128)(2,1)S(1)}, u32[]{:S(2)}, u32[]{:S(2)}) collective-permute-start(bf16[4,512,256]{2,1,0:T(8,128)(2,1)S(1)} %input_partial.3), channel_id=1, source_target_pairs={{0,1},{1,0},{2,3},{3,2},{4,5},{5,4},{6,7},{7,6},{8,9},{9,8},{10,11... | collective-permute-start | bytes 3145736 | tf_op jit(solution)/shard_map/ppermute | solution.py:501
  83.2 6.8 %collective-permute-start.24 = (bf16[512,128]{1,0:T(8,128)(2,1)S(1)}, bf16[512,128]{1,0:T(8,128)(2,1)S(1)}, u32[]{:S(2)}, u32[]{:S(2)}) collective-permute-start(bf16[512,128]{1,0:T(8,128)(2,1)S(1)} %get-tuple-element.49), channel_id=1, source_target_pairs={{0,2},{1,3},{2,0},{3,1},{4,6},{5,7},{6,4},{7,5},{8,10},{9,11},{10,... | collective-permute-start | bytes 393224 | tf_op jit(solution)/shard_map/ppermute | solution.py:501
  84.8 6.7 %collective-permute-start.25 = (bf16[512,128]{1,0:T(8,128)(2,1)S(1)}, bf16[512,128]{1,0:T(8,128)(2,1)S(1)}, u32[]{:S(2)}, u32[]{:S(2)}) collective-permute-start(bf16[512,128]{1,0:T(8,128)(2,1)S(1)} %get-tuple-element.50), channel_id=1, source_target_pairs={{0,4},{1,5},{2,6},{3,7},{4,0},{5,1},{6,2},{7,3},{8,12},{9,13},{10,... | collective-permute-start | bytes 393224 | tf_op jit(solution)/shard_map/ppermute | solution.py:501
  86.5 7.4 %collective-permute-start.26 = (bf16[512,128]{1,0:T(8,128)(2,1)S(1)}, bf16[512,128]{1,0:T(8,128)(2,1)S(1)}, u32[]{:S(2)}, u32[]{:S(2)}) collective-permute-start(bf16[512,128]{1,0:T(8,128)(2,1)S(1)} %get-tuple-element.51), channel_id=1, source_target_pairs={{0,6},{1,7},{2,4},{3,5},{4,2},{5,3},{6,0},{7,1},{8,14},{9,15},{10,... | collective-permute-start | bytes 393224 | tf_op jit(solution)/shard_map/ppermute | solution.py:501
  86.8 9.0 %collective-permute-start.21 = (bf16[512,128]{1,0:T(8,128)(2,1)S(1)}, bf16[512,128]{1,0:T(8,128)(2,1)S(1)}, u32[]{:S(2)}, u32[]{:S(2)}) collective-permute-start(bf16[512,128]{1,0:T(8,128)(2,1)S(1)} %get-tuple-element.45), channel_id=1, source_target_pairs={{0,2},{1,3},{2,0},{3,1},{4,6},{5,7},{6,4},{7,5},{8,10},{9,11},{10,... | collective-permute-start | bytes 393224 | tf_op jit(solution)/shard_map/ppermute | solution.py:501
  88.3 8.5 %collective-permute-start.22 = (bf16[512,128]{1,0:T(8,128)(2,1)S(1)}, bf16[512,128]{1,0:T(8,128)(2,1)S(1)}, u32[]{:S(2)}, u32[]{:S(2)}) collective-permute-start(bf16[512,128]{1,0:T(8,128)(2,1)S(1)} %get-tuple-element.46), channel_id=1, source_target_pairs={{0,4},{1,5},{2,6},{3,7},{4,0},{5,1},{6,2},{7,3},{8,12},{9,13},{10,... | collective-permute-start | bytes 393224 | tf_op jit(solution)/shard_map/ppermute | solution.py:501
  90.0 8.5 %collective-permute-start.23 = (bf16[512,128]{1,0:T(8,128)(2,1)S(1)}, bf16[512,128]{1,0:T(8,128)(2,1)S(1)}, u32[]{:S(2)}, u32[]{:S(2)}) collective-permute-start(bf16[512,128]{1,0:T(8,128)(2,1)S(1)} %get-tuple-element.47), channel_id=1, source_target_pairs={{0,6},{1,7},{2,4},{3,5},{4,2},{5,3},{6,0},{7,1},{8,14},{9,15},{10,... | collective-permute-start | bytes 393224 | tf_op jit(solution)/shard_map/ppermute | solution.py:501
  93.9 5.0 %collective-permute-start.27 = (bf16[512,128]{1,0:T(8,128)(2,1)S(1)}, bf16[512,128]{1,0:T(8,128)(2,1)S(1)}, u32[]{:S(2)}, u32[]{:S(2)}) collective-permute-start(bf16[512,128]{1,0:T(8,128)(2,1)S(1)} %total.3), channel_id=1, source_target_pairs={{0,16},{16,0},{1,17},{17,1},{2,18},{18,2},{3,19},{19,3},{4,20},{20... | collective-permute-start | bytes 393224 | tf_op jit(solution)/shard_map/ppermute | solution.py:505
  99.0 10.2 %collective-permute-start.28 = (bf16[512,128]{1,0:T(8,128)(2,1)S(1)}, bf16[512,128]{1,0:T(8,128)(2,1)S(1)}, u32[]{:S(2)}, u32[]{:S(2)}) collective-permute-start(bf16[512,128]{1,0:T(8,128)(2,1)S(1)} %get-tuple-element.53), channel_id=1, source_target_pairs={{0,8},{1,9},{2,10},{3,11},{4,12},{5,13},{6,14},{7,15},{8,0},{9,1},... | collective-permute-start | bytes 393224 | tf_op jit(solution)/shard_map/ppermute | solution.py:501

commit v3 on v2

--- a/solution.py
+++ b/solution.py
@@ -77,7 +77,8 @@
     )(in_hbm(first), in_hbm(second))
 
 
-def own_kernel(both_ref, turned_ref, crossed_ref, *out_refs):
+def own_kernel(both_ref, turned_ref, crossed_ref, *refs):
+    out_refs = refs[-2:]
     run = both_ref.shape[0] // 2
     home = at_home()
     for n, out_ref in enumerate(out_refs):
@@ -94,17 +95,35 @@
             out_ref[run:] = crossed_ref[at]
 
 
-def own_slices(both, turned, crossed):
+def own_slices(both, turned, crossed, *earlier):
     out = jax.ShapeDtypeStruct(both.shape, both.dtype)
     return pl.pallas_call(
         own_kernel,
-        in_specs=[VMEM_SPEC] * 3,
+        in_specs=[VMEM_SPEC] * 3 + [LATER_SPEC] * len(earlier),
         out_specs=[VMEM_SPEC] * 2,
         out_shape=[out, out],
         compiler_params=params(8),
         cost_estimate=cost(0, 10 * both.size),
         name="own_slices",
-    )(both, turned, crossed)
+    )(both, turned, crossed, *earlier)
+
+
+def relay_kernel(*refs):
+    del refs
+
+
+def relayed(arrays, *earlier):
+    count = len(arrays)
+    return pl.pallas_call(
+        relay_kernel,
+        in_specs=[LATER_SPEC] * (count + len(earlier)),
+        out_specs=[LATER_SPEC] * count,
+        out_shape=[jax.ShapeDtypeStruct(array.shape, array.dtype) for array in arrays],
+        input_output_aliases={n: n for n in range(count)},
+        compiler_params=params(8),
+        cost_estimate=cost(0, 0),
+        name="relayed",
+    )(*arrays, *earlier)
 
 
 def in_vmem(array):
@@ -205,49 +224,29 @@
         held[:, piece_rows(masks, n, ref.shape[1])] = ref[...]
 
 
-def proj_part(runs, held_ref, w_ref, out_ref):
-    run = held_ref.shape[0] // runs
-    total = jnp.dot(held_ref[...], w_ref[...], preferred_element_type=F32)
-    for h, start in enumerate(run_starts(runs, run)):
-        out_ref[:, pl.ds(start, run)] = total[h * run : (h + 1) * run].T.astype(BF16)
-
-
-def first_proj_kernel(masks, runs, *refs):
-    xs, (key_ref, value_ref, key_out, value_out, held_ref) = refs[:-5], refs[-5:]
-    assembled(masks, xs, held_ref)
-    proj_part(runs, held_ref, key_ref, key_out)
-    proj_part(runs, held_ref, value_ref, value_out)
-
-
-def more_proj_kernel(runs, held_ref, w_ref, out_ref):
-    proj_part(runs, held_ref, w_ref, out_ref)
+def proj_kernel(masks, runs, *refs):
+    xs, (out_ref, held) = refs[:-5], refs[-2:]
+    assembled(masks, xs, held)
+    run = held.shape[0] // runs
+    for j, w_ref in enumerate(refs[-5:-2]):
+        total = jnp.dot(held[...], w_ref[...], preferred_element_type=F32)
+        for h, start in enumerate(run_starts(runs, run)):
+            out_ref[j, :, pl.ds(start, run)] = total[h * run : (h + 1) * run].T.astype(BF16)
 
 
 def proj_partial(xs, masks, runs, weights):
     tokens = xs[0].shape[0]
     depth, channels = weights[0].shape
-    flops = 2 * tokens * depth * channels
-    weights = [in_vmem(weight) for weight in weights]
-    part = jax.ShapeDtypeStruct((channels, tokens), BF16)
-    *keys, held = pl.pallas_call(
-        functools.partial(first_proj_kernel, masks, runs),
-        in_specs=[VMEM_SPEC] * (len(xs) + 2),
-        out_specs=[VMEM_SPEC] * 3,
-        out_shape=[part, part, pltpu.VMEM((tokens, depth), BF16)],
+    return pl.pallas_call(
+        functools.partial(proj_kernel, masks, runs),
+        in_specs=[VMEM_SPEC] * (len(xs) + 3),
+        out_specs=VMEM_SPEC,
+        out_shape=jax.ShapeDtypeStruct((3, channels, tokens), BF16),
+        scratch_shapes=[pltpu.VMEM((tokens, depth), BF16)],
         compiler_params=params(16),
-        cost_estimate=cost(2 * flops, 4 * depth * channels),
-        name="proj_keys_values",
-    )(*xs, *weights[1:])
-    others = pl.pallas_call(
-        functools.partial(more_proj_kernel, runs),
-        in_specs=[VMEM_SPEC] * 2,
-        out_specs=VMEM_SPEC,
-        out_shape=part,
-        compiler_params=params(16),
-        cost_estimate=cost(flops, 2 * depth * channels),
-        name="proj_queries",
-    )(held, weights[0])
-    return keys, others
+        cost_estimate=cost(6 * tokens * depth * channels, 6 * depth * channels),
+        name="proj_partial",
+    )(*xs, *[in_vmem(weight) for weight in weights])
 
 
 def grad_z_kernel(masks, runs, *refs):
@@ -338,18 +337,17 @@
     return jnp.concatenate([array[i * rows : (i + 1) * rows] for i in range(blocks)], 1)
 
 
-def summed(refs):
-    total = refs[0][...].astype(F32)
+def summed(refs, part):
+    total = refs[0][part].astype(F32)
     for ref in refs[1:]:
-        total = total + ref[...].astype(F32)
+        total = total + ref[part].astype(F32)
     return total.astype(BF16)
 
 
 def conv_kernel(parts, groups, *refs):
-    keys, values, queries = (refs[n * parts : (n + 1) * parts] for n in range(3))
-    past_ref, proj_ref, prod_ref, conv_ref = refs[3 * parts :]
-    key, value = summed(keys), summed(values)
-    proj_ref[0] = summed(queries)
+    shares, (past_ref, proj_ref, prod_ref, conv_ref) = refs[:parts], refs[parts:]
+    key, value = summed(shares, 1), summed(shares, 2)
+    proj_ref[0] = summed(shares, 0)
     proj_ref[1] = key
     proj_ref[2] = value
     product = (key.astype(F32) * value.astype(F32)).astype(BF16)
@@ -362,19 +360,20 @@
         conv_ref[rows] = unstacked(result, tokens // BLOCK)
 
 
-def conv_forward(keys, values, queries, past):
-    channels, tokens = keys[0].shape
+def conv_forward(shares, past):
+    _, channels, tokens = shares[0].shape
     groups = past.shape[0]
     steps = max(1, groups // 8)
     chunk = channels // steps
-    parts = len(keys)
+    parts = len(shares)
+    three = pl.BlockSpec((3, chunk, tokens), lambda i: (0, i, 0))
     one = pl.BlockSpec((chunk, tokens), lambda i: (i, 0))
     return pl.pallas_call(
         functools.partial(conv_kernel, parts, groups // steps),
         grid=(steps,),
-        in_specs=[one] * (3 * parts)
+        in_specs=[three] * parts
         + [pl.BlockSpec((groups // steps,) + past.shape[1:], lambda i: (i, 0, 0))],
-        out_specs=[pl.BlockSpec((3, chunk, tokens), lambda i: (0, i, 0)), one, one],
+        out_specs=[three, one, one],
         out_shape=[
             jax.ShapeDtypeStruct((3, channels, tokens), BF16),
             jax.ShapeDtypeStruct((channels, tokens), BF16),
@@ -383,7 +382,7 @@
         compiler_params=params(16),
         cost_estimate=cost(4 * channels * tokens * BLOCK * 8, channels * tokens * 24),
         name="conv_forward",
-    )(*keys, *values, *queries, past)
+    )(*shares, past)
 
 
 def conv_back_kernel(parts, groups, *refs):
@@ -639,16 +638,16 @@
 def on_small_slice(tokens, values, scales, filters, out_weight, cotangent):
     rows = tokens.shape[1]
     both = stacked(tokens, cotangent)
-    token_own, cot_own = own_slices(both, *first_stage(both))
+    turned, crossed = first_stage(both)
+    weights, out_held, ready = prepared(values, scales, out_weight, both)
+    past, later = toeplitz(filters, both)
+    token_own, cot_own = own_slices(both, turned, crossed, ready, past)
     token_same = second_stage(token_own)
-    weights, out_held, ready = prepared(values, scales, out_weight, token_own)
-    past, later = toeplitz(filters, token_own)
-    cot_own = copied(cot_own, ready, past, *token_same[1:])
+    cot_own = copied(cot_own, *token_same[1:])
     cot_same = second_stage(cot_own)
-    keys, queries = proj_partial(both_cores(token_same), MINE + OTHERS, 2, weights)
-    proj, product, conv = conv_forward(
-        *[[part, other_row(part)] for part in (*keys, queries)], past
-    )
+    proj_part = proj_partial(both_cores(token_same), MINE + OTHERS, 2, weights)
+    cot_same = list(relayed(cot_same, proj_part))
+    proj, product, conv = conv_forward([proj_part, other_row(proj_part)], past)
     z_part = grad_z_partial(both_cores(cot_same), MINE + OTHERS, 2, out_held)
     grad_proj, grad = conv_backward([z_part, other_row(z_part)], proj, conv, later)
     others = input_partial(OTHERS, 4, rows, weights, grad_proj)
@@ -673,8 +672,8 @@
 
     weights, out_held, _ = prepared(values, scales, out_weight)
     past, later = toeplitz(filters)
-    keys, queries = proj_partial(gather(tokens), None, 1, weights)
-    proj, product, conv = conv_forward(*[shares(part) for part in (*keys, queries)], past)
+    proj_part = proj_partial(gather(tokens), None, 1, weights)
+    proj, product, conv = conv_forward(shares(proj_part), past)
     z_part = grad_z_partial(gather(cotangent), None, 1, out_held)
     grad_proj, grad = conv_backward(shares(z_part), proj, conv, later)
     partial = input_partial(None, pieces, piece, weights, grad_proj)

time: 110 us -> 98 us (0.89)
  waiting for transfers between devices: 44.5 us -> 35.1 us
  starting transfers between devices: 37.4 us -> 34.7 us
    ppermute x5 -> x3, waiting for transfers between devices: 18.1 us -> 10.4 us  [other_row(): return lax.ppermute(array, 'fsdp', [(0, 1), (1, 0)])]
    ppermute x22, starting transfers between devices: 26.2 us -> 19.7 us  [across(): return lax.ppermute(array, 'tensor', [(i, i ^ mask) for i in range(16)])]
    ppermute x2, waiting for transfers between devices: 4.94 us -> 0.01 us  [in_square(): return lax.ppermute(array, ('fsdp', 'tensor'), pairs)]
    ppermute x22, waiting for transfers between devices: 21.4 us -> 24.7 us  [across(): return lax.ppermute(array, 'tensor', [(i, i ^ mask) for i in range(16)])]
    ppermute x2, starting transfers between devices: 4.75 us -> 7.29 us  [in_square(): return lax.ppermute(array, ('fsdp', 'tensor'), pairs)]
    ppermute x5 -> x3, starting transfers between devices: 6.39 us -> 7.71 us  [other_row(): return lax.ppermute(array, 'fsdp', [(0, 1), (1, 0)])]
  transfers between devices with their start and end apart: 29 -> 27, of which waited for: 15 -> 18; matrix products, arithmetic and copies ran while one was open for 0% -> 0% of each run, Pallas kernels for 19% -> 21%
where the time goes in v3:
time: 98 us; the launch traced here: 97.8 us
  waiting for transfers between devices  35.1 us (36%)
  starting transfers between devices  34.7 us (35%)
  Pallas kernels  25.6 us (26%)
  local copies, waits for them, and re-layouts  1.6 us (2%)
    ppermute x22, waiting for transfers between devices, across(): return lax.ppermute(array, 'tensor', [(i, i ^ mask) for i in range(16)])  24.7 us
    ppermute x22, starting transfers between devices, across(): return lax.ppermute(array, 'tensor', [(i, i ^ mask) for i in range(16)])  19.7 us
    ppermute x3, waiting for transfers between devices, other_row(): return lax.ppermute(array, 'fsdp', [(0, 1), (1, 0)])  10.4 us
    ppermute x3, starting transfers between devices, other_row(): return lax.ppermute(array, 'fsdp', [(0, 1), (1, 0)])  7.71 us
    ppermute x2, starting transfers between devices, in_square(): return lax.ppermute(array, ('fsdp', 'tensor'), pairs)  7.29 us
    pallas_call x1, Pallas kernels, prepared(): pl.pallas_call(prepare_kernel, in_specs=[LATER_SPEC, VMEM_SPEC, LATER_SPE...  6.18 us
    pallas_call x1, Pallas kernels, taps_gradient(): pl.pallas_call(functools.partial(taps_kernel, groups // steps), grid=(ste...  5.31 us
    pallas_call x1, Pallas kernels, proj_partial(): pl.pallas_call(functools.partial(proj_kernel, masks, runs), in_specs=[VME...  3.79 us
  transfers between devices with their start and end apart: 27, of which 18 were waited for; matrix products, arithmetic and copies ran while one was open for 0% of the time, Pallas kernels for 21%

profile of v3, /device:TPU:0, one launch (start us, length us, event | category | flops | bytes accessed | tf_op | source)
XLA Modules:
  0.0 97.8 jit_solution(9583943283515001093)
XLA Ops:
  0.6 1.0 %stacked.1.refs_0_.both_ref = bf16[256,512]{1,0:T(8,128)(2,1)S(1)} custom-call(bf16[128,512]{1,0:T(8,128)(2,1)} %first_ref.1, bf16[128,512]{1,0:T(8,128)(2,1)} %second_ref.1), custom_call_target="tpu_custom_call" | custom-call | bytes 128 | tf_op jit(solution)/shard_map/stacked/pallas_call | solution.py:68
  2.3 6.6 %collective-permute-start = (bf16[256,512]{1,0:T(8,128)(2,1)S(1)}, bf16[256,512]{1,0:T(8,128)(2,1)S(1)}, u32[]{:S(2)}, u32[]{:S(2)}) collective-permute-start(bf16[256,512]{1,0:T(8,128)(2,1)S(1)} %stacked.1.refs_0_.both_ref), channel_id=1, source_target_pairs={{0,8},{1,9},{2,10},{3,11},{4,12},{5,13},{6,14},{7,15},{8,24},{9,25... | collective-permute-start | bytes 786440 | tf_op jit(solution)/shard_map/ppermute | solution.py:514
  9.6 1.0 %toeplitz.1 = (bf16[32,256,128]{2,1,0:T(8,128)(2,1)S(1)}, bf16[32,256,128]{2,1,0:T(8,128)(2,1)S(1)}) custom-call(f32[32,128]{1,0:T(8,128)S(1)} %copy-done.1, bf16[256,512]{1,0:T(8,128)(2,1)S(1)} %stacked.1.refs_0_.both_ref), custom_call_target="tpu_custom_call" | custom-call | flops 2000 | bytes 1024 | tf_op jit(solution)/shard_map/toeplitz/pallas_call | solution.py:303
  10.7 0.9 copy-done
  11.6 6.2 %prepare.1 = (bf16[4096,512]{1,0:T(8,128)(2,1)S(1)}, bf16[4096,512]{1,0:T(8,128)(2,1)S(1)}, bf16[4096,512]{1,0:T(8,128)(2,1)S(1)}, bf16[512,4096]{1,0:T(8,128)(2,1)S(1)}, f32[8,128]{1,0:T(8,128)S(1)}) custom-call(bf16[3,4096,512]{2,1,0:T(8,128)(2,1)} %bitcast.6, bf16[3,32,512]{2,1,0:T(8,128)(2,1)S(1)} %bitcast.5, bf16[512,4096]{1,0:T(8,128)(2,1)} %ow_ref.1, ...), custom_call_target="tpu_custom_call" | custom-call | flops 6144 | bytes 6144 | tf_op jit(solution)/shard_map/prepare/pallas_call | solution.py:180
  17.9 4.5 %collective-permute-start.4 = (bf16[256,512]{1,0:T(8,128)(2,1)S(1)}, bf16[256,512]{1,0:T(8,128)(2,1)S(1)}, u32[]{:S(2)}, u32[]{:S(2)}) collective-permute-start(bf16[256,512]{1,0:T(8,128)(2,1)S(1)} %get-tuple-element.36.refs_0_), channel_id=1, source_target_pairs={{0,6},{1,7},{2,4},{3,5},{4,2},{5,3},{6,0},{7,1},{8,14},{9,15},{10,... | collective-permute-start | bytes 786440 | tf_op jit(solution)/shard_map/ppermute | solution.py:500
  23.0 6.5 %collective-permute-done.4.refs_2_.refs_3_ = bf16[256,512]{1,0:T(8,128)(2,1)S(1)} collective-permute-done((bf16[256,512]{1,0:T(8,128)(2,1)S(1)}, bf16[256,512]{1,0:T(8,128)(2,1)S(1)}, u32[]{:S(2)}, u32[]{:S(2)}) %collective-permute-start.4) | collective-permute-done | bytes 262176 | tf_op jit(solution)/shard_map/ppermute | solution.py:500
  29.5 4.3 %collective-permute-done.3.refs_1_.refs_2_ = bf16[256,512]{1,0:T(8,128)(2,1)S(1)} collective-permute-done((bf16[256,512]{1,0:T(8,128)(2,1)S(1)}, bf16[256,512]{1,0:T(8,128)(2,1)S(1)}, u32[]{:S(2)}, u32[]{:S(2)}) %collective-permute-start.3) | collective-permute-done | bytes 262176 | tf_op jit(solution)/shard_map/ppermute | solution.py:500
  34.5 2.7 %collective-permute-start.7 = (bf16[256,512]{1,0:T(8,128)(2,1)S(1)}, bf16[256,512]{1,0:T(8,128)(2,1)S(1)}, u32[]{:S(2)}, u32[]{:S(2)}) collective-permute-start(bf16[256,512]{1,0:T(8,128)(2,1)S(1)} %copied.1.refs_0_), channel_id=1, source_target_pairs={{0,6},{1,7},{2,4},{3,5},{4,2},{5,3},{6,0},{7,1},{8,14},{9,15},{10,... | collective-permute-start | bytes 786440 | tf_op jit(solution)/shard_map/ppermute | solution.py:500
  37.2 1.2 %collective-permute-start.5 = (bf16[256,512]{1,0:T(8,128)(2,1)S(1)}, bf16[256,512]{1,0:T(8,128)(2,1)S(1)}, u32[]{:S(2)}, u32[]{:S(2)}) collective-permute-start(bf16[256,512]{1,0:T(8,128)(2,1)S(1)} %copied.1.refs_0_), channel_id=1, source_target_pairs={{0,2},{1,3},{2,0},{3,1},{4,6},{5,7},{6,4},{7,5},{8,10},{9,11},{10,... | collective-permute-start | bytes 786440 | tf_op jit(solution)/shard_map/ppermute | solution.py:500
  38.4 3.8 %proj_partial.1.refs_4_.refs_0_ = bf16[3,512,256]{2,1,0:T(8,128)(2,1)S(1)} custom-call(bf16[256,512]{1,0:T(8,128)(2,1)S(1)} %get-tuple-element.36.refs_0_, bf16[256,512]{1,0:T(8,128)(2,1)S(1)} %collective-permute-done.2.refs_0_.refs_1_, bf16[256,512]{1,0:T(8,128)(2,1)S(1)} %collective-permute-done.3.refs_1_.refs_2_, ...), custom_call_target="tpu_custom_call" | custom-call | flops 786432 | bytes 3072 | tf_op jit(solution)/shard_map/proj_partial/pallas_call | solution.py:240
  42.2 3.0 %collective-permute-start.17 = (bf16[3,512,256]{2,1,0:T(8,128)(2,1)S(1)}, bf16[3,512,256]{2,1,0:T(8,128)(2,1)S(1)}, u32[]{:S(2)}, u32[]{:S(2)}) collective-permute-start(bf16[3,512,256]{2,1,0:T(8,128)(2,1)S(1)} %proj_partial.1.refs_4_.refs_0_), channel_id=1, source_target_pairs={{0,16},{16,0},{1,17},{17,1},{2,18},{18,2},{3,19},{19,3},{4,20},{20... | collective-permute-start | bytes 2359304 | tf_op jit(solution)/shard_map/ppermute | solution.py:504
  45.2 3.9 %collective-permute-done.6.refs_2_ = bf16[256,512]{1,0:T(8,128)(2,1)S(1)} collective-permute-done((bf16[256,512]{1,0:T(8,128)(2,1)S(1)}, bf16[256,512]{1,0:T(8,128)(2,1)S(1)}, u32[]{:S(2)}, u32[]{:S(2)}) %collective-permute-start.6) | collective-permute-done | bytes 262176 | tf_op jit(solution)/shard_map/ppermute | solution.py:500
  52.4 1.5 %grad_z_partial.1.refs_0_ = bf16[512,256]{1,0:T(8,128)(2,1)S(1)} custom-call(bf16[256,512]{1,0:T(8,128)(2,1)S(1)} %get-tuple-element.37.refs_0_, bf16[256,512]{1,0:T(8,128)(2,1)S(1)} %get-tuple-element.38.refs_1_, bf16[256,512]{1,0:T(8,128)(2,1)S(1)} %get-tuple-element.39.refs_2_, bf16[256,512]{1,0:T(8,128)(2,1)S(1)} %get-tuple-element.40.refs_3_, ...), custom_call_target="tpu_custom_call" | custom-call | flops 262144 | bytes 1024 | tf_op jit(solution)/shard_map/grad_z_partial/pallas_call | solution.py:266
  53.9 2.9 %collective-permute-start.16 = (bf16[512,256]{1,0:T(8,128)(2,1)S(1)}, bf16[512,256]{1,0:T(8,128)(2,1)S(1)}, u32[]{:S(2)}, u32[]{:S(2)}) collective-permute-start(bf16[512,256]{1,0:T(8,128)(2,1)S(1)} %grad_z_partial.1.refs_0_), channel_id=1, source_target_pairs={{0,16},{16,0},{1,17},{17,1},{2,18},{18,2},{3,19},{19,3},{4,20},{20... | collective-permute-start | bytes 786440 | tf_op jit(solution)/shard_map/ppermute | solution.py:504
  56.8 6.9 %collective-permute-done.17.refs_1_ = bf16[3,512,256]{2,1,0:T(8,128)(2,1)S(1)} collective-permute-done((bf16[3,512,256]{2,1,0:T(8,128)(2,1)S(1)}, bf16[3,512,256]{2,1,0:T(8,128)(2,1)S(1)}, u32[]{:S(2)}, u32[]{:S(2)}) %collective-permute-start.17) | collective-permute-done | bytes 786464 | tf_op jit(solution)/shard_map/ppermute | solution.py:504
  63.7 1.1 %conv_forward.1 = (bf16[3,512,256]{2,1,0:T(8,128)(2,1)S(1)}, bf16[512,256]{1,0:T(8,128)(2,1)S(1)}, f32[512,256]{1,0:T(8,128)S(1)}) custom-call(bf16[3,512,256]{2,1,0:T(8,128)(2,1)S(1)} %proj_partial.1.refs_4_.refs_0_, bf16[3,512,256]{2,1,0:T(8,128)(2,1)S(1)} %collective-permute-done.17.refs_1_, bf16[32,256,128]{2,1,0:T(8,128)(2,1)S(1)} %get-tuple-element.34.refs_1_.refs_2_), custom_call_target="tpu_custom_call" | custom-call | flops 131072 | bytes 768 | tf_op jit(solution)/shard_map/conv_forward/pallas_call | solution.py:371
  64.7 3.0 %collective-permute-done.16.refs_1_ = bf16[512,256]{1,0:T(8,128)(2,1)S(1)} collective-permute-done((bf16[512,256]{1,0:T(8,128)(2,1)S(1)}, bf16[512,256]{1,0:T(8,128)(2,1)S(1)}, u32[]{:S(2)}, u32[]{:S(2)}) %collective-permute-start.16) | collective-permute-done | bytes 262176 | tf_op jit(solution)/shard_map/ppermute | solution.py:504
  67.7 1.0 %conv_backward.1 = (bf16[3,512,256]{2,1,0:T(8,128)(2,1)S(1)}, bf16[512,256]{1,0:T(8,128)(2,1)S(1)}) custom-call(bf16[512,256]{1,0:T(8,128)(2,1)S(1)} %grad_z_partial.1.refs_0_, bf16[512,256]{1,0:T(8,128)(2,1)S(1)} %collective-permute-done.16.refs_1_, bf16[3,512,256]{2,1,0:T(8,128)(2,1)S(1)} %get-tuple-element.42.refs_2_, ...), custom_call_target="tpu_custom_call" | custom-call | flops 131072 | bytes 768 | tf_op jit(solution)/shard_map/conv_backward/pallas_call | solution.py:414
  68.7 1.8 %input_partial.3 = bf16[4,512,256]{2,1,0:T(8,128)(2,1)S(1)} custom-call(bf16[4096,512]{1,0:T(8,128)(2,1)S(1)} %get-tuple-element.30.refs_8_.refs_0_, bf16[4096,512]{1,0:T(8,128)(2,1)S(1)} %get-tuple-element.31.refs_9_.refs_1_, bf16[4096,512]{1,0:T(8,128)(2,1)S(1)} %get-tuple-element.32.refs_10_.refs_2_, bf16[1536,256]{1,0:T(8,128)(2,1)S(1)} %bitcast.3), custom_call_target="tpu_custom_call" | custom-call | flops 393216 | bytes 1792 | tf_op jit(solution)/shard_map/input_partial/pallas_call | solution.py:486
  70.5 1.8 %input_partial.2.same_ref = bf16[4,512,256]{2,1,0:T(8,128)(2,1)S(1)} custom-call(bf16[4096,512]{1,0:T(8,128)(2,1)S(1)} %get-tuple-element.30.refs_8_.refs_0_, bf16[4096,512]{1,0:T(8,128)(2,1)S(1)} %get-tuple-element.31.refs_9_.refs_1_, bf16[4096,512]{1,0:T(8,128)(2,1)S(1)} %get-tuple-element.32.refs_10_.refs_2_, bf16[1536,256]{1,0:T(8,128)(2,1)S(1)} %bitcast.4), custom_call_target="tpu_custom_call" | custom-call | flops 393216 | bytes 1792 | tf_op jit(solution)/shard_map/input_partial/pallas_call | solution.py:486
  72.3 0.9 collective-permute-done.18.got_ref
  73.4 1.5 %collective-permute-start.22 = (bf16[512,128]{1,0:T(8,128)(2,1)S(1)}, bf16[512,128]{1,0:T(8,128)(2,1)S(1)}, u32[]{:S(2)}, u32[]{:S(2)}) collective-permute-start(bf16[512,128]{1,0:T(8,128)(2,1)S(1)} %get-tuple-element.51), channel_id=1, source_target_pairs={{0,2},{1,3},{2,0},{3,1},{4,6},{5,7},{6,4},{7,5},{8,10},{9,11},{10,... | collective-permute-start | bytes 393224 | tf_op jit(solution)/shard_map/ppermute | solution.py:500
  75.6 1.3 %collective-permute-start.24 = (bf16[512,128]{1,0:T(8,128)(2,1)S(1)}, bf16[512,128]{1,0:T(8,128)(2,1)S(1)}, u32[]{:S(2)}, u32[]{:S(2)}) collective-permute-start(bf16[512,128]{1,0:T(8,128)(2,1)S(1)} %get-tuple-element.53), channel_id=1, source_target_pairs={{0,6},{1,7},{2,4},{3,5},{4,2},{5,3},{6,0},{7,1},{8,14},{9,15},{10,... | collective-permute-start | bytes 393224 | tf_op jit(solution)/shard_map/ppermute | solution.py:500
  77.0 1.4 %collective-permute-start.19 = (bf16[512,128]{1,0:T(8,128)(2,1)S(1)}, bf16[512,128]{1,0:T(8,128)(2,1)S(1)}, u32[]{:S(2)}, u32[]{:S(2)}) collective-permute-start(bf16[512,128]{1,0:T(8,128)(2,1)S(1)} %get-tuple-element.47), channel_id=1, source_target_pairs={{0,2},{1,3},{2,0},{3,1},{4,6},{5,7},{6,4},{7,5},{8,10},{9,11},{10,... | collective-permute-start | bytes 393224 | tf_op jit(solution)/shard_map/ppermute | solution.py:500
  79.2 1.6 %collective-permute-start.21 = (bf16[512,128]{1,0:T(8,128)(2,1)S(1)}, bf16[512,128]{1,0:T(8,128)(2,1)S(1)}, u32[]{:S(2)}, u32[]{:S(2)}) collective-permute-start(bf16[512,128]{1,0:T(8,128)(2,1)S(1)} %get-tuple-element.49), channel_id=1, source_target_pairs={{0,6},{1,7},{2,4},{3,5},{4,2},{5,3},{6,0},{7,1},{8,14},{9,15},{10,... | collective-permute-start | bytes 393224 | tf_op jit(solution)/shard_map/ppermute | solution.py:500
  81.3 2.9 %collective-permute-done.24.refs_3_ = bf16[512,128]{1,0:T(8,128)(2,1)S(1)} collective-permute-done((bf16[512,128]{1,0:T(8,128)(2,1)S(1)}, bf16[512,128]{1,0:T(8,128)(2,1)S(1)}, u32[]{:S(2)}, u32[]{:S(2)}) %collective-permute-start.24) | collective-permute-done | bytes 131104 | tf_op jit(solution)/shard_map/ppermute | solution.py:500
  84.2 1.8 %collective-permute-start.25 = (bf16[512,128]{1,0:T(8,128)(2,1)S(1)}, bf16[512,128]{1,0:T(8,128)(2,1)S(1)}, u32[]{:S(2)}, u32[]{:S(2)}) collective-permute-start(bf16[512,128]{1,0:T(8,128)(2,1)S(1)} %total.3), channel_id=1, source_target_pairs={{0,16},{16,0},{1,17},{17,1},{2,18},{18,2},{3,19},{19,3},{4,20},{20... | collective-permute-start | bytes 393224 | tf_op jit(solution)/shard_map/ppermute | solution.py:504
  86.0 0.9 collective-permute-done.20.refs_2_
  86.9 1.7 %collective-permute-done.21.refs_3_ = bf16[512,128]{1,0:T(8,128)(2,1)S(1)} collective-permute-done((bf16[512,128]{1,0:T(8,128)(2,1)S(1)}, bf16[512,128]{1,0:T(8,128)(2,1)S(1)}, u32[]{:S(2)}, u32[]{:S(2)}) %collective-permute-start.21) | collective-permute-done | bytes 131104 | tf_op jit(solution)/shard_map/ppermute | solution.py:500
  89.3 2.3 %collective-permute-start.26 = (bf16[512,128]{1,0:T(8,128)(2,1)S(1)}, bf16[512,128]{1,0:T(8,128)(2,1)S(1)}, u32[]{:S(2)}, u32[]{:S(2)}) collective-permute-start(bf16[512,128]{1,0:T(8,128)(2,1)S(1)} %get-tuple-element.55), channel_id=1, source_target_pairs={{0,8},{1,9},{2,10},{3,11},{4,12},{5,13},{6,14},{7,15},{8,0},{9,1},... | collective-permute-start | bytes 393224 | tf_op jit(solution)/shard_map/ppermute | solution.py:500
  91.6 5.3 %taps_gradient.1 = f32[32,128]{1,0:T(8,128)} custom-call(bf16[512,256]{1,0:T(8,128)(2,1)S(1)} %get-tuple-element.56.prod_ref, bf16[512,256]{1,0:T(8,128)(2,1)S(1)} %get-tuple-element.57.grad_ref), custom_call_target="tpu_custom_call" | custom-call | flops 131072 | bytes 768 | tf_op jit(solution)/shard_map/taps_gradient/pallas_call | solution.py:463
  (44 shorter events, 10.1 us)
Async XLA Ops:
  1.6 16.1 %collective-permute-start.1 = (bf16[256,512]{1,0:T(8,128)(2,1)S(1)}, bf16[256,512]{1,0:T(8,128)(2,1)S(1)}, u32[]{:S(2)}, u32[]{:S(2)}) collective-permute-start(bf16[256,512]{1,0:T(8,128)(2,1)S(1)} %stacked.1.refs_0_.both_ref), channel_id=1, source_target_pairs={{8,16},{9,17},{10,18},{11,19},{12,20},{13,21},{14,22},{15,23},{16,... | collective-permute-start | bytes 786440 | tf_op jit(solution)/shard_map/ppermute | solution.py:514
  2.3 15.5 %collective-permute-start = (bf16[256,512]{1,0:T(8,128)(2,1)S(1)}, bf16[256,512]{1,0:T(8,128)(2,1)S(1)}, u32[]{:S(2)}, u32[]{:S(2)}) collective-permute-start(bf16[256,512]{1,0:T(8,128)(2,1)S(1)} %stacked.1.refs_0_.both_ref), channel_id=1, source_target_pairs={{0,8},{1,9},{2,10},{3,11},{4,12},{5,13},{6,14},{7,15},{8,24},{9,25... | collective-permute-start | bytes 786440 | tf_op jit(solution)/shard_map/ppermute | solution.py:514
  8.9 0.7 copy-start.1
  10.7 0.9 copy-start
  17.9 11.6 %collective-permute-start.4 = (bf16[256,512]{1,0:T(8,128)(2,1)S(1)}, bf16[256,512]{1,0:T(8,128)(2,1)S(1)}, u32[]{:S(2)}, u32[]{:S(2)}) collective-permute-start(bf16[256,512]{1,0:T(8,128)(2,1)S(1)} %get-tuple-element.36.refs_0_), channel_id=1, source_target_pairs={{0,6},{1,7},{2,4},{3,5},{4,2},{5,3},{6,0},{7,1},{8,14},{9,15},{10,... | collective-permute-start | bytes 786440 | tf_op jit(solution)/shard_map/ppermute | solution.py:500
  22.3 11.4 %collective-permute-start.3 = (bf16[256,512]{1,0:T(8,128)(2,1)S(1)}, bf16[256,512]{1,0:T(8,128)(2,1)S(1)}, u32[]{:S(2)}, u32[]{:S(2)}) collective-permute-start(bf16[256,512]{1,0:T(8,128)(2,1)S(1)} %get-tuple-element.36.refs_0_), channel_id=1, source_target_pairs={{0,4},{1,5},{2,6},{3,7},{4,0},{5,1},{6,2},{7,3},{8,12},{9,13},{10,... | collective-permute-start | bytes 786440 | tf_op jit(solution)/shard_map/ppermute | solution.py:500
  22.3 12.1 %collective-permute-start.2 = (bf16[256,512]{1,0:T(8,128)(2,1)S(1)}, bf16[256,512]{1,0:T(8,128)(2,1)S(1)}, u32[]{:S(2)}, u32[]{:S(2)}) collective-permute-start(bf16[256,512]{1,0:T(8,128)(2,1)S(1)} %get-tuple-element.36.refs_0_), channel_id=1, source_target_pairs={{0,2},{1,3},{2,0},{3,1},{4,6},{5,7},{6,4},{7,5},{8,10},{9,11},{10,... | collective-permute-start | bytes 786440 | tf_op jit(solution)/shard_map/ppermute | solution.py:500
  23.0 14.2 %collective-permute-start.8 = (bf16[256,512]{1,0:T(8,128)(2,1)S(1)}, bf16[256,512]{1,0:T(8,128)(2,1)S(1)}, u32[]{:S(2)}, u32[]{:S(2)}) collective-permute-start(bf16[256,512]{1,0:T(8,128)(2,1)S(1)} %get-tuple-element.36.refs_0_), channel_id=1, source_target_pairs={{0,1},{1,0},{2,3},{3,2},{4,5},{5,4},{6,7},{7,6},{8,9},{9,8},{10,11... | collective-permute-start | bytes 786440 | tf_op jit(solution)/shard_map/ppermute | solution.py:500
  29.5 7.7 %collective-permute-start.11 = (bf16[256,512]{1,0:T(8,128)(2,1)S(1)}, bf16[256,512]{1,0:T(8,128)(2,1)S(1)}, u32[]{:S(2)}, u32[]{:S(2)}) collective-permute-start(bf16[256,512]{1,0:T(8,128)(2,1)S(1)} %collective-permute-done.4.refs_2_.refs_3_), channel_id=1, source_target_pairs={{0,1},{1,0},{2,3},{3,2},{4,5},{5,4},{6,7},{7,6},{8,9},{9,8},{10,11... | collective-permute-start | bytes 786440 | tf_op jit(solution)/shard_map/ppermute | solution.py:500
  33.7 4.6 %collective-permute-start.10 = (bf16[256,512]{1,0:T(8,128)(2,1)S(1)}, bf16[256,512]{1,0:T(8,128)(2,1)S(1)}, u32[]{:S(2)}, u32[]{:S(2)}) collective-permute-start(bf16[256,512]{1,0:T(8,128)(2,1)S(1)} %collective-permute-done.3.refs_1_.refs_2_), channel_id=1, source_target_pairs={{0,1},{1,0},{2,3},{3,2},{4,5},{5,4},{6,7},{7,6},{8,9},{9,8},{10,11... | collective-permute-start | bytes 786440 | tf_op jit(solution)/shard_map/ppermute | solution.py:500
  34.4 3.9 %collective-permute-start.9 = (bf16[256,512]{1,0:T(8,128)(2,1)S(1)}, bf16[256,512]{1,0:T(8,128)(2,1)S(1)}, u32[]{:S(2)}, u32[]{:S(2)}) collective-permute-start(bf16[256,512]{1,0:T(8,128)(2,1)S(1)} %collective-permute-done.2.refs_0_.refs_1_), channel_id=1, source_target_pairs={{0,1},{1,0},{2,3},{3,2},{4,5},{5,4},{6,7},{7,6},{8,9},{9,8},{10,11... | collective-permute-start | bytes 786440 | tf_op jit(solution)/shard_map/ppermute | solution.py:500
  34.5 10.7 %collective-permute-start.7 = (bf16[256,512]{1,0:T(8,128)(2,1)S(1)}, bf16[256,512]{1,0:T(8,128)(2,1)S(1)}, u32[]{:S(2)}, u32[]{:S(2)}) collective-permute-start(bf16[256,512]{1,0:T(8,128)(2,1)S(1)} %copied.1.refs_0_), channel_id=1, source_target_pairs={{0,6},{1,7},{2,4},{3,5},{4,2},{5,3},{6,0},{7,1},{8,14},{9,15},{10,... | collective-permute-start | bytes 786440 | tf_op jit(solution)/shard_map/ppermute | solution.py:500
  37.2 11.9 %collective-permute-start.6 = (bf16[256,512]{1,0:T(8,128)(2,1)S(1)}, bf16[256,512]{1,0:T(8,128)(2,1)S(1)}, u32[]{:S(2)}, u32[]{:S(2)}) collective-permute-start(bf16[256,512]{1,0:T(8,128)(2,1)S(1)} %copied.1.refs_0_), channel_id=1, source_target_pairs={{0,4},{1,5},{2,6},{3,7},{4,0},{5,1},{6,2},{7,3},{8,12},{9,13},{10,... | collective-permute-start | bytes 786440 | tf_op jit(solution)/shard_map/ppermute | solution.py:500
  37.2 12.6 %collective-permute-start.5 = (bf16[256,512]{1,0:T(8,128)(2,1)S(1)}, bf16[256,512]{1,0:T(8,128)(2,1)S(1)}, u32[]{:S(2)}, u32[]{:S(2)}) collective-permute-start(bf16[256,512]{1,0:T(8,128)(2,1)S(1)} %copied.1.refs_0_), channel_id=1, source_target_pairs={{0,2},{1,3},{2,0},{3,1},{4,6},{5,7},{6,4},{7,5},{8,10},{9,11},{10,... | collective-permute-start | bytes 786440 | tf_op jit(solution)/shard_map/ppermute | solution.py:500
  42.2 21.5 %collective-permute-start.17 = (bf16[3,512,256]{2,1,0:T(8,128)(2,1)S(1)}, bf16[3,512,256]{2,1,0:T(8,128)(2,1)S(1)}, u32[]{:S(2)}, u32[]{:S(2)}) collective-permute-start(bf16[3,512,256]{2,1,0:T(8,128)(2,1)S(1)} %proj_partial.1.refs_4_.refs_0_), channel_id=1, source_target_pairs={{0,16},{16,0},{1,17},{17,1},{2,18},{18,2},{3,19},{19,3},{4,20},{20... | collective-permute-start | bytes 2359304 | tf_op jit(solution)/shard_map/ppermute | solution.py:504
  49.8 1.5 %collective-permute-start.12 = (bf16[256,512]{1,0:T(8,128)(2,1)S(1)}, bf16[256,512]{1,0:T(8,128)(2,1)S(1)}, u32[]{:S(2)}, u32[]{:S(2)}) collective-permute-start(bf16[256,512]{1,0:T(8,128)(2,1)S(1)} %get-tuple-element.37.refs_0_), channel_id=1, source_target_pairs={{0,1},{1,0},{2,3},{3,2},{4,5},{5,4},{6,7},{7,6},{8,9},{9,8},{10,11... | collective-permute-start | bytes 786440 | tf_op jit(solution)/shard_map/ppermute | solution.py:500
  49.8 1.9 %collective-permute-start.13 = (bf16[256,512]{1,0:T(8,128)(2,1)S(1)}, bf16[256,512]{1,0:T(8,128)(2,1)S(1)}, u32[]{:S(2)}, u32[]{:S(2)}) collective-permute-start(bf16[256,512]{1,0:T(8,128)(2,1)S(1)} %get-tuple-element.38.refs_1_), channel_id=1, source_target_pairs={{0,1},{1,0},{2,3},{3,2},{4,5},{5,4},{6,7},{7,6},{8,9},{9,8},{10,11... | collective-permute-start | bytes 786440 | tf_op jit(solution)/shard_map/ppermute | solution.py:500
  50.3 1.8 %collective-permute-start.14 = (bf16[256,512]{1,0:T(8,128)(2,1)S(1)}, bf16[256,512]{1,0:T(8,128)(2,1)S(1)}, u32[]{:S(2)}, u32[]{:S(2)}) collective-permute-start(bf16[256,512]{1,0:T(8,128)(2,1)S(1)} %get-tuple-element.39.refs_2_), channel_id=1, source_target_pairs={{0,1},{1,0},{2,3},{3,2},{4,5},{5,4},{6,7},{7,6},{8,9},{9,8},{10,11... | collective-permute-start | bytes 786440 | tf_op jit(solution)/shard_map/ppermute | solution.py:500
  50.3 2.1 %collective-permute-start.15 = (bf16[256,512]{1,0:T(8,128)(2,1)S(1)}, bf16[256,512]{1,0:T(8,128)(2,1)S(1)}, u32[]{:S(2)}, u32[]{:S(2)}) collective-permute-start(bf16[256,512]{1,0:T(8,128)(2,1)S(1)} %get-tuple-element.40.refs_3_), channel_id=1, source_target_pairs={{0,1},{1,0},{2,3},{3,2},{4,5},{5,4},{6,7},{7,6},{8,9},{9,8},{10,11... | collective-permute-start | bytes 786440 | tf_op jit(solution)/shard_map/ppermute | solution.py:500
  53.9 13.8 %collective-permute-start.16 = (bf16[512,256]{1,0:T(8,128)(2,1)S(1)}, bf16[512,256]{1,0:T(8,128)(2,1)S(1)}, u32[]{:S(2)}, u32[]{:S(2)}) collective-permute-start(bf16[512,256]{1,0:T(8,128)(2,1)S(1)} %grad_z_partial.1.refs_0_), channel_id=1, source_target_pairs={{0,16},{16,0},{1,17},{17,1},{2,18},{18,2},{3,19},{19,3},{4,20},{20... | collective-permute-start | bytes 786440 | tf_op jit(solution)/shard_map/ppermute | solution.py:504
  70.5 2.7 %collective-permute-start.18 = (bf16[4,512,256]{2,1,0:T(8,128)(2,1)S(1)}, bf16[4,512,256]{2,1,0:T(8,128)(2,1)S(1)}, u32[]{:S(2)}, u32[]{:S(2)}) collective-permute-start(bf16[4,512,256]{2,1,0:T(8,128)(2,1)S(1)} %input_partial.3), channel_id=1, source_target_pairs={{0,1},{1,0},{2,3},{3,2},{4,5},{5,4},{6,7},{7,6},{8,9},{9,8},{10,11... | collective-permute-start | bytes 3145736 | tf_op jit(solution)/shard_map/ppermute | solution.py:500
  73.4 5.7 %collective-permute-start.22 = (bf16[512,128]{1,0:T(8,128)(2,1)S(1)}, bf16[512,128]{1,0:T(8,128)(2,1)S(1)}, u32[]{:S(2)}, u32[]{:S(2)}) collective-permute-start(bf16[512,128]{1,0:T(8,128)(2,1)S(1)} %get-tuple-element.51), channel_id=1, source_target_pairs={{0,2},{1,3},{2,0},{3,1},{4,6},{5,7},{6,4},{7,5},{8,10},{9,11},{10,... | collective-permute-start | bytes 393224 | tf_op jit(solution)/shard_map/ppermute | solution.py:500
  74.9 6.4 %collective-permute-start.23 = (bf16[512,128]{1,0:T(8,128)(2,1)S(1)}, bf16[512,128]{1,0:T(8,128)(2,1)S(1)}, u32[]{:S(2)}, u32[]{:S(2)}) collective-permute-start(bf16[512,128]{1,0:T(8,128)(2,1)S(1)} %get-tuple-element.52), channel_id=1, source_target_pairs={{0,4},{1,5},{2,6},{3,7},{4,0},{5,1},{6,2},{7,3},{8,12},{9,13},{10,... | collective-permute-start | bytes 393224 | tf_op jit(solution)/shard_map/ppermute | solution.py:500
  75.6 8.5 %collective-permute-start.24 = (bf16[512,128]{1,0:T(8,128)(2,1)S(1)}, bf16[512,128]{1,0:T(8,128)(2,1)S(1)}, u32[]{:S(2)}, u32[]{:S(2)}) collective-permute-start(bf16[512,128]{1,0:T(8,128)(2,1)S(1)} %get-tuple-element.53), channel_id=1, source_target_pairs={{0,6},{1,7},{2,4},{3,5},{4,2},{5,3},{6,0},{7,1},{8,14},{9,15},{10,... | collective-permute-start | bytes 393224 | tf_op jit(solution)/shard_map/ppermute | solution.py:500
  77.0 9.0 %collective-permute-start.19 = (bf16[512,128]{1,0:T(8,128)(2,1)S(1)}, bf16[512,128]{1,0:T(8,128)(2,1)S(1)}, u32[]{:S(2)}, u32[]{:S(2)}) collective-permute-start(bf16[512,128]{1,0:T(8,128)(2,1)S(1)} %get-tuple-element.47), channel_id=1, source_target_pairs={{0,2},{1,3},{2,0},{3,1},{4,6},{5,7},{6,4},{7,5},{8,10},{9,11},{10,... | collective-permute-start | bytes 393224 | tf_op jit(solution)/shard_map/ppermute | solution.py:500
  78.4 8.5 %collective-permute-start.20 = (bf16[512,128]{1,0:T(8,128)(2,1)S(1)}, bf16[512,128]{1,0:T(8,128)(2,1)S(1)}, u32[]{:S(2)}, u32[]{:S(2)}) collective-permute-start(bf16[512,128]{1,0:T(8,128)(2,1)S(1)} %get-tuple-element.48), channel_id=1, source_target_pairs={{0,4},{1,5},{2,6},{3,7},{4,0},{5,1},{6,2},{7,3},{8,12},{9,13},{10,... | collective-permute-start | bytes 393224 | tf_op jit(solution)/shard_map/ppermute | solution.py:500
  79.2 9.5 %collective-permute-start.21 = (bf16[512,128]{1,0:T(8,128)(2,1)S(1)}, bf16[512,128]{1,0:T(8,128)(2,1)S(1)}, u32[]{:S(2)}, u32[]{:S(2)}) collective-permute-start(bf16[512,128]{1,0:T(8,128)(2,1)S(1)} %get-tuple-element.49), channel_id=1, source_target_pairs={{0,6},{1,7},{2,4},{3,5},{4,2},{5,3},{6,0},{7,1},{8,14},{9,15},{10,... | collective-permute-start | bytes 393224 | tf_op jit(solution)/shard_map/ppermute | solution.py:500
  84.2 5.0 %collective-permute-start.25 = (bf16[512,128]{1,0:T(8,128)(2,1)S(1)}, bf16[512,128]{1,0:T(8,128)(2,1)S(1)}, u32[]{:S(2)}, u32[]{:S(2)}) collective-permute-start(bf16[512,128]{1,0:T(8,128)(2,1)S(1)} %total.3), channel_id=1, source_target_pairs={{0,16},{16,0},{1,17},{17,1},{2,18},{18,2},{3,19},{19,3},{4,20},{20... | collective-permute-start | bytes 393224 | tf_op jit(solution)/shard_map/ppermute | solution.py:504
  89.3 7.7 %collective-permute-start.26 = (bf16[512,128]{1,0:T(8,128)(2,1)S(1)}, bf16[512,128]{1,0:T(8,128)(2,1)S(1)}, u32[]{:S(2)}, u32[]{:S(2)}) collective-permute-start(bf16[512,128]{1,0:T(8,128)(2,1)S(1)} %get-tuple-element.55), channel_id=1, source_target_pairs={{0,8},{1,9},{2,10},{3,11},{4,12},{5,13},{6,14},{7,15},{8,0},{9,1},... | collective-permute-start | bytes 393224 | tf_op jit(solution)/shard_map/ppermute | solution.py:500

commit v4 on v3

--- a/solution.py
+++ b/solution.py
@@ -51,61 +51,35 @@
     return lax.axis_index("tensor") // Z1 == lax.axis_index("fsdp")
 
 
-def stack_kernel(first_ref, second_ref, out_ref, sems):
-    run = first_ref.shape[0]
-    copies = [
-        pltpu.make_async_copy(ref, out_ref.at[pl.ds(n * run, run), :], sems.at[n])
-        for n, ref in enumerate((first_ref, second_ref))
-    ]
-    for copy in copies:
+def own_kernel(array_ref, turned_ref, crossed_ref, *refs):
+    out_ref, sem = refs[-2:]
+    run = array_ref.shape[0]
+    home = at_home()
+
+    @pl.when(home)
+    def _():
+        copy = pltpu.make_async_copy(array_ref, out_ref.at[pl.ds(0, run), :], sem)
         copy.start()
-    for copy in copies:
+        out_ref[run:] = turned_ref[...]
         copy.wait()
 
-
-def stacked(first, second):
-    shape = (2 * first.shape[0], first.shape[1])
-    return pl.pallas_call(
-        stack_kernel,
-        in_specs=[LATER_SPEC] * 2,
+    @pl.when(jnp.logical_not(home))
+    def _():
+        out_ref[:run] = turned_ref[...]
+        out_ref[run:] = crossed_ref[...]
+
+
+def own_slice(array, turned, crossed, *earlier):
+    return pl.pallas_call(
+        own_kernel,
+        in_specs=[LATER_SPEC] + [VMEM_SPEC] * 2 + [LATER_SPEC] * len(earlier),
         out_specs=VMEM_SPEC,
-        out_shape=pltpu.VMEM(shape, first.dtype),
-        scratch_shapes=[pltpu.SemaphoreType.DMA((2,))],
+        out_shape=jax.ShapeDtypeStruct((2 * array.shape[0], array.shape[1]), array.dtype),
+        scratch_shapes=[pltpu.SemaphoreType.DMA],
         compiler_params=params(8),
-        cost_estimate=cost(0, 8 * first.size),
-        name="stacked",
-    )(in_hbm(first), in_hbm(second))
-
-
-def own_kernel(both_ref, turned_ref, crossed_ref, *refs):
-    out_refs = refs[-2:]
-    run = both_ref.shape[0] // 2
-    home = at_home()
-    for n, out_ref in enumerate(out_refs):
-        at = slice(n * run, (n + 1) * run)
-
-        @pl.when(home)
-        def _(out_ref=out_ref, at=at):
-            out_ref[:run] = both_ref[at]
-            out_ref[run:] = turned_ref[at]
-
-        @pl.when(jnp.logical_not(home))
-        def _(out_ref=out_ref, at=at):
-            out_ref[:run] = turned_ref[at]
-            out_ref[run:] = crossed_ref[at]
-
-
-def own_slices(both, turned, crossed, *earlier):
-    out = jax.ShapeDtypeStruct(both.shape, both.dtype)
-    return pl.pallas_call(
-        own_kernel,
-        in_specs=[VMEM_SPEC] * 3 + [LATER_SPEC] * len(earlier),
-        out_specs=[VMEM_SPEC] * 2,
-        out_shape=[out, out],
-        compiler_params=params(8),
-        cost_estimate=cost(0, 10 * both.size),
-        name="own_slices",
-    )(both, turned, crossed, *earlier)
+        cost_estimate=cost(0, 10 * array.size),
+        name="own_slice",
+    )(array, turned, crossed, *earlier)
 
 
 def relay_kernel(*refs):
@@ -437,20 +411,29 @@
     channels, tokens = prod_ref.shape
     per = channels // groups
     blocks = tokens // BLOCK
+
+    def cut(ref, i):
+        return ref[:, i * BLOCK : (i + 1) * BLOCK]
+
+    turned = [
+        jnp.dot(cut(prod_ref, i), flip, preferred_element_type=F32).astype(BF16)
+        for i in range(blocks)
+    ]
+    grad = [cut(grad_ref, i) for i in range(blocks)]
+
+    def correlated(earlier, later, rows):
+        return lax.dot_general(
+            jnp.concatenate([block[rows] for block in earlier], 0),
+            jnp.concatenate([block[rows] for block in later], 0),
+            (((0,), (0,)), ((), ())),
+            preferred_element_type=F32,
+        )
+
     for g in range(groups):
         rows = slice(g * per, (g + 1) * per)
-        product, grad = prod_ref[rows, :], grad_ref[rows, :]
-        turned = jnp.dot(
-            jnp.concatenate([block_of(product, i) for i in range(blocks)], 0),
-            flip,
-            preferred_element_type=F32,
-        )
-        earlier = paired(unstacked(turned.astype(BF16), blocks), -1)
-        later = jnp.concatenate([block_of(grad, i) for i in range(blocks)], 0)
-        both = lax.dot_general(
-            earlier, later, (((0,), (0,)), ((), ())), preferred_element_type=F32
-        )
-        folded = jnp.where(row + lane >= BLOCK - 1, both[BLOCK:], both[:BLOCK])
+        within = correlated(turned, grad, rows)
+        before = correlated(turned[:-1], grad[1:], rows)
+        folded = jnp.where(row + lane >= BLOCK - 1, within, before)
         out_ref[g : g + 1, :] = jnp.sum(sheared(folded), axis=0, keepdims=True)
     out_ref[...] = pltpu.roll(out_ref[...], 1, 1) / TOK_DEV
 
@@ -637,13 +620,14 @@
 
 def on_small_slice(tokens, values, scales, filters, out_weight, cotangent):
     rows = tokens.shape[1]
-    both = stacked(tokens, cotangent)
-    turned, crossed = first_stage(both)
-    weights, out_held, ready = prepared(values, scales, out_weight, both)
-    past, later = toeplitz(filters, both)
-    token_own, cot_own = own_slices(both, turned, crossed, ready, past)
+    token_stage = first_stage(tokens)
+    weights, out_held, ready = prepared(values, scales, out_weight)
+    token_own = own_slice(in_hbm(tokens), *token_stage, ready)
     token_same = second_stage(token_own)
-    cot_own = copied(cot_own, *token_same[1:])
+    past, later = toeplitz(filters, token_own)
+    cotangent = copied(cotangent, past)
+    cot_own = own_slice(cotangent, *first_stage(cotangent))
+    *token_same, cot_own = relayed([*token_same, cot_own])
     cot_same = second_stage(cot_own)
     proj_part = proj_partial(both_cores(token_same), MINE + OTHERS, 2, weights)
     cot_same = list(relayed(cot_same, proj_part))

time: 98 us -> 96.1 us (0.981)
  starting transfers between devices: 34.7 us -> 41.6 us
  waiting for transfers between devices: 35.1 us -> 29.1 us
  Pallas kernels: 25.6 us -> 23.6 us
    ppermute x22, waiting for transfers between devices: 24.7 us -> 14.1 us  [across(): return lax.ppermute(array, 'tensor', [(i, i ^ mask) for i in range(16)])]
    ppermute x2 -> x4, starting transfers between devices: 7.29 us -> 12.4 us  [in_square(): return lax.ppermute(array, ('fsdp', 'tensor'), pairs)]
    ppermute x2 -> x4, waiting for transfers between devices: 0.01 us -> 4.07 us  [in_square(): return lax.ppermute(array, ('fsdp', 'tensor'), pairs)]
    pallas_call x1, Pallas kernels: 5.31 us -> 3.22 us  [taps_gradient(): pl.pallas_call(functools.partial(taps_kernel, groups // steps), grid=(ste...]
    ppermute x3, starting transfers between devices: 7.71 us -> 9.39 us  [other_row(): return lax.ppermute(array, 'fsdp', [(0, 1), (1, 0)])]
  transfers between devices with their start and end apart: 27 -> 29, of which waited for: 18 -> 16; matrix products, arithmetic and copies ran while one was open for 0% -> 0% of each run, Pallas kernels for 21% -> 20%
where the time goes in v4:
time: 96.1 us; the launch traced here: 95.9 us
  starting transfers between devices  41.6 us (43%)
  waiting for transfers between devices  29.1 us (30%)
  Pallas kernels  23.6 us (25%)
    ppermute x22, starting transfers between devices, across(): return lax.ppermute(array, 'tensor', [(i, i ^ mask) for i in range(16)])  19.8 us
    ppermute x22, waiting for transfers between devices, across(): return lax.ppermute(array, 'tensor', [(i, i ^ mask) for i in range(16)])  14.1 us
    ppermute x4, starting transfers between devices, in_square(): return lax.ppermute(array, ('fsdp', 'tensor'), pairs)  12.4 us
    ppermute x3, waiting for transfers between devices, other_row(): return lax.ppermute(array, 'fsdp', [(0, 1), (1, 0)])  10.9 us
    ppermute x3, starting transfers between devices, other_row(): return lax.ppermute(array, 'fsdp', [(0, 1), (1, 0)])  9.39 us
    pallas_call x1, Pallas kernels, prepared(): pl.pallas_call(prepare_kernel, in_specs=[LATER_SPEC, VMEM_SPEC, LATER_SPE...  6.23 us
    ppermute x4, waiting for transfers between devices, in_square(): return lax.ppermute(array, ('fsdp', 'tensor'), pairs)  4.07 us
    pallas_call x1, Pallas kernels, proj_partial(): pl.pallas_call(functools.partial(proj_kernel, masks, runs), in_specs=[VME...  3.78 us
  transfers between devices with their start and end apart: 29, of which 16 were waited for; matrix products, arithmetic and copies ran while one was open for 0% of the time, Pallas kernels for 20%

profile of v4, /device:TPU:0, one launch (start us, length us, event | category | flops | bytes accessed | tf_op | source)
XLA Modules:
  0.0 95.9 jit_solution(6992241119177159554)
XLA Ops:
  0.6 4.1 %collective-permute-start = (bf16[128,512]{1,0:T(8,128)(2,1)}, bf16[128,512]{1,0:T(8,128)(2,1)S(1)}, u32[]{:S(2)}, u32[]{:S(2)}) collective-permute-start(bf16[128,512]{1,0:T(8,128)(2,1)} %array_ref.1), channel_id=1, source_target_pairs={{0,8},{1,9},{2,10},{3,11},{4,12},{5,13},{6,14},{7,15},{8,24},{9,25... | collective-permute-start | bytes 393224 | tf_op jit(solution)/shard_map/ppermute | solution.py:497
  5.4 0.9 copy-done.1
  6.3 6.2 %prepare.1 = (bf16[4096,512]{1,0:T(8,128)(2,1)S(1)}, bf16[4096,512]{1,0:T(8,128)(2,1)S(1)}, bf16[4096,512]{1,0:T(8,128)(2,1)S(1)}, bf16[512,4096]{1,0:T(8,128)(2,1)S(1)}, f32[8,128]{1,0:T(8,128)S(1)}) custom-call(bf16[3,4096,512]{2,1,0:T(8,128)(2,1)} %bitcast.6, bf16[3,32,512]{2,1,0:T(8,128)(2,1)S(1)} %bitcast.5, bf16[512,4096]{1,0:T(8,128)(2,1)} %ow_ref.1), custom_call_target="tpu_custom_call" | custom-call | flops 6144 | bytes 6144 | tf_op jit(solution)/shard_map/prepare/pallas_call | solution.py:154
  12.5 0.9 own_slice.2.refs_0_
  13.5 2.6 %collective-permute-start.4 = (bf16[256,512]{1,0:T(8,128)(2,1)S(1)}, bf16[256,512]{1,0:T(8,128)(2,1)S(1)}, u32[]{:S(2)}, u32[]{:S(2)}) collective-permute-start(bf16[256,512]{1,0:T(8,128)(2,1)S(1)} %own_slice.2.refs_0_), channel_id=1, source_target_pairs={{0,6},{1,7},{2,4},{3,5},{4,2},{5,3},{6,0},{7,1},{8,14},{9,15},{10,... | collective-permute-start | bytes 786440 | tf_op jit(solution)/shard_map/ppermute | solution.py:483
  17.0 1.0 %toeplitz.1 = (bf16[32,256,128]{2,1,0:T(8,128)(2,1)S(1)}, bf16[32,256,128]{2,1,0:T(8,128)(2,1)S(1)}) custom-call(f32[32,128]{1,0:T(8,128)S(1)} %copy-done.2, bf16[256,512]{1,0:T(8,128)(2,1)S(1)} %own_slice.2.refs_0_), custom_call_target="tpu_custom_call" | custom-call | flops 2000 | bytes 1024 | tf_op jit(solution)/shard_map/toeplitz/pallas_call | solution.py:277
  18.8 7.0 %collective-permute-start.5 = (bf16[128,512]{1,0:T(8,128)(2,1)S(1)}, bf16[128,512]{1,0:T(8,128)(2,1)S(1)}, u32[]{:S(2)}, u32[]{:S(2)}) collective-permute-start(bf16[128,512]{1,0:T(8,128)(2,1)S(1)} %copied.1.array_ref), channel_id=1, source_target_pairs={{0,8},{1,9},{2,10},{3,11},{4,12},{5,13},{6,14},{7,15},{8,24},{9,25... | collective-permute-start | bytes 393224 | tf_op jit(solution)/shard_map/ppermute | solution.py:497
  25.8 4.1 %collective-permute-done.5.turned_ref = bf16[128,512]{1,0:T(8,128)(2,1)S(1)} collective-permute-done((bf16[128,512]{1,0:T(8,128)(2,1)S(1)}, bf16[128,512]{1,0:T(8,128)(2,1)S(1)}, u32[]{:S(2)}, u32[]{:S(2)}) %collective-permute-start.5) | collective-permute-done | bytes 131104 | tf_op jit(solution)/shard_map/ppermute | solution.py:497
  31.7 1.9 %collective-permute-start.9 = (bf16[256,512]{1,0:T(8,128)(2,1)S(1)}, bf16[256,512]{1,0:T(8,128)(2,1)S(1)}, u32[]{:S(2)}, u32[]{:S(2)}) collective-permute-start(bf16[256,512]{1,0:T(8,128)(2,1)S(1)} %get-tuple-element.38.refs_0_), channel_id=1, source_target_pairs={{0,6},{1,7},{2,4},{3,5},{4,2},{5,3},{6,0},{7,1},{8,14},{9,15},{10,... | collective-permute-start | bytes 786440 | tf_op jit(solution)/shard_map/ppermute | solution.py:483
  33.8 1.5 %collective-permute-start.7 = (bf16[256,512]{1,0:T(8,128)(2,1)S(1)}, bf16[256,512]{1,0:T(8,128)(2,1)S(1)}, u32[]{:S(2)}, u32[]{:S(2)}) collective-permute-start(bf16[256,512]{1,0:T(8,128)(2,1)S(1)} %get-tuple-element.38.refs_0_), channel_id=1, source_target_pairs={{0,2},{1,3},{2,0},{3,1},{4,6},{5,7},{6,4},{7,5},{8,10},{9,11},{10,... | collective-permute-start | bytes 786440 | tf_op jit(solution)/shard_map/ppermute | solution.py:483
  35.2 3.8 %proj_partial.1.refs_4_.refs_0_ = bf16[3,512,256]{2,1,0:T(8,128)(2,1)S(1)} custom-call(bf16[256,512]{1,0:T(8,128)(2,1)S(1)} %get-tuple-element.39.refs_0_, bf16[256,512]{1,0:T(8,128)(2,1)S(1)} %get-tuple-element.40.refs_1_, bf16[256,512]{1,0:T(8,128)(2,1)S(1)} %get-tuple-element.41.refs_2_, bf16[256,512]{1,0:T(8,128)(2,1)S(1)} %get-tuple-element.42.refs_3_, ...), custom_call_target="tpu_custom_call" | custom-call | flops 786432 | bytes 3072 | tf_op jit(solution)/shard_map/proj_partial/pallas_call | solution.py:214
  39.0 3.9 %collective-permute-start.19 = (bf16[3,512,256]{2,1,0:T(8,128)(2,1)S(1)}, bf16[3,512,256]{2,1,0:T(8,128)(2,1)S(1)}, u32[]{:S(2)}, u32[]{:S(2)}) collective-permute-start(bf16[3,512,256]{2,1,0:T(8,128)(2,1)S(1)} %proj_partial.1.refs_4_.refs_0_), channel_id=1, source_target_pairs={{0,16},{16,0},{1,17},{17,1},{2,18},{18,2},{3,19},{19,3},{4,20},{20... | collective-permute-start | bytes 2359304 | tf_op jit(solution)/shard_map/ppermute | solution.py:487
  42.9 2.7 %collective-permute-done.8.refs_2_ = bf16[256,512]{1,0:T(8,128)(2,1)S(1)} collective-permute-done((bf16[256,512]{1,0:T(8,128)(2,1)S(1)}, bf16[256,512]{1,0:T(8,128)(2,1)S(1)}, u32[]{:S(2)}, u32[]{:S(2)}) %collective-permute-start.8) | collective-permute-done | bytes 262176 | tf_op jit(solution)/shard_map/ppermute | solution.py:483
  49.2 1.4 %grad_z_partial.1.refs_0_ = bf16[512,256]{1,0:T(8,128)(2,1)S(1)} custom-call(bf16[256,512]{1,0:T(8,128)(2,1)S(1)} %get-tuple-element.43.refs_0_, bf16[256,512]{1,0:T(8,128)(2,1)S(1)} %get-tuple-element.44.refs_1_, bf16[256,512]{1,0:T(8,128)(2,1)S(1)} %get-tuple-element.45.refs_2_, bf16[256,512]{1,0:T(8,128)(2,1)S(1)} %get-tuple-element.46.refs_3_, ...), custom_call_target="tpu_custom_call" | custom-call | flops 262144 | bytes 1024 | tf_op jit(solution)/shard_map/grad_z_partial/pallas_call | solution.py:240
  50.6 3.7 %collective-permute-start.18 = (bf16[512,256]{1,0:T(8,128)(2,1)S(1)}, bf16[512,256]{1,0:T(8,128)(2,1)S(1)}, u32[]{:S(2)}, u32[]{:S(2)}) collective-permute-start(bf16[512,256]{1,0:T(8,128)(2,1)S(1)} %grad_z_partial.1.refs_0_), channel_id=1, source_target_pairs={{0,16},{16,0},{1,17},{17,1},{2,18},{18,2},{3,19},{19,3},{4,20},{20... | collective-permute-start | bytes 786440 | tf_op jit(solution)/shard_map/ppermute | solution.py:487
  54.3 7.0 %collective-permute-done.19.refs_1_ = bf16[3,512,256]{2,1,0:T(8,128)(2,1)S(1)} collective-permute-done((bf16[3,512,256]{2,1,0:T(8,128)(2,1)S(1)}, bf16[3,512,256]{2,1,0:T(8,128)(2,1)S(1)}, u32[]{:S(2)}, u32[]{:S(2)}) %collective-permute-start.19) | collective-permute-done | bytes 786464 | tf_op jit(solution)/shard_map/ppermute | solution.py:487
  61.3 1.1 %conv_forward.1 = (bf16[3,512,256]{2,1,0:T(8,128)(2,1)S(1)}, bf16[512,256]{1,0:T(8,128)(2,1)S(1)}, f32[512,256]{1,0:T(8,128)S(1)}) custom-call(bf16[3,512,256]{2,1,0:T(8,128)(2,1)S(1)} %proj_partial.1.refs_4_.refs_0_, bf16[3,512,256]{2,1,0:T(8,128)(2,1)S(1)} %collective-permute-done.19.refs_1_, bf16[32,256,128]{2,1,0:T(8,128)(2,1)S(1)} %get-tuple-element.37.refs_0_.refs_2_), custom_call_target="tpu_custom_call" | custom-call | flops 131072 | bytes 768 | tf_op jit(solution)/shard_map/conv_forward/pallas_call | solution.py:345
  62.4 3.4 %collective-permute-done.18.refs_1_ = bf16[512,256]{1,0:T(8,128)(2,1)S(1)} collective-permute-done((bf16[512,256]{1,0:T(8,128)(2,1)S(1)}, bf16[512,256]{1,0:T(8,128)(2,1)S(1)}, u32[]{:S(2)}, u32[]{:S(2)}) %collective-permute-start.18) | collective-permute-done | bytes 262176 | tf_op jit(solution)/shard_map/ppermute | solution.py:487
  65.8 1.0 %conv_backward.1 = (bf16[3,512,256]{2,1,0:T(8,128)(2,1)S(1)}, bf16[512,256]{1,0:T(8,128)(2,1)S(1)}) custom-call(bf16[512,256]{1,0:T(8,128)(2,1)S(1)} %grad_z_partial.1.refs_0_, bf16[512,256]{1,0:T(8,128)(2,1)S(1)} %collective-permute-done.18.refs_1_, bf16[3,512,256]{2,1,0:T(8,128)(2,1)S(1)} %get-tuple-element.48.refs_2_, ...), custom_call_target="tpu_custom_call" | custom-call | flops 131072 | bytes 768 | tf_op jit(solution)/shard_map/conv_backward/pallas_call | solution.py:388
  66.9 1.8 %input_partial.3 = bf16[4,512,256]{2,1,0:T(8,128)(2,1)S(1)} custom-call(bf16[4096,512]{1,0:T(8,128)(2,1)S(1)} %get-tuple-element.33.refs_8_.refs_0_, bf16[4096,512]{1,0:T(8,128)(2,1)S(1)} %get-tuple-element.34.refs_9_.refs_1_, bf16[4096,512]{1,0:T(8,128)(2,1)S(1)} %get-tuple-element.35.refs_10_.refs_2_, bf16[1536,256]{1,0:T(8,128)(2,1)S(1)} %bitcast.3), custom_call_target="tpu_custom_call" | custom-call | flops 393216 | bytes 1792 | tf_op jit(solution)/shard_map/input_partial/pallas_call | solution.py:469
  68.7 1.8 %input_partial.2.same_ref = bf16[4,512,256]{2,1,0:T(8,128)(2,1)S(1)} custom-call(bf16[4096,512]{1,0:T(8,128)(2,1)S(1)} %get-tuple-element.33.refs_8_.refs_0_, bf16[4096,512]{1,0:T(8,128)(2,1)S(1)} %get-tuple-element.34.refs_9_.refs_1_, bf16[4096,512]{1,0:T(8,128)(2,1)S(1)} %get-tuple-element.35.refs_10_.refs_2_, bf16[1536,256]{1,0:T(8,128)(2,1)S(1)} %bitcast.4), custom_call_target="tpu_custom_call" | custom-call | flops 393216 | bytes 1792 | tf_op jit(solution)/shard_map/input_partial/pallas_call | solution.py:469
  71.6 1.0 %collective-permute-start.24 = (bf16[512,128]{1,0:T(8,128)(2,1)S(1)}, bf16[512,128]{1,0:T(8,128)(2,1)S(1)}, u32[]{:S(2)}, u32[]{:S(2)}) collective-permute-start(bf16[512,128]{1,0:T(8,128)(2,1)S(1)} %get-tuple-element.57), channel_id=1, source_target_pairs={{0,2},{1,3},{2,0},{3,1},{4,6},{5,7},{6,4},{7,5},{8,10},{9,11},{10,... | collective-permute-start | bytes 393224 | tf_op jit(solution)/shard_map/ppermute | solution.py:483
  72.6 1.7 %collective-permute-start.25 = (bf16[512,128]{1,0:T(8,128)(2,1)S(1)}, bf16[512,128]{1,0:T(8,128)(2,1)S(1)}, u32[]{:S(2)}, u32[]{:S(2)}) collective-permute-start(bf16[512,128]{1,0:T(8,128)(2,1)S(1)} %get-tuple-element.58), channel_id=1, source_target_pairs={{0,4},{1,5},{2,6},{3,7},{4,0},{5,1},{6,2},{7,3},{8,12},{9,13},{10,... | collective-permute-start | bytes 393224 | tf_op jit(solution)/shard_map/ppermute | solution.py:483
  75.2 1.0 %collective-permute-start.21 = (bf16[512,128]{1,0:T(8,128)(2,1)S(1)}, bf16[512,128]{1,0:T(8,128)(2,1)S(1)}, u32[]{:S(2)}, u32[]{:S(2)}) collective-permute-start(bf16[512,128]{1,0:T(8,128)(2,1)S(1)} %get-tuple-element.53), channel_id=1, source_target_pairs={{0,2},{1,3},{2,0},{3,1},{4,6},{5,7},{6,4},{7,5},{8,10},{9,11},{10,... | collective-permute-start | bytes 393224 | tf_op jit(solution)/shard_map/ppermute | solution.py:483
  76.1 1.7 %collective-permute-start.22 = (bf16[512,128]{1,0:T(8,128)(2,1)S(1)}, bf16[512,128]{1,0:T(8,128)(2,1)S(1)}, u32[]{:S(2)}, u32[]{:S(2)}) collective-permute-start(bf16[512,128]{1,0:T(8,128)(2,1)S(1)} %get-tuple-element.54), channel_id=1, source_target_pairs={{0,4},{1,5},{2,6},{3,7},{4,0},{5,1},{6,2},{7,3},{8,12},{9,13},{10,... | collective-permute-start | bytes 393224 | tf_op jit(solution)/shard_map/ppermute | solution.py:483
  77.8 1.6 %collective-permute-start.23 = (bf16[512,128]{1,0:T(8,128)(2,1)S(1)}, bf16[512,128]{1,0:T(8,128)(2,1)S(1)}, u32[]{:S(2)}, u32[]{:S(2)}) collective-permute-start(bf16[512,128]{1,0:T(8,128)(2,1)S(1)} %get-tuple-element.55), channel_id=1, source_target_pairs={{0,6},{1,7},{2,4},{3,5},{4,2},{5,3},{6,0},{7,1},{8,14},{9,15},{10,... | collective-permute-start | bytes 393224 | tf_op jit(solution)/shard_map/ppermute | solution.py:483
  79.4 2.9 %collective-permute-done.26.refs_3_ = bf16[512,128]{1,0:T(8,128)(2,1)S(1)} collective-permute-done((bf16[512,128]{1,0:T(8,128)(2,1)S(1)}, bf16[512,128]{1,0:T(8,128)(2,1)S(1)}, u32[]{:S(2)}, u32[]{:S(2)}) %collective-permute-start.26) | collective-permute-done | bytes 131104 | tf_op jit(solution)/shard_map/ppermute | solution.py:483
  82.3 1.8 %collective-permute-start.27 = (bf16[512,128]{1,0:T(8,128)(2,1)S(1)}, bf16[512,128]{1,0:T(8,128)(2,1)S(1)}, u32[]{:S(2)}, u32[]{:S(2)}) collective-permute-start(bf16[512,128]{1,0:T(8,128)(2,1)S(1)} %total.3), channel_id=1, source_target_pairs={{0,16},{16,0},{1,17},{17,1},{2,18},{18,2},{3,19},{19,3},{4,20},{20... | collective-permute-start | bytes 393224 | tf_op jit(solution)/shard_map/ppermute | solution.py:487
  84.6 2.2 %collective-permute-done.23.refs_3_ = bf16[512,128]{1,0:T(8,128)(2,1)S(1)} collective-permute-done((bf16[512,128]{1,0:T(8,128)(2,1)S(1)}, bf16[512,128]{1,0:T(8,128)(2,1)S(1)}, u32[]{:S(2)}, u32[]{:S(2)}) %collective-permute-start.23) | collective-permute-done | bytes 131104 | tf_op jit(solution)/shard_map/ppermute | solution.py:483
  87.4 2.8 %collective-permute-start.28 = (bf16[512,128]{1,0:T(8,128)(2,1)S(1)}, bf16[512,128]{1,0:T(8,128)(2,1)S(1)}, u32[]{:S(2)}, u32[]{:S(2)}) collective-permute-start(bf16[512,128]{1,0:T(8,128)(2,1)S(1)} %get-tuple-element.61), channel_id=1, source_target_pairs={{0,8},{1,9},{2,10},{3,11},{4,12},{5,13},{6,14},{7,15},{8,0},{9,1},... | collective-permute-start | bytes 393224 | tf_op jit(solution)/shard_map/ppermute | solution.py:483
  90.2 3.2 %taps_gradient.1 = f32[32,128]{1,0:T(8,128)} custom-call(bf16[512,256]{1,0:T(8,128)(2,1)S(1)} %get-tuple-element.62.prod_ref, bf16[512,256]{1,0:T(8,128)(2,1)S(1)} %get-tuple-element.63.grad_ref), custom_call_target="tpu_custom_call" | custom-call | flops 131072 | bytes 768 | tf_op jit(solution)/shard_map/taps_gradient/pallas_call | solution.py:446
  93.4 1.7 %collective-permute-done.28.got_ref = bf16[512,128]{1,0:T(8,128)(2,1)S(1)} collective-permute-done((bf16[512,128]{1,0:T(8,128)(2,1)S(1)}, bf16[512,128]{1,0:T(8,128)(2,1)S(1)}, u32[]{:S(2)}, u32[]{:S(2)}) %collective-permute-start.28) | collective-permute-done | bytes 131104 | tf_op jit(solution)/shard_map/ppermute | solution.py:483
  (51 shorter events, 11.8 us)
Async XLA Ops:
  0.6 11.9 %collective-permute-start = (bf16[128,512]{1,0:T(8,128)(2,1)}, bf16[128,512]{1,0:T(8,128)(2,1)S(1)}, u32[]{:S(2)}, u32[]{:S(2)}) collective-permute-start(bf16[128,512]{1,0:T(8,128)(2,1)} %array_ref.1), channel_id=1, source_target_pairs={{0,8},{1,9},{2,10},{3,11},{4,12},{5,13},{6,14},{7,15},{8,24},{9,25... | collective-permute-start | bytes 393224 | tf_op jit(solution)/shard_map/ppermute | solution.py:497
  4.7 7.8 %collective-permute-start.1 = (bf16[128,512]{1,0:T(8,128)(2,1)}, bf16[128,512]{1,0:T(8,128)(2,1)S(1)}, u32[]{:S(2)}, u32[]{:S(2)}) collective-permute-start(bf16[128,512]{1,0:T(8,128)(2,1)} %array_ref.1), channel_id=1, source_target_pairs={{8,16},{9,17},{10,18},{11,19},{12,20},{13,21},{14,22},{15,23},{16,... | collective-permute-start | bytes 393224 | tf_op jit(solution)/shard_map/ppermute | solution.py:497
  5.4 0.9 copy-start.1
  6.3 10.8 %copy-start.2 = (f32[32,128]{1,0:T(8,128)S(1)}, f32[32,128]{1,0:T(8,128)}, u32[]{:S(2)}) copy-start(f32[32,128]{1,0:T(8,128)} %taps_ref.1) | copy-start | bytes 49156
  6.3 11.8 %copy-start = (bf16[128,512]{1,0:T(8,128)(2,1)S(1)}, bf16[128,512]{1,0:T(8,128)(2,1)}, u32[]{:S(2)}) copy-start(bf16[128,512]{1,0:T(8,128)(2,1)} %in_ref.1) | copy-start | bytes 393220
  13.5 16.5 %collective-permute-start.4 = (bf16[256,512]{1,0:T(8,128)(2,1)S(1)}, bf16[256,512]{1,0:T(8,128)(2,1)S(1)}, u32[]{:S(2)}, u32[]{:S(2)}) collective-permute-start(bf16[256,512]{1,0:T(8,128)(2,1)S(1)} %own_slice.2.refs_0_), channel_id=1, source_target_pairs={{0,6},{1,7},{2,4},{3,5},{4,2},{5,3},{6,0},{7,1},{8,14},{9,15},{10,... | collective-permute-start | bytes 786440 | tf_op jit(solution)/shard_map/ppermute | solution.py:483
  16.0 14.7 %collective-permute-start.3 = (bf16[256,512]{1,0:T(8,128)(2,1)S(1)}, bf16[256,512]{1,0:T(8,128)(2,1)S(1)}, u32[]{:S(2)}, u32[]{:S(2)}) collective-permute-start(bf16[256,512]{1,0:T(8,128)(2,1)S(1)} %own_slice.2.refs_0_), channel_id=1, source_target_pairs={{0,4},{1,5},{2,6},{3,7},{4,0},{5,1},{6,2},{7,3},{8,12},{9,13},{10,... | collective-permute-start | bytes 786440 | tf_op jit(solution)/shard_map/ppermute | solution.py:483
  16.5 14.2 %collective-permute-start.2 = (bf16[256,512]{1,0:T(8,128)(2,1)S(1)}, bf16[256,512]{1,0:T(8,128)(2,1)S(1)}, u32[]{:S(2)}, u32[]{:S(2)}) collective-permute-start(bf16[256,512]{1,0:T(8,128)(2,1)S(1)} %own_slice.2.refs_0_), channel_id=1, source_target_pairs={{0,2},{1,3},{2,0},{3,1},{4,6},{5,7},{6,4},{7,5},{8,10},{9,11},{10,... | collective-permute-start | bytes 786440 | tf_op jit(solution)/shard_map/ppermute | solution.py:483
  18.1 7.7 %collective-permute-start.6 = (bf16[128,512]{1,0:T(8,128)(2,1)S(1)}, bf16[128,512]{1,0:T(8,128)(2,1)S(1)}, u32[]{:S(2)}, u32[]{:S(2)}) collective-permute-start(bf16[128,512]{1,0:T(8,128)(2,1)S(1)} %copied.1.array_ref), channel_id=1, source_target_pairs={{8,16},{9,17},{10,18},{11,19},{12,20},{13,21},{14,22},{15,23},{16,... | collective-permute-start | bytes 393224 | tf_op jit(solution)/shard_map/ppermute | solution.py:497
  18.8 11.1 %collective-permute-start.5 = (bf16[128,512]{1,0:T(8,128)(2,1)S(1)}, bf16[128,512]{1,0:T(8,128)(2,1)S(1)}, u32[]{:S(2)}, u32[]{:S(2)}) collective-permute-start(bf16[128,512]{1,0:T(8,128)(2,1)S(1)} %copied.1.array_ref), channel_id=1, source_target_pairs={{0,8},{1,9},{2,10},{3,11},{4,12},{5,13},{6,14},{7,15},{8,24},{9,25... | collective-permute-start | bytes 393224 | tf_op jit(solution)/shard_map/ppermute | solution.py:497
  30.7 3.0 %collective-permute-start.10 = (bf16[256,512]{1,0:T(8,128)(2,1)S(1)}, bf16[256,512]{1,0:T(8,128)(2,1)S(1)}, u32[]{:S(2)}, u32[]{:S(2)}) collective-permute-start(bf16[256,512]{1,0:T(8,128)(2,1)S(1)} %get-tuple-element.39.refs_0_), channel_id=1, source_target_pairs={{0,1},{1,0},{2,3},{3,2},{4,5},{5,4},{6,7},{7,6},{8,9},{9,8},{10,11... | collective-permute-start | bytes 786440 | tf_op jit(solution)/shard_map/ppermute | solution.py:483
  30.7 3.1 %collective-permute-start.11 = (bf16[256,512]{1,0:T(8,128)(2,1)S(1)}, bf16[256,512]{1,0:T(8,128)(2,1)S(1)}, u32[]{:S(2)}, u32[]{:S(2)}) collective-permute-start(bf16[256,512]{1,0:T(8,128)(2,1)S(1)} %get-tuple-element.40.refs_1_), channel_id=1, source_target_pairs={{0,1},{1,0},{2,3},{3,2},{4,5},{5,4},{6,7},{7,6},{8,9},{9,8},{10,11... | collective-permute-start | bytes 786440 | tf_op jit(solution)/shard_map/ppermute | solution.py:483
  31.2 4.0 %collective-permute-start.12 = (bf16[256,512]{1,0:T(8,128)(2,1)S(1)}, bf16[256,512]{1,0:T(8,128)(2,1)S(1)}, u32[]{:S(2)}, u32[]{:S(2)}) collective-permute-start(bf16[256,512]{1,0:T(8,128)(2,1)S(1)} %get-tuple-element.41.refs_2_), channel_id=1, source_target_pairs={{0,1},{1,0},{2,3},{3,2},{4,5},{5,4},{6,7},{7,6},{8,9},{9,8},{10,11... | collective-permute-start | bytes 786440 | tf_op jit(solution)/shard_map/ppermute | solution.py:483
  31.3 4.0 %collective-permute-start.13 = (bf16[256,512]{1,0:T(8,128)(2,1)S(1)}, bf16[256,512]{1,0:T(8,128)(2,1)S(1)}, u32[]{:S(2)}, u32[]{:S(2)}) collective-permute-start(bf16[256,512]{1,0:T(8,128)(2,1)S(1)} %get-tuple-element.42.refs_3_), channel_id=1, source_target_pairs={{0,1},{1,0},{2,3},{3,2},{4,5},{5,4},{6,7},{7,6},{8,9},{9,8},{10,11... | collective-permute-start | bytes 786440 | tf_op jit(solution)/shard_map/ppermute | solution.py:483
  31.7 11.2 %collective-permute-start.9 = (bf16[256,512]{1,0:T(8,128)(2,1)S(1)}, bf16[256,512]{1,0:T(8,128)(2,1)S(1)}, u32[]{:S(2)}, u32[]{:S(2)}) collective-permute-start(bf16[256,512]{1,0:T(8,128)(2,1)S(1)} %get-tuple-element.38.refs_0_), channel_id=1, source_target_pairs={{0,6},{1,7},{2,4},{3,5},{4,2},{5,3},{6,0},{7,1},{8,14},{9,15},{10,... | collective-permute-start | bytes 786440 | tf_op jit(solution)/shard_map/ppermute | solution.py:483
  33.7 12.0 %collective-permute-start.8 = (bf16[256,512]{1,0:T(8,128)(2,1)S(1)}, bf16[256,512]{1,0:T(8,128)(2,1)S(1)}, u32[]{:S(2)}, u32[]{:S(2)}) collective-permute-start(bf16[256,512]{1,0:T(8,128)(2,1)S(1)} %get-tuple-element.38.refs_0_), channel_id=1, source_target_pairs={{0,4},{1,5},{2,6},{3,7},{4,0},{5,1},{6,2},{7,3},{8,12},{9,13},{10,... | collective-permute-start | bytes 786440 | tf_op jit(solution)/shard_map/ppermute | solution.py:483
  33.8 12.8 %collective-permute-start.7 = (bf16[256,512]{1,0:T(8,128)(2,1)S(1)}, bf16[256,512]{1,0:T(8,128)(2,1)S(1)}, u32[]{:S(2)}, u32[]{:S(2)}) collective-permute-start(bf16[256,512]{1,0:T(8,128)(2,1)S(1)} %get-tuple-element.38.refs_0_), channel_id=1, source_target_pairs={{0,2},{1,3},{2,0},{3,1},{4,6},{5,7},{6,4},{7,5},{8,10},{9,11},{10,... | collective-permute-start | bytes 786440 | tf_op jit(solution)/shard_map/ppermute | solution.py:483
  39.0 22.3 %collective-permute-start.19 = (bf16[3,512,256]{2,1,0:T(8,128)(2,1)S(1)}, bf16[3,512,256]{2,1,0:T(8,128)(2,1)S(1)}, u32[]{:S(2)}, u32[]{:S(2)}) collective-permute-start(bf16[3,512,256]{2,1,0:T(8,128)(2,1)S(1)} %proj_partial.1.refs_4_.refs_0_), channel_id=1, source_target_pairs={{0,16},{16,0},{1,17},{17,1},{2,18},{18,2},{3,19},{19,3},{4,20},{20... | collective-permute-start | bytes 2359304 | tf_op jit(solution)/shard_map/ppermute | solution.py:487
  46.5 1.5 %collective-permute-start.14 = (bf16[256,512]{1,0:T(8,128)(2,1)S(1)}, bf16[256,512]{1,0:T(8,128)(2,1)S(1)}, u32[]{:S(2)}, u32[]{:S(2)}) collective-permute-start(bf16[256,512]{1,0:T(8,128)(2,1)S(1)} %get-tuple-element.43.refs_0_), channel_id=1, source_target_pairs={{0,1},{1,0},{2,3},{3,2},{4,5},{5,4},{6,7},{7,6},{8,9},{9,8},{10,11... | collective-permute-start | bytes 786440 | tf_op jit(solution)/shard_map/ppermute | solution.py:483
  46.5 1.9 %collective-permute-start.15 = (bf16[256,512]{1,0:T(8,128)(2,1)S(1)}, bf16[256,512]{1,0:T(8,128)(2,1)S(1)}, u32[]{:S(2)}, u32[]{:S(2)}) collective-permute-start(bf16[256,512]{1,0:T(8,128)(2,1)S(1)} %get-tuple-element.44.refs_1_), channel_id=1, source_target_pairs={{0,1},{1,0},{2,3},{3,2},{4,5},{5,4},{6,7},{7,6},{8,9},{9,8},{10,11... | collective-permute-start | bytes 786440 | tf_op jit(solution)/shard_map/ppermute | solution.py:483
  47.0 1.8 %collective-permute-start.16 = (bf16[256,512]{1,0:T(8,128)(2,1)S(1)}, bf16[256,512]{1,0:T(8,128)(2,1)S(1)}, u32[]{:S(2)}, u32[]{:S(2)}) collective-permute-start(bf16[256,512]{1,0:T(8,128)(2,1)S(1)} %get-tuple-element.45.refs_2_), channel_id=1, source_target_pairs={{0,1},{1,0},{2,3},{3,2},{4,5},{5,4},{6,7},{7,6},{8,9},{9,8},{10,11... | collective-permute-start | bytes 786440 | tf_op jit(solution)/shard_map/ppermute | solution.py:483
  47.1 2.1 %collective-permute-start.17 = (bf16[256,512]{1,0:T(8,128)(2,1)S(1)}, bf16[256,512]{1,0:T(8,128)(2,1)S(1)}, u32[]{:S(2)}, u32[]{:S(2)}) collective-permute-start(bf16[256,512]{1,0:T(8,128)(2,1)S(1)} %get-tuple-element.46.refs_3_), channel_id=1, source_target_pairs={{0,1},{1,0},{2,3},{3,2},{4,5},{5,4},{6,7},{7,6},{8,9},{9,8},{10,11... | collective-permute-start | bytes 786440 | tf_op jit(solution)/shard_map/ppermute | solution.py:483
  50.6 15.2 %collective-permute-start.18 = (bf16[512,256]{1,0:T(8,128)(2,1)S(1)}, bf16[512,256]{1,0:T(8,128)(2,1)S(1)}, u32[]{:S(2)}, u32[]{:S(2)}) collective-permute-start(bf16[512,256]{1,0:T(8,128)(2,1)S(1)} %grad_z_partial.1.refs_0_), channel_id=1, source_target_pairs={{0,16},{16,0},{1,17},{17,1},{2,18},{18,2},{3,19},{19,3},{4,20},{20... | collective-permute-start | bytes 786440 | tf_op jit(solution)/shard_map/ppermute | solution.py:487
  68.6 2.7 %collective-permute-start.20 = (bf16[4,512,256]{2,1,0:T(8,128)(2,1)S(1)}, bf16[4,512,256]{2,1,0:T(8,128)(2,1)S(1)}, u32[]{:S(2)}, u32[]{:S(2)}) collective-permute-start(bf16[4,512,256]{2,1,0:T(8,128)(2,1)S(1)} %input_partial.3), channel_id=1, source_target_pairs={{0,1},{1,0},{2,3},{3,2},{4,5},{5,4},{6,7},{7,6},{8,9},{9,8},{10,11... | collective-permute-start | bytes 3145736 | tf_op jit(solution)/shard_map/ppermute | solution.py:483
  71.6 6.2 %collective-permute-start.24 = (bf16[512,128]{1,0:T(8,128)(2,1)S(1)}, bf16[512,128]{1,0:T(8,128)(2,1)S(1)}, u32[]{:S(2)}, u32[]{:S(2)}) collective-permute-start(bf16[512,128]{1,0:T(8,128)(2,1)S(1)} %get-tuple-element.57), channel_id=1, source_target_pairs={{0,2},{1,3},{2,0},{3,1},{4,6},{5,7},{6,4},{7,5},{8,10},{9,11},{10,... | collective-permute-start | bytes 393224 | tf_op jit(solution)/shard_map/ppermute | solution.py:483
  72.6 6.8 %collective-permute-start.25 = (bf16[512,128]{1,0:T(8,128)(2,1)S(1)}, bf16[512,128]{1,0:T(8,128)(2,1)S(1)}, u32[]{:S(2)}, u32[]{:S(2)}) collective-permute-start(bf16[512,128]{1,0:T(8,128)(2,1)S(1)} %get-tuple-element.58), channel_id=1, source_target_pairs={{0,4},{1,5},{2,6},{3,7},{4,0},{5,1},{6,2},{7,3},{8,12},{9,13},{10,... | collective-permute-start | bytes 393224 | tf_op jit(solution)/shard_map/ppermute | solution.py:483
  74.3 8.0 %collective-permute-start.26 = (bf16[512,128]{1,0:T(8,128)(2,1)S(1)}, bf16[512,128]{1,0:T(8,128)(2,1)S(1)}, u32[]{:S(2)}, u32[]{:S(2)}) collective-permute-start(bf16[512,128]{1,0:T(8,128)(2,1)S(1)} %get-tuple-element.59), channel_id=1, source_target_pairs={{0,6},{1,7},{2,4},{3,5},{4,2},{5,3},{6,0},{7,1},{8,14},{9,15},{10,... | collective-permute-start | bytes 393224 | tf_op jit(solution)/shard_map/ppermute | solution.py:483
  75.2 9.0 %collective-permute-start.21 = (bf16[512,128]{1,0:T(8,128)(2,1)S(1)}, bf16[512,128]{1,0:T(8,128)(2,1)S(1)}, u32[]{:S(2)}, u32[]{:S(2)}) collective-permute-start(bf16[512,128]{1,0:T(8,128)(2,1)S(1)} %get-tuple-element.53), channel_id=1, source_target_pairs={{0,2},{1,3},{2,0},{3,1},{4,6},{5,7},{6,4},{7,5},{8,10},{9,11},{10,... | collective-permute-start | bytes 393224 | tf_op jit(solution)/shard_map/ppermute | solution.py:483
  76.1 8.5 %collective-permute-start.22 = (bf16[512,128]{1,0:T(8,128)(2,1)S(1)}, bf16[512,128]{1,0:T(8,128)(2,1)S(1)}, u32[]{:S(2)}, u32[]{:S(2)}) collective-permute-start(bf16[512,128]{1,0:T(8,128)(2,1)S(1)} %get-tuple-element.54), channel_id=1, source_target_pairs={{0,4},{1,5},{2,6},{3,7},{4,0},{5,1},{6,2},{7,3},{8,12},{9,13},{10,... | collective-permute-start | bytes 393224 | tf_op jit(solution)/shard_map/ppermute | solution.py:483
  77.8 9.0 %collective-permute-start.23 = (bf16[512,128]{1,0:T(8,128)(2,1)S(1)}, bf16[512,128]{1,0:T(8,128)(2,1)S(1)}, u32[]{:S(2)}, u32[]{:S(2)}) collective-permute-start(bf16[512,128]{1,0:T(8,128)(2,1)S(1)} %get-tuple-element.55), channel_id=1, source_target_pairs={{0,6},{1,7},{2,4},{3,5},{4,2},{5,3},{6,0},{7,1},{8,14},{9,15},{10,... | collective-permute-start | bytes 393224 | tf_op jit(solution)/shard_map/ppermute | solution.py:483
  82.3 5.0 %collective-permute-start.27 = (bf16[512,128]{1,0:T(8,128)(2,1)S(1)}, bf16[512,128]{1,0:T(8,128)(2,1)S(1)}, u32[]{:S(2)}, u32[]{:S(2)}) collective-permute-start(bf16[512,128]{1,0:T(8,128)(2,1)S(1)} %total.3), channel_id=1, source_target_pairs={{0,16},{16,0},{1,17},{17,1},{2,18},{18,2},{3,19},{19,3},{4,20},{20... | collective-permute-start | bytes 393224 | tf_op jit(solution)/shard_map/ppermute | solution.py:487
  87.4 7.8 %collective-permute-start.28 = (bf16[512,128]{1,0:T(8,128)(2,1)S(1)}, bf16[512,128]{1,0:T(8,128)(2,1)S(1)}, u32[]{:S(2)}, u32[]{:S(2)}) collective-permute-start(bf16[512,128]{1,0:T(8,128)(2,1)S(1)} %get-tuple-element.61), channel_id=1, source_target_pairs={{0,8},{1,9},{2,10},{3,11},{4,12},{5,13},{6,14},{7,15},{8,0},{9,1},... | collective-permute-start | bytes 393224 | tf_op jit(solution)/shard_map/ppermute | solution.py:483

commit v5 on v4

--- a/solution.py
+++ b/solution.py
@@ -107,8 +107,8 @@
 AHEAD = 3
 
 
-def prepare_kernel(v_ref, s_ref, ow_ref, *refs):
-    weights, (ow_out, done_ref, held, ins, in_sems, ow_sem) = refs[-9:-6], refs[-6:]
+def prepare_kernel(v_ref, s_ref, *refs):
+    weights, (done_ref, raw, held, ins, in_sems, s_sem) = refs[-9:-6], refs[-6:]
     piece = ins.shape[2]
     pieces = v_ref.shape[1] // piece
 
@@ -121,12 +121,13 @@
             v_ref.at[j, rows(i), :], ins.at[slot, j], in_sems.at[slot, j]
         )
 
+    scales = pltpu.make_async_copy(s_ref, raw, s_sem)
+    scales.start()
     for i in range(min(AHEAD, pieces)):
         for j in range(3):
             fetch(i, j).start()
-    whole = pltpu.make_async_copy(ow_ref, ow_out, ow_sem)
-    whole.start()
-    held[...] = s_ref[...].astype(F32)
+    scales.wait()
+    held[...] = raw[...].astype(F32)
     done_ref[...] = jnp.zeros(done_ref.shape, F32)
 
     def one(i, carry):
@@ -145,19 +146,19 @@
         return carry
 
     lax.fori_loop(0, pieces, one, 0)
-    whole.wait()
-
-
-def prepared(values, scales, out_weight, *earlier):
+
+
+def prepared(values, scales, *earlier):
     _, rows, channels = values.shape
     piece = min(rows, 512)
-    *weights, out_held, ready = pl.pallas_call(
+    *weights, ready = pl.pallas_call(
         prepare_kernel,
-        in_specs=[LATER_SPEC, VMEM_SPEC, LATER_SPEC] + [LATER_SPEC] * len(earlier),
-        out_specs=[VMEM_SPEC] * 5,
+        in_specs=[LATER_SPEC] * (2 + len(earlier)),
+        out_specs=[VMEM_SPEC] * 4,
         out_shape=[pltpu.VMEM((rows, channels), BF16)] * 3
-        + [pltpu.VMEM(out_weight.shape, BF16), jax.ShapeDtypeStruct((8, 128), F32)],
+        + [jax.ShapeDtypeStruct((8, 128), F32)],
         scratch_shapes=[
+            pltpu.VMEM(scales.shape, BF16),
             pltpu.VMEM(scales.shape, F32),
             pltpu.VMEM((AHEAD, 3, piece, channels), BF16),
             pltpu.SemaphoreType.DMA((AHEAD, 3)),
@@ -166,8 +167,8 @@
         compiler_params=params(16),
         cost_estimate=cost(values.size * 4, 4 * values.size),
         name="prepare",
-    )(in_hbm(values), scales, in_hbm(out_weight), *earlier)
-    return weights, out_held, ready
+    )(in_hbm(values), in_hbm(scales), *earlier)
+    return weights, ready
 
 
 Z1, Z0, X, CORE = 8, 4, 2, 1
@@ -193,34 +194,76 @@
     return pl.ds(pl.multiple_of(slices_of(masks)[n] * rows, BLOCK), rows)
 
 
+def load_kernel(in_ref, *refs):
+    out_ref, sem = refs[-2:]
+    copy = pltpu.make_async_copy(in_ref, out_ref, sem)
+    copy.start()
+    copy.wait()
+
+
+def loaded(array, *earlier):
+    return pl.pallas_call(
+        load_kernel,
+        in_specs=[LATER_SPEC] * (1 + len(earlier)),
+        out_specs=VMEM_SPEC,
+        out_shape=pltpu.VMEM(array.shape, array.dtype),
+        scratch_shapes=[pltpu.SemaphoreType.DMA],
+        compiler_params=params(8),
+        cost_estimate=cost(0, 4 * array.size),
+        name="loaded",
+    )(in_hbm(array), *earlier)
+
+
 def assembled(masks, refs, held):
     for n, ref in enumerate(refs):
         held[:, piece_rows(masks, n, ref.shape[1])] = ref[...]
 
 
-def proj_kernel(masks, runs, *refs):
-    xs, (out_ref, held) = refs[:-5], refs[-2:]
-    assembled(masks, xs, held)
-    run = held.shape[0] // runs
-    for j, w_ref in enumerate(refs[-5:-2]):
-        total = jnp.dot(held[...], w_ref[...], preferred_element_type=F32)
-        for h, start in enumerate(run_starts(runs, run)):
-            out_ref[j, :, pl.ds(start, run)] = total[h * run : (h + 1) * run].T.astype(BF16)
+def proj_part(runs, held_ref, w_ref, out_ref):
+    run = held_ref.shape[0] // runs
+    total = jnp.dot(held_ref[...], w_ref[...], preferred_element_type=F32)
+    for h, start in enumerate(run_starts(runs, run)):
+        out_ref[:, pl.ds(start, run)] = total[h * run : (h + 1) * run].T.astype(BF16)
+
+
+def pair_kernel(masks, runs, *refs):
+    xs, (key_ref, value_ref, out_ref, held_ref) = refs[:-4], refs[-4:]
+    assembled(masks, xs, held_ref)
+    proj_part(runs, held_ref, key_ref, out_ref.at[0])
+    proj_part(runs, held_ref, value_ref, out_ref.at[1])
+
+
+def query_kernel(runs, held_ref, w_ref, out_ref):
+    proj_part(runs, held_ref, w_ref, out_ref)
 
 
 def proj_partial(xs, masks, runs, weights):
     tokens = xs[0].shape[0]
     depth, channels = weights[0].shape
-    return pl.pallas_call(
-        functools.partial(proj_kernel, masks, runs),
-        in_specs=[VMEM_SPEC] * (len(xs) + 3),
+    flops = 2 * tokens * depth * channels
+    weights = [in_vmem(weight) for weight in weights]
+    pair, held = pl.pallas_call(
+        functools.partial(pair_kernel, masks, runs),
+        in_specs=[VMEM_SPEC] * (len(xs) + 2),
+        out_specs=[VMEM_SPEC] * 2,
+        out_shape=[
+            jax.ShapeDtypeStruct((2, channels, tokens), BF16),
+            pltpu.VMEM((tokens, depth), BF16),
+        ],
+        compiler_params=params(16),
+        cost_estimate=cost(2 * flops, 4 * depth * channels),
+        name="proj_pair",
+    )(*xs, *weights[1:])
+    queries = pl.pallas_call(
+        functools.partial(query_kernel, runs),
+        in_specs=[VMEM_SPEC] * 2,
         out_specs=VMEM_SPEC,
-        out_shape=jax.ShapeDtypeStruct((3, channels, tokens), BF16),
-        scratch_shapes=[pltpu.VMEM((tokens, depth), BF16)],
-        compiler_params=params(16),
-        cost_estimate=cost(6 * tokens * depth * channels, 6 * depth * channels),
-        name="proj_partial",
-    )(*xs, *[in_vmem(weight) for weight in weights])
+        out_shape=jax.ShapeDtypeStruct((channels, tokens), BF16),
+        compiler_params=params(16),
+        cost_estimate=cost(flops, 2 * depth * channels),
+        name="proj_queries",
+    )(held, weights[0])
+    return pair, queries
 
 
 def grad_z_kernel(masks, runs, *refs):
@@ -311,7 +354,7 @@
     return jnp.concatenate([array[i * rows : (i + 1) * rows] for i in range(blocks)], 1)
 
 
-def summed(refs, part):
+def summed(refs, part=...):
     total = refs[0][part].astype(F32)
     for ref in refs[1:]:
         total = total + ref[part].astype(F32)
@@ -319,11 +362,10 @@
 
 
 def conv_kernel(parts, groups, *refs):
-    shares, (past_ref, proj_ref, prod_ref, conv_ref) = refs[:parts], refs[parts:]
-    key, value = summed(shares, 1), summed(shares, 2)
-    proj_ref[0] = summed(shares, 0)
-    proj_ref[1] = key
-    proj_ref[2] = value
+    shares, (past_ref, pair_ref, prod_ref, conv_ref) = refs[:parts], refs[parts:]
+    key, value = summed(shares, 0), summed(shares, 1)
+    pair_ref[0] = key
+    pair_ref[1] = value
     product = (key.astype(F32) * value.astype(F32)).astype(BF16)
     prod_ref[...] = product
     channels, tokens = product.shape
@@ -337,19 +379,19 @@
 def conv_forward(shares, past):
     _, channels, tokens = shares[0].shape
     groups = past.shape[0]
-    steps = max(1, groups // 8)
+    steps = max(1, groups // 16)
     chunk = channels // steps
     parts = len(shares)
-    three = pl.BlockSpec((3, chunk, tokens), lambda i: (0, i, 0))
+    two = pl.BlockSpec((2, chunk, tokens), lambda i: (0, i, 0))
     one = pl.BlockSpec((chunk, tokens), lambda i: (i, 0))
     return pl.pallas_call(
         functools.partial(conv_kernel, parts, groups // steps),
         grid=(steps,),
-        in_specs=[three] * parts
+        in_specs=[two] * parts
         + [pl.BlockSpec((groups // steps,) + past.shape[1:], lambda i: (i, 0, 0))],
-        out_specs=[three, one, one],
+        out_specs=[two, one, one],
         out_shape=[
-            jax.ShapeDtypeStruct((3, channels, tokens), BF16),
+            jax.ShapeDtypeStruct((2, channels, tokens), BF16),
             jax.ShapeDtypeStruct((channels, tokens), BF16),
             jax.ShapeDtypeStruct((channels, tokens), F32),
         ],
@@ -360,12 +402,13 @@
 
 
 def conv_back_kernel(parts, groups, *refs):
-    partials, (proj_ref, conv_ref, next_ref, out_ref, grad_ref) = refs[:parts], refs[parts:]
-    grad_z = partials[0][...].astype(F32)
-    for ref in partials[1:]:
+    shares, queries = refs[:parts], refs[parts : 2 * parts]
+    pair_ref, conv_ref, next_ref, out_ref, grad_ref = refs[2 * parts :]
+    grad_z = shares[0][...].astype(F32)
+    for ref in shares[1:]:
         grad_z = grad_z + ref[...].astype(F32)
     out_ref[0] = (grad_z * conv_ref[...]).astype(BF16)
-    grad = (grad_z * proj_ref[0].astype(F32)).astype(BF16)
+    grad = (grad_z * summed(queries).astype(F32)).astype(BF16)
     grad_ref[...] = grad
     channels, tokens = grad.shape
     per = channels // groups
@@ -373,24 +416,24 @@
         rows = slice(g * per, (g + 1) * per)
         result = jnp.dot(paired(grad[rows], 1), next_ref[g], preferred_element_type=F32)
         result = unstacked(result, tokens // BLOCK)
-        out_ref[1, rows] = (result * proj_ref[2, rows].astype(F32)).astype(BF16)
-        out_ref[2, rows] = (result * proj_ref[1, rows].astype(F32)).astype(BF16)
-
-
-def conv_backward(partials, proj, conv, after):
+        out_ref[1, rows] = (result * pair_ref[1, rows].astype(F32)).astype(BF16)
+        out_ref[2, rows] = (result * pair_ref[0, rows].astype(F32)).astype(BF16)
+
+
+def conv_backward(shares, queries, pair, conv, after):
     channels, tokens = conv.shape
     groups = after.shape[0]
-    steps = max(1, groups // 8)
+    steps = max(1, groups // 16)
     chunk = channels // steps
-    parts = len(partials)
+    parts = len(shares)
     three = pl.BlockSpec((3, chunk, tokens), lambda i: (0, i, 0))
     one = pl.BlockSpec((chunk, tokens), lambda i: (i, 0))
     return pl.pallas_call(
         functools.partial(conv_back_kernel, parts, groups // steps),
         grid=(steps,),
-        in_specs=[one] * parts
+        in_specs=[one] * (2 * parts)
         + [
-            three,
+            pl.BlockSpec((2, chunk, tokens), lambda i: (0, i, 0)),
             one,
             pl.BlockSpec((groups // steps,) + after.shape[1:], lambda i: (i, 0, 0)),
         ],
@@ -402,7 +445,7 @@
         compiler_params=params(16),
         cost_estimate=cost(4 * channels * tokens * BLOCK * 8, channels * tokens * 24),
         name="conv_backward",
-    )(*partials, proj, conv, after)
+    )(*shares, *queries, pair, conv, after)
 
 
 def taps_kernel(groups, prod_ref, grad_ref, out_ref):
@@ -621,19 +664,22 @@
 def on_small_slice(tokens, values, scales, filters, out_weight, cotangent):
     rows = tokens.shape[1]
     token_stage = first_stage(tokens)
-    weights, out_held, ready = prepared(values, scales, out_weight)
+    weights, ready = prepared(values, scales)
     token_own = own_slice(in_hbm(tokens), *token_stage, ready)
     token_same = second_stage(token_own)
     past, later = toeplitz(filters, token_own)
-    cotangent = copied(cotangent, past)
+    out_held = loaded(out_weight, past)
+    cotangent = copied(cotangent, token_own)
     cot_own = own_slice(cotangent, *first_stage(cotangent))
-    *token_same, cot_own = relayed([*token_same, cot_own])
+    *token_same, cot_own = relayed([*token_same, cot_own], out_held)
     cot_same = second_stage(cot_own)
-    proj_part = proj_partial(both_cores(token_same), MINE + OTHERS, 2, weights)
-    cot_same = list(relayed(cot_same, proj_part))
-    proj, product, conv = conv_forward([proj_part, other_row(proj_part)], past)
+    pair, queries = proj_partial(both_cores(token_same), MINE + OTHERS, 2, weights)
+    cot_same = list(relayed(cot_same, queries))
+    pair, product, conv = conv_forward([pair, other_row(pair)], past)
     z_part = grad_z_partial(both_cores(cot_same), MINE + OTHERS, 2, out_held)
-    grad_proj, grad = conv_backward([z_part, other_row(z_part)], proj, conv, later)
+    grad_proj, grad = conv_backward(
+        [z_part, other_row(z_part)], [queries, other_row(queries)], pair, conv, later
+    )
     others = input_partial(OTHERS, 4, rows, weights, grad_proj)
     same = input_partial(MINE, 4, rows, weights, grad_proj)
     return scattered(same, others), taps_gradient(product, grad, filters.shape[0])
@@ -654,12 +700,13 @@
         every = lax.all_gather(array, "fsdp", axis=0)
         return [every[i] for i in range(count)]
 
-    weights, out_held, _ = prepared(values, scales, out_weight)
+    weights, _ = prepared(values, scales)
+    out_held = loaded(out_weight)
     past, later = toeplitz(filters)
-    proj_part = proj_partial(gather(tokens), None, 1, weights)
-    proj, product, conv = conv_forward(shares(proj_part), past)
+    pair, queries = proj_partial(gather(tokens), None, 1, weights)
+    pair, product, conv = conv_forward(shares(pair), past)
     z_part = grad_z_partial(gather(cotangent), None, 1, out_held)
-    grad_proj, grad = conv_backward(shares(z_part), proj, conv, later)
+    grad_proj, grad = conv_backward(shares(z_part), shares(queries), pair, conv, later)
     partial = input_partial(None, pieces, piece, weights, grad_proj)
     partial = partial.reshape(rows, partial.shape[2]).astype(F32)
     partial = lax.all_to_all(partial, "fsdp", 1, 0, tiled=True)

time: 96.1 us -> 95.4 us (level)
  waiting for transfers between devices: 29.1 us -> 25.3 us
  starting transfers between devices: 41.6 us -> 44.1 us
  Pallas kernels: 23.6 us -> 24.9 us
    ppermute x3 -> x4, starting transfers between devices: 9.39 us -> 14.1 us  [other_row(): return lax.ppermute(array, 'fsdp', [(0, 1), (1, 0)])]
    pallas_call x2 -> x4, Pallas kernels: 10 us -> 12 us  [the longest x1 5.89 us: prepared(): pl.pallas_call(prepare_kernel, in_specs=[LATER_SPEC] * (2 + len(earlier))...]
    ppermute x22, waiting for transfers between devices: 14.1 us -> 12.2 us  [across(): return lax.ppermute(array, 'tensor', [(i, i ^ mask) for i in range(16)])]
    ppermute x4, starting transfers between devices: 12.4 us -> 10.7 us  [in_square(): return lax.ppermute(array, ('fsdp', 'tensor'), pairs)]
    ppermute x3 -> x4, waiting for transfers between devices: 10.9 us -> 9.33 us  [other_row(): return lax.ppermute(array, 'fsdp', [(0, 1), (1, 0)])]
  transfers between devices with their start and end apart: 29 -> 30, of which waited for: 16 -> 12; matrix products, arithmetic and copies ran while one was open for 0% -> 0% of each run, Pallas kernels for 20% -> 22%
where the time goes in v5:
time: 95.4 us; the launch traced here: 95.2 us
  starting transfers between devices  44.1 us (46%)
  waiting for transfers between devices  25.3 us (27%)
  Pallas kernels  24.9 us (26%)
    ppermute x22, starting transfers between devices, across(): return lax.ppermute(array, 'tensor', [(i, i ^ mask) for i in range(16)])  19.3 us
    ppermute x4, starting transfers between devices, other_row(): return lax.ppermute(array, 'fsdp', [(0, 1), (1, 0)])  14.1 us
    ppermute x22, waiting for transfers between devices, across(): return lax.ppermute(array, 'tensor', [(i, i ^ mask) for i in range(16)])  12.2 us
    ppermute x4, starting transfers between devices, in_square(): return lax.ppermute(array, ('fsdp', 'tensor'), pairs)  10.7 us
    ppermute x4, waiting for transfers between devices, other_row(): return lax.ppermute(array, 'fsdp', [(0, 1), (1, 0)])  9.33 us
    pallas_call x1, Pallas kernels, prepared(): pl.pallas_call(prepare_kernel, in_specs=[LATER_SPEC] * (2 + len(earlier))...  5.89 us
    ppermute x4, waiting for transfers between devices, in_square(): return lax.ppermute(array, ('fsdp', 'tensor'), pairs)  3.76 us
    pallas_call x2, Pallas kernels, input_partial(): pl.pallas_call(functools.partial(input_kernel, masks), in_specs=[VMEM_SPE...  3.57 us
  transfers between devices with their start and end apart: 30, of which 12 were waited for; matrix products, arithmetic and copies ran while one was open for 0% of the time, Pallas kernels for 22%

profile of v5, /device:TPU:0, one launch (start us, length us, event | category | flops | bytes accessed | tf_op | source)
XLA Modules:
  0.0 95.2 jit_solution(4770445094110836483)
XLA Ops:
  0.6 4.1 %collective-permute-start = (bf16[128,512]{1,0:T(8,128)(2,1)}, bf16[128,512]{1,0:T(8,128)(2,1)S(1)}, u32[]{:S(2)}, u32[]{:S(2)}) collective-permute-start(bf16[128,512]{1,0:T(8,128)(2,1)} %array_ref.1), channel_id=1, source_target_pairs={{0,8},{1,9},{2,10},{3,11},{4,12},{5,13},{6,14},{7,15},{8,24},{9,25... | collective-permute-start | bytes 393224 | tf_op jit(solution)/shard_map/ppermute | solution.py:540
  5.4 5.9 %prepare.1 = (bf16[4096,512]{1,0:T(8,128)(2,1)S(1)}, bf16[4096,512]{1,0:T(8,128)(2,1)S(1)}, bf16[4096,512]{1,0:T(8,128)(2,1)S(1)}, f32[8,128]{1,0:T(8,128)S(1)}) custom-call(bf16[3,4096,512]{2,1,0:T(8,128)(2,1)} %bitcast.5, bf16[3,32,512]{2,1,0:T(8,128)(2,1)} %bitcast.6), custom_call_target="tpu_custom_call" | custom-call | flops 6144 | bytes 6144 | tf_op jit(solution)/shard_map/prepare/pallas_call | solution.py:154
  12.3 1.6 %collective-permute-start.2 = (bf16[256,512]{1,0:T(8,128)(2,1)S(1)}, bf16[256,512]{1,0:T(8,128)(2,1)S(1)}, u32[]{:S(2)}, u32[]{:S(2)}) collective-permute-start(bf16[256,512]{1,0:T(8,128)(2,1)S(1)} %own_slice.2.refs_0_), channel_id=1, source_target_pairs={{0,2},{1,3},{2,0},{3,1},{4,6},{5,7},{6,4},{7,5},{8,10},{9,11},{10,... | collective-permute-start | bytes 786440 | tf_op jit(solution)/shard_map/ppermute | solution.py:526
  13.8 1.6 %collective-permute-start.3 = (bf16[256,512]{1,0:T(8,128)(2,1)S(1)}, bf16[256,512]{1,0:T(8,128)(2,1)S(1)}, u32[]{:S(2)}, u32[]{:S(2)}) collective-permute-start(bf16[256,512]{1,0:T(8,128)(2,1)S(1)} %own_slice.2.refs_0_), channel_id=1, source_target_pairs={{0,4},{1,5},{2,6},{3,7},{4,0},{5,1},{6,2},{7,3},{8,12},{9,13},{10,... | collective-permute-start | bytes 786440 | tf_op jit(solution)/shard_map/ppermute | solution.py:526
  15.8 5.3 %collective-permute-start.5 = (bf16[128,512]{1,0:T(8,128)(2,1)S(1)}, bf16[128,512]{1,0:T(8,128)(2,1)S(1)}, u32[]{:S(2)}, u32[]{:S(2)}) collective-permute-start(bf16[128,512]{1,0:T(8,128)(2,1)S(1)} %copied.1.array_ref), channel_id=1, source_target_pairs={{0,8},{1,9},{2,10},{3,11},{4,12},{5,13},{6,14},{7,15},{8,24},{9,25... | collective-permute-start | bytes 393224 | tf_op jit(solution)/shard_map/ppermute | solution.py:540
  21.8 1.1 %toeplitz.1 = (bf16[32,256,128]{2,1,0:T(8,128)(2,1)S(1)}, bf16[32,256,128]{2,1,0:T(8,128)(2,1)S(1)}) custom-call(f32[32,128]{1,0:T(8,128)S(1)} %copy-done.1, bf16[256,512]{1,0:T(8,128)(2,1)S(1)} %own_slice.2.refs_0_), custom_call_target="tpu_custom_call" | custom-call | flops 2000 | bytes 1024 | tf_op jit(solution)/shard_map/toeplitz/pallas_call | solution.py:320
  22.9 2.2 %loaded.1.refs_5_.refs_8_ = bf16[512,4096]{1,0:T(8,128)(2,1)S(1)} custom-call(bf16[512,4096]{1,0:T(8,128)(2,1)} %in_ref.3, bf16[32,256,128]{2,1,0:T(8,128)(2,1)S(1)} %get-tuple-element.38.refs_0_.refs_2_), custom_call_target="tpu_custom_call" | custom-call | bytes 2048 | tf_op jit(solution)/shard_map/loaded/pallas_call | solution.py:205
  25.1 3.8 %collective-permute-done.5.turned_ref = bf16[128,512]{1,0:T(8,128)(2,1)S(1)} collective-permute-done((bf16[128,512]{1,0:T(8,128)(2,1)S(1)}, bf16[128,512]{1,0:T(8,128)(2,1)S(1)}, u32[]{:S(2)}, u32[]{:S(2)}) %collective-permute-start.5) | collective-permute-done | bytes 131104 | tf_op jit(solution)/shard_map/ppermute | solution.py:540
  30.7 1.5 %collective-permute-start.7 = (bf16[256,512]{1,0:T(8,128)(2,1)S(1)}, bf16[256,512]{1,0:T(8,128)(2,1)S(1)}, u32[]{:S(2)}, u32[]{:S(2)}) collective-permute-start(bf16[256,512]{1,0:T(8,128)(2,1)S(1)} %get-tuple-element.39.refs_0_), channel_id=1, source_target_pairs={{0,2},{1,3},{2,0},{3,1},{4,6},{5,7},{6,4},{7,5},{8,10},{9,11},{10,... | collective-permute-start | bytes 786440 | tf_op jit(solution)/shard_map/ppermute | solution.py:526
  32.4 1.8 %collective-permute-start.9 = (bf16[256,512]{1,0:T(8,128)(2,1)S(1)}, bf16[256,512]{1,0:T(8,128)(2,1)S(1)}, u32[]{:S(2)}, u32[]{:S(2)}) collective-permute-start(bf16[256,512]{1,0:T(8,128)(2,1)S(1)} %get-tuple-element.39.refs_0_), channel_id=1, source_target_pairs={{0,6},{1,7},{2,4},{3,5},{4,2},{5,3},{6,0},{7,1},{8,14},{9,15},{10,... | collective-permute-start | bytes 786440 | tf_op jit(solution)/shard_map/ppermute | solution.py:526
  34.2 2.5 %proj_pair.1 = (bf16[2,512,256]{2,1,0:T(8,128)(2,1)S(1)}, bf16[256,4096]{1,0:T(8,128)(2,1)S(1)}) custom-call(bf16[256,512]{1,0:T(8,128)(2,1)S(1)} %get-tuple-element.40.refs_0_, bf16[256,512]{1,0:T(8,128)(2,1)S(1)} %get-tuple-element.41.refs_1_, bf16[256,512]{1,0:T(8,128)(2,1)S(1)} %get-tuple-element.42.refs_2_, ...), custom_call_target="tpu_custom_call" | custom-call | flops 524288 | bytes 2048 | tf_op jit(solution)/shard_map/proj_pair/pallas_call | solution.py:245
  36.8 5.6 %collective-permute-start.20 = (bf16[2,512,256]{2,1,0:T(8,128)(2,1)S(1)}, bf16[2,512,256]{2,1,0:T(8,128)(2,1)S(1)}, u32[]{:S(2)}, u32[]{:S(2)}) collective-permute-start(bf16[2,512,256]{2,1,0:T(8,128)(2,1)S(1)} %get-tuple-element.49.refs_0_), channel_id=1, source_target_pairs={{0,16},{16,0},{1,17},{17,1},{2,18},{18,2},{3,19},{19,3},{4,20},{20... | collective-permute-start | bytes 1572872 | tf_op jit(solution)/shard_map/ppermute | solution.py:530
  42.4 1.3 %proj_queries.1.refs_4_.refs_2_ = bf16[512,256]{1,0:T(8,128)(2,1)S(1)} custom-call(bf16[256,4096]{1,0:T(8,128)(2,1)S(1)} %get-tuple-element.44.held_ref, bf16[4096,512]{1,0:T(8,128)(2,1)S(1)} %get-tuple-element.34.w_ref.refs_0_), custom_call_target="tpu_custom_call" | custom-call | flops 262144 | bytes 1024 | tf_op jit(solution)/shard_map/proj_queries/pallas_call | solution.py:257
  43.7 2.4 %collective-permute-done.9.refs_3_ = bf16[256,512]{1,0:T(8,128)(2,1)S(1)} collective-permute-done((bf16[256,512]{1,0:T(8,128)(2,1)S(1)}, bf16[256,512]{1,0:T(8,128)(2,1)S(1)}, u32[]{:S(2)}, u32[]{:S(2)}) %collective-permute-start.9) | collective-permute-done | bytes 262176 | tf_op jit(solution)/shard_map/ppermute | solution.py:526
  47.7 5.5 %collective-permute-start.19 = (bf16[512,256]{1,0:T(8,128)(2,1)S(1)}, bf16[512,256]{1,0:T(8,128)(2,1)S(1)}, u32[]{:S(2)}, u32[]{:S(2)}) collective-permute-start(bf16[512,256]{1,0:T(8,128)(2,1)S(1)} %proj_queries.1.refs_4_.refs_2_), channel_id=1, source_target_pairs={{0,16},{16,0},{1,17},{17,1},{2,18},{18,2},{3,19},{19,3},{4,20},{20... | collective-permute-start | bytes 786440 | tf_op jit(solution)/shard_map/ppermute | solution.py:530
  53.1 1.5 %grad_z_partial.1.refs_0_ = bf16[512,256]{1,0:T(8,128)(2,1)S(1)} custom-call(bf16[256,512]{1,0:T(8,128)(2,1)S(1)} %get-tuple-element.45.refs_0_, bf16[256,512]{1,0:T(8,128)(2,1)S(1)} %get-tuple-element.46.refs_1_, bf16[256,512]{1,0:T(8,128)(2,1)S(1)} %get-tuple-element.47.refs_2_, bf16[256,512]{1,0:T(8,128)(2,1)S(1)} %get-tuple-element.48.refs_3_, ...), custom_call_target="tpu_custom_call" | custom-call | flops 262144 | bytes 1024 | tf_op jit(solution)/shard_map/grad_z_partial/pallas_call | solution.py:283
  54.6 1.2 %collective-permute-start.18 = (bf16[512,256]{1,0:T(8,128)(2,1)S(1)}, bf16[512,256]{1,0:T(8,128)(2,1)S(1)}, u32[]{:S(2)}, u32[]{:S(2)}) collective-permute-start(bf16[512,256]{1,0:T(8,128)(2,1)S(1)} %grad_z_partial.1.refs_0_), channel_id=1, source_target_pairs={{0,16},{16,0},{1,17},{17,1},{2,18},{18,2},{3,19},{19,3},{4,20},{20... | collective-permute-start | bytes 786440 | tf_op jit(solution)/shard_map/ppermute | solution.py:530
  56.5 3.7 %collective-permute-done.19.refs_3_ = bf16[512,256]{1,0:T(8,128)(2,1)S(1)} collective-permute-done((bf16[512,256]{1,0:T(8,128)(2,1)S(1)}, bf16[512,256]{1,0:T(8,128)(2,1)S(1)}, u32[]{:S(2)}, u32[]{:S(2)}) %collective-permute-start.19) | collective-permute-done | bytes 262176 | tf_op jit(solution)/shard_map/ppermute | solution.py:530
  60.2 5.1 %collective-permute-done.18.refs_1_ = bf16[512,256]{1,0:T(8,128)(2,1)S(1)} collective-permute-done((bf16[512,256]{1,0:T(8,128)(2,1)S(1)}, bf16[512,256]{1,0:T(8,128)(2,1)S(1)}, u32[]{:S(2)}, u32[]{:S(2)}) %collective-permute-start.18) | collective-permute-done | bytes 262176 | tf_op jit(solution)/shard_map/ppermute | solution.py:530
  66.1 1.8 %input_partial.3 = bf16[4,512,256]{2,1,0:T(8,128)(2,1)S(1)} custom-call(bf16[4096,512]{1,0:T(8,128)(2,1)S(1)} %get-tuple-element.34.w_ref.refs_0_, bf16[4096,512]{1,0:T(8,128)(2,1)S(1)} %get-tuple-element.35.refs_8_.refs_1_, bf16[4096,512]{1,0:T(8,128)(2,1)S(1)} %get-tuple-element.36.refs_9_.refs_2_, bf16[1536,256]{1,0:T(8,128)(2,1)S(1)} %bitcast.3), custom_call_target="tpu_custom_call" | custom-call | flops 393216 | bytes 1792 | tf_op jit(solution)/shard_map/input_partial/pallas_call | solution.py:512
  67.9 1.8 %input_partial.2.same_ref = bf16[4,512,256]{2,1,0:T(8,128)(2,1)S(1)} custom-call(bf16[4096,512]{1,0:T(8,128)(2,1)S(1)} %get-tuple-element.34.w_ref.refs_0_, bf16[4096,512]{1,0:T(8,128)(2,1)S(1)} %get-tuple-element.35.refs_8_.refs_1_, bf16[4096,512]{1,0:T(8,128)(2,1)S(1)} %get-tuple-element.36.refs_9_.refs_2_, bf16[1536,256]{1,0:T(8,128)(2,1)S(1)} %bitcast.4), custom_call_target="tpu_custom_call" | custom-call | flops 393216 | bytes 1792 | tf_op jit(solution)/shard_map/input_partial/pallas_call | solution.py:512
  70.8 1.1 %collective-permute-start.25 = (bf16[512,128]{1,0:T(8,128)(2,1)S(1)}, bf16[512,128]{1,0:T(8,128)(2,1)S(1)}, u32[]{:S(2)}, u32[]{:S(2)}) collective-permute-start(bf16[512,128]{1,0:T(8,128)(2,1)S(1)} %get-tuple-element.59), channel_id=1, source_target_pairs={{0,2},{1,3},{2,0},{3,1},{4,6},{5,7},{6,4},{7,5},{8,10},{9,11},{10,... | collective-permute-start | bytes 393224 | tf_op jit(solution)/shard_map/ppermute | solution.py:526
  71.9 1.5 %collective-permute-start.26 = (bf16[512,128]{1,0:T(8,128)(2,1)S(1)}, bf16[512,128]{1,0:T(8,128)(2,1)S(1)}, u32[]{:S(2)}, u32[]{:S(2)}) collective-permute-start(bf16[512,128]{1,0:T(8,128)(2,1)S(1)} %get-tuple-element.60), channel_id=1, source_target_pairs={{0,4},{1,5},{2,6},{3,7},{4,0},{5,1},{6,2},{7,3},{8,12},{9,13},{10,... | collective-permute-start | bytes 393224 | tf_op jit(solution)/shard_map/ppermute | solution.py:526
  74.4 1.0 %collective-permute-start.22 = (bf16[512,128]{1,0:T(8,128)(2,1)S(1)}, bf16[512,128]{1,0:T(8,128)(2,1)S(1)}, u32[]{:S(2)}, u32[]{:S(2)}) collective-permute-start(bf16[512,128]{1,0:T(8,128)(2,1)S(1)} %get-tuple-element.55), channel_id=1, source_target_pairs={{0,2},{1,3},{2,0},{3,1},{4,6},{5,7},{6,4},{7,5},{8,10},{9,11},{10,... | collective-permute-start | bytes 393224 | tf_op jit(solution)/shard_map/ppermute | solution.py:526
  75.4 1.5 %collective-permute-start.23 = (bf16[512,128]{1,0:T(8,128)(2,1)S(1)}, bf16[512,128]{1,0:T(8,128)(2,1)S(1)}, u32[]{:S(2)}, u32[]{:S(2)}) collective-permute-start(bf16[512,128]{1,0:T(8,128)(2,1)S(1)} %get-tuple-element.56), channel_id=1, source_target_pairs={{0,4},{1,5},{2,6},{3,7},{4,0},{5,1},{6,2},{7,3},{8,12},{9,13},{10,... | collective-permute-start | bytes 393224 | tf_op jit(solution)/shard_map/ppermute | solution.py:526
  77.0 1.6 %collective-permute-start.24 = (bf16[512,128]{1,0:T(8,128)(2,1)S(1)}, bf16[512,128]{1,0:T(8,128)(2,1)S(1)}, u32[]{:S(2)}, u32[]{:S(2)}) collective-permute-start(bf16[512,128]{1,0:T(8,128)(2,1)S(1)} %get-tuple-element.57), channel_id=1, source_target_pairs={{0,6},{1,7},{2,4},{3,5},{4,2},{5,3},{6,0},{7,1},{8,14},{9,15},{10,... | collective-permute-start | bytes 393224 | tf_op jit(solution)/shard_map/ppermute | solution.py:526
  78.6 2.9 %collective-permute-done.27.refs_3_ = bf16[512,128]{1,0:T(8,128)(2,1)S(1)} collective-permute-done((bf16[512,128]{1,0:T(8,128)(2,1)S(1)}, bf16[512,128]{1,0:T(8,128)(2,1)S(1)}, u32[]{:S(2)}, u32[]{:S(2)}) %collective-permute-start.27) | collective-permute-done | bytes 131104 | tf_op jit(solution)/shard_map/ppermute | solution.py:526
  81.6 1.8 %collective-permute-start.28 = (bf16[512,128]{1,0:T(8,128)(2,1)S(1)}, bf16[512,128]{1,0:T(8,128)(2,1)S(1)}, u32[]{:S(2)}, u32[]{:S(2)}) collective-permute-start(bf16[512,128]{1,0:T(8,128)(2,1)S(1)} %total.3), channel_id=1, source_target_pairs={{0,16},{16,0},{1,17},{17,1},{2,18},{18,2},{3,19},{19,3},{4,20},{20... | collective-permute-start | bytes 393224 | tf_op jit(solution)/shard_map/ppermute | solution.py:530
  83.8 2.3 %collective-permute-done.24.refs_3_ = bf16[512,128]{1,0:T(8,128)(2,1)S(1)} collective-permute-done((bf16[512,128]{1,0:T(8,128)(2,1)S(1)}, bf16[512,128]{1,0:T(8,128)(2,1)S(1)}, u32[]{:S(2)}, u32[]{:S(2)}) %collective-permute-start.24) | collective-permute-done | bytes 131104 | tf_op jit(solution)/shard_map/ppermute | solution.py:526
  86.6 2.4 %collective-permute-start.29 = (bf16[512,128]{1,0:T(8,128)(2,1)S(1)}, bf16[512,128]{1,0:T(8,128)(2,1)S(1)}, u32[]{:S(2)}, u32[]{:S(2)}) collective-permute-start(bf16[512,128]{1,0:T(8,128)(2,1)S(1)} %get-tuple-element.63), channel_id=1, source_target_pairs={{0,8},{1,9},{2,10},{3,11},{4,12},{5,13},{6,14},{7,15},{8,0},{9,1},... | collective-permute-start | bytes 393224 | tf_op jit(solution)/shard_map/ppermute | solution.py:526
  89.0 3.2 %taps_gradient.1 = f32[32,128]{1,0:T(8,128)} custom-call(bf16[512,256]{1,0:T(8,128)(2,1)S(1)} %get-tuple-element.64.prod_ref, bf16[512,256]{1,0:T(8,128)(2,1)S(1)} %get-tuple-element.65.grad_ref), custom_call_target="tpu_custom_call" | custom-call | flops 131072 | bytes 768 | tf_op jit(solution)/shard_map/taps_gradient/pallas_call | solution.py:489
  92.3 2.1 %collective-permute-done.29.got_ref = bf16[512,128]{1,0:T(8,128)(2,1)S(1)} collective-permute-done((bf16[512,128]{1,0:T(8,128)(2,1)S(1)}, bf16[512,128]{1,0:T(8,128)(2,1)S(1)}, u32[]{:S(2)}, u32[]{:S(2)}) %collective-permute-start.29) | collective-permute-done | bytes 131104 | tf_op jit(solution)/shard_map/ppermute | solution.py:526
  (53 shorter events, 11.6 us)
Async XLA Ops:
  0.6 10.7 %collective-permute-start = (bf16[128,512]{1,0:T(8,128)(2,1)}, bf16[128,512]{1,0:T(8,128)(2,1)S(1)}, u32[]{:S(2)}, u32[]{:S(2)}) collective-permute-start(bf16[128,512]{1,0:T(8,128)(2,1)} %array_ref.1), channel_id=1, source_target_pairs={{0,8},{1,9},{2,10},{3,11},{4,12},{5,13},{6,14},{7,15},{8,24},{9,25... | collective-permute-start | bytes 393224 | tf_op jit(solution)/shard_map/ppermute | solution.py:540
  4.7 6.6 %collective-permute-start.1 = (bf16[128,512]{1,0:T(8,128)(2,1)}, bf16[128,512]{1,0:T(8,128)(2,1)S(1)}, u32[]{:S(2)}, u32[]{:S(2)}) collective-permute-start(bf16[128,512]{1,0:T(8,128)(2,1)} %array_ref.1), channel_id=1, source_target_pairs={{8,16},{9,17},{10,18},{11,19},{12,20},{13,21},{14,22},{15,23},{16,... | collective-permute-start | bytes 393224 | tf_op jit(solution)/shard_map/ppermute | solution.py:540
  5.4 10.4 %copy-start = (bf16[128,512]{1,0:T(8,128)(2,1)S(1)}, bf16[128,512]{1,0:T(8,128)(2,1)}, u32[]{:S(2)}) copy-start(bf16[128,512]{1,0:T(8,128)(2,1)} %in_ref.2) | copy-start | bytes 393220
  5.4 16.4 %copy-start.1 = (f32[32,128]{1,0:T(8,128)S(1)}, f32[32,128]{1,0:T(8,128)}, u32[]{:S(2)}) copy-start(f32[32,128]{1,0:T(8,128)} %taps_ref.1) | copy-start | bytes 49156
  12.3 16.7 %collective-permute-start.2 = (bf16[256,512]{1,0:T(8,128)(2,1)S(1)}, bf16[256,512]{1,0:T(8,128)(2,1)S(1)}, u32[]{:S(2)}, u32[]{:S(2)}) collective-permute-start(bf16[256,512]{1,0:T(8,128)(2,1)S(1)} %own_slice.2.refs_0_), channel_id=1, source_target_pairs={{0,2},{1,3},{2,0},{3,1},{4,6},{5,7},{6,4},{7,5},{8,10},{9,11},{10,... | collective-permute-start | bytes 786440 | tf_op jit(solution)/shard_map/ppermute | solution.py:526
  13.8 15.2 %collective-permute-start.3 = (bf16[256,512]{1,0:T(8,128)(2,1)S(1)}, bf16[256,512]{1,0:T(8,128)(2,1)S(1)}, u32[]{:S(2)}, u32[]{:S(2)}) collective-permute-start(bf16[256,512]{1,0:T(8,128)(2,1)S(1)} %own_slice.2.refs_0_), channel_id=1, source_target_pairs={{0,4},{1,5},{2,6},{3,7},{4,0},{5,1},{6,2},{7,3},{8,12},{9,13},{10,... | collective-permute-start | bytes 786440 | tf_op jit(solution)/shard_map/ppermute | solution.py:526
  15.4 14.3 %collective-permute-start.4 = (bf16[256,512]{1,0:T(8,128)(2,1)S(1)}, bf16[256,512]{1,0:T(8,128)(2,1)S(1)}, u32[]{:S(2)}, u32[]{:S(2)}) collective-permute-start(bf16[256,512]{1,0:T(8,128)(2,1)S(1)} %own_slice.2.refs_0_), channel_id=1, source_target_pairs={{0,6},{1,7},{2,4},{3,5},{4,2},{5,3},{6,0},{7,1},{8,14},{9,15},{10,... | collective-permute-start | bytes 786440 | tf_op jit(solution)/shard_map/ppermute | solution.py:526
  15.8 13.0 %collective-permute-start.5 = (bf16[128,512]{1,0:T(8,128)(2,1)S(1)}, bf16[128,512]{1,0:T(8,128)(2,1)S(1)}, u32[]{:S(2)}, u32[]{:S(2)}) collective-permute-start(bf16[128,512]{1,0:T(8,128)(2,1)S(1)} %copied.1.array_ref), channel_id=1, source_target_pairs={{0,8},{1,9},{2,10},{3,11},{4,12},{5,13},{6,14},{7,15},{8,24},{9,25... | collective-permute-start | bytes 393224 | tf_op jit(solution)/shard_map/ppermute | solution.py:540
  21.1 7.7 %collective-permute-start.6 = (bf16[128,512]{1,0:T(8,128)(2,1)S(1)}, bf16[128,512]{1,0:T(8,128)(2,1)S(1)}, u32[]{:S(2)}, u32[]{:S(2)}) collective-permute-start(bf16[128,512]{1,0:T(8,128)(2,1)S(1)} %copied.1.array_ref), channel_id=1, source_target_pairs={{8,16},{9,17},{10,18},{11,19},{12,20},{13,21},{14,22},{15,23},{16,... | collective-permute-start | bytes 393224 | tf_op jit(solution)/shard_map/ppermute | solution.py:540
  29.7 2.5 %collective-permute-start.10 = (bf16[256,512]{1,0:T(8,128)(2,1)S(1)}, bf16[256,512]{1,0:T(8,128)(2,1)S(1)}, u32[]{:S(2)}, u32[]{:S(2)}) collective-permute-start(bf16[256,512]{1,0:T(8,128)(2,1)S(1)} %get-tuple-element.40.refs_0_), channel_id=1, source_target_pairs={{0,1},{1,0},{2,3},{3,2},{4,5},{5,4},{6,7},{7,6},{8,9},{9,8},{10,11... | collective-permute-start | bytes 786440 | tf_op jit(solution)/shard_map/ppermute | solution.py:526
  29.7 2.7 %collective-permute-start.11 = (bf16[256,512]{1,0:T(8,128)(2,1)S(1)}, bf16[256,512]{1,0:T(8,128)(2,1)S(1)}, u32[]{:S(2)}, u32[]{:S(2)}) collective-permute-start(bf16[256,512]{1,0:T(8,128)(2,1)S(1)} %get-tuple-element.41.refs_1_), channel_id=1, source_target_pairs={{0,1},{1,0},{2,3},{3,2},{4,5},{5,4},{6,7},{7,6},{8,9},{9,8},{10,11... | collective-permute-start | bytes 786440 | tf_op jit(solution)/shard_map/ppermute | solution.py:526
  30.2 4.0 %collective-permute-start.12 = (bf16[256,512]{1,0:T(8,128)(2,1)S(1)}, bf16[256,512]{1,0:T(8,128)(2,1)S(1)}, u32[]{:S(2)}, u32[]{:S(2)}) collective-permute-start(bf16[256,512]{1,0:T(8,128)(2,1)S(1)} %get-tuple-element.42.refs_2_), channel_id=1, source_target_pairs={{0,1},{1,0},{2,3},{3,2},{4,5},{5,4},{6,7},{7,6},{8,9},{9,8},{10,11... | collective-permute-start | bytes 786440 | tf_op jit(solution)/shard_map/ppermute | solution.py:526
  30.2 4.0 %collective-permute-start.13 = (bf16[256,512]{1,0:T(8,128)(2,1)S(1)}, bf16[256,512]{1,0:T(8,128)(2,1)S(1)}, u32[]{:S(2)}, u32[]{:S(2)}) collective-permute-start(bf16[256,512]{1,0:T(8,128)(2,1)S(1)} %get-tuple-element.43.refs_3_), channel_id=1, source_target_pairs={{0,1},{1,0},{2,3},{3,2},{4,5},{5,4},{6,7},{7,6},{8,9},{9,8},{10,11... | collective-permute-start | bytes 786440 | tf_op jit(solution)/shard_map/ppermute | solution.py:526
  30.7 13.0 %collective-permute-start.7 = (bf16[256,512]{1,0:T(8,128)(2,1)S(1)}, bf16[256,512]{1,0:T(8,128)(2,1)S(1)}, u32[]{:S(2)}, u32[]{:S(2)}) collective-permute-start(bf16[256,512]{1,0:T(8,128)(2,1)S(1)} %get-tuple-element.39.refs_0_), channel_id=1, source_target_pairs={{0,2},{1,3},{2,0},{3,1},{4,6},{5,7},{6,4},{7,5},{8,10},{9,11},{10,... | collective-permute-start | bytes 786440 | tf_op jit(solution)/shard_map/ppermute | solution.py:526
  32.2 11.5 %collective-permute-start.8 = (bf16[256,512]{1,0:T(8,128)(2,1)S(1)}, bf16[256,512]{1,0:T(8,128)(2,1)S(1)}, u32[]{:S(2)}, u32[]{:S(2)}) collective-permute-start(bf16[256,512]{1,0:T(8,128)(2,1)S(1)} %get-tuple-element.39.refs_0_), channel_id=1, source_target_pairs={{0,4},{1,5},{2,6},{3,7},{4,0},{5,1},{6,2},{7,3},{8,12},{9,13},{10,... | collective-permute-start | bytes 786440 | tf_op jit(solution)/shard_map/ppermute | solution.py:526
  32.4 13.7 %collective-permute-start.9 = (bf16[256,512]{1,0:T(8,128)(2,1)S(1)}, bf16[256,512]{1,0:T(8,128)(2,1)S(1)}, u32[]{:S(2)}, u32[]{:S(2)}) collective-permute-start(bf16[256,512]{1,0:T(8,128)(2,1)S(1)} %get-tuple-element.39.refs_0_), channel_id=1, source_target_pairs={{0,6},{1,7},{2,4},{3,5},{4,2},{5,3},{6,0},{7,1},{8,14},{9,15},{10,... | collective-permute-start | bytes 786440 | tf_op jit(solution)/shard_map/ppermute | solution.py:526
  36.8 19.0 %collective-permute-start.20 = (bf16[2,512,256]{2,1,0:T(8,128)(2,1)S(1)}, bf16[2,512,256]{2,1,0:T(8,128)(2,1)S(1)}, u32[]{:S(2)}, u32[]{:S(2)}) collective-permute-start(bf16[2,512,256]{2,1,0:T(8,128)(2,1)S(1)} %get-tuple-element.49.refs_0_), channel_id=1, source_target_pairs={{0,16},{16,0},{1,17},{17,1},{2,18},{18,2},{3,19},{19,3},{4,20},{20... | collective-permute-start | bytes 1572872 | tf_op jit(solution)/shard_map/ppermute | solution.py:530
  46.1 1.5 %collective-permute-start.14 = (bf16[256,512]{1,0:T(8,128)(2,1)S(1)}, bf16[256,512]{1,0:T(8,128)(2,1)S(1)}, u32[]{:S(2)}, u32[]{:S(2)}) collective-permute-start(bf16[256,512]{1,0:T(8,128)(2,1)S(1)} %get-tuple-element.45.refs_0_), channel_id=1, source_target_pairs={{0,1},{1,0},{2,3},{3,2},{4,5},{5,4},{6,7},{7,6},{8,9},{9,8},{10,11... | collective-permute-start | bytes 786440 | tf_op jit(solution)/shard_map/ppermute | solution.py:526
  46.1 7.0 %collective-permute-start.15 = (bf16[256,512]{1,0:T(8,128)(2,1)S(1)}, bf16[256,512]{1,0:T(8,128)(2,1)S(1)}, u32[]{:S(2)}, u32[]{:S(2)}) collective-permute-start(bf16[256,512]{1,0:T(8,128)(2,1)S(1)} %get-tuple-element.46.refs_1_), channel_id=1, source_target_pairs={{0,1},{1,0},{2,3},{3,2},{4,5},{5,4},{6,7},{7,6},{8,9},{9,8},{10,11... | collective-permute-start | bytes 786440 | tf_op jit(solution)/shard_map/ppermute | solution.py:526
  46.6 6.5 %collective-permute-start.16 = (bf16[256,512]{1,0:T(8,128)(2,1)S(1)}, bf16[256,512]{1,0:T(8,128)(2,1)S(1)}, u32[]{:S(2)}, u32[]{:S(2)}) collective-permute-start(bf16[256,512]{1,0:T(8,128)(2,1)S(1)} %get-tuple-element.47.refs_2_), channel_id=1, source_target_pairs={{0,1},{1,0},{2,3},{3,2},{4,5},{5,4},{6,7},{7,6},{8,9},{9,8},{10,11... | collective-permute-start | bytes 786440 | tf_op jit(solution)/shard_map/ppermute | solution.py:526
  46.6 6.5 %collective-permute-start.17 = (bf16[256,512]{1,0:T(8,128)(2,1)S(1)}, bf16[256,512]{1,0:T(8,128)(2,1)S(1)}, u32[]{:S(2)}, u32[]{:S(2)}) collective-permute-start(bf16[256,512]{1,0:T(8,128)(2,1)S(1)} %get-tuple-element.48.refs_3_), channel_id=1, source_target_pairs={{0,1},{1,0},{2,3},{3,2},{4,5},{5,4},{6,7},{7,6},{8,9},{9,8},{10,11... | collective-permute-start | bytes 786440 | tf_op jit(solution)/shard_map/ppermute | solution.py:526
  47.7 12.5 %collective-permute-start.19 = (bf16[512,256]{1,0:T(8,128)(2,1)S(1)}, bf16[512,256]{1,0:T(8,128)(2,1)S(1)}, u32[]{:S(2)}, u32[]{:S(2)}) collective-permute-start(bf16[512,256]{1,0:T(8,128)(2,1)S(1)} %proj_queries.1.refs_4_.refs_2_), channel_id=1, source_target_pairs={{0,16},{16,0},{1,17},{17,1},{2,18},{18,2},{3,19},{19,3},{4,20},{20... | collective-permute-start | bytes 786440 | tf_op jit(solution)/shard_map/ppermute | solution.py:530
  54.6 10.7 %collective-permute-start.18 = (bf16[512,256]{1,0:T(8,128)(2,1)S(1)}, bf16[512,256]{1,0:T(8,128)(2,1)S(1)}, u32[]{:S(2)}, u32[]{:S(2)}) collective-permute-start(bf16[512,256]{1,0:T(8,128)(2,1)S(1)} %grad_z_partial.1.refs_0_), channel_id=1, source_target_pairs={{0,16},{16,0},{1,17},{17,1},{2,18},{18,2},{3,19},{19,3},{4,20},{20... | collective-permute-start | bytes 786440 | tf_op jit(solution)/shard_map/ppermute | solution.py:530
  67.9 2.7 %collective-permute-start.21 = (bf16[4,512,256]{2,1,0:T(8,128)(2,1)S(1)}, bf16[4,512,256]{2,1,0:T(8,128)(2,1)S(1)}, u32[]{:S(2)}, u32[]{:S(2)}) collective-permute-start(bf16[4,512,256]{2,1,0:T(8,128)(2,1)S(1)} %input_partial.3), channel_id=1, source_target_pairs={{0,1},{1,0},{2,3},{3,2},{4,5},{5,4},{6,7},{7,6},{8,9},{9,8},{10,11... | collective-permute-start | bytes 3145736 | tf_op jit(solution)/shard_map/ppermute | solution.py:526
  70.8 6.2 %collective-permute-start.25 = (bf16[512,128]{1,0:T(8,128)(2,1)S(1)}, bf16[512,128]{1,0:T(8,128)(2,1)S(1)}, u32[]{:S(2)}, u32[]{:S(2)}) collective-permute-start(bf16[512,128]{1,0:T(8,128)(2,1)S(1)} %get-tuple-element.59), channel_id=1, source_target_pairs={{0,2},{1,3},{2,0},{3,1},{4,6},{5,7},{6,4},{7,5},{8,10},{9,11},{10,... | collective-permute-start | bytes 393224 | tf_op jit(solution)/shard_map/ppermute | solution.py:526
  71.9 6.6 %collective-permute-start.26 = (bf16[512,128]{1,0:T(8,128)(2,1)S(1)}, bf16[512,128]{1,0:T(8,128)(2,1)S(1)}, u32[]{:S(2)}, u32[]{:S(2)}) collective-permute-start(bf16[512,128]{1,0:T(8,128)(2,1)S(1)} %get-tuple-element.60), channel_id=1, source_target_pairs={{0,4},{1,5},{2,6},{3,7},{4,0},{5,1},{6,2},{7,3},{8,12},{9,13},{10,... | collective-permute-start | bytes 393224 | tf_op jit(solution)/shard_map/ppermute | solution.py:526
  73.5 8.0 %collective-permute-start.27 = (bf16[512,128]{1,0:T(8,128)(2,1)S(1)}, bf16[512,128]{1,0:T(8,128)(2,1)S(1)}, u32[]{:S(2)}, u32[]{:S(2)}) collective-permute-start(bf16[512,128]{1,0:T(8,128)(2,1)S(1)} %get-tuple-element.61), channel_id=1, source_target_pairs={{0,6},{1,7},{2,4},{3,5},{4,2},{5,3},{6,0},{7,1},{8,14},{9,15},{10,... | collective-permute-start | bytes 393224 | tf_op jit(solution)/shard_map/ppermute | solution.py:526
  74.4 9.0 %collective-permute-start.22 = (bf16[512,128]{1,0:T(8,128)(2,1)S(1)}, bf16[512,128]{1,0:T(8,128)(2,1)S(1)}, u32[]{:S(2)}, u32[]{:S(2)}) collective-permute-start(bf16[512,128]{1,0:T(8,128)(2,1)S(1)} %get-tuple-element.55), channel_id=1, source_target_pairs={{0,2},{1,3},{2,0},{3,1},{4,6},{5,7},{6,4},{7,5},{8,10},{9,11},{10,... | collective-permute-start | bytes 393224 | tf_op jit(solution)/shard_map/ppermute | solution.py:526
  75.4 8.3 %collective-permute-start.23 = (bf16[512,128]{1,0:T(8,128)(2,1)S(1)}, bf16[512,128]{1,0:T(8,128)(2,1)S(1)}, u32[]{:S(2)}, u32[]{:S(2)}) collective-permute-start(bf16[512,128]{1,0:T(8,128)(2,1)S(1)} %get-tuple-element.56), channel_id=1, source_target_pairs={{0,4},{1,5},{2,6},{3,7},{4,0},{5,1},{6,2},{7,3},{8,12},{9,13},{10,... | collective-permute-start | bytes 393224 | tf_op jit(solution)/shard_map/ppermute | solution.py:526
  77.0 9.1 %collective-permute-start.24 = (bf16[512,128]{1,0:T(8,128)(2,1)S(1)}, bf16[512,128]{1,0:T(8,128)(2,1)S(1)}, u32[]{:S(2)}, u32[]{:S(2)}) collective-permute-start(bf16[512,128]{1,0:T(8,128)(2,1)S(1)} %get-tuple-element.57), channel_id=1, source_target_pairs={{0,6},{1,7},{2,4},{3,5},{4,2},{5,3},{6,0},{7,1},{8,14},{9,15},{10,... | collective-permute-start | bytes 393224 | tf_op jit(solution)/shard_map/ppermute | solution.py:526
  81.6 5.0 %collective-permute-start.28 = (bf16[512,128]{1,0:T(8,128)(2,1)S(1)}, bf16[512,128]{1,0:T(8,128)(2,1)S(1)}, u32[]{:S(2)}, u32[]{:S(2)}) collective-permute-start(bf16[512,128]{1,0:T(8,128)(2,1)S(1)} %total.3), channel_id=1, source_target_pairs={{0,16},{16,0},{1,17},{17,1},{2,18},{18,2},{3,19},{19,3},{4,20},{20... | collective-permute-start | bytes 393224 | tf_op jit(solution)/shard_map/ppermute | solution.py:530
  86.6 7.8 %collective-permute-start.29 = (bf16[512,128]{1,0:T(8,128)(2,1)S(1)}, bf16[512,128]{1,0:T(8,128)(2,1)S(1)}, u32[]{:S(2)}, u32[]{:S(2)}) collective-permute-start(bf16[512,128]{1,0:T(8,128)(2,1)S(1)} %get-tuple-element.63), channel_id=1, source_target_pairs={{0,8},{1,9},{2,10},{3,11},{4,12},{5,13},{6,14},{7,15},{8,0},{9,1},... | collective-permute-start | bytes 393224 | tf_op jit(solution)/shard_map/ppermute | solution.py:526

commit v6 on v5

--- a/solution.py
+++ b/solution.py
@@ -172,7 +172,7 @@
 
 
 Z1, Z0, X, CORE = 8, 4, 2, 1
-MINE = (0, X, Z0, X + Z0)
+MINE = (0, Z0, X, X + Z0)
 OTHERS = tuple(mask + CORE for mask in MINE)
 
 
@@ -671,7 +671,8 @@
     out_held = loaded(out_weight, past)
     cotangent = copied(cotangent, token_own)
     cot_own = own_slice(cotangent, *first_stage(cotangent))
-    *token_same, cot_own = relayed([*token_same, cot_own], out_held)
+    late = relayed([token_same[3]], out_held, cot_own)
+    token_same = [*token_same[:3], *late]
     cot_same = second_stage(cot_own)
     pair, queries = proj_partial(both_cores(token_same), MINE + OTHERS, 2, weights)
     cot_same = list(relayed(cot_same, queries))

time: 95.4 us -> 93.5 us (0.980)
  starting transfers between devices: 44.1 us -> 37.9 us
  waiting for transfers between devices: 25.3 us -> 29.5 us
    ppermute x22, waiting for transfers between devices: 12.2 us -> 20.3 us  [across(): return lax.ppermute(array, 'tensor', [(i, i ^ mask) for i in range(16)])]
    ppermute x4, starting transfers between devices: 14.1 us -> 7.14 us  [other_row(): return lax.ppermute(array, 'fsdp', [(0, 1), (1, 0)])]
    ppermute x4, waiting for transfers between devices: 3.76 us -> 0.01 us  [in_square(): return lax.ppermute(array, ('fsdp', 'tensor'), pairs)]
where the time goes in v6:
time: 93.5 us; the launch traced here: 93.3 us
  starting transfers between devices  37.9 us (41%)
  waiting for transfers between devices  29.5 us (32%)
  Pallas kernels  25 us (27%)
    ppermute x22, waiting for transfers between devices, across(): return lax.ppermute(array, 'tensor', [(i, i ^ mask) for i in range(16)])  20.3 us
    ppermute x22, starting transfers between devices, across(): return lax.ppermute(array, 'tensor', [(i, i ^ mask) for i in range(16)])  19.7 us
    ppermute x4, starting transfers between devices, in_square(): return lax.ppermute(array, ('fsdp', 'tensor'), pairs)  11.1 us
    ppermute x4, waiting for transfers between devices, other_row(): return lax.ppermute(array, 'fsdp', [(0, 1), (1, 0)])  9.19 us
    ppermute x4, starting transfers between devices, other_row(): return lax.ppermute(array, 'fsdp', [(0, 1), (1, 0)])  7.14 us
    pallas_call x1, Pallas kernels, prepared(): pl.pallas_call(prepare_kernel, in_specs=[LATER_SPEC] * (2 + len(earlier))...  5.89 us
    pallas_call x2, Pallas kernels, input_partial(): pl.pallas_call(functools.partial(input_kernel, masks), in_specs=[VMEM_SPE...  3.57 us
    pallas_call x1, Pallas kernels, taps_gradient(): pl.pallas_call(functools.partial(taps_kernel, groups // steps), grid=(ste...  3.22 us
  transfers between devices with their start and end apart: 30, of which 12 were waited for; matrix products, arithmetic and copies ran while one was open for 0% of the time, Pallas kernels for 22%

profile of v6, /device:TPU:0, one launch (start us, length us, event | category | flops | bytes accessed | tf_op | source)
XLA Modules:
  0.0 93.3 jit_solution(8499019497975544330)
XLA Ops:
  0.6 4.1 %collective-permute-start = (bf16[128,512]{1,0:T(8,128)(2,1)}, bf16[128,512]{1,0:T(8,128)(2,1)S(1)}, u32[]{:S(2)}, u32[]{:S(2)}) collective-permute-start(bf16[128,512]{1,0:T(8,128)(2,1)} %array_ref.1), channel_id=1, source_target_pairs={{0,8},{1,9},{2,10},{3,11},{4,12},{5,13},{6,14},{7,15},{8,24},{9,25... | collective-permute-start | bytes 393224 | tf_op jit(solution)/shard_map/ppermute | solution.py:540
  5.4 5.9 %prepare.1 = (bf16[4096,512]{1,0:T(8,128)(2,1)S(1)}, bf16[4096,512]{1,0:T(8,128)(2,1)S(1)}, bf16[4096,512]{1,0:T(8,128)(2,1)S(1)}, f32[8,128]{1,0:T(8,128)S(1)}) custom-call(bf16[3,4096,512]{2,1,0:T(8,128)(2,1)} %bitcast.5, bf16[3,32,512]{2,1,0:T(8,128)(2,1)} %bitcast.6), custom_call_target="tpu_custom_call" | custom-call | flops 6144 | bytes 6144 | tf_op jit(solution)/shard_map/prepare/pallas_call | solution.py:154
  11.3 0.9 own_slice.2.refs_0_
  12.3 2.6 %collective-permute-start.9 = (bf16[256,512]{1,0:T(8,128)(2,1)S(1)}, bf16[256,512]{1,0:T(8,128)(2,1)S(1)}, u32[]{:S(2)}, u32[]{:S(2)}) collective-permute-start(bf16[256,512]{1,0:T(8,128)(2,1)S(1)} %own_slice.2.refs_0_), channel_id=1, source_target_pairs={{0,6},{1,7},{2,4},{3,5},{4,2},{5,3},{6,0},{7,1},{8,14},{9,15},{10,... | collective-permute-start | bytes 786440 | tf_op jit(solution)/shard_map/ppermute | solution.py:526
  14.8 5.7 %collective-permute-start.2 = (bf16[128,512]{1,0:T(8,128)(2,1)S(1)}, bf16[128,512]{1,0:T(8,128)(2,1)S(1)}, u32[]{:S(2)}, u32[]{:S(2)}) collective-permute-start(bf16[128,512]{1,0:T(8,128)(2,1)S(1)} %copied.1.array_ref), channel_id=1, source_target_pairs={{0,8},{1,9},{2,10},{3,11},{4,12},{5,13},{6,14},{7,15},{8,24},{9,25... | collective-permute-start | bytes 393224 | tf_op jit(solution)/shard_map/ppermute | solution.py:540
  21.9 1.0 %toeplitz.1 = (bf16[32,256,128]{2,1,0:T(8,128)(2,1)S(1)}, bf16[32,256,128]{2,1,0:T(8,128)(2,1)S(1)}) custom-call(f32[32,128]{1,0:T(8,128)S(1)} %copy-done.1, bf16[256,512]{1,0:T(8,128)(2,1)S(1)} %own_slice.2.refs_0_), custom_call_target="tpu_custom_call" | custom-call | flops 2000 | bytes 1024 | tf_op jit(solution)/shard_map/toeplitz/pallas_call | solution.py:320
  22.9 2.2 %loaded.1.refs_1_.refs_8_ = bf16[512,4096]{1,0:T(8,128)(2,1)S(1)} custom-call(bf16[512,4096]{1,0:T(8,128)(2,1)} %in_ref.3, bf16[32,256,128]{2,1,0:T(8,128)(2,1)S(1)} %get-tuple-element.33.refs_0_.refs_2_), custom_call_target="tpu_custom_call" | custom-call | bytes 2048 | tf_op jit(solution)/shard_map/loaded/pallas_call | solution.py:205
  26.0 5.4 %collective-permute-done.7.refs_1_ = bf16[256,512]{1,0:T(8,128)(2,1)S(1)} collective-permute-done((bf16[256,512]{1,0:T(8,128)(2,1)S(1)}, bf16[256,512]{1,0:T(8,128)(2,1)S(1)}, u32[]{:S(2)}, u32[]{:S(2)}) %collective-permute-start.7) | collective-permute-done | bytes 262176 | tf_op jit(solution)/shard_map/ppermute | solution.py:526
  32.4 3.0 %collective-permute-start.6 = (bf16[256,512]{1,0:T(8,128)(2,1)S(1)}, bf16[256,512]{1,0:T(8,128)(2,1)S(1)}, u32[]{:S(2)}, u32[]{:S(2)}) collective-permute-start(bf16[256,512]{1,0:T(8,128)(2,1)S(1)} %own_slice.3.refs_2_.refs_0_), channel_id=1, source_target_pairs={{0,6},{1,7},{2,4},{3,5},{4,2},{5,3},{6,0},{7,1},{8,14},{9,15},{10,... | collective-permute-start | bytes 786440 | tf_op jit(solution)/shard_map/ppermute | solution.py:526
  35.4 2.5 %proj_pair.1 = (bf16[2,512,256]{2,1,0:T(8,128)(2,1)S(1)}, bf16[256,4096]{1,0:T(8,128)(2,1)S(1)}) custom-call(bf16[256,512]{1,0:T(8,128)(2,1)S(1)} %own_slice.2.refs_0_, bf16[256,512]{1,0:T(8,128)(2,1)S(1)} %collective-permute-done.7.refs_1_, bf16[256,512]{1,0:T(8,128)(2,1)S(1)} %collective-permute-done.8.refs_2_, bf16[256,512]{1,0:T(8,128)(2,1)S(1)} %relayed.2.refs_3_, ...), custom_call_target="tpu_custom_call" | custom-call | flops 524288 | bytes 2048 | tf_op jit(solution)/shard_map/proj_pair/pallas_call | solution.py:245
  38.0 1.3 %collective-permute-start.20 = (bf16[2,512,256]{2,1,0:T(8,128)(2,1)S(1)}, bf16[2,512,256]{2,1,0:T(8,128)(2,1)S(1)}, u32[]{:S(2)}, u32[]{:S(2)}) collective-permute-start(bf16[2,512,256]{2,1,0:T(8,128)(2,1)S(1)} %get-tuple-element.39.refs_0_), channel_id=1, source_target_pairs={{0,16},{16,0},{1,17},{17,1},{2,18},{18,2},{3,19},{19,3},{4,20},{20... | collective-permute-start | bytes 1572872 | tf_op jit(solution)/shard_map/ppermute | solution.py:530
  39.3 1.3 %proj_queries.1.refs_4_.refs_2_ = bf16[512,256]{1,0:T(8,128)(2,1)S(1)} custom-call(bf16[256,4096]{1,0:T(8,128)(2,1)S(1)} %get-tuple-element.34.held_ref, bf16[4096,512]{1,0:T(8,128)(2,1)S(1)} %get-tuple-element.29.w_ref.refs_0_), custom_call_target="tpu_custom_call" | custom-call | flops 262144 | bytes 1024 | tf_op jit(solution)/shard_map/proj_queries/pallas_call | solution.py:257
  41.1 4.7 %collective-permute-done.5.refs_2_ = bf16[256,512]{1,0:T(8,128)(2,1)S(1)} collective-permute-done((bf16[256,512]{1,0:T(8,128)(2,1)S(1)}, bf16[256,512]{1,0:T(8,128)(2,1)S(1)}, u32[]{:S(2)}, u32[]{:S(2)}) %collective-permute-start.5) | collective-permute-done | bytes 262176 | tf_op jit(solution)/shard_map/ppermute | solution.py:526
  47.4 2.9 %collective-permute-start.19 = (bf16[512,256]{1,0:T(8,128)(2,1)S(1)}, bf16[512,256]{1,0:T(8,128)(2,1)S(1)}, u32[]{:S(2)}, u32[]{:S(2)}) collective-permute-start(bf16[512,256]{1,0:T(8,128)(2,1)S(1)} %proj_queries.1.refs_4_.refs_2_), channel_id=1, source_target_pairs={{0,16},{16,0},{1,17},{17,1},{2,18},{18,2},{3,19},{19,3},{4,20},{20... | collective-permute-start | bytes 786440 | tf_op jit(solution)/shard_map/ppermute | solution.py:530
  50.3 1.5 %grad_z_partial.1.refs_0_ = bf16[512,256]{1,0:T(8,128)(2,1)S(1)} custom-call(bf16[256,512]{1,0:T(8,128)(2,1)S(1)} %get-tuple-element.35.refs_0_, bf16[256,512]{1,0:T(8,128)(2,1)S(1)} %get-tuple-element.36.refs_1_, bf16[256,512]{1,0:T(8,128)(2,1)S(1)} %get-tuple-element.37.refs_2_, bf16[256,512]{1,0:T(8,128)(2,1)S(1)} %get-tuple-element.38.refs_3_, ...), custom_call_target="tpu_custom_call" | custom-call | flops 262144 | bytes 1024 | tf_op jit(solution)/shard_map/grad_z_partial/pallas_call | solution.py:283
  51.8 1.2 %collective-permute-start.18 = (bf16[512,256]{1,0:T(8,128)(2,1)S(1)}, bf16[512,256]{1,0:T(8,128)(2,1)S(1)}, u32[]{:S(2)}, u32[]{:S(2)}) collective-permute-start(bf16[512,256]{1,0:T(8,128)(2,1)S(1)} %grad_z_partial.1.refs_0_), channel_id=1, source_target_pairs={{0,16},{16,0},{1,17},{17,1},{2,18},{18,2},{3,19},{19,3},{4,20},{20... | collective-permute-start | bytes 786440 | tf_op jit(solution)/shard_map/ppermute | solution.py:530
  53.6 3.7 %collective-permute-done.19.refs_3_ = bf16[512,256]{1,0:T(8,128)(2,1)S(1)} collective-permute-done((bf16[512,256]{1,0:T(8,128)(2,1)S(1)}, bf16[512,256]{1,0:T(8,128)(2,1)S(1)}, u32[]{:S(2)}, u32[]{:S(2)}) %collective-permute-start.19) | collective-permute-done | bytes 262176 | tf_op jit(solution)/shard_map/ppermute | solution.py:530
  57.4 5.1 %collective-permute-done.18.refs_1_ = bf16[512,256]{1,0:T(8,128)(2,1)S(1)} collective-permute-done((bf16[512,256]{1,0:T(8,128)(2,1)S(1)}, bf16[512,256]{1,0:T(8,128)(2,1)S(1)}, u32[]{:S(2)}, u32[]{:S(2)}) %collective-permute-start.18) | collective-permute-done | bytes 262176 | tf_op jit(solution)/shard_map/ppermute | solution.py:530
  63.2 1.8 %input_partial.3 = bf16[4,512,256]{2,1,0:T(8,128)(2,1)S(1)} custom-call(bf16[4096,512]{1,0:T(8,128)(2,1)S(1)} %get-tuple-element.29.w_ref.refs_0_, bf16[4096,512]{1,0:T(8,128)(2,1)S(1)} %get-tuple-element.30.refs_8_.refs_1_, bf16[4096,512]{1,0:T(8,128)(2,1)S(1)} %get-tuple-element.31.refs_9_.refs_2_, bf16[1536,256]{1,0:T(8,128)(2,1)S(1)} %bitcast.3), custom_call_target="tpu_custom_call" | custom-call | flops 393216 | bytes 1792 | tf_op jit(solution)/shard_map/input_partial/pallas_call | solution.py:512
  65.1 1.8 %input_partial.2.same_ref = bf16[4,512,256]{2,1,0:T(8,128)(2,1)S(1)} custom-call(bf16[4096,512]{1,0:T(8,128)(2,1)S(1)} %get-tuple-element.29.w_ref.refs_0_, bf16[4096,512]{1,0:T(8,128)(2,1)S(1)} %get-tuple-element.30.refs_8_.refs_1_, bf16[4096,512]{1,0:T(8,128)(2,1)S(1)} %get-tuple-element.31.refs_9_.refs_2_, bf16[1536,256]{1,0:T(8,128)(2,1)S(1)} %bitcast.4), custom_call_target="tpu_custom_call" | custom-call | flops 393216 | bytes 1792 | tf_op jit(solution)/shard_map/input_partial/pallas_call | solution.py:512
  66.9 0.9 collective-permute-done.21.got_ref
  68.0 1.4 %collective-permute-start.25 = (bf16[512,128]{1,0:T(8,128)(2,1)S(1)}, bf16[512,128]{1,0:T(8,128)(2,1)S(1)}, u32[]{:S(2)}, u32[]{:S(2)}) collective-permute-start(bf16[512,128]{1,0:T(8,128)(2,1)S(1)} %get-tuple-element.49), channel_id=1, source_target_pairs={{0,4},{1,5},{2,6},{3,7},{4,0},{5,1},{6,2},{7,3},{8,12},{9,13},{10,... | collective-permute-start | bytes 393224 | tf_op jit(solution)/shard_map/ppermute | solution.py:526
  69.8 1.7 %collective-permute-start.27 = (bf16[512,128]{1,0:T(8,128)(2,1)S(1)}, bf16[512,128]{1,0:T(8,128)(2,1)S(1)}, u32[]{:S(2)}, u32[]{:S(2)}) collective-permute-start(bf16[512,128]{1,0:T(8,128)(2,1)S(1)} %get-tuple-element.51), channel_id=1, source_target_pairs={{0,6},{1,7},{2,4},{3,5},{4,2},{5,3},{6,0},{7,1},{8,14},{9,15},{10,... | collective-permute-start | bytes 393224 | tf_op jit(solution)/shard_map/ppermute | solution.py:526
  71.5 1.3 %collective-permute-start.22 = (bf16[512,128]{1,0:T(8,128)(2,1)S(1)}, bf16[512,128]{1,0:T(8,128)(2,1)S(1)}, u32[]{:S(2)}, u32[]{:S(2)}) collective-permute-start(bf16[512,128]{1,0:T(8,128)(2,1)S(1)} %get-tuple-element.45), channel_id=1, source_target_pairs={{0,4},{1,5},{2,6},{3,7},{4,0},{5,1},{6,2},{7,3},{8,12},{9,13},{10,... | collective-permute-start | bytes 393224 | tf_op jit(solution)/shard_map/ppermute | solution.py:526
  73.3 0.8 collective-permute-done.25.refs_1_
  74.2 1.5 %collective-permute-start.24 = (bf16[512,128]{1,0:T(8,128)(2,1)S(1)}, bf16[512,128]{1,0:T(8,128)(2,1)S(1)}, u32[]{:S(2)}, u32[]{:S(2)}) collective-permute-start(bf16[512,128]{1,0:T(8,128)(2,1)S(1)} %get-tuple-element.47), channel_id=1, source_target_pairs={{0,6},{1,7},{2,4},{3,5},{4,2},{5,3},{6,0},{7,1},{8,14},{9,15},{10,... | collective-permute-start | bytes 393224 | tf_op jit(solution)/shard_map/ppermute | solution.py:526
  75.6 2.7 %collective-permute-done.26.refs_2_ = bf16[512,128]{1,0:T(8,128)(2,1)S(1)} collective-permute-done((bf16[512,128]{1,0:T(8,128)(2,1)S(1)}, bf16[512,128]{1,0:T(8,128)(2,1)S(1)}, u32[]{:S(2)}, u32[]{:S(2)}) %collective-permute-start.26) | collective-permute-done | bytes 131104 | tf_op jit(solution)/shard_map/ppermute | solution.py:526
  78.4 1.8 %collective-permute-start.28 = (bf16[512,128]{1,0:T(8,128)(2,1)S(1)}, bf16[512,128]{1,0:T(8,128)(2,1)S(1)}, u32[]{:S(2)}, u32[]{:S(2)}) collective-permute-start(bf16[512,128]{1,0:T(8,128)(2,1)S(1)} %total.3), channel_id=1, source_target_pairs={{0,16},{16,0},{1,17},{17,1},{2,18},{18,2},{3,19},{19,3},{4,20},{20... | collective-permute-start | bytes 393224 | tf_op jit(solution)/shard_map/ppermute | solution.py:530
  80.2 2.8 %collective-permute-done.23.refs_2_ = bf16[512,128]{1,0:T(8,128)(2,1)S(1)} collective-permute-done((bf16[512,128]{1,0:T(8,128)(2,1)S(1)}, bf16[512,128]{1,0:T(8,128)(2,1)S(1)}, u32[]{:S(2)}, u32[]{:S(2)}) %collective-permute-start.23) | collective-permute-done | bytes 131104 | tf_op jit(solution)/shard_map/ppermute | solution.py:526
  83.5 4.0 %collective-permute-start.29 = (bf16[512,128]{1,0:T(8,128)(2,1)S(1)}, bf16[512,128]{1,0:T(8,128)(2,1)S(1)}, u32[]{:S(2)}, u32[]{:S(2)}) collective-permute-start(bf16[512,128]{1,0:T(8,128)(2,1)S(1)} %get-tuple-element.53), channel_id=1, source_target_pairs={{0,8},{1,9},{2,10},{3,11},{4,12},{5,13},{6,14},{7,15},{8,0},{9,1},... | collective-permute-start | bytes 393224 | tf_op jit(solution)/shard_map/ppermute | solution.py:526
  87.4 3.2 %taps_gradient.1 = f32[32,128]{1,0:T(8,128)} custom-call(bf16[512,256]{1,0:T(8,128)(2,1)S(1)} %get-tuple-element.54.prod_ref, bf16[512,256]{1,0:T(8,128)(2,1)S(1)} %get-tuple-element.55.grad_ref), custom_call_target="tpu_custom_call" | custom-call | flops 131072 | bytes 768 | tf_op jit(solution)/shard_map/taps_gradient/pallas_call | solution.py:489
  90.7 1.8 %collective-permute-done.29.got_ref = bf16[512,128]{1,0:T(8,128)(2,1)S(1)} collective-permute-done((bf16[512,128]{1,0:T(8,128)(2,1)S(1)}, bf16[512,128]{1,0:T(8,128)(2,1)S(1)}, u32[]{:S(2)}, u32[]{:S(2)}) %collective-permute-start.29) | collective-permute-done | bytes 131104 | tf_op jit(solution)/shard_map/ppermute | solution.py:526
  (53 shorter events, 9.9 us)
Async XLA Ops:
  0.6 10.7 %collective-permute-start = (bf16[128,512]{1,0:T(8,128)(2,1)}, bf16[128,512]{1,0:T(8,128)(2,1)S(1)}, u32[]{:S(2)}, u32[]{:S(2)}) collective-permute-start(bf16[128,512]{1,0:T(8,128)(2,1)} %array_ref.1), channel_id=1, source_target_pairs={{0,8},{1,9},{2,10},{3,11},{4,12},{5,13},{6,14},{7,15},{8,24},{9,25... | collective-permute-start | bytes 393224 | tf_op jit(solution)/shard_map/ppermute | solution.py:540
  4.7 6.6 %collective-permute-start.1 = (bf16[128,512]{1,0:T(8,128)(2,1)}, bf16[128,512]{1,0:T(8,128)(2,1)S(1)}, u32[]{:S(2)}, u32[]{:S(2)}) collective-permute-start(bf16[128,512]{1,0:T(8,128)(2,1)} %array_ref.1), channel_id=1, source_target_pairs={{8,16},{9,17},{10,18},{11,19},{12,20},{13,21},{14,22},{15,23},{16,... | collective-permute-start | bytes 393224 | tf_op jit(solution)/shard_map/ppermute | solution.py:540
  5.4 9.4 %copy-start = (bf16[128,512]{1,0:T(8,128)(2,1)S(1)}, bf16[128,512]{1,0:T(8,128)(2,1)}, u32[]{:S(2)}) copy-start(bf16[128,512]{1,0:T(8,128)(2,1)} %in_ref.2) | copy-start | bytes 393220
  5.4 16.5 %copy-start.1 = (f32[32,128]{1,0:T(8,128)S(1)}, f32[32,128]{1,0:T(8,128)}, u32[]{:S(2)}) copy-start(f32[32,128]{1,0:T(8,128)} %taps_ref.1) | copy-start | bytes 49156
  12.3 13.2 %collective-permute-start.9 = (bf16[256,512]{1,0:T(8,128)(2,1)S(1)}, bf16[256,512]{1,0:T(8,128)(2,1)S(1)}, u32[]{:S(2)}, u32[]{:S(2)}) collective-permute-start(bf16[256,512]{1,0:T(8,128)(2,1)S(1)} %own_slice.2.refs_0_), channel_id=1, source_target_pairs={{0,6},{1,7},{2,4},{3,5},{4,2},{5,3},{6,0},{7,1},{8,14},{9,15},{10,... | collective-permute-start | bytes 786440 | tf_op jit(solution)/shard_map/ppermute | solution.py:526
  14.8 10.3 %collective-permute-start.2 = (bf16[128,512]{1,0:T(8,128)(2,1)S(1)}, bf16[128,512]{1,0:T(8,128)(2,1)S(1)}, u32[]{:S(2)}, u32[]{:S(2)}) collective-permute-start(bf16[128,512]{1,0:T(8,128)(2,1)S(1)} %copied.1.array_ref), channel_id=1, source_target_pairs={{0,8},{1,9},{2,10},{3,11},{4,12},{5,13},{6,14},{7,15},{8,24},{9,25... | collective-permute-start | bytes 393224 | tf_op jit(solution)/shard_map/ppermute | solution.py:540
  20.6 4.7 %collective-permute-start.3 = (bf16[128,512]{1,0:T(8,128)(2,1)S(1)}, bf16[128,512]{1,0:T(8,128)(2,1)S(1)}, u32[]{:S(2)}, u32[]{:S(2)}) collective-permute-start(bf16[128,512]{1,0:T(8,128)(2,1)S(1)} %copied.1.array_ref), channel_id=1, source_target_pairs={{8,16},{9,17},{10,18},{11,19},{12,20},{13,21},{14,22},{15,23},{16,... | collective-permute-start | bytes 393224 | tf_op jit(solution)/shard_map/ppermute | solution.py:540
  21.2 10.2 %collective-permute-start.7 = (bf16[256,512]{1,0:T(8,128)(2,1)S(1)}, bf16[256,512]{1,0:T(8,128)(2,1)S(1)}, u32[]{:S(2)}, u32[]{:S(2)}) collective-permute-start(bf16[256,512]{1,0:T(8,128)(2,1)S(1)} %own_slice.2.refs_0_), channel_id=1, source_target_pairs={{0,4},{1,5},{2,6},{3,7},{4,0},{5,1},{6,2},{7,3},{8,12},{9,13},{10,... | collective-permute-start | bytes 786440 | tf_op jit(solution)/shard_map/ppermute | solution.py:526
  21.3 10.1 %collective-permute-start.8 = (bf16[256,512]{1,0:T(8,128)(2,1)S(1)}, bf16[256,512]{1,0:T(8,128)(2,1)S(1)}, u32[]{:S(2)}, u32[]{:S(2)}) collective-permute-start(bf16[256,512]{1,0:T(8,128)(2,1)S(1)} %own_slice.2.refs_0_), channel_id=1, source_target_pairs={{0,2},{1,3},{2,0},{3,1},{4,6},{5,7},{6,4},{7,5},{8,10},{9,11},{10,... | collective-permute-start | bytes 786440 | tf_op jit(solution)/shard_map/ppermute | solution.py:526
  25.2 6.8 %collective-permute-start.10 = (bf16[256,512]{1,0:T(8,128)(2,1)S(1)}, bf16[256,512]{1,0:T(8,128)(2,1)S(1)}, u32[]{:S(2)}, u32[]{:S(2)}) collective-permute-start(bf16[256,512]{1,0:T(8,128)(2,1)S(1)} %own_slice.2.refs_0_), channel_id=1, source_target_pairs={{0,1},{1,0},{2,3},{3,2},{4,5},{5,4},{6,7},{7,6},{8,9},{9,8},{10,11... | collective-permute-start | bytes 786440 | tf_op jit(solution)/shard_map/ppermute | solution.py:526
  25.5 7.0 %collective-permute-start.13 = (bf16[256,512]{1,0:T(8,128)(2,1)S(1)}, bf16[256,512]{1,0:T(8,128)(2,1)S(1)}, u32[]{:S(2)}, u32[]{:S(2)}) collective-permute-start(bf16[256,512]{1,0:T(8,128)(2,1)S(1)} %relayed.2.refs_3_), channel_id=1, source_target_pairs={{0,1},{1,0},{2,3},{3,2},{4,5},{5,4},{6,7},{7,6},{8,9},{9,8},{10,11... | collective-permute-start | bytes 786440 | tf_op jit(solution)/shard_map/ppermute | solution.py:526
  31.4 4.0 %collective-permute-start.11 = (bf16[256,512]{1,0:T(8,128)(2,1)S(1)}, bf16[256,512]{1,0:T(8,128)(2,1)S(1)}, u32[]{:S(2)}, u32[]{:S(2)}) collective-permute-start(bf16[256,512]{1,0:T(8,128)(2,1)S(1)} %collective-permute-done.7.refs_1_), channel_id=1, source_target_pairs={{0,1},{1,0},{2,3},{3,2},{4,5},{5,4},{6,7},{7,6},{8,9},{9,8},{10,11... | collective-permute-start | bytes 786440 | tf_op jit(solution)/shard_map/ppermute | solution.py:526
  31.4 4.0 %collective-permute-start.12 = (bf16[256,512]{1,0:T(8,128)(2,1)S(1)}, bf16[256,512]{1,0:T(8,128)(2,1)S(1)}, u32[]{:S(2)}, u32[]{:S(2)}) collective-permute-start(bf16[256,512]{1,0:T(8,128)(2,1)S(1)} %collective-permute-done.8.refs_2_), channel_id=1, source_target_pairs={{0,1},{1,0},{2,3},{3,2},{4,5},{5,4},{6,7},{7,6},{8,9},{9,8},{10,11... | collective-permute-start | bytes 786440 | tf_op jit(solution)/shard_map/ppermute | solution.py:526
  31.9 9.2 %collective-permute-start.4 = (bf16[256,512]{1,0:T(8,128)(2,1)S(1)}, bf16[256,512]{1,0:T(8,128)(2,1)S(1)}, u32[]{:S(2)}, u32[]{:S(2)}) collective-permute-start(bf16[256,512]{1,0:T(8,128)(2,1)S(1)} %own_slice.3.refs_2_.refs_0_), channel_id=1, source_target_pairs={{0,4},{1,5},{2,6},{3,7},{4,0},{5,1},{6,2},{7,3},{8,12},{9,13},{10,... | collective-permute-start | bytes 786440 | tf_op jit(solution)/shard_map/ppermute | solution.py:526
  32.0 13.9 %collective-permute-start.5 = (bf16[256,512]{1,0:T(8,128)(2,1)S(1)}, bf16[256,512]{1,0:T(8,128)(2,1)S(1)}, u32[]{:S(2)}, u32[]{:S(2)}) collective-permute-start(bf16[256,512]{1,0:T(8,128)(2,1)S(1)} %own_slice.3.refs_2_.refs_0_), channel_id=1, source_target_pairs={{0,2},{1,3},{2,0},{3,1},{4,6},{5,7},{6,4},{7,5},{8,10},{9,11},{10,... | collective-permute-start | bytes 786440 | tf_op jit(solution)/shard_map/ppermute | solution.py:526
  32.4 13.4 %collective-permute-start.6 = (bf16[256,512]{1,0:T(8,128)(2,1)S(1)}, bf16[256,512]{1,0:T(8,128)(2,1)S(1)}, u32[]{:S(2)}, u32[]{:S(2)}) collective-permute-start(bf16[256,512]{1,0:T(8,128)(2,1)S(1)} %own_slice.3.refs_2_.refs_0_), channel_id=1, source_target_pairs={{0,6},{1,7},{2,4},{3,5},{4,2},{5,3},{6,0},{7,1},{8,14},{9,15},{10,... | collective-permute-start | bytes 786440 | tf_op jit(solution)/shard_map/ppermute | solution.py:526
  38.0 14.9 %collective-permute-start.20 = (bf16[2,512,256]{2,1,0:T(8,128)(2,1)S(1)}, bf16[2,512,256]{2,1,0:T(8,128)(2,1)S(1)}, u32[]{:S(2)}, u32[]{:S(2)}) collective-permute-start(bf16[2,512,256]{2,1,0:T(8,128)(2,1)S(1)} %get-tuple-element.39.refs_0_), channel_id=1, source_target_pairs={{0,16},{16,0},{1,17},{17,1},{2,18},{18,2},{3,19},{19,3},{4,20},{20... | collective-permute-start | bytes 1572872 | tf_op jit(solution)/shard_map/ppermute | solution.py:530
  45.9 1.5 %collective-permute-start.14 = (bf16[256,512]{1,0:T(8,128)(2,1)S(1)}, bf16[256,512]{1,0:T(8,128)(2,1)S(1)}, u32[]{:S(2)}, u32[]{:S(2)}) collective-permute-start(bf16[256,512]{1,0:T(8,128)(2,1)S(1)} %get-tuple-element.35.refs_0_), channel_id=1, source_target_pairs={{0,1},{1,0},{2,3},{3,2},{4,5},{5,4},{6,7},{7,6},{8,9},{9,8},{10,11... | collective-permute-start | bytes 786440 | tf_op jit(solution)/shard_map/ppermute | solution.py:526
  45.9 4.4 %collective-permute-start.15 = (bf16[256,512]{1,0:T(8,128)(2,1)S(1)}, bf16[256,512]{1,0:T(8,128)(2,1)S(1)}, u32[]{:S(2)}, u32[]{:S(2)}) collective-permute-start(bf16[256,512]{1,0:T(8,128)(2,1)S(1)} %get-tuple-element.36.refs_1_), channel_id=1, source_target_pairs={{0,1},{1,0},{2,3},{3,2},{4,5},{5,4},{6,7},{7,6},{8,9},{9,8},{10,11... | collective-permute-start | bytes 786440 | tf_op jit(solution)/shard_map/ppermute | solution.py:526
  46.4 3.9 %collective-permute-start.16 = (bf16[256,512]{1,0:T(8,128)(2,1)S(1)}, bf16[256,512]{1,0:T(8,128)(2,1)S(1)}, u32[]{:S(2)}, u32[]{:S(2)}) collective-permute-start(bf16[256,512]{1,0:T(8,128)(2,1)S(1)} %get-tuple-element.37.refs_2_), channel_id=1, source_target_pairs={{0,1},{1,0},{2,3},{3,2},{4,5},{5,4},{6,7},{7,6},{8,9},{9,8},{10,11... | collective-permute-start | bytes 786440 | tf_op jit(solution)/shard_map/ppermute | solution.py:526
  46.4 3.9 %collective-permute-start.17 = (bf16[256,512]{1,0:T(8,128)(2,1)S(1)}, bf16[256,512]{1,0:T(8,128)(2,1)S(1)}, u32[]{:S(2)}, u32[]{:S(2)}) collective-permute-start(bf16[256,512]{1,0:T(8,128)(2,1)S(1)} %get-tuple-element.38.refs_3_), channel_id=1, source_target_pairs={{0,1},{1,0},{2,3},{3,2},{4,5},{5,4},{6,7},{7,6},{8,9},{9,8},{10,11... | collective-permute-start | bytes 786440 | tf_op jit(solution)/shard_map/ppermute | solution.py:526
  47.4 10.0 %collective-permute-start.19 = (bf16[512,256]{1,0:T(8,128)(2,1)S(1)}, bf16[512,256]{1,0:T(8,128)(2,1)S(1)}, u32[]{:S(2)}, u32[]{:S(2)}) collective-permute-start(bf16[512,256]{1,0:T(8,128)(2,1)S(1)} %proj_queries.1.refs_4_.refs_2_), channel_id=1, source_target_pairs={{0,16},{16,0},{1,17},{17,1},{2,18},{18,2},{3,19},{19,3},{4,20},{20... | collective-permute-start | bytes 786440 | tf_op jit(solution)/shard_map/ppermute | solution.py:530
  51.8 10.7 %collective-permute-start.18 = (bf16[512,256]{1,0:T(8,128)(2,1)S(1)}, bf16[512,256]{1,0:T(8,128)(2,1)S(1)}, u32[]{:S(2)}, u32[]{:S(2)}) collective-permute-start(bf16[512,256]{1,0:T(8,128)(2,1)S(1)} %grad_z_partial.1.refs_0_), channel_id=1, source_target_pairs={{0,16},{16,0},{1,17},{17,1},{2,18},{18,2},{3,19},{19,3},{4,20},{20... | collective-permute-start | bytes 786440 | tf_op jit(solution)/shard_map/ppermute | solution.py:530
  65.0 2.7 %collective-permute-start.21 = (bf16[4,512,256]{2,1,0:T(8,128)(2,1)S(1)}, bf16[4,512,256]{2,1,0:T(8,128)(2,1)S(1)}, u32[]{:S(2)}, u32[]{:S(2)}) collective-permute-start(bf16[4,512,256]{2,1,0:T(8,128)(2,1)S(1)} %input_partial.3), channel_id=1, source_target_pairs={{0,1},{1,0},{2,3},{3,2},{4,5},{5,4},{6,7},{7,6},{8,9},{9,8},{10,11... | collective-permute-start | bytes 3145736 | tf_op jit(solution)/shard_map/ppermute | solution.py:526
  68.0 6.2 %collective-permute-start.25 = (bf16[512,128]{1,0:T(8,128)(2,1)S(1)}, bf16[512,128]{1,0:T(8,128)(2,1)S(1)}, u32[]{:S(2)}, u32[]{:S(2)}) collective-permute-start(bf16[512,128]{1,0:T(8,128)(2,1)S(1)} %get-tuple-element.49), channel_id=1, source_target_pairs={{0,4},{1,5},{2,6},{3,7},{4,0},{5,1},{6,2},{7,3},{8,12},{9,13},{10,... | collective-permute-start | bytes 393224 | tf_op jit(solution)/shard_map/ppermute | solution.py:526
  69.4 9.0 %collective-permute-start.26 = (bf16[512,128]{1,0:T(8,128)(2,1)S(1)}, bf16[512,128]{1,0:T(8,128)(2,1)S(1)}, u32[]{:S(2)}, u32[]{:S(2)}) collective-permute-start(bf16[512,128]{1,0:T(8,128)(2,1)S(1)} %get-tuple-element.50), channel_id=1, source_target_pairs={{0,2},{1,3},{2,0},{3,1},{4,6},{5,7},{6,4},{7,5},{8,10},{9,11},{10,... | collective-permute-start | bytes 393224 | tf_op jit(solution)/shard_map/ppermute | solution.py:526
  69.8 8.5 %collective-permute-start.27 = (bf16[512,128]{1,0:T(8,128)(2,1)S(1)}, bf16[512,128]{1,0:T(8,128)(2,1)S(1)}, u32[]{:S(2)}, u32[]{:S(2)}) collective-permute-start(bf16[512,128]{1,0:T(8,128)(2,1)S(1)} %get-tuple-element.51), channel_id=1, source_target_pairs={{0,6},{1,7},{2,4},{3,5},{4,2},{5,3},{6,0},{7,1},{8,14},{9,15},{10,... | collective-permute-start | bytes 393224 | tf_op jit(solution)/shard_map/ppermute | solution.py:526
  71.5 8.7 %collective-permute-start.22 = (bf16[512,128]{1,0:T(8,128)(2,1)S(1)}, bf16[512,128]{1,0:T(8,128)(2,1)S(1)}, u32[]{:S(2)}, u32[]{:S(2)}) collective-permute-start(bf16[512,128]{1,0:T(8,128)(2,1)S(1)} %get-tuple-element.45), channel_id=1, source_target_pairs={{0,4},{1,5},{2,6},{3,7},{4,0},{5,1},{6,2},{7,3},{8,12},{9,13},{10,... | collective-permute-start | bytes 393224 | tf_op jit(solution)/shard_map/ppermute | solution.py:526
  72.8 10.2 %collective-permute-start.23 = (bf16[512,128]{1,0:T(8,128)(2,1)S(1)}, bf16[512,128]{1,0:T(8,128)(2,1)S(1)}, u32[]{:S(2)}, u32[]{:S(2)}) collective-permute-start(bf16[512,128]{1,0:T(8,128)(2,1)S(1)} %get-tuple-element.46), channel_id=1, source_target_pairs={{0,2},{1,3},{2,0},{3,1},{4,6},{5,7},{6,4},{7,5},{8,10},{9,11},{10,... | collective-permute-start | bytes 393224 | tf_op jit(solution)/shard_map/ppermute | solution.py:526
  74.2 8.9 %collective-permute-start.24 = (bf16[512,128]{1,0:T(8,128)(2,1)S(1)}, bf16[512,128]{1,0:T(8,128)(2,1)S(1)}, u32[]{:S(2)}, u32[]{:S(2)}) collective-permute-start(bf16[512,128]{1,0:T(8,128)(2,1)S(1)} %get-tuple-element.47), channel_id=1, source_target_pairs={{0,6},{1,7},{2,4},{3,5},{4,2},{5,3},{6,0},{7,1},{8,14},{9,15},{10,... | collective-permute-start | bytes 393224 | tf_op jit(solution)/shard_map/ppermute | solution.py:526
  78.4 5.0 %collective-permute-start.28 = (bf16[512,128]{1,0:T(8,128)(2,1)S(1)}, bf16[512,128]{1,0:T(8,128)(2,1)S(1)}, u32[]{:S(2)}, u32[]{:S(2)}) collective-permute-start(bf16[512,128]{1,0:T(8,128)(2,1)S(1)} %total.3), channel_id=1, source_target_pairs={{0,16},{16,0},{1,17},{17,1},{2,18},{18,2},{3,19},{19,3},{4,20},{20... | collective-permute-start | bytes 393224 | tf_op jit(solution)/shard_map/ppermute | solution.py:530
  83.5 9.0 %collective-permute-start.29 = (bf16[512,128]{1,0:T(8,128)(2,1)S(1)}, bf16[512,128]{1,0:T(8,128)(2,1)S(1)}, u32[]{:S(2)}, u32[]{:S(2)}) collective-permute-start(bf16[512,128]{1,0:T(8,128)(2,1)S(1)} %get-tuple-element.53), channel_id=1, source_target_pairs={{0,8},{1,9},{2,10},{3,11},{4,12},{5,13},{6,14},{7,15},{8,0},{9,1},... | collective-permute-start | bytes 393224 | tf_op jit(solution)/shard_map/ppermute | solution.py:526

commit v7 on v6

--- a/solution.py
+++ b/solution.py
@@ -268,10 +268,15 @@
 
 def grad_z_kernel(masks, runs, *refs):
     xs, (w_ref, out_ref, held) = refs[:-3], refs[-3:]
-    assembled(masks, xs, held)
-    total = lax.dot_general(
-        w_ref[...], held[...], (((1,), (1,)), ((), ())), preferred_element_type=F32
-    )
+    total = None
+    for n, x_ref in enumerate(xs):
+        term = lax.dot_general(
+            w_ref[:, piece_rows(masks, n, x_ref.shape[1])],
+            x_ref[...],
+            (((1,), (1,)), ((), ())),
+            preferred_element_type=F32,
+        )
+        total = term if total is None else total + term
     run = total.shape[1] // runs
     for h, start in enumerate(run_starts(runs, run)):
         out_ref[:, pl.ds(start, run)] = total[:, h * run : (h + 1) * run].astype(BF16)
@@ -379,7 +384,7 @@
 def conv_forward(shares, past):
     _, channels, tokens = shares[0].shape
     groups = past.shape[0]
-    steps = max(1, groups // 16)
+    steps = max(1, groups // 32)
     chunk = channels // steps
     parts = len(shares)
     two = pl.BlockSpec((2, chunk, tokens), lambda i: (0, i, 0))
@@ -423,7 +428,7 @@
 def conv_backward(shares, queries, pair, conv, after):
     channels, tokens = conv.shape
     groups = after.shape[0]
-    steps = max(1, groups // 16)
+    steps = max(1, groups // 32)
     chunk = channels // steps
     parts = len(shares)
     three = pl.BlockSpec((3, chunk, tokens), lambda i: (0, i, 0))
@@ -552,37 +557,40 @@
     return in_square(array, from_turn), in_square(array, over_diagonal)
 
 
-def second_stage(own):
-    return [own] + [across(own, mask) for mask in MINE[1:]]
+def second_stage(own, order=(1, 2, 3)):
+    got = {n: across(own, MINE[n]) for n in order}
+    return [own] + [got[n] for n in (1, 2, 3)]
 
 
 def both_cores(same):
     return same + [across(piece, CORE) for piece in same]
 
 
-def split_kernel(same_ref, got_ref, *out_refs):
+def split_kernel(parts, same_ref, *refs):
+    got_refs, out_refs = refs[:parts], refs[parts:]
     pieces = same_ref.shape[0]
+    got = [ref.at[n] for ref in got_refs for n in range(ref.shape[0])]
     y = lax.axis_index("fsdp")
     leave = pl.ds(pl.multiple_of((1 - y) * TOK_DEV, BLOCK), TOK_DEV)
     stay = pl.ds(pl.multiple_of(y * TOK_DEV, BLOCK), TOK_DEV)
     for n in range(pieces):
         for at, out_ref in ((leave, out_refs[n]), (stay, out_refs[pieces + n])):
-            total = same_ref[n, :, at].astype(F32) + got_ref[n, :, at].astype(F32)
+            total = same_ref[n, :, at].astype(F32) + got[n][:, at].astype(F32)
             out_ref[...] = total.astype(BF16)
 
 
-def split(same, got):
+def split(same, *got):
     pieces, rows, _ = same.shape
     out = jax.ShapeDtypeStruct((rows, TOK_DEV), BF16)
     halves = pl.pallas_call(
-        split_kernel,
-        in_specs=[VMEM_SPEC] * 2,
+        functools.partial(split_kernel, len(got)),
+        in_specs=[VMEM_SPEC] * (1 + len(got)),
         out_specs=[VMEM_SPEC] * (2 * pieces),
         out_shape=[out] * (2 * pieces),
         compiler_params=params(8),
         cost_estimate=cost(0, 6 * same.size),
         name="split",
-    )(same, got)
+    )(same, *got)
     return halves[:pieces], halves[pieces:]
 
 
@@ -605,31 +613,36 @@
     )(*pieces)
 
 
-def sides_kernel(near_ref, far_ref, keep_ref, send_ref):
+def sides_kernel(*refs):
+    far_ref, keep_ref, send_ref = refs[-3:]
     home = at_home()
+    near = refs[0][...].astype(F32)
+    for ref in refs[1:-3]:
+        near = near + ref[...].astype(F32)
+    near = near.astype(BF16)
 
     @pl.when(home)
     def _():
-        keep_ref[...] = near_ref[...]
+        keep_ref[...] = near
         send_ref[...] = far_ref[...]
 
     @pl.when(jnp.logical_not(home))
     def _():
         keep_ref[...] = far_ref[...]
-        send_ref[...] = near_ref[...]
-
-
-def sides(near, far):
-    out = jax.ShapeDtypeStruct(near.shape, BF16)
+        send_ref[...] = near
+
+
+def sides(pieces, far):
+    out = jax.ShapeDtypeStruct(far.shape, BF16)
     return pl.pallas_call(
         sides_kernel,
-        in_specs=[VMEM_SPEC] * 2,
+        in_specs=[VMEM_SPEC] * (len(pieces) + 1),
         out_specs=[VMEM_SPEC] * 2,
         out_shape=[out] * 2,
         compiler_params=params(8),
-        cost_estimate=cost(0, 8 * near.size),
+        cost_estimate=cost(0, 8 * far.size),
         name="sides",
-    )(near, far)
+    )(*pieces, far)
 
 
 def last_kernel(keep_ref, got_ref, out_ref):
@@ -653,11 +666,11 @@
     return [pieces[0]] + [across(piece, mask) for piece, mask in zip(pieces[1:], MINE[1:])]
 
 
-def scattered(same, others):
-    leave, stay = split(same, across(others, CORE))
+def scattered(same, *others):
+    leave, stay = split(same, *[across(part, CORE) for part in others])
     leave, stay = moved(leave), moved(stay)
     far = other_row(total_of(leave))
-    keep, send = sides(total_of(stay), far)
+    keep, send = sides(stay, far)
     return last_sum(keep, across(send, Z1))
 
 
@@ -666,24 +679,28 @@
     token_stage = first_stage(tokens)
     weights, ready = prepared(values, scales)
     token_own = own_slice(in_hbm(tokens), *token_stage, ready)
-    token_same = second_stage(token_own)
+    token_same = second_stage(token_own, (2, 1, 3))
     past, later = toeplitz(filters, token_own)
     out_held = loaded(out_weight, past)
     cotangent = copied(cotangent, token_own)
     cot_own = own_slice(cotangent, *first_stage(cotangent))
     late = relayed([token_same[3]], out_held, cot_own)
     token_same = [*token_same[:3], *late]
+    xs = both_cores(token_same)
     cot_same = second_stage(cot_own)
-    pair, queries = proj_partial(both_cores(token_same), MINE + OTHERS, 2, weights)
+    pair, queries = proj_partial(xs, MINE + OTHERS, 2, weights)
     cot_same = list(relayed(cot_same, queries))
     pair, product, conv = conv_forward([pair, other_row(pair)], past)
     z_part = grad_z_partial(both_cores(cot_same), MINE + OTHERS, 2, out_held)
     grad_proj, grad = conv_backward(
         [z_part, other_row(z_part)], [queries, other_row(queries)], pair, conv, later
     )
-    others = input_partial(OTHERS, 4, rows, weights, grad_proj)
+    others = [
+        input_partial(masks, len(masks), rows, weights, grad_proj)
+        for masks in (OTHERS[:3], OTHERS[3:])
+    ]
     same = input_partial(MINE, 4, rows, weights, grad_proj)
-    return scattered(same, others), taps_gradient(product, grad, filters.shape[0])
+    return scattered(same, *others), taps_gradient(product, grad, filters.shape[0])
 
 
 def on_any_slice(tokens, values, scales, filters, out_weight, cotangent):

time: 93.5 us -> 92.8 us (level)
    ppermute x22 -> x23, waiting for transfers between devices: 20.3 us -> 18.9 us  [across(): return lax.ppermute(array, 'tensor', [(i, i ^ mask) for i in range(16)])]
    ppermute x22 -> x23, starting transfers between devices: 19.7 us -> 20.3 us  [across(): return lax.ppermute(array, 'tensor', [(i, i ^ mask) for i in range(16)])]
    pallas_call x2 -> x3, Pallas kernels: 3.57 us -> 3.74 us  [input_partial(): pl.pallas_call(functools.partial(input_kernel, masks), in_specs=[VMEM_SPE...]
  transfers between devices with their start and end apart: 30 -> 31, of which waited for: 12 -> 11; matrix products, arithmetic and copies ran while one was open for 0% -> 0% of each run, Pallas kernels for 22% -> 22%
where the time goes in v7:
time: 92.8 us; the launch traced here: 92.6 us
  starting transfers between devices  38.5 us (41%)
  waiting for transfers between devices  28.7 us (31%)
  Pallas kernels  24.5 us (26%)
    ppermute x23, starting transfers between devices, across(): return lax.ppermute(array, 'tensor', [(i, i ^ mask) for i in range(16)])  20.3 us
    ppermute x23, waiting for transfers between devices, across(): return lax.ppermute(array, 'tensor', [(i, i ^ mask) for i in range(16)])  18.9 us
    ppermute x4, starting transfers between devices, in_square(): return lax.ppermute(array, ('fsdp', 'tensor'), pairs)  11.1 us
    ppermute x4, waiting for transfers between devices, other_row(): return lax.ppermute(array, 'fsdp', [(0, 1), (1, 0)])  9.82 us
    ppermute x4, starting transfers between devices, other_row(): return lax.ppermute(array, 'fsdp', [(0, 1), (1, 0)])  7.15 us
    pallas_call x1, Pallas kernels, prepared(): pl.pallas_call(prepare_kernel, in_specs=[LATER_SPEC] * (2 + len(earlier))...  5.89 us
    pallas_call x3, Pallas kernels, input_partial(): pl.pallas_call(functools.partial(input_kernel, masks), in_specs=[VMEM_SPE...  3.74 us
    pallas_call x1, Pallas kernels, taps_gradient(): pl.pallas_call(functools.partial(taps_kernel, groups // steps), grid=(ste...  3.22 us
  transfers between devices with their start and end apart: 31, of which 11 were waited for; matrix products, arithmetic and copies ran while one was open for 0% of the time, Pallas kernels for 22%

profile of v7, /device:TPU:0, one launch (start us, length us, event | category | flops | bytes accessed | tf_op | source)
XLA Modules:
  0.0 92.6 jit_solution(2127959523653145791)
XLA Ops:
  0.6 4.1 %collective-permute-start = (bf16[128,512]{1,0:T(8,128)(2,1)}, bf16[128,512]{1,0:T(8,128)(2,1)S(1)}, u32[]{:S(2)}, u32[]{:S(2)}) collective-permute-start(bf16[128,512]{1,0:T(8,128)(2,1)} %array_ref.1), channel_id=1, source_target_pairs={{0,8},{1,9},{2,10},{3,11},{4,12},{5,13},{6,14},{7,15},{8,24},{9,25... | collective-permute-start | bytes 393224 | tf_op jit(solution)/shard_map/ppermute | solution.py:545
  5.4 5.9 %prepare.1 = (bf16[4096,512]{1,0:T(8,128)(2,1)S(1)}, bf16[4096,512]{1,0:T(8,128)(2,1)S(1)}, bf16[4096,512]{1,0:T(8,128)(2,1)S(1)}, f32[8,128]{1,0:T(8,128)S(1)}) custom-call(bf16[3,4096,512]{2,1,0:T(8,128)(2,1)} %bitcast.6, bf16[3,32,512]{2,1,0:T(8,128)(2,1)} %bitcast.7), custom_call_target="tpu_custom_call" | custom-call | flops 6144 | bytes 6144 | tf_op jit(solution)/shard_map/prepare/pallas_call | solution.py:154
  11.3 0.9 %own_slice.2.refs_0_ = bf16[256,512]{1,0:T(8,128)(2,1)S(1)} custom-call(bf16[128,512]{1,0:T(8,128)(2,1)} %array_ref.1, bf16[128,512]{1,0:T(8,128)(2,1)S(1)} %collective-permute-done.turned_ref, bf16[128,512]{1,0:T(8,128)(2,1)S(1)} %collective-permute-done.1.crossed_ref, f32[8,128]{1,0:T(8,128)S(1)} %get-tuple-element.32.refs_0_), custom_call_target="tpu_custom_call" | custom-call | bytes 160 | tf_op jit(solution)/shard_map/own_slice/pallas_call | solution.py:73
  12.3 2.6 %collective-permute-start.9 = (bf16[256,512]{1,0:T(8,128)(2,1)S(1)}, bf16[256,512]{1,0:T(8,128)(2,1)S(1)}, u32[]{:S(2)}, u32[]{:S(2)}) collective-permute-start(bf16[256,512]{1,0:T(8,128)(2,1)S(1)} %own_slice.2.refs_0_), channel_id=1, source_target_pairs={{0,6},{1,7},{2,4},{3,5},{4,2},{5,3},{6,0},{7,1},{8,14},{9,15},{10,... | collective-permute-start | bytes 786440 | tf_op jit(solution)/shard_map/ppermute | solution.py:531
  14.8 5.7 %collective-permute-start.2 = (bf16[128,512]{1,0:T(8,128)(2,1)S(1)}, bf16[128,512]{1,0:T(8,128)(2,1)S(1)}, u32[]{:S(2)}, u32[]{:S(2)}) collective-permute-start(bf16[128,512]{1,0:T(8,128)(2,1)S(1)} %copied.1.array_ref), channel_id=1, source_target_pairs={{0,8},{1,9},{2,10},{3,11},{4,12},{5,13},{6,14},{7,15},{8,24},{9,25... | collective-permute-start | bytes 393224 | tf_op jit(solution)/shard_map/ppermute | solution.py:545
  21.9 1.0 %toeplitz.1 = (bf16[32,256,128]{2,1,0:T(8,128)(2,1)S(1)}, bf16[32,256,128]{2,1,0:T(8,128)(2,1)S(1)}) custom-call(f32[32,128]{1,0:T(8,128)S(1)} %copy-done.1, bf16[256,512]{1,0:T(8,128)(2,1)S(1)} %own_slice.2.refs_0_), custom_call_target="tpu_custom_call" | custom-call | flops 2000 | bytes 1024 | tf_op jit(solution)/shard_map/toeplitz/pallas_call | solution.py:325
  22.9 2.2 %loaded.1.refs_1_.refs_8_ = bf16[512,4096]{1,0:T(8,128)(2,1)S(1)} custom-call(bf16[512,4096]{1,0:T(8,128)(2,1)} %in_ref.3, bf16[32,256,128]{2,1,0:T(8,128)(2,1)S(1)} %get-tuple-element.33.refs_0_.refs_2_), custom_call_target="tpu_custom_call" | custom-call | bytes 2048 | tf_op jit(solution)/shard_map/loaded/pallas_call | solution.py:205
  26.0 5.4 %collective-permute-done.7.refs_1_ = bf16[256,512]{1,0:T(8,128)(2,1)S(1)} collective-permute-done((bf16[256,512]{1,0:T(8,128)(2,1)S(1)}, bf16[256,512]{1,0:T(8,128)(2,1)S(1)}, u32[]{:S(2)}, u32[]{:S(2)}) %collective-permute-start.7) | collective-permute-done | bytes 262176 | tf_op jit(solution)/shard_map/ppermute | solution.py:531
  32.4 3.0 %collective-permute-start.6 = (bf16[256,512]{1,0:T(8,128)(2,1)S(1)}, bf16[256,512]{1,0:T(8,128)(2,1)S(1)}, u32[]{:S(2)}, u32[]{:S(2)}) collective-permute-start(bf16[256,512]{1,0:T(8,128)(2,1)S(1)} %own_slice.3.refs_2_.refs_0_), channel_id=1, source_target_pairs={{0,6},{1,7},{2,4},{3,5},{4,2},{5,3},{6,0},{7,1},{8,14},{9,15},{10,... | collective-permute-start | bytes 786440 | tf_op jit(solution)/shard_map/ppermute | solution.py:531
  35.4 2.5 %proj_pair.1 = (bf16[2,512,256]{2,1,0:T(8,128)(2,1)S(1)}, bf16[256,4096]{1,0:T(8,128)(2,1)S(1)}) custom-call(bf16[256,512]{1,0:T(8,128)(2,1)S(1)} %own_slice.2.refs_0_, bf16[256,512]{1,0:T(8,128)(2,1)S(1)} %collective-permute-done.7.refs_1_, bf16[256,512]{1,0:T(8,128)(2,1)S(1)} %collective-permute-done.8.refs_2_, bf16[256,512]{1,0:T(8,128)(2,1)S(1)} %relayed.2.refs_3_, ...), custom_call_target="tpu_custom_call" | custom-call | flops 524288 | bytes 2048 | tf_op jit(solution)/shard_map/proj_pair/pallas_call | solution.py:245
  38.0 1.3 %collective-permute-start.20 = (bf16[2,512,256]{2,1,0:T(8,128)(2,1)S(1)}, bf16[2,512,256]{2,1,0:T(8,128)(2,1)S(1)}, u32[]{:S(2)}, u32[]{:S(2)}) collective-permute-start(bf16[2,512,256]{2,1,0:T(8,128)(2,1)S(1)} %get-tuple-element.39.refs_0_), channel_id=1, source_target_pairs={{0,16},{16,0},{1,17},{17,1},{2,18},{18,2},{3,19},{19,3},{4,20},{20... | collective-permute-start | bytes 1572872 | tf_op jit(solution)/shard_map/ppermute | solution.py:535
  39.3 1.3 %proj_queries.1.refs_4_.refs_2_ = bf16[512,256]{1,0:T(8,128)(2,1)S(1)} custom-call(bf16[256,4096]{1,0:T(8,128)(2,1)S(1)} %get-tuple-element.34.held_ref, bf16[4096,512]{1,0:T(8,128)(2,1)S(1)} %get-tuple-element.29.w_ref.refs_0_), custom_call_target="tpu_custom_call" | custom-call | flops 262144 | bytes 1024 | tf_op jit(solution)/shard_map/proj_queries/pallas_call | solution.py:257
  41.1 4.7 %collective-permute-done.5.refs_2_ = bf16[256,512]{1,0:T(8,128)(2,1)S(1)} collective-permute-done((bf16[256,512]{1,0:T(8,128)(2,1)S(1)}, bf16[256,512]{1,0:T(8,128)(2,1)S(1)}, u32[]{:S(2)}, u32[]{:S(2)}) %collective-permute-start.5) | collective-permute-done | bytes 262176 | tf_op jit(solution)/shard_map/ppermute | solution.py:531
  47.4 2.9 %collective-permute-start.19 = (bf16[512,256]{1,0:T(8,128)(2,1)S(1)}, bf16[512,256]{1,0:T(8,128)(2,1)S(1)}, u32[]{:S(2)}, u32[]{:S(2)}) collective-permute-start(bf16[512,256]{1,0:T(8,128)(2,1)S(1)} %proj_queries.1.refs_4_.refs_2_), channel_id=1, source_target_pairs={{0,16},{16,0},{1,17},{17,1},{2,18},{18,2},{3,19},{19,3},{4,20},{20... | collective-permute-start | bytes 786440 | tf_op jit(solution)/shard_map/ppermute | solution.py:535
  50.3 1.3 %grad_z_partial.1.refs_0_ = bf16[512,256]{1,0:T(8,128)(2,1)S(1)} custom-call(bf16[256,512]{1,0:T(8,128)(2,1)S(1)} %get-tuple-element.35.refs_0_, bf16[256,512]{1,0:T(8,128)(2,1)S(1)} %get-tuple-element.36.refs_1_, bf16[256,512]{1,0:T(8,128)(2,1)S(1)} %get-tuple-element.37.refs_2_, bf16[256,512]{1,0:T(8,128)(2,1)S(1)} %get-tuple-element.38.refs_3_, ...), custom_call_target="tpu_custom_call" | custom-call | flops 262144 | bytes 1024 | tf_op jit(solution)/shard_map/grad_z_partial/pallas_call | solution.py:288
  51.6 1.2 %collective-permute-start.18 = (bf16[512,256]{1,0:T(8,128)(2,1)S(1)}, bf16[512,256]{1,0:T(8,128)(2,1)S(1)}, u32[]{:S(2)}, u32[]{:S(2)}) collective-permute-start(bf16[512,256]{1,0:T(8,128)(2,1)S(1)} %grad_z_partial.1.refs_0_), channel_id=1, source_target_pairs={{0,16},{16,0},{1,17},{17,1},{2,18},{18,2},{3,19},{19,3},{4,20},{20... | collective-permute-start | bytes 786440 | tf_op jit(solution)/shard_map/ppermute | solution.py:535
  53.2 4.2 %collective-permute-done.19.refs_3_ = bf16[512,256]{1,0:T(8,128)(2,1)S(1)} collective-permute-done((bf16[512,256]{1,0:T(8,128)(2,1)S(1)}, bf16[512,256]{1,0:T(8,128)(2,1)S(1)}, u32[]{:S(2)}, u32[]{:S(2)}) %collective-permute-start.19) | collective-permute-done | bytes 262176 | tf_op jit(solution)/shard_map/ppermute | solution.py:535
  57.4 5.1 %collective-permute-done.18.refs_1_ = bf16[512,256]{1,0:T(8,128)(2,1)S(1)} collective-permute-done((bf16[512,256]{1,0:T(8,128)(2,1)S(1)}, bf16[512,256]{1,0:T(8,128)(2,1)S(1)}, u32[]{:S(2)}, u32[]{:S(2)}) %collective-permute-start.18) | collective-permute-done | bytes 262176 | tf_op jit(solution)/shard_map/ppermute | solution.py:535
  63.0 1.4 %input_partial.4 = bf16[3,512,256]{2,1,0:T(8,128)(2,1)S(1)} custom-call(bf16[4096,512]{1,0:T(8,128)(2,1)S(1)} %get-tuple-element.29.w_ref.refs_0_, bf16[4096,512]{1,0:T(8,128)(2,1)S(1)} %get-tuple-element.30.refs_8_.refs_1_, bf16[4096,512]{1,0:T(8,128)(2,1)S(1)} %get-tuple-element.31.refs_9_.refs_2_, bf16[1536,256]{1,0:T(8,128)(2,1)S(1)} %bitcast.3), custom_call_target="tpu_custom_call" | custom-call | flops 294912 | bytes 1344 | tf_op jit(solution)/shard_map/input_partial/pallas_call | solution.py:517
  65.6 1.8 %input_partial.3.same_ref = bf16[4,512,256]{2,1,0:T(8,128)(2,1)S(1)} custom-call(bf16[4096,512]{1,0:T(8,128)(2,1)S(1)} %get-tuple-element.29.w_ref.refs_0_, bf16[4096,512]{1,0:T(8,128)(2,1)S(1)} %get-tuple-element.30.refs_8_.refs_1_, bf16[4096,512]{1,0:T(8,128)(2,1)S(1)} %get-tuple-element.31.refs_9_.refs_2_, bf16[1536,256]{1,0:T(8,128)(2,1)S(1)} %bitcast.5), custom_call_target="tpu_custom_call" | custom-call | flops 393216 | bytes 1792 | tf_op jit(solution)/shard_map/input_partial/pallas_call | solution.py:517
  67.7 1.4 %collective-permute-start.26 = (bf16[512,128]{1,0:T(8,128)(2,1)S(1)}, bf16[512,128]{1,0:T(8,128)(2,1)S(1)}, u32[]{:S(2)}, u32[]{:S(2)}) collective-permute-start(bf16[512,128]{1,0:T(8,128)(2,1)S(1)} %get-tuple-element.49), channel_id=1, source_target_pairs={{0,4},{1,5},{2,6},{3,7},{4,0},{5,1},{6,2},{7,3},{8,12},{9,13},{10,... | collective-permute-start | bytes 393224 | tf_op jit(solution)/shard_map/ppermute | solution.py:531
  69.5 1.7 %collective-permute-start.28 = (bf16[512,128]{1,0:T(8,128)(2,1)S(1)}, bf16[512,128]{1,0:T(8,128)(2,1)S(1)}, u32[]{:S(2)}, u32[]{:S(2)}) collective-permute-start(bf16[512,128]{1,0:T(8,128)(2,1)S(1)} %get-tuple-element.51), channel_id=1, source_target_pairs={{0,6},{1,7},{2,4},{3,5},{4,2},{5,3},{6,0},{7,1},{8,14},{9,15},{10,... | collective-permute-start | bytes 393224 | tf_op jit(solution)/shard_map/ppermute | solution.py:531
  71.2 1.3 %collective-permute-start.23 = (bf16[512,128]{1,0:T(8,128)(2,1)S(1)}, bf16[512,128]{1,0:T(8,128)(2,1)S(1)}, u32[]{:S(2)}, u32[]{:S(2)}) collective-permute-start(bf16[512,128]{1,0:T(8,128)(2,1)S(1)} %get-tuple-element.45), channel_id=1, source_target_pairs={{0,4},{1,5},{2,6},{3,7},{4,0},{5,1},{6,2},{7,3},{8,12},{9,13},{10,... | collective-permute-start | bytes 393224 | tf_op jit(solution)/shard_map/ppermute | solution.py:531
  73.0 0.7 collective-permute-done.26.refs_1_
  73.7 1.6 %collective-permute-start.25 = (bf16[512,128]{1,0:T(8,128)(2,1)S(1)}, bf16[512,128]{1,0:T(8,128)(2,1)S(1)}, u32[]{:S(2)}, u32[]{:S(2)}) collective-permute-start(bf16[512,128]{1,0:T(8,128)(2,1)S(1)} %get-tuple-element.47), channel_id=1, source_target_pairs={{0,6},{1,7},{2,4},{3,5},{4,2},{5,3},{6,0},{7,1},{8,14},{9,15},{10,... | collective-permute-start | bytes 393224 | tf_op jit(solution)/shard_map/ppermute | solution.py:531
  75.3 2.7 %collective-permute-done.27.refs_2_ = bf16[512,128]{1,0:T(8,128)(2,1)S(1)} collective-permute-done((bf16[512,128]{1,0:T(8,128)(2,1)S(1)}, bf16[512,128]{1,0:T(8,128)(2,1)S(1)}, u32[]{:S(2)}, u32[]{:S(2)}) %collective-permute-start.27) | collective-permute-done | bytes 131104 | tf_op jit(solution)/shard_map/ppermute | solution.py:531
  78.1 1.8 %collective-permute-start.29 = (bf16[512,128]{1,0:T(8,128)(2,1)S(1)}, bf16[512,128]{1,0:T(8,128)(2,1)S(1)}, u32[]{:S(2)}, u32[]{:S(2)}) collective-permute-start(bf16[512,128]{1,0:T(8,128)(2,1)S(1)} %total.1), channel_id=1, source_target_pairs={{0,16},{16,0},{1,17},{17,1},{2,18},{18,2},{3,19},{19,3},{4,20},{20... | collective-permute-start | bytes 393224 | tf_op jit(solution)/shard_map/ppermute | solution.py:535
  79.9 2.7 %collective-permute-done.24.refs_2_ = bf16[512,128]{1,0:T(8,128)(2,1)S(1)} collective-permute-done((bf16[512,128]{1,0:T(8,128)(2,1)S(1)}, bf16[512,128]{1,0:T(8,128)(2,1)S(1)}, u32[]{:S(2)}, u32[]{:S(2)}) %collective-permute-start.24) | collective-permute-done | bytes 131104 | tf_op jit(solution)/shard_map/ppermute | solution.py:531
  83.2 3.9 %collective-permute-start.30 = (bf16[512,128]{1,0:T(8,128)(2,1)S(1)}, bf16[512,128]{1,0:T(8,128)(2,1)S(1)}, u32[]{:S(2)}, u32[]{:S(2)}) collective-permute-start(bf16[512,128]{1,0:T(8,128)(2,1)S(1)} %get-tuple-element.53), channel_id=1, source_target_pairs={{0,8},{1,9},{2,10},{3,11},{4,12},{5,13},{6,14},{7,15},{8,0},{9,1},... | collective-permute-start | bytes 393224 | tf_op jit(solution)/shard_map/ppermute | solution.py:531
  87.1 3.2 %taps_gradient.1 = f32[32,128]{1,0:T(8,128)} custom-call(bf16[512,256]{1,0:T(8,128)(2,1)S(1)} %get-tuple-element.54.prod_ref, bf16[512,256]{1,0:T(8,128)(2,1)S(1)} %get-tuple-element.55.grad_ref), custom_call_target="tpu_custom_call" | custom-call | flops 131072 | bytes 768 | tf_op jit(solution)/shard_map/taps_gradient/pallas_call | solution.py:494
  90.3 1.5 %collective-permute-done.30.got_ref = bf16[512,128]{1,0:T(8,128)(2,1)S(1)} collective-permute-done((bf16[512,128]{1,0:T(8,128)(2,1)S(1)}, bf16[512,128]{1,0:T(8,128)(2,1)S(1)}, u32[]{:S(2)}, u32[]{:S(2)}) %collective-permute-start.30) | collective-permute-done | bytes 131104 | tf_op jit(solution)/shard_map/ppermute | solution.py:531
  91.8 0.8 last_sum.1
  (55 shorter events, 9.9 us)
Async XLA Ops:
  0.6 10.7 %collective-permute-start = (bf16[128,512]{1,0:T(8,128)(2,1)}, bf16[128,512]{1,0:T(8,128)(2,1)S(1)}, u32[]{:S(2)}, u32[]{:S(2)}) collective-permute-start(bf16[128,512]{1,0:T(8,128)(2,1)} %array_ref.1), channel_id=1, source_target_pairs={{0,8},{1,9},{2,10},{3,11},{4,12},{5,13},{6,14},{7,15},{8,24},{9,25... | collective-permute-start | bytes 393224 | tf_op jit(solution)/shard_map/ppermute | solution.py:545
  4.7 6.6 %collective-permute-start.1 = (bf16[128,512]{1,0:T(8,128)(2,1)}, bf16[128,512]{1,0:T(8,128)(2,1)S(1)}, u32[]{:S(2)}, u32[]{:S(2)}) collective-permute-start(bf16[128,512]{1,0:T(8,128)(2,1)} %array_ref.1), channel_id=1, source_target_pairs={{8,16},{9,17},{10,18},{11,19},{12,20},{13,21},{14,22},{15,23},{16,... | collective-permute-start | bytes 393224 | tf_op jit(solution)/shard_map/ppermute | solution.py:545
  5.4 16.5 %copy-start.1 = (f32[32,128]{1,0:T(8,128)S(1)}, f32[32,128]{1,0:T(8,128)}, u32[]{:S(2)}) copy-start(f32[32,128]{1,0:T(8,128)} %taps_ref.1) | copy-start | bytes 49156
  12.3 13.2 %collective-permute-start.9 = (bf16[256,512]{1,0:T(8,128)(2,1)S(1)}, bf16[256,512]{1,0:T(8,128)(2,1)S(1)}, u32[]{:S(2)}, u32[]{:S(2)}) collective-permute-start(bf16[256,512]{1,0:T(8,128)(2,1)S(1)} %own_slice.2.refs_0_), channel_id=1, source_target_pairs={{0,6},{1,7},{2,4},{3,5},{4,2},{5,3},{6,0},{7,1},{8,14},{9,15},{10,... | collective-permute-start | bytes 786440 | tf_op jit(solution)/shard_map/ppermute | solution.py:531
  14.8 10.3 %collective-permute-start.2 = (bf16[128,512]{1,0:T(8,128)(2,1)S(1)}, bf16[128,512]{1,0:T(8,128)(2,1)S(1)}, u32[]{:S(2)}, u32[]{:S(2)}) collective-permute-start(bf16[128,512]{1,0:T(8,128)(2,1)S(1)} %copied.1.array_ref), channel_id=1, source_target_pairs={{0,8},{1,9},{2,10},{3,11},{4,12},{5,13},{6,14},{7,15},{8,24},{9,25... | collective-permute-start | bytes 393224 | tf_op jit(solution)/shard_map/ppermute | solution.py:545
  20.6 4.7 %collective-permute-start.3 = (bf16[128,512]{1,0:T(8,128)(2,1)S(1)}, bf16[128,512]{1,0:T(8,128)(2,1)S(1)}, u32[]{:S(2)}, u32[]{:S(2)}) collective-permute-start(bf16[128,512]{1,0:T(8,128)(2,1)S(1)} %copied.1.array_ref), channel_id=1, source_target_pairs={{8,16},{9,17},{10,18},{11,19},{12,20},{13,21},{14,22},{15,23},{16,... | collective-permute-start | bytes 393224 | tf_op jit(solution)/shard_map/ppermute | solution.py:545
  21.2 10.2 %collective-permute-start.7 = (bf16[256,512]{1,0:T(8,128)(2,1)S(1)}, bf16[256,512]{1,0:T(8,128)(2,1)S(1)}, u32[]{:S(2)}, u32[]{:S(2)}) collective-permute-start(bf16[256,512]{1,0:T(8,128)(2,1)S(1)} %own_slice.2.refs_0_), channel_id=1, source_target_pairs={{0,4},{1,5},{2,6},{3,7},{4,0},{5,1},{6,2},{7,3},{8,12},{9,13},{10,... | collective-permute-start | bytes 786440 | tf_op jit(solution)/shard_map/ppermute | solution.py:531
  21.3 10.1 %collective-permute-start.8 = (bf16[256,512]{1,0:T(8,128)(2,1)S(1)}, bf16[256,512]{1,0:T(8,128)(2,1)S(1)}, u32[]{:S(2)}, u32[]{:S(2)}) collective-permute-start(bf16[256,512]{1,0:T(8,128)(2,1)S(1)} %own_slice.2.refs_0_), channel_id=1, source_target_pairs={{0,2},{1,3},{2,0},{3,1},{4,6},{5,7},{6,4},{7,5},{8,10},{9,11},{10,... | collective-permute-start | bytes 786440 | tf_op jit(solution)/shard_map/ppermute | solution.py:531
  25.2 6.8 %collective-permute-start.10 = (bf16[256,512]{1,0:T(8,128)(2,1)S(1)}, bf16[256,512]{1,0:T(8,128)(2,1)S(1)}, u32[]{:S(2)}, u32[]{:S(2)}) collective-permute-start(bf16[256,512]{1,0:T(8,128)(2,1)S(1)} %own_slice.2.refs_0_), channel_id=1, source_target_pairs={{0,1},{1,0},{2,3},{3,2},{4,5},{5,4},{6,7},{7,6},{8,9},{9,8},{10,11... | collective-permute-start | bytes 786440 | tf_op jit(solution)/shard_map/ppermute | solution.py:531
  25.5 7.0 %collective-permute-start.13 = (bf16[256,512]{1,0:T(8,128)(2,1)S(1)}, bf16[256,512]{1,0:T(8,128)(2,1)S(1)}, u32[]{:S(2)}, u32[]{:S(2)}) collective-permute-start(bf16[256,512]{1,0:T(8,128)(2,1)S(1)} %relayed.2.refs_3_), channel_id=1, source_target_pairs={{0,1},{1,0},{2,3},{3,2},{4,5},{5,4},{6,7},{7,6},{8,9},{9,8},{10,11... | collective-permute-start | bytes 786440 | tf_op jit(solution)/shard_map/ppermute | solution.py:531
  31.4 4.0 %collective-permute-start.11 = (bf16[256,512]{1,0:T(8,128)(2,1)S(1)}, bf16[256,512]{1,0:T(8,128)(2,1)S(1)}, u32[]{:S(2)}, u32[]{:S(2)}) collective-permute-start(bf16[256,512]{1,0:T(8,128)(2,1)S(1)} %collective-permute-done.7.refs_1_), channel_id=1, source_target_pairs={{0,1},{1,0},{2,3},{3,2},{4,5},{5,4},{6,7},{7,6},{8,9},{9,8},{10,11... | collective-permute-start | bytes 786440 | tf_op jit(solution)/shard_map/ppermute | solution.py:531
  31.4 4.0 %collective-permute-start.12 = (bf16[256,512]{1,0:T(8,128)(2,1)S(1)}, bf16[256,512]{1,0:T(8,128)(2,1)S(1)}, u32[]{:S(2)}, u32[]{:S(2)}) collective-permute-start(bf16[256,512]{1,0:T(8,128)(2,1)S(1)} %collective-permute-done.8.refs_2_), channel_id=1, source_target_pairs={{0,1},{1,0},{2,3},{3,2},{4,5},{5,4},{6,7},{7,6},{8,9},{9,8},{10,11... | collective-permute-start | bytes 786440 | tf_op jit(solution)/shard_map/ppermute | solution.py:531
  31.9 9.2 %collective-permute-start.4 = (bf16[256,512]{1,0:T(8,128)(2,1)S(1)}, bf16[256,512]{1,0:T(8,128)(2,1)S(1)}, u32[]{:S(2)}, u32[]{:S(2)}) collective-permute-start(bf16[256,512]{1,0:T(8,128)(2,1)S(1)} %own_slice.3.refs_2_.refs_0_), channel_id=1, source_target_pairs={{0,4},{1,5},{2,6},{3,7},{4,0},{5,1},{6,2},{7,3},{8,12},{9,13},{10,... | collective-permute-start | bytes 786440 | tf_op jit(solution)/shard_map/ppermute | solution.py:531
  32.0 13.9 %collective-permute-start.5 = (bf16[256,512]{1,0:T(8,128)(2,1)S(1)}, bf16[256,512]{1,0:T(8,128)(2,1)S(1)}, u32[]{:S(2)}, u32[]{:S(2)}) collective-permute-start(bf16[256,512]{1,0:T(8,128)(2,1)S(1)} %own_slice.3.refs_2_.refs_0_), channel_id=1, source_target_pairs={{0,2},{1,3},{2,0},{3,1},{4,6},{5,7},{6,4},{7,5},{8,10},{9,11},{10,... | collective-permute-start | bytes 786440 | tf_op jit(solution)/shard_map/ppermute | solution.py:531
  32.4 13.4 %collective-permute-start.6 = (bf16[256,512]{1,0:T(8,128)(2,1)S(1)}, bf16[256,512]{1,0:T(8,128)(2,1)S(1)}, u32[]{:S(2)}, u32[]{:S(2)}) collective-permute-start(bf16[256,512]{1,0:T(8,128)(2,1)S(1)} %own_slice.3.refs_2_.refs_0_), channel_id=1, source_target_pairs={{0,6},{1,7},{2,4},{3,5},{4,2},{5,3},{6,0},{7,1},{8,14},{9,15},{10,... | collective-permute-start | bytes 786440 | tf_op jit(solution)/shard_map/ppermute | solution.py:531
  38.0 14.8 %collective-permute-start.20 = (bf16[2,512,256]{2,1,0:T(8,128)(2,1)S(1)}, bf16[2,512,256]{2,1,0:T(8,128)(2,1)S(1)}, u32[]{:S(2)}, u32[]{:S(2)}) collective-permute-start(bf16[2,512,256]{2,1,0:T(8,128)(2,1)S(1)} %get-tuple-element.39.refs_0_), channel_id=1, source_target_pairs={{0,16},{16,0},{1,17},{17,1},{2,18},{18,2},{3,19},{19,3},{4,20},{20... | collective-permute-start | bytes 1572872 | tf_op jit(solution)/shard_map/ppermute | solution.py:535
  45.9 1.5 %collective-permute-start.14 = (bf16[256,512]{1,0:T(8,128)(2,1)S(1)}, bf16[256,512]{1,0:T(8,128)(2,1)S(1)}, u32[]{:S(2)}, u32[]{:S(2)}) collective-permute-start(bf16[256,512]{1,0:T(8,128)(2,1)S(1)} %get-tuple-element.35.refs_0_), channel_id=1, source_target_pairs={{0,1},{1,0},{2,3},{3,2},{4,5},{5,4},{6,7},{7,6},{8,9},{9,8},{10,11... | collective-permute-start | bytes 786440 | tf_op jit(solution)/shard_map/ppermute | solution.py:531
  45.9 4.4 %collective-permute-start.15 = (bf16[256,512]{1,0:T(8,128)(2,1)S(1)}, bf16[256,512]{1,0:T(8,128)(2,1)S(1)}, u32[]{:S(2)}, u32[]{:S(2)}) collective-permute-start(bf16[256,512]{1,0:T(8,128)(2,1)S(1)} %get-tuple-element.36.refs_1_), channel_id=1, source_target_pairs={{0,1},{1,0},{2,3},{3,2},{4,5},{5,4},{6,7},{7,6},{8,9},{9,8},{10,11... | collective-permute-start | bytes 786440 | tf_op jit(solution)/shard_map/ppermute | solution.py:531
  46.4 3.9 %collective-permute-start.16 = (bf16[256,512]{1,0:T(8,128)(2,1)S(1)}, bf16[256,512]{1,0:T(8,128)(2,1)S(1)}, u32[]{:S(2)}, u32[]{:S(2)}) collective-permute-start(bf16[256,512]{1,0:T(8,128)(2,1)S(1)} %get-tuple-element.37.refs_2_), channel_id=1, source_target_pairs={{0,1},{1,0},{2,3},{3,2},{4,5},{5,4},{6,7},{7,6},{8,9},{9,8},{10,11... | collective-permute-start | bytes 786440 | tf_op jit(solution)/shard_map/ppermute | solution.py:531
  46.4 3.9 %collective-permute-start.17 = (bf16[256,512]{1,0:T(8,128)(2,1)S(1)}, bf16[256,512]{1,0:T(8,128)(2,1)S(1)}, u32[]{:S(2)}, u32[]{:S(2)}) collective-permute-start(bf16[256,512]{1,0:T(8,128)(2,1)S(1)} %get-tuple-element.38.refs_3_), channel_id=1, source_target_pairs={{0,1},{1,0},{2,3},{3,2},{4,5},{5,4},{6,7},{7,6},{8,9},{9,8},{10,11... | collective-permute-start | bytes 786440 | tf_op jit(solution)/shard_map/ppermute | solution.py:531
  47.4 10.0 %collective-permute-start.19 = (bf16[512,256]{1,0:T(8,128)(2,1)S(1)}, bf16[512,256]{1,0:T(8,128)(2,1)S(1)}, u32[]{:S(2)}, u32[]{:S(2)}) collective-permute-start(bf16[512,256]{1,0:T(8,128)(2,1)S(1)} %proj_queries.1.refs_4_.refs_2_), channel_id=1, source_target_pairs={{0,16},{16,0},{1,17},{17,1},{2,18},{18,2},{3,19},{19,3},{4,20},{20... | collective-permute-start | bytes 786440 | tf_op jit(solution)/shard_map/ppermute | solution.py:535
  51.6 10.9 %collective-permute-start.18 = (bf16[512,256]{1,0:T(8,128)(2,1)S(1)}, bf16[512,256]{1,0:T(8,128)(2,1)S(1)}, u32[]{:S(2)}, u32[]{:S(2)}) collective-permute-start(bf16[512,256]{1,0:T(8,128)(2,1)S(1)} %grad_z_partial.1.refs_0_), channel_id=1, source_target_pairs={{0,16},{16,0},{1,17},{17,1},{2,18},{18,2},{3,19},{19,3},{4,20},{20... | collective-permute-start | bytes 786440 | tf_op jit(solution)/shard_map/ppermute | solution.py:535
  64.4 3.0 %collective-permute-start.21 = (bf16[3,512,256]{2,1,0:T(8,128)(2,1)S(1)}, bf16[3,512,256]{2,1,0:T(8,128)(2,1)S(1)}, u32[]{:S(2)}, u32[]{:S(2)}) collective-permute-start(bf16[3,512,256]{2,1,0:T(8,128)(2,1)S(1)} %input_partial.4), channel_id=1, source_target_pairs={{0,1},{1,0},{2,3},{3,2},{4,5},{5,4},{6,7},{7,6},{8,9},{9,8},{10,11... | collective-permute-start | bytes 2359304 | tf_op jit(solution)/shard_map/ppermute | solution.py:531
  65.0 2.4 %collective-permute-start.22 = (bf16[1,512,256]{2,1,0:T(8,128)(2,1)S(1)}, bf16[1,512,256]{2,1,0:T(8,128)(2,1)S(1)}, u32[]{:S(2)}, u32[]{:S(2)}) collective-permute-start(bf16[1,512,256]{2,1,0:T(8,128)(2,1)S(1)} %input_partial.5), channel_id=1, source_target_pairs={{0,1},{1,0},{2,3},{3,2},{4,5},{5,4},{6,7},{7,6},{8,9},{9,8},{10,11... | collective-permute-start | bytes 786440 | tf_op jit(solution)/shard_map/ppermute | solution.py:531
  67.7 6.1 %collective-permute-start.26 = (bf16[512,128]{1,0:T(8,128)(2,1)S(1)}, bf16[512,128]{1,0:T(8,128)(2,1)S(1)}, u32[]{:S(2)}, u32[]{:S(2)}) collective-permute-start(bf16[512,128]{1,0:T(8,128)(2,1)S(1)} %get-tuple-element.49), channel_id=1, source_target_pairs={{0,4},{1,5},{2,6},{3,7},{4,0},{5,1},{6,2},{7,3},{8,12},{9,13},{10,... | collective-permute-start | bytes 393224 | tf_op jit(solution)/shard_map/ppermute | solution.py:531
  69.0 9.0 %collective-permute-start.27 = (bf16[512,128]{1,0:T(8,128)(2,1)S(1)}, bf16[512,128]{1,0:T(8,128)(2,1)S(1)}, u32[]{:S(2)}, u32[]{:S(2)}) collective-permute-start(bf16[512,128]{1,0:T(8,128)(2,1)S(1)} %get-tuple-element.50), channel_id=1, source_target_pairs={{0,2},{1,3},{2,0},{3,1},{4,6},{5,7},{6,4},{7,5},{8,10},{9,11},{10,... | collective-permute-start | bytes 393224 | tf_op jit(solution)/shard_map/ppermute | solution.py:531
  69.5 8.5 %collective-permute-start.28 = (bf16[512,128]{1,0:T(8,128)(2,1)S(1)}, bf16[512,128]{1,0:T(8,128)(2,1)S(1)}, u32[]{:S(2)}, u32[]{:S(2)}) collective-permute-start(bf16[512,128]{1,0:T(8,128)(2,1)S(1)} %get-tuple-element.51), channel_id=1, source_target_pairs={{0,6},{1,7},{2,4},{3,5},{4,2},{5,3},{6,0},{7,1},{8,14},{9,15},{10,... | collective-permute-start | bytes 393224 | tf_op jit(solution)/shard_map/ppermute | solution.py:531
  71.2 8.7 %collective-permute-start.23 = (bf16[512,128]{1,0:T(8,128)(2,1)S(1)}, bf16[512,128]{1,0:T(8,128)(2,1)S(1)}, u32[]{:S(2)}, u32[]{:S(2)}) collective-permute-start(bf16[512,128]{1,0:T(8,128)(2,1)S(1)} %get-tuple-element.45), channel_id=1, source_target_pairs={{0,4},{1,5},{2,6},{3,7},{4,0},{5,1},{6,2},{7,3},{8,12},{9,13},{10,... | collective-permute-start | bytes 393224 | tf_op jit(solution)/shard_map/ppermute | solution.py:531
  72.5 10.1 %collective-permute-start.24 = (bf16[512,128]{1,0:T(8,128)(2,1)S(1)}, bf16[512,128]{1,0:T(8,128)(2,1)S(1)}, u32[]{:S(2)}, u32[]{:S(2)}) collective-permute-start(bf16[512,128]{1,0:T(8,128)(2,1)S(1)} %get-tuple-element.46), channel_id=1, source_target_pairs={{0,2},{1,3},{2,0},{3,1},{4,6},{5,7},{6,4},{7,5},{8,10},{9,11},{10,... | collective-permute-start | bytes 393224 | tf_op jit(solution)/shard_map/ppermute | solution.py:531
  73.7 8.9 %collective-permute-start.25 = (bf16[512,128]{1,0:T(8,128)(2,1)S(1)}, bf16[512,128]{1,0:T(8,128)(2,1)S(1)}, u32[]{:S(2)}, u32[]{:S(2)}) collective-permute-start(bf16[512,128]{1,0:T(8,128)(2,1)S(1)} %get-tuple-element.47), channel_id=1, source_target_pairs={{0,6},{1,7},{2,4},{3,5},{4,2},{5,3},{6,0},{7,1},{8,14},{9,15},{10,... | collective-permute-start | bytes 393224 | tf_op jit(solution)/shard_map/ppermute | solution.py:531
  78.1 5.0 %collective-permute-start.29 = (bf16[512,128]{1,0:T(8,128)(2,1)S(1)}, bf16[512,128]{1,0:T(8,128)(2,1)S(1)}, u32[]{:S(2)}, u32[]{:S(2)}) collective-permute-start(bf16[512,128]{1,0:T(8,128)(2,1)S(1)} %total.1), channel_id=1, source_target_pairs={{0,16},{16,0},{1,17},{17,1},{2,18},{18,2},{3,19},{19,3},{4,20},{20... | collective-permute-start | bytes 393224 | tf_op jit(solution)/shard_map/ppermute | solution.py:535
  83.2 8.6 %collective-permute-start.30 = (bf16[512,128]{1,0:T(8,128)(2,1)S(1)}, bf16[512,128]{1,0:T(8,128)(2,1)S(1)}, u32[]{:S(2)}, u32[]{:S(2)}) collective-permute-start(bf16[512,128]{1,0:T(8,128)(2,1)S(1)} %get-tuple-element.53), channel_id=1, source_target_pairs={{0,8},{1,9},{2,10},{3,11},{4,12},{5,13},{6,14},{7,15},{8,0},{9,1},... | collective-permute-start | bytes 393224 | tf_op jit(solution)/shard_map/ppermute | solution.py:531
  (1 other events, 9.4 us)

commit v8 on v7

--- a/solution.py
+++ b/solution.py
@@ -223,7 +223,7 @@
     run = held_ref.shape[0] // runs
     total = jnp.dot(held_ref[...], w_ref[...], preferred_element_type=F32)
     for h, start in enumerate(run_starts(runs, run)):
-        out_ref[:, pl.ds(start, run)] = total[h * run : (h + 1) * run].T.astype(BF16)
+        out_ref[:, pl.ds(start, run)] = total[h * run : (h + 1) * run].astype(BF16).T
 
 
 def pair_kernel(masks, runs, *refs):
@@ -647,7 +647,7 @@
 
 def last_kernel(keep_ref, got_ref, out_ref):
     total = keep_ref[...].astype(F32) + got_ref[...].astype(F32)
-    out_ref[...] = total.T.astype(BF16)
+    out_ref[...] = total.astype(BF16).T
 
 
 def last_sum(keep, got):

time: 92.8 us -> 92.8 us (level)
  no operation moved by 1% of the time
where the time goes in v8:
time: 92.8 us; the launch traced here: 92.6 us
  starting transfers between devices  38.5 us (41%)
  waiting for transfers between devices  28.7 us (31%)
  Pallas kernels  24.5 us (26%)
    ppermute x23, starting transfers between devices, across(): return lax.ppermute(array, 'tensor', [(i, i ^ mask) for i in range(16)])  20.3 us
    ppermute x23, waiting for transfers between devices, across(): return lax.ppermute(array, 'tensor', [(i, i ^ mask) for i in range(16)])  18.8 us
    ppermute x4, starting transfers between devices, in_square(): return lax.ppermute(array, ('fsdp', 'tensor'), pairs)  11.1 us
    ppermute x4, waiting for transfers between devices, other_row(): return lax.ppermute(array, 'fsdp', [(0, 1), (1, 0)])  9.88 us
    ppermute x4, starting transfers between devices, other_row(): return lax.ppermute(array, 'fsdp', [(0, 1), (1, 0)])  7.13 us
    pallas_call x1, Pallas kernels, prepared(): pl.pallas_call(prepare_kernel, in_specs=[LATER_SPEC] * (2 + len(earlier))...  5.89 us
    pallas_call x3, Pallas kernels, input_partial(): pl.pallas_call(functools.partial(input_kernel, masks), in_specs=[VMEM_SPE...  3.74 us
    pallas_call x1, Pallas kernels, taps_gradient(): pl.pallas_call(functools.partial(taps_kernel, groups // steps), grid=(ste...  3.22 us
  transfers between devices with their start and end apart: 31, of which 11 were waited for; matrix products, arithmetic and copies ran while one was open for 0% of the time, Pallas kernels for 22%

profile of v8, /device:TPU:0, one launch (start us, length us, event | category | flops | bytes accessed | tf_op | source)
XLA Modules:
  0.0 92.6 jit_solution(7538618729017573751)
XLA Ops:
  0.6 4.1 %collective-permute-start = (bf16[128,512]{1,0:T(8,128)(2,1)}, bf16[128,512]{1,0:T(8,128)(2,1)S(1)}, u32[]{:S(2)}, u32[]{:S(2)}) collective-permute-start(bf16[128,512]{1,0:T(8,128)(2,1)} %array_ref.1), channel_id=1, source_target_pairs={{0,8},{1,9},{2,10},{3,11},{4,12},{5,13},{6,14},{7,15},{8,24},{9,25... | collective-permute-start | bytes 393224 | tf_op jit(solution)/shard_map/ppermute | solution.py:545
  5.4 5.9 %prepare.1 = (bf16[4096,512]{1,0:T(8,128)(2,1)S(1)}, bf16[4096,512]{1,0:T(8,128)(2,1)S(1)}, bf16[4096,512]{1,0:T(8,128)(2,1)S(1)}, f32[8,128]{1,0:T(8,128)S(1)}) custom-call(bf16[3,4096,512]{2,1,0:T(8,128)(2,1)} %bitcast.6, bf16[3,32,512]{2,1,0:T(8,128)(2,1)} %bitcast.7), custom_call_target="tpu_custom_call" | custom-call | flops 6144 | bytes 6144 | tf_op jit(solution)/shard_map/prepare/pallas_call | solution.py:154
  11.3 0.9 %own_slice.2.refs_0_ = bf16[256,512]{1,0:T(8,128)(2,1)S(1)} custom-call(bf16[128,512]{1,0:T(8,128)(2,1)} %array_ref.1, bf16[128,512]{1,0:T(8,128)(2,1)S(1)} %collective-permute-done.turned_ref, bf16[128,512]{1,0:T(8,128)(2,1)S(1)} %collective-permute-done.1.crossed_ref, f32[8,128]{1,0:T(8,128)S(1)} %get-tuple-element.32.refs_0_), custom_call_target="tpu_custom_call" | custom-call | bytes 160 | tf_op jit(solution)/shard_map/own_slice/pallas_call | solution.py:73
  12.3 2.6 %collective-permute-start.9 = (bf16[256,512]{1,0:T(8,128)(2,1)S(1)}, bf16[256,512]{1,0:T(8,128)(2,1)S(1)}, u32[]{:S(2)}, u32[]{:S(2)}) collective-permute-start(bf16[256,512]{1,0:T(8,128)(2,1)S(1)} %own_slice.2.refs_0_), channel_id=1, source_target_pairs={{0,6},{1,7},{2,4},{3,5},{4,2},{5,3},{6,0},{7,1},{8,14},{9,15},{10,... | collective-permute-start | bytes 786440 | tf_op jit(solution)/shard_map/ppermute | solution.py:531
  14.8 5.7 %collective-permute-start.2 = (bf16[128,512]{1,0:T(8,128)(2,1)S(1)}, bf16[128,512]{1,0:T(8,128)(2,1)S(1)}, u32[]{:S(2)}, u32[]{:S(2)}) collective-permute-start(bf16[128,512]{1,0:T(8,128)(2,1)S(1)} %copied.1.array_ref), channel_id=1, source_target_pairs={{0,8},{1,9},{2,10},{3,11},{4,12},{5,13},{6,14},{7,15},{8,24},{9,25... | collective-permute-start | bytes 393224 | tf_op jit(solution)/shard_map/ppermute | solution.py:545
  21.9 1.0 %toeplitz.1 = (bf16[32,256,128]{2,1,0:T(8,128)(2,1)S(1)}, bf16[32,256,128]{2,1,0:T(8,128)(2,1)S(1)}) custom-call(f32[32,128]{1,0:T(8,128)S(1)} %copy-done.1, bf16[256,512]{1,0:T(8,128)(2,1)S(1)} %own_slice.2.refs_0_), custom_call_target="tpu_custom_call" | custom-call | flops 2000 | bytes 1024 | tf_op jit(solution)/shard_map/toeplitz/pallas_call | solution.py:325
  22.9 2.2 %loaded.1.refs_1_.refs_8_ = bf16[512,4096]{1,0:T(8,128)(2,1)S(1)} custom-call(bf16[512,4096]{1,0:T(8,128)(2,1)} %in_ref.3, bf16[32,256,128]{2,1,0:T(8,128)(2,1)S(1)} %get-tuple-element.33.refs_0_.refs_2_), custom_call_target="tpu_custom_call" | custom-call | bytes 2048 | tf_op jit(solution)/shard_map/loaded/pallas_call | solution.py:205
  26.0 5.4 %collective-permute-done.7.refs_1_ = bf16[256,512]{1,0:T(8,128)(2,1)S(1)} collective-permute-done((bf16[256,512]{1,0:T(8,128)(2,1)S(1)}, bf16[256,512]{1,0:T(8,128)(2,1)S(1)}, u32[]{:S(2)}, u32[]{:S(2)}) %collective-permute-start.7) | collective-permute-done | bytes 262176 | tf_op jit(solution)/shard_map/ppermute | solution.py:531
  32.4 3.0 %collective-permute-start.6 = (bf16[256,512]{1,0:T(8,128)(2,1)S(1)}, bf16[256,512]{1,0:T(8,128)(2,1)S(1)}, u32[]{:S(2)}, u32[]{:S(2)}) collective-permute-start(bf16[256,512]{1,0:T(8,128)(2,1)S(1)} %own_slice.3.refs_2_.refs_0_), channel_id=1, source_target_pairs={{0,6},{1,7},{2,4},{3,5},{4,2},{5,3},{6,0},{7,1},{8,14},{9,15},{10,... | collective-permute-start | bytes 786440 | tf_op jit(solution)/shard_map/ppermute | solution.py:531
  35.4 2.6 %proj_pair.1 = (bf16[2,512,256]{2,1,0:T(8,128)(2,1)S(1)}, bf16[256,4096]{1,0:T(8,128)(2,1)S(1)}) custom-call(bf16[256,512]{1,0:T(8,128)(2,1)S(1)} %own_slice.2.refs_0_, bf16[256,512]{1,0:T(8,128)(2,1)S(1)} %collective-permute-done.7.refs_1_, bf16[256,512]{1,0:T(8,128)(2,1)S(1)} %collective-permute-done.8.refs_2_, bf16[256,512]{1,0:T(8,128)(2,1)S(1)} %relayed.2.refs_3_, ...), custom_call_target="tpu_custom_call" | custom-call | flops 524288 | bytes 2048 | tf_op jit(solution)/shard_map/proj_pair/pallas_call | solution.py:245
  38.0 1.3 %collective-permute-start.20 = (bf16[2,512,256]{2,1,0:T(8,128)(2,1)S(1)}, bf16[2,512,256]{2,1,0:T(8,128)(2,1)S(1)}, u32[]{:S(2)}, u32[]{:S(2)}) collective-permute-start(bf16[2,512,256]{2,1,0:T(8,128)(2,1)S(1)} %get-tuple-element.39.refs_0_), channel_id=1, source_target_pairs={{0,16},{16,0},{1,17},{17,1},{2,18},{18,2},{3,19},{19,3},{4,20},{20... | collective-permute-start | bytes 1572872 | tf_op jit(solution)/shard_map/ppermute | solution.py:535
  39.3 1.3 %proj_queries.1.refs_4_.refs_2_ = bf16[512,256]{1,0:T(8,128)(2,1)S(1)} custom-call(bf16[256,4096]{1,0:T(8,128)(2,1)S(1)} %get-tuple-element.34.held_ref, bf16[4096,512]{1,0:T(8,128)(2,1)S(1)} %get-tuple-element.29.w_ref.refs_0_), custom_call_target="tpu_custom_call" | custom-call | flops 262144 | bytes 1024 | tf_op jit(solution)/shard_map/proj_queries/pallas_call | solution.py:257
  41.1 4.7 %collective-permute-done.5.refs_2_ = bf16[256,512]{1,0:T(8,128)(2,1)S(1)} collective-permute-done((bf16[256,512]{1,0:T(8,128)(2,1)S(1)}, bf16[256,512]{1,0:T(8,128)(2,1)S(1)}, u32[]{:S(2)}, u32[]{:S(2)}) %collective-permute-start.5) | collective-permute-done | bytes 262176 | tf_op jit(solution)/shard_map/ppermute | solution.py:531
  47.4 2.9 %collective-permute-start.19 = (bf16[512,256]{1,0:T(8,128)(2,1)S(1)}, bf16[512,256]{1,0:T(8,128)(2,1)S(1)}, u32[]{:S(2)}, u32[]{:S(2)}) collective-permute-start(bf16[512,256]{1,0:T(8,128)(2,1)S(1)} %proj_queries.1.refs_4_.refs_2_), channel_id=1, source_target_pairs={{0,16},{16,0},{1,17},{17,1},{2,18},{18,2},{3,19},{19,3},{4,20},{20... | collective-permute-start | bytes 786440 | tf_op jit(solution)/shard_map/ppermute | solution.py:535
  50.3 1.3 %grad_z_partial.1.refs_0_ = bf16[512,256]{1,0:T(8,128)(2,1)S(1)} custom-call(bf16[256,512]{1,0:T(8,128)(2,1)S(1)} %get-tuple-element.35.refs_0_, bf16[256,512]{1,0:T(8,128)(2,1)S(1)} %get-tuple-element.36.refs_1_, bf16[256,512]{1,0:T(8,128)(2,1)S(1)} %get-tuple-element.37.refs_2_, bf16[256,512]{1,0:T(8,128)(2,1)S(1)} %get-tuple-element.38.refs_3_, ...), custom_call_target="tpu_custom_call" | custom-call | flops 262144 | bytes 1024 | tf_op jit(solution)/shard_map/grad_z_partial/pallas_call | solution.py:288
  51.6 1.2 %collective-permute-start.18 = (bf16[512,256]{1,0:T(8,128)(2,1)S(1)}, bf16[512,256]{1,0:T(8,128)(2,1)S(1)}, u32[]{:S(2)}, u32[]{:S(2)}) collective-permute-start(bf16[512,256]{1,0:T(8,128)(2,1)S(1)} %grad_z_partial.1.refs_0_), channel_id=1, source_target_pairs={{0,16},{16,0},{1,17},{17,1},{2,18},{18,2},{3,19},{19,3},{4,20},{20... | collective-permute-start | bytes 786440 | tf_op jit(solution)/shard_map/ppermute | solution.py:535
  53.2 4.2 %collective-permute-done.19.refs_3_ = bf16[512,256]{1,0:T(8,128)(2,1)S(1)} collective-permute-done((bf16[512,256]{1,0:T(8,128)(2,1)S(1)}, bf16[512,256]{1,0:T(8,128)(2,1)S(1)}, u32[]{:S(2)}, u32[]{:S(2)}) %collective-permute-start.19) | collective-permute-done | bytes 262176 | tf_op jit(solution)/shard_map/ppermute | solution.py:535
  57.4 5.1 %collective-permute-done.18.refs_1_ = bf16[512,256]{1,0:T(8,128)(2,1)S(1)} collective-permute-done((bf16[512,256]{1,0:T(8,128)(2,1)S(1)}, bf16[512,256]{1,0:T(8,128)(2,1)S(1)}, u32[]{:S(2)}, u32[]{:S(2)}) %collective-permute-start.18) | collective-permute-done | bytes 262176 | tf_op jit(solution)/shard_map/ppermute | solution.py:535
  63.0 1.4 %input_partial.4 = bf16[3,512,256]{2,1,0:T(8,128)(2,1)S(1)} custom-call(bf16[4096,512]{1,0:T(8,128)(2,1)S(1)} %get-tuple-element.29.w_ref.refs_0_, bf16[4096,512]{1,0:T(8,128)(2,1)S(1)} %get-tuple-element.30.refs_8_.refs_1_, bf16[4096,512]{1,0:T(8,128)(2,1)S(1)} %get-tuple-element.31.refs_9_.refs_2_, bf16[1536,256]{1,0:T(8,128)(2,1)S(1)} %bitcast.3), custom_call_target="tpu_custom_call" | custom-call | flops 294912 | bytes 1344 | tf_op jit(solution)/shard_map/input_partial/pallas_call | solution.py:517
  65.6 1.8 %input_partial.3.same_ref = bf16[4,512,256]{2,1,0:T(8,128)(2,1)S(1)} custom-call(bf16[4096,512]{1,0:T(8,128)(2,1)S(1)} %get-tuple-element.29.w_ref.refs_0_, bf16[4096,512]{1,0:T(8,128)(2,1)S(1)} %get-tuple-element.30.refs_8_.refs_1_, bf16[4096,512]{1,0:T(8,128)(2,1)S(1)} %get-tuple-element.31.refs_9_.refs_2_, bf16[1536,256]{1,0:T(8,128)(2,1)S(1)} %bitcast.5), custom_call_target="tpu_custom_call" | custom-call | flops 393216 | bytes 1792 | tf_op jit(solution)/shard_map/input_partial/pallas_call | solution.py:517
  67.7 1.4 %collective-permute-start.26 = (bf16[512,128]{1,0:T(8,128)(2,1)S(1)}, bf16[512,128]{1,0:T(8,128)(2,1)S(1)}, u32[]{:S(2)}, u32[]{:S(2)}) collective-permute-start(bf16[512,128]{1,0:T(8,128)(2,1)S(1)} %get-tuple-element.49), channel_id=1, source_target_pairs={{0,4},{1,5},{2,6},{3,7},{4,0},{5,1},{6,2},{7,3},{8,12},{9,13},{10,... | collective-permute-start | bytes 393224 | tf_op jit(solution)/shard_map/ppermute | solution.py:531
  69.5 1.7 %collective-permute-start.28 = (bf16[512,128]{1,0:T(8,128)(2,1)S(1)}, bf16[512,128]{1,0:T(8,128)(2,1)S(1)}, u32[]{:S(2)}, u32[]{:S(2)}) collective-permute-start(bf16[512,128]{1,0:T(8,128)(2,1)S(1)} %get-tuple-element.51), channel_id=1, source_target_pairs={{0,6},{1,7},{2,4},{3,5},{4,2},{5,3},{6,0},{7,1},{8,14},{9,15},{10,... | collective-permute-start | bytes 393224 | tf_op jit(solution)/shard_map/ppermute | solution.py:531
  71.2 1.3 %collective-permute-start.23 = (bf16[512,128]{1,0:T(8,128)(2,1)S(1)}, bf16[512,128]{1,0:T(8,128)(2,1)S(1)}, u32[]{:S(2)}, u32[]{:S(2)}) collective-permute-start(bf16[512,128]{1,0:T(8,128)(2,1)S(1)} %get-tuple-element.45), channel_id=1, source_target_pairs={{0,4},{1,5},{2,6},{3,7},{4,0},{5,1},{6,2},{7,3},{8,12},{9,13},{10,... | collective-permute-start | bytes 393224 | tf_op jit(solution)/shard_map/ppermute | solution.py:531
  73.0 0.7 collective-permute-done.26.refs_1_
  73.7 1.6 %collective-permute-start.25 = (bf16[512,128]{1,0:T(8,128)(2,1)S(1)}, bf16[512,128]{1,0:T(8,128)(2,1)S(1)}, u32[]{:S(2)}, u32[]{:S(2)}) collective-permute-start(bf16[512,128]{1,0:T(8,128)(2,1)S(1)} %get-tuple-element.47), channel_id=1, source_target_pairs={{0,6},{1,7},{2,4},{3,5},{4,2},{5,3},{6,0},{7,1},{8,14},{9,15},{10,... | collective-permute-start | bytes 393224 | tf_op jit(solution)/shard_map/ppermute | solution.py:531
  75.3 2.8 %collective-permute-done.27.refs_2_ = bf16[512,128]{1,0:T(8,128)(2,1)S(1)} collective-permute-done((bf16[512,128]{1,0:T(8,128)(2,1)S(1)}, bf16[512,128]{1,0:T(8,128)(2,1)S(1)}, u32[]{:S(2)}, u32[]{:S(2)}) %collective-permute-start.27) | collective-permute-done | bytes 131104 | tf_op jit(solution)/shard_map/ppermute | solution.py:531
  78.2 1.8 %collective-permute-start.29 = (bf16[512,128]{1,0:T(8,128)(2,1)S(1)}, bf16[512,128]{1,0:T(8,128)(2,1)S(1)}, u32[]{:S(2)}, u32[]{:S(2)}) collective-permute-start(bf16[512,128]{1,0:T(8,128)(2,1)S(1)} %total.1), channel_id=1, source_target_pairs={{0,16},{16,0},{1,17},{17,1},{2,18},{18,2},{3,19},{19,3},{4,20},{20... | collective-permute-start | bytes 393224 | tf_op jit(solution)/shard_map/ppermute | solution.py:535
  79.9 2.7 %collective-permute-done.24.refs_2_ = bf16[512,128]{1,0:T(8,128)(2,1)S(1)} collective-permute-done((bf16[512,128]{1,0:T(8,128)(2,1)S(1)}, bf16[512,128]{1,0:T(8,128)(2,1)S(1)}, u32[]{:S(2)}, u32[]{:S(2)}) %collective-permute-start.24) | collective-permute-done | bytes 131104 | tf_op jit(solution)/shard_map/ppermute | solution.py:531
  83.3 3.8 %collective-permute-start.30 = (bf16[512,128]{1,0:T(8,128)(2,1)S(1)}, bf16[512,128]{1,0:T(8,128)(2,1)S(1)}, u32[]{:S(2)}, u32[]{:S(2)}) collective-permute-start(bf16[512,128]{1,0:T(8,128)(2,1)S(1)} %get-tuple-element.53), channel_id=1, source_target_pairs={{0,8},{1,9},{2,10},{3,11},{4,12},{5,13},{6,14},{7,15},{8,0},{9,1},... | collective-permute-start | bytes 393224 | tf_op jit(solution)/shard_map/ppermute | solution.py:531
  87.1 3.2 %taps_gradient.1 = f32[32,128]{1,0:T(8,128)} custom-call(bf16[512,256]{1,0:T(8,128)(2,1)S(1)} %get-tuple-element.54.prod_ref, bf16[512,256]{1,0:T(8,128)(2,1)S(1)} %get-tuple-element.55.grad_ref), custom_call_target="tpu_custom_call" | custom-call | flops 131072 | bytes 768 | tf_op jit(solution)/shard_map/taps_gradient/pallas_call | solution.py:494
  90.3 1.5 %collective-permute-done.30.got_ref = bf16[512,128]{1,0:T(8,128)(2,1)S(1)} collective-permute-done((bf16[512,128]{1,0:T(8,128)(2,1)S(1)}, bf16[512,128]{1,0:T(8,128)(2,1)S(1)}, u32[]{:S(2)}, u32[]{:S(2)}) %collective-permute-start.30) | collective-permute-done | bytes 131104 | tf_op jit(solution)/shard_map/ppermute | solution.py:531
  91.8 0.7 last_sum.1
  (55 shorter events, 10.0 us)
Async XLA Ops:
  0.6 10.7 %collective-permute-start = (bf16[128,512]{1,0:T(8,128)(2,1)}, bf16[128,512]{1,0:T(8,128)(2,1)S(1)}, u32[]{:S(2)}, u32[]{:S(2)}) collective-permute-start(bf16[128,512]{1,0:T(8,128)(2,1)} %array_ref.1), channel_id=1, source_target_pairs={{0,8},{1,9},{2,10},{3,11},{4,12},{5,13},{6,14},{7,15},{8,24},{9,25... | collective-permute-start | bytes 393224 | tf_op jit(solution)/shard_map/ppermute | solution.py:545
  4.7 6.6 %collective-permute-start.1 = (bf16[128,512]{1,0:T(8,128)(2,1)}, bf16[128,512]{1,0:T(8,128)(2,1)S(1)}, u32[]{:S(2)}, u32[]{:S(2)}) collective-permute-start(bf16[128,512]{1,0:T(8,128)(2,1)} %array_ref.1), channel_id=1, source_target_pairs={{8,16},{9,17},{10,18},{11,19},{12,20},{13,21},{14,22},{15,23},{16,... | collective-permute-start | bytes 393224 | tf_op jit(solution)/shard_map/ppermute | solution.py:545
  5.4 16.5 %copy-start.1 = (f32[32,128]{1,0:T(8,128)S(1)}, f32[32,128]{1,0:T(8,128)}, u32[]{:S(2)}) copy-start(f32[32,128]{1,0:T(8,128)} %taps_ref.1) | copy-start | bytes 49156
  12.3 13.2 %collective-permute-start.9 = (bf16[256,512]{1,0:T(8,128)(2,1)S(1)}, bf16[256,512]{1,0:T(8,128)(2,1)S(1)}, u32[]{:S(2)}, u32[]{:S(2)}) collective-permute-start(bf16[256,512]{1,0:T(8,128)(2,1)S(1)} %own_slice.2.refs_0_), channel_id=1, source_target_pairs={{0,6},{1,7},{2,4},{3,5},{4,2},{5,3},{6,0},{7,1},{8,14},{9,15},{10,... | collective-permute-start | bytes 786440 | tf_op jit(solution)/shard_map/ppermute | solution.py:531
  14.8 10.3 %collective-permute-start.2 = (bf16[128,512]{1,0:T(8,128)(2,1)S(1)}, bf16[128,512]{1,0:T(8,128)(2,1)S(1)}, u32[]{:S(2)}, u32[]{:S(2)}) collective-permute-start(bf16[128,512]{1,0:T(8,128)(2,1)S(1)} %copied.1.array_ref), channel_id=1, source_target_pairs={{0,8},{1,9},{2,10},{3,11},{4,12},{5,13},{6,14},{7,15},{8,24},{9,25... | collective-permute-start | bytes 393224 | tf_op jit(solution)/shard_map/ppermute | solution.py:545
  20.6 4.7 %collective-permute-start.3 = (bf16[128,512]{1,0:T(8,128)(2,1)S(1)}, bf16[128,512]{1,0:T(8,128)(2,1)S(1)}, u32[]{:S(2)}, u32[]{:S(2)}) collective-permute-start(bf16[128,512]{1,0:T(8,128)(2,1)S(1)} %copied.1.array_ref), channel_id=1, source_target_pairs={{8,16},{9,17},{10,18},{11,19},{12,20},{13,21},{14,22},{15,23},{16,... | collective-permute-start | bytes 393224 | tf_op jit(solution)/shard_map/ppermute | solution.py:545
  21.2 10.2 %collective-permute-start.7 = (bf16[256,512]{1,0:T(8,128)(2,1)S(1)}, bf16[256,512]{1,0:T(8,128)(2,1)S(1)}, u32[]{:S(2)}, u32[]{:S(2)}) collective-permute-start(bf16[256,512]{1,0:T(8,128)(2,1)S(1)} %own_slice.2.refs_0_), channel_id=1, source_target_pairs={{0,4},{1,5},{2,6},{3,7},{4,0},{5,1},{6,2},{7,3},{8,12},{9,13},{10,... | collective-permute-start | bytes 786440 | tf_op jit(solution)/shard_map/ppermute | solution.py:531
  21.3 10.1 %collective-permute-start.8 = (bf16[256,512]{1,0:T(8,128)(2,1)S(1)}, bf16[256,512]{1,0:T(8,128)(2,1)S(1)}, u32[]{:S(2)}, u32[]{:S(2)}) collective-permute-start(bf16[256,512]{1,0:T(8,128)(2,1)S(1)} %own_slice.2.refs_0_), channel_id=1, source_target_pairs={{0,2},{1,3},{2,0},{3,1},{4,6},{5,7},{6,4},{7,5},{8,10},{9,11},{10,... | collective-permute-start | bytes 786440 | tf_op jit(solution)/shard_map/ppermute | solution.py:531
  25.2 6.8 %collective-permute-start.10 = (bf16[256,512]{1,0:T(8,128)(2,1)S(1)}, bf16[256,512]{1,0:T(8,128)(2,1)S(1)}, u32[]{:S(2)}, u32[]{:S(2)}) collective-permute-start(bf16[256,512]{1,0:T(8,128)(2,1)S(1)} %own_slice.2.refs_0_), channel_id=1, source_target_pairs={{0,1},{1,0},{2,3},{3,2},{4,5},{5,4},{6,7},{7,6},{8,9},{9,8},{10,11... | collective-permute-start | bytes 786440 | tf_op jit(solution)/shard_map/ppermute | solution.py:531
  25.5 7.0 %collective-permute-start.13 = (bf16[256,512]{1,0:T(8,128)(2,1)S(1)}, bf16[256,512]{1,0:T(8,128)(2,1)S(1)}, u32[]{:S(2)}, u32[]{:S(2)}) collective-permute-start(bf16[256,512]{1,0:T(8,128)(2,1)S(1)} %relayed.2.refs_3_), channel_id=1, source_target_pairs={{0,1},{1,0},{2,3},{3,2},{4,5},{5,4},{6,7},{7,6},{8,9},{9,8},{10,11... | collective-permute-start | bytes 786440 | tf_op jit(solution)/shard_map/ppermute | solution.py:531
  31.4 4.0 %collective-permute-start.11 = (bf16[256,512]{1,0:T(8,128)(2,1)S(1)}, bf16[256,512]{1,0:T(8,128)(2,1)S(1)}, u32[]{:S(2)}, u32[]{:S(2)}) collective-permute-start(bf16[256,512]{1,0:T(8,128)(2,1)S(1)} %collective-permute-done.7.refs_1_), channel_id=1, source_target_pairs={{0,1},{1,0},{2,3},{3,2},{4,5},{5,4},{6,7},{7,6},{8,9},{9,8},{10,11... | collective-permute-start | bytes 786440 | tf_op jit(solution)/shard_map/ppermute | solution.py:531
  31.4 4.0 %collective-permute-start.12 = (bf16[256,512]{1,0:T(8,128)(2,1)S(1)}, bf16[256,512]{1,0:T(8,128)(2,1)S(1)}, u32[]{:S(2)}, u32[]{:S(2)}) collective-permute-start(bf16[256,512]{1,0:T(8,128)(2,1)S(1)} %collective-permute-done.8.refs_2_), channel_id=1, source_target_pairs={{0,1},{1,0},{2,3},{3,2},{4,5},{5,4},{6,7},{7,6},{8,9},{9,8},{10,11... | collective-permute-start | bytes 786440 | tf_op jit(solution)/shard_map/ppermute | solution.py:531
  31.9 9.2 %collective-permute-start.4 = (bf16[256,512]{1,0:T(8,128)(2,1)S(1)}, bf16[256,512]{1,0:T(8,128)(2,1)S(1)}, u32[]{:S(2)}, u32[]{:S(2)}) collective-permute-start(bf16[256,512]{1,0:T(8,128)(2,1)S(1)} %own_slice.3.refs_2_.refs_0_), channel_id=1, source_target_pairs={{0,4},{1,5},{2,6},{3,7},{4,0},{5,1},{6,2},{7,3},{8,12},{9,13},{10,... | collective-permute-start | bytes 786440 | tf_op jit(solution)/shard_map/ppermute | solution.py:531
  32.0 13.9 %collective-permute-start.5 = (bf16[256,512]{1,0:T(8,128)(2,1)S(1)}, bf16[256,512]{1,0:T(8,128)(2,1)S(1)}, u32[]{:S(2)}, u32[]{:S(2)}) collective-permute-start(bf16[256,512]{1,0:T(8,128)(2,1)S(1)} %own_slice.3.refs_2_.refs_0_), channel_id=1, source_target_pairs={{0,2},{1,3},{2,0},{3,1},{4,6},{5,7},{6,4},{7,5},{8,10},{9,11},{10,... | collective-permute-start | bytes 786440 | tf_op jit(solution)/shard_map/ppermute | solution.py:531
  32.4 13.4 %collective-permute-start.6 = (bf16[256,512]{1,0:T(8,128)(2,1)S(1)}, bf16[256,512]{1,0:T(8,128)(2,1)S(1)}, u32[]{:S(2)}, u32[]{:S(2)}) collective-permute-start(bf16[256,512]{1,0:T(8,128)(2,1)S(1)} %own_slice.3.refs_2_.refs_0_), channel_id=1, source_target_pairs={{0,6},{1,7},{2,4},{3,5},{4,2},{5,3},{6,0},{7,1},{8,14},{9,15},{10,... | collective-permute-start | bytes 786440 | tf_op jit(solution)/shard_map/ppermute | solution.py:531
  38.0 14.8 %collective-permute-start.20 = (bf16[2,512,256]{2,1,0:T(8,128)(2,1)S(1)}, bf16[2,512,256]{2,1,0:T(8,128)(2,1)S(1)}, u32[]{:S(2)}, u32[]{:S(2)}) collective-permute-start(bf16[2,512,256]{2,1,0:T(8,128)(2,1)S(1)} %get-tuple-element.39.refs_0_), channel_id=1, source_target_pairs={{0,16},{16,0},{1,17},{17,1},{2,18},{18,2},{3,19},{19,3},{4,20},{20... | collective-permute-start | bytes 1572872 | tf_op jit(solution)/shard_map/ppermute | solution.py:535
  45.9 1.5 %collective-permute-start.14 = (bf16[256,512]{1,0:T(8,128)(2,1)S(1)}, bf16[256,512]{1,0:T(8,128)(2,1)S(1)}, u32[]{:S(2)}, u32[]{:S(2)}) collective-permute-start(bf16[256,512]{1,0:T(8,128)(2,1)S(1)} %get-tuple-element.35.refs_0_), channel_id=1, source_target_pairs={{0,1},{1,0},{2,3},{3,2},{4,5},{5,4},{6,7},{7,6},{8,9},{9,8},{10,11... | collective-permute-start | bytes 786440 | tf_op jit(solution)/shard_map/ppermute | solution.py:531
  45.9 4.4 %collective-permute-start.15 = (bf16[256,512]{1,0:T(8,128)(2,1)S(1)}, bf16[256,512]{1,0:T(8,128)(2,1)S(1)}, u32[]{:S(2)}, u32[]{:S(2)}) collective-permute-start(bf16[256,512]{1,0:T(8,128)(2,1)S(1)} %get-tuple-element.36.refs_1_), channel_id=1, source_target_pairs={{0,1},{1,0},{2,3},{3,2},{4,5},{5,4},{6,7},{7,6},{8,9},{9,8},{10,11... | collective-permute-start | bytes 786440 | tf_op jit(solution)/shard_map/ppermute | solution.py:531
  46.4 3.9 %collective-permute-start.16 = (bf16[256,512]{1,0:T(8,128)(2,1)S(1)}, bf16[256,512]{1,0:T(8,128)(2,1)S(1)}, u32[]{:S(2)}, u32[]{:S(2)}) collective-permute-start(bf16[256,512]{1,0:T(8,128)(2,1)S(1)} %get-tuple-element.37.refs_2_), channel_id=1, source_target_pairs={{0,1},{1,0},{2,3},{3,2},{4,5},{5,4},{6,7},{7,6},{8,9},{9,8},{10,11... | collective-permute-start | bytes 786440 | tf_op jit(solution)/shard_map/ppermute | solution.py:531
  46.4 3.9 %collective-permute-start.17 = (bf16[256,512]{1,0:T(8,128)(2,1)S(1)}, bf16[256,512]{1,0:T(8,128)(2,1)S(1)}, u32[]{:S(2)}, u32[]{:S(2)}) collective-permute-start(bf16[256,512]{1,0:T(8,128)(2,1)S(1)} %get-tuple-element.38.refs_3_), channel_id=1, source_target_pairs={{0,1},{1,0},{2,3},{3,2},{4,5},{5,4},{6,7},{7,6},{8,9},{9,8},{10,11... | collective-permute-start | bytes 786440 | tf_op jit(solution)/shard_map/ppermute | solution.py:531
  47.4 10.0 %collective-permute-start.19 = (bf16[512,256]{1,0:T(8,128)(2,1)S(1)}, bf16[512,256]{1,0:T(8,128)(2,1)S(1)}, u32[]{:S(2)}, u32[]{:S(2)}) collective-permute-start(bf16[512,256]{1,0:T(8,128)(2,1)S(1)} %proj_queries.1.refs_4_.refs_2_), channel_id=1, source_target_pairs={{0,16},{16,0},{1,17},{17,1},{2,18},{18,2},{3,19},{19,3},{4,20},{20... | collective-permute-start | bytes 786440 | tf_op jit(solution)/shard_map/ppermute | solution.py:535
  51.6 10.9 %collective-permute-start.18 = (bf16[512,256]{1,0:T(8,128)(2,1)S(1)}, bf16[512,256]{1,0:T(8,128)(2,1)S(1)}, u32[]{:S(2)}, u32[]{:S(2)}) collective-permute-start(bf16[512,256]{1,0:T(8,128)(2,1)S(1)} %grad_z_partial.1.refs_0_), channel_id=1, source_target_pairs={{0,16},{16,0},{1,17},{17,1},{2,18},{18,2},{3,19},{19,3},{4,20},{20... | collective-permute-start | bytes 786440 | tf_op jit(solution)/shard_map/ppermute | solution.py:535
  64.4 3.0 %collective-permute-start.21 = (bf16[3,512,256]{2,1,0:T(8,128)(2,1)S(1)}, bf16[3,512,256]{2,1,0:T(8,128)(2,1)S(1)}, u32[]{:S(2)}, u32[]{:S(2)}) collective-permute-start(bf16[3,512,256]{2,1,0:T(8,128)(2,1)S(1)} %input_partial.4), channel_id=1, source_target_pairs={{0,1},{1,0},{2,3},{3,2},{4,5},{5,4},{6,7},{7,6},{8,9},{9,8},{10,11... | collective-permute-start | bytes 2359304 | tf_op jit(solution)/shard_map/ppermute | solution.py:531
  65.0 2.4 %collective-permute-start.22 = (bf16[1,512,256]{2,1,0:T(8,128)(2,1)S(1)}, bf16[1,512,256]{2,1,0:T(8,128)(2,1)S(1)}, u32[]{:S(2)}, u32[]{:S(2)}) collective-permute-start(bf16[1,512,256]{2,1,0:T(8,128)(2,1)S(1)} %input_partial.5), channel_id=1, source_target_pairs={{0,1},{1,0},{2,3},{3,2},{4,5},{5,4},{6,7},{7,6},{8,9},{9,8},{10,11... | collective-permute-start | bytes 786440 | tf_op jit(solution)/shard_map/ppermute | solution.py:531
  67.7 6.0 %collective-permute-start.26 = (bf16[512,128]{1,0:T(8,128)(2,1)S(1)}, bf16[512,128]{1,0:T(8,128)(2,1)S(1)}, u32[]{:S(2)}, u32[]{:S(2)}) collective-permute-start(bf16[512,128]{1,0:T(8,128)(2,1)S(1)} %get-tuple-element.49), channel_id=1, source_target_pairs={{0,4},{1,5},{2,6},{3,7},{4,0},{5,1},{6,2},{7,3},{8,12},{9,13},{10,... | collective-permute-start | bytes 393224 | tf_op jit(solution)/shard_map/ppermute | solution.py:531
  69.0 9.0 %collective-permute-start.27 = (bf16[512,128]{1,0:T(8,128)(2,1)S(1)}, bf16[512,128]{1,0:T(8,128)(2,1)S(1)}, u32[]{:S(2)}, u32[]{:S(2)}) collective-permute-start(bf16[512,128]{1,0:T(8,128)(2,1)S(1)} %get-tuple-element.50), channel_id=1, source_target_pairs={{0,2},{1,3},{2,0},{3,1},{4,6},{5,7},{6,4},{7,5},{8,10},{9,11},{10,... | collective-permute-start | bytes 393224 | tf_op jit(solution)/shard_map/ppermute | solution.py:531
  69.5 8.5 %collective-permute-start.28 = (bf16[512,128]{1,0:T(8,128)(2,1)S(1)}, bf16[512,128]{1,0:T(8,128)(2,1)S(1)}, u32[]{:S(2)}, u32[]{:S(2)}) collective-permute-start(bf16[512,128]{1,0:T(8,128)(2,1)S(1)} %get-tuple-element.51), channel_id=1, source_target_pairs={{0,6},{1,7},{2,4},{3,5},{4,2},{5,3},{6,0},{7,1},{8,14},{9,15},{10,... | collective-permute-start | bytes 393224 | tf_op jit(solution)/shard_map/ppermute | solution.py:531
  71.2 8.7 %collective-permute-start.23 = (bf16[512,128]{1,0:T(8,128)(2,1)S(1)}, bf16[512,128]{1,0:T(8,128)(2,1)S(1)}, u32[]{:S(2)}, u32[]{:S(2)}) collective-permute-start(bf16[512,128]{1,0:T(8,128)(2,1)S(1)} %get-tuple-element.45), channel_id=1, source_target_pairs={{0,4},{1,5},{2,6},{3,7},{4,0},{5,1},{6,2},{7,3},{8,12},{9,13},{10,... | collective-permute-start | bytes 393224 | tf_op jit(solution)/shard_map/ppermute | solution.py:531
  72.5 10.1 %collective-permute-start.24 = (bf16[512,128]{1,0:T(8,128)(2,1)S(1)}, bf16[512,128]{1,0:T(8,128)(2,1)S(1)}, u32[]{:S(2)}, u32[]{:S(2)}) collective-permute-start(bf16[512,128]{1,0:T(8,128)(2,1)S(1)} %get-tuple-element.46), channel_id=1, source_target_pairs={{0,2},{1,3},{2,0},{3,1},{4,6},{5,7},{6,4},{7,5},{8,10},{9,11},{10,... | collective-permute-start | bytes 393224 | tf_op jit(solution)/shard_map/ppermute | solution.py:531
  73.7 8.9 %collective-permute-start.25 = (bf16[512,128]{1,0:T(8,128)(2,1)S(1)}, bf16[512,128]{1,0:T(8,128)(2,1)S(1)}, u32[]{:S(2)}, u32[]{:S(2)}) collective-permute-start(bf16[512,128]{1,0:T(8,128)(2,1)S(1)} %get-tuple-element.47), channel_id=1, source_target_pairs={{0,6},{1,7},{2,4},{3,5},{4,2},{5,3},{6,0},{7,1},{8,14},{9,15},{10,... | collective-permute-start | bytes 393224 | tf_op jit(solution)/shard_map/ppermute | solution.py:531
  78.2 5.0 %collective-permute-start.29 = (bf16[512,128]{1,0:T(8,128)(2,1)S(1)}, bf16[512,128]{1,0:T(8,128)(2,1)S(1)}, u32[]{:S(2)}, u32[]{:S(2)}) collective-permute-start(bf16[512,128]{1,0:T(8,128)(2,1)S(1)} %total.1), channel_id=1, source_target_pairs={{0,16},{16,0},{1,17},{17,1},{2,18},{18,2},{3,19},{19,3},{4,20},{20... | collective-permute-start | bytes 393224 | tf_op jit(solution)/shard_map/ppermute | solution.py:535
  83.3 8.5 %collective-permute-start.30 = (bf16[512,128]{1,0:T(8,128)(2,1)S(1)}, bf16[512,128]{1,0:T(8,128)(2,1)S(1)}, u32[]{:S(2)}, u32[]{:S(2)}) collective-permute-start(bf16[512,128]{1,0:T(8,128)(2,1)S(1)} %get-tuple-element.53), channel_id=1, source_target_pairs={{0,8},{1,9},{2,10},{3,11},{4,12},{5,13},{6,14},{7,15},{8,0},{9,1},... | collective-permute-start | bytes 393224 | tf_op jit(solution)/shard_map/ppermute | solution.py:531
  (1 other events, 9.4 us)

commit v9 on v8

--- a/solution.py
+++ b/solution.py
@@ -320,7 +320,7 @@
 
 def toeplitz(filters, *earlier):
     groups, taps = filters.shape
-    step = min(8, groups)
+    step = min(16, groups)
     shape = pltpu.VMEM((groups, 2 * BLOCK, taps), BF16)
     return pl.pallas_call(
         toeplitz_kernel,

time: 92.8 us -> 92.8 us (level)
  no operation moved by 1% of the time
where the time goes in v9:
time: 92.8 us; the launch traced here: 92.6 us
  starting transfers between devices  38.5 us (41%)
  waiting for transfers between devices  28.9 us (31%)
  Pallas kernels  24.3 us (26%)
    ppermute x23, starting transfers between devices, across(): return lax.ppermute(array, 'tensor', [(i, i ^ mask) for i in range(16)])  20.3 us
    ppermute x23, waiting for transfers between devices, across(): return lax.ppermute(array, 'tensor', [(i, i ^ mask) for i in range(16)])  19 us
    ppermute x4, starting transfers between devices, in_square(): return lax.ppermute(array, ('fsdp', 'tensor'), pairs)  11.1 us
    ppermute x4, waiting for transfers between devices, other_row(): return lax.ppermute(array, 'fsdp', [(0, 1), (1, 0)])  9.88 us
    ppermute x4, starting transfers between devices, other_row(): return lax.ppermute(array, 'fsdp', [(0, 1), (1, 0)])  7.13 us
    pallas_call x1, Pallas kernels, prepared(): pl.pallas_call(prepare_kernel, in_specs=[LATER_SPEC] * (2 + len(earlier))...  5.89 us
    pallas_call x3, Pallas kernels, input_partial(): pl.pallas_call(functools.partial(input_kernel, masks), in_specs=[VMEM_SPE...  3.74 us
    pallas_call x1, Pallas kernels, taps_gradient(): pl.pallas_call(functools.partial(taps_kernel, groups // steps), grid=(ste...  3.22 us
  transfers between devices with their start and end apart: 31, of which 11 were waited for; matrix products, arithmetic and copies ran while one was open for 0% of the time, Pallas kernels for 22%

profile of v9, /device:TPU:0, one launch (start us, length us, event | category | flops | bytes accessed | tf_op | source)
XLA Modules:
  0.0 92.6 jit_solution(46701653430196181)
XLA Ops:
  0.6 4.1 %collective-permute-start = (bf16[128,512]{1,0:T(8,128)(2,1)}, bf16[128,512]{1,0:T(8,128)(2,1)S(1)}, u32[]{:S(2)}, u32[]{:S(2)}) collective-permute-start(bf16[128,512]{1,0:T(8,128)(2,1)} %array_ref.1), channel_id=1, source_target_pairs={{0,8},{1,9},{2,10},{3,11},{4,12},{5,13},{6,14},{7,15},{8,24},{9,25... | collective-permute-start | bytes 393224 | tf_op jit(solution)/shard_map/ppermute | solution.py:545
  5.4 5.9 %prepare.1 = (bf16[4096,512]{1,0:T(8,128)(2,1)S(1)}, bf16[4096,512]{1,0:T(8,128)(2,1)S(1)}, bf16[4096,512]{1,0:T(8,128)(2,1)S(1)}, f32[8,128]{1,0:T(8,128)S(1)}) custom-call(bf16[3,4096,512]{2,1,0:T(8,128)(2,1)} %bitcast.6, bf16[3,32,512]{2,1,0:T(8,128)(2,1)} %bitcast.7), custom_call_target="tpu_custom_call" | custom-call | flops 6144 | bytes 6144 | tf_op jit(solution)/shard_map/prepare/pallas_call | solution.py:154
  11.3 0.9 %own_slice.2.refs_0_ = bf16[256,512]{1,0:T(8,128)(2,1)S(1)} custom-call(bf16[128,512]{1,0:T(8,128)(2,1)} %array_ref.1, bf16[128,512]{1,0:T(8,128)(2,1)S(1)} %collective-permute-done.turned_ref, bf16[128,512]{1,0:T(8,128)(2,1)S(1)} %collective-permute-done.1.crossed_ref, f32[8,128]{1,0:T(8,128)S(1)} %get-tuple-element.32.refs_0_), custom_call_target="tpu_custom_call" | custom-call | bytes 160 | tf_op jit(solution)/shard_map/own_slice/pallas_call | solution.py:73
  12.3 2.6 %collective-permute-start.9 = (bf16[256,512]{1,0:T(8,128)(2,1)S(1)}, bf16[256,512]{1,0:T(8,128)(2,1)S(1)}, u32[]{:S(2)}, u32[]{:S(2)}) collective-permute-start(bf16[256,512]{1,0:T(8,128)(2,1)S(1)} %own_slice.2.refs_0_), channel_id=1, source_target_pairs={{0,6},{1,7},{2,4},{3,5},{4,2},{5,3},{6,0},{7,1},{8,14},{9,15},{10,... | collective-permute-start | bytes 786440 | tf_op jit(solution)/shard_map/ppermute | solution.py:531
  14.8 5.7 %collective-permute-start.2 = (bf16[128,512]{1,0:T(8,128)(2,1)S(1)}, bf16[128,512]{1,0:T(8,128)(2,1)S(1)}, u32[]{:S(2)}, u32[]{:S(2)}) collective-permute-start(bf16[128,512]{1,0:T(8,128)(2,1)S(1)} %copied.1.array_ref), channel_id=1, source_target_pairs={{0,8},{1,9},{2,10},{3,11},{4,12},{5,13},{6,14},{7,15},{8,24},{9,25... | collective-permute-start | bytes 393224 | tf_op jit(solution)/shard_map/ppermute | solution.py:545
  21.9 0.9 toeplitz.1
  22.8 2.2 %loaded.1.refs_1_.refs_8_ = bf16[512,4096]{1,0:T(8,128)(2,1)S(1)} custom-call(bf16[512,4096]{1,0:T(8,128)(2,1)} %in_ref.3, bf16[32,256,128]{2,1,0:T(8,128)(2,1)S(1)} %get-tuple-element.33.refs_0_.refs_2_), custom_call_target="tpu_custom_call" | custom-call | bytes 2048 | tf_op jit(solution)/shard_map/loaded/pallas_call | solution.py:205
  25.8 5.6 %collective-permute-done.7.refs_1_ = bf16[256,512]{1,0:T(8,128)(2,1)S(1)} collective-permute-done((bf16[256,512]{1,0:T(8,128)(2,1)S(1)}, bf16[256,512]{1,0:T(8,128)(2,1)S(1)}, u32[]{:S(2)}, u32[]{:S(2)}) %collective-permute-start.7) | collective-permute-done | bytes 262176 | tf_op jit(solution)/shard_map/ppermute | solution.py:531
  32.4 3.0 %collective-permute-start.6 = (bf16[256,512]{1,0:T(8,128)(2,1)S(1)}, bf16[256,512]{1,0:T(8,128)(2,1)S(1)}, u32[]{:S(2)}, u32[]{:S(2)}) collective-permute-start(bf16[256,512]{1,0:T(8,128)(2,1)S(1)} %own_slice.3.refs_2_.refs_0_), channel_id=1, source_target_pairs={{0,6},{1,7},{2,4},{3,5},{4,2},{5,3},{6,0},{7,1},{8,14},{9,15},{10,... | collective-permute-start | bytes 786440 | tf_op jit(solution)/shard_map/ppermute | solution.py:531
  35.4 2.6 %proj_pair.1 = (bf16[2,512,256]{2,1,0:T(8,128)(2,1)S(1)}, bf16[256,4096]{1,0:T(8,128)(2,1)S(1)}) custom-call(bf16[256,512]{1,0:T(8,128)(2,1)S(1)} %own_slice.2.refs_0_, bf16[256,512]{1,0:T(8,128)(2,1)S(1)} %collective-permute-done.7.refs_1_, bf16[256,512]{1,0:T(8,128)(2,1)S(1)} %collective-permute-done.8.refs_2_, bf16[256,512]{1,0:T(8,128)(2,1)S(1)} %relayed.2.refs_3_, ...), custom_call_target="tpu_custom_call" | custom-call | flops 524288 | bytes 2048 | tf_op jit(solution)/shard_map/proj_pair/pallas_call | solution.py:245
  38.0 1.3 %collective-permute-start.20 = (bf16[2,512,256]{2,1,0:T(8,128)(2,1)S(1)}, bf16[2,512,256]{2,1,0:T(8,128)(2,1)S(1)}, u32[]{:S(2)}, u32[]{:S(2)}) collective-permute-start(bf16[2,512,256]{2,1,0:T(8,128)(2,1)S(1)} %get-tuple-element.39.refs_0_), channel_id=1, source_target_pairs={{0,16},{16,0},{1,17},{17,1},{2,18},{18,2},{3,19},{19,3},{4,20},{20... | collective-permute-start | bytes 1572872 | tf_op jit(solution)/shard_map/ppermute | solution.py:535
  39.3 1.3 %proj_queries.1.refs_4_.refs_2_ = bf16[512,256]{1,0:T(8,128)(2,1)S(1)} custom-call(bf16[256,4096]{1,0:T(8,128)(2,1)S(1)} %get-tuple-element.34.held_ref, bf16[4096,512]{1,0:T(8,128)(2,1)S(1)} %get-tuple-element.29.w_ref.refs_0_), custom_call_target="tpu_custom_call" | custom-call | flops 262144 | bytes 1024 | tf_op jit(solution)/shard_map/proj_queries/pallas_call | solution.py:257
  41.1 4.7 %collective-permute-done.5.refs_2_ = bf16[256,512]{1,0:T(8,128)(2,1)S(1)} collective-permute-done((bf16[256,512]{1,0:T(8,128)(2,1)S(1)}, bf16[256,512]{1,0:T(8,128)(2,1)S(1)}, u32[]{:S(2)}, u32[]{:S(2)}) %collective-permute-start.5) | collective-permute-done | bytes 262176 | tf_op jit(solution)/shard_map/ppermute | solution.py:531
  47.4 2.9 %collective-permute-start.19 = (bf16[512,256]{1,0:T(8,128)(2,1)S(1)}, bf16[512,256]{1,0:T(8,128)(2,1)S(1)}, u32[]{:S(2)}, u32[]{:S(2)}) collective-permute-start(bf16[512,256]{1,0:T(8,128)(2,1)S(1)} %proj_queries.1.refs_4_.refs_2_), channel_id=1, source_target_pairs={{0,16},{16,0},{1,17},{17,1},{2,18},{18,2},{3,19},{19,3},{4,20},{20... | collective-permute-start | bytes 786440 | tf_op jit(solution)/shard_map/ppermute | solution.py:535
  50.3 1.3 %grad_z_partial.1.refs_0_ = bf16[512,256]{1,0:T(8,128)(2,1)S(1)} custom-call(bf16[256,512]{1,0:T(8,128)(2,1)S(1)} %get-tuple-element.35.refs_0_, bf16[256,512]{1,0:T(8,128)(2,1)S(1)} %get-tuple-element.36.refs_1_, bf16[256,512]{1,0:T(8,128)(2,1)S(1)} %get-tuple-element.37.refs_2_, bf16[256,512]{1,0:T(8,128)(2,1)S(1)} %get-tuple-element.38.refs_3_, ...), custom_call_target="tpu_custom_call" | custom-call | flops 262144 | bytes 1024 | tf_op jit(solution)/shard_map/grad_z_partial/pallas_call | solution.py:288
  51.6 1.2 %collective-permute-start.18 = (bf16[512,256]{1,0:T(8,128)(2,1)S(1)}, bf16[512,256]{1,0:T(8,128)(2,1)S(1)}, u32[]{:S(2)}, u32[]{:S(2)}) collective-permute-start(bf16[512,256]{1,0:T(8,128)(2,1)S(1)} %grad_z_partial.1.refs_0_), channel_id=1, source_target_pairs={{0,16},{16,0},{1,17},{17,1},{2,18},{18,2},{3,19},{19,3},{4,20},{20... | collective-permute-start | bytes 786440 | tf_op jit(solution)/shard_map/ppermute | solution.py:535
  53.2 4.2 %collective-permute-done.19.refs_3_ = bf16[512,256]{1,0:T(8,128)(2,1)S(1)} collective-permute-done((bf16[512,256]{1,0:T(8,128)(2,1)S(1)}, bf16[512,256]{1,0:T(8,128)(2,1)S(1)}, u32[]{:S(2)}, u32[]{:S(2)}) %collective-permute-start.19) | collective-permute-done | bytes 262176 | tf_op jit(solution)/shard_map/ppermute | solution.py:535
  57.4 5.1 %collective-permute-done.18.refs_1_ = bf16[512,256]{1,0:T(8,128)(2,1)S(1)} collective-permute-done((bf16[512,256]{1,0:T(8,128)(2,1)S(1)}, bf16[512,256]{1,0:T(8,128)(2,1)S(1)}, u32[]{:S(2)}, u32[]{:S(2)}) %collective-permute-start.18) | collective-permute-done | bytes 262176 | tf_op jit(solution)/shard_map/ppermute | solution.py:535
  63.0 1.4 %input_partial.4 = bf16[3,512,256]{2,1,0:T(8,128)(2,1)S(1)} custom-call(bf16[4096,512]{1,0:T(8,128)(2,1)S(1)} %get-tuple-element.29.w_ref.refs_0_, bf16[4096,512]{1,0:T(8,128)(2,1)S(1)} %get-tuple-element.30.refs_8_.refs_1_, bf16[4096,512]{1,0:T(8,128)(2,1)S(1)} %get-tuple-element.31.refs_9_.refs_2_, bf16[1536,256]{1,0:T(8,128)(2,1)S(1)} %bitcast.3), custom_call_target="tpu_custom_call" | custom-call | flops 294912 | bytes 1344 | tf_op jit(solution)/shard_map/input_partial/pallas_call | solution.py:517
  65.6 1.8 %input_partial.3.same_ref = bf16[4,512,256]{2,1,0:T(8,128)(2,1)S(1)} custom-call(bf16[4096,512]{1,0:T(8,128)(2,1)S(1)} %get-tuple-element.29.w_ref.refs_0_, bf16[4096,512]{1,0:T(8,128)(2,1)S(1)} %get-tuple-element.30.refs_8_.refs_1_, bf16[4096,512]{1,0:T(8,128)(2,1)S(1)} %get-tuple-element.31.refs_9_.refs_2_, bf16[1536,256]{1,0:T(8,128)(2,1)S(1)} %bitcast.5), custom_call_target="tpu_custom_call" | custom-call | flops 393216 | bytes 1792 | tf_op jit(solution)/shard_map/input_partial/pallas_call | solution.py:517
  67.7 1.4 %collective-permute-start.26 = (bf16[512,128]{1,0:T(8,128)(2,1)S(1)}, bf16[512,128]{1,0:T(8,128)(2,1)S(1)}, u32[]{:S(2)}, u32[]{:S(2)}) collective-permute-start(bf16[512,128]{1,0:T(8,128)(2,1)S(1)} %get-tuple-element.49), channel_id=1, source_target_pairs={{0,4},{1,5},{2,6},{3,7},{4,0},{5,1},{6,2},{7,3},{8,12},{9,13},{10,... | collective-permute-start | bytes 393224 | tf_op jit(solution)/shard_map/ppermute | solution.py:531
  69.5 1.7 %collective-permute-start.28 = (bf16[512,128]{1,0:T(8,128)(2,1)S(1)}, bf16[512,128]{1,0:T(8,128)(2,1)S(1)}, u32[]{:S(2)}, u32[]{:S(2)}) collective-permute-start(bf16[512,128]{1,0:T(8,128)(2,1)S(1)} %get-tuple-element.51), channel_id=1, source_target_pairs={{0,6},{1,7},{2,4},{3,5},{4,2},{5,3},{6,0},{7,1},{8,14},{9,15},{10,... | collective-permute-start | bytes 393224 | tf_op jit(solution)/shard_map/ppermute | solution.py:531
  71.2 1.3 %collective-permute-start.23 = (bf16[512,128]{1,0:T(8,128)(2,1)S(1)}, bf16[512,128]{1,0:T(8,128)(2,1)S(1)}, u32[]{:S(2)}, u32[]{:S(2)}) collective-permute-start(bf16[512,128]{1,0:T(8,128)(2,1)S(1)} %get-tuple-element.45), channel_id=1, source_target_pairs={{0,4},{1,5},{2,6},{3,7},{4,0},{5,1},{6,2},{7,3},{8,12},{9,13},{10,... | collective-permute-start | bytes 393224 | tf_op jit(solution)/shard_map/ppermute | solution.py:531
  73.0 0.7 collective-permute-done.26.refs_1_
  73.7 1.6 %collective-permute-start.25 = (bf16[512,128]{1,0:T(8,128)(2,1)S(1)}, bf16[512,128]{1,0:T(8,128)(2,1)S(1)}, u32[]{:S(2)}, u32[]{:S(2)}) collective-permute-start(bf16[512,128]{1,0:T(8,128)(2,1)S(1)} %get-tuple-element.47), channel_id=1, source_target_pairs={{0,6},{1,7},{2,4},{3,5},{4,2},{5,3},{6,0},{7,1},{8,14},{9,15},{10,... | collective-permute-start | bytes 393224 | tf_op jit(solution)/shard_map/ppermute | solution.py:531
  75.3 2.8 %collective-permute-done.27.refs_2_ = bf16[512,128]{1,0:T(8,128)(2,1)S(1)} collective-permute-done((bf16[512,128]{1,0:T(8,128)(2,1)S(1)}, bf16[512,128]{1,0:T(8,128)(2,1)S(1)}, u32[]{:S(2)}, u32[]{:S(2)}) %collective-permute-start.27) | collective-permute-done | bytes 131104 | tf_op jit(solution)/shard_map/ppermute | solution.py:531
  78.2 1.8 %collective-permute-start.29 = (bf16[512,128]{1,0:T(8,128)(2,1)S(1)}, bf16[512,128]{1,0:T(8,128)(2,1)S(1)}, u32[]{:S(2)}, u32[]{:S(2)}) collective-permute-start(bf16[512,128]{1,0:T(8,128)(2,1)S(1)} %total.1), channel_id=1, source_target_pairs={{0,16},{16,0},{1,17},{17,1},{2,18},{18,2},{3,19},{19,3},{4,20},{20... | collective-permute-start | bytes 393224 | tf_op jit(solution)/shard_map/ppermute | solution.py:535
  79.9 2.7 %collective-permute-done.24.refs_2_ = bf16[512,128]{1,0:T(8,128)(2,1)S(1)} collective-permute-done((bf16[512,128]{1,0:T(8,128)(2,1)S(1)}, bf16[512,128]{1,0:T(8,128)(2,1)S(1)}, u32[]{:S(2)}, u32[]{:S(2)}) %collective-permute-start.24) | collective-permute-done | bytes 131104 | tf_op jit(solution)/shard_map/ppermute | solution.py:531
  83.3 3.8 %collective-permute-start.30 = (bf16[512,128]{1,0:T(8,128)(2,1)S(1)}, bf16[512,128]{1,0:T(8,128)(2,1)S(1)}, u32[]{:S(2)}, u32[]{:S(2)}) collective-permute-start(bf16[512,128]{1,0:T(8,128)(2,1)S(1)} %get-tuple-element.53), channel_id=1, source_target_pairs={{0,8},{1,9},{2,10},{3,11},{4,12},{5,13},{6,14},{7,15},{8,0},{9,1},... | collective-permute-start | bytes 393224 | tf_op jit(solution)/shard_map/ppermute | solution.py:531
  87.1 3.2 %taps_gradient.1 = f32[32,128]{1,0:T(8,128)} custom-call(bf16[512,256]{1,0:T(8,128)(2,1)S(1)} %get-tuple-element.54.prod_ref, bf16[512,256]{1,0:T(8,128)(2,1)S(1)} %get-tuple-element.55.grad_ref), custom_call_target="tpu_custom_call" | custom-call | flops 131072 | bytes 768 | tf_op jit(solution)/shard_map/taps_gradient/pallas_call | solution.py:494
  90.3 1.5 %collective-permute-done.30.got_ref = bf16[512,128]{1,0:T(8,128)(2,1)S(1)} collective-permute-done((bf16[512,128]{1,0:T(8,128)(2,1)S(1)}, bf16[512,128]{1,0:T(8,128)(2,1)S(1)}, u32[]{:S(2)}, u32[]{:S(2)}) %collective-permute-start.30) | collective-permute-done | bytes 131104 | tf_op jit(solution)/shard_map/ppermute | solution.py:531
  91.8 0.7 last_sum.1
  (55 shorter events, 10.0 us)
Async XLA Ops:
  0.6 10.7 %collective-permute-start = (bf16[128,512]{1,0:T(8,128)(2,1)}, bf16[128,512]{1,0:T(8,128)(2,1)S(1)}, u32[]{:S(2)}, u32[]{:S(2)}) collective-permute-start(bf16[128,512]{1,0:T(8,128)(2,1)} %array_ref.1), channel_id=1, source_target_pairs={{0,8},{1,9},{2,10},{3,11},{4,12},{5,13},{6,14},{7,15},{8,24},{9,25... | collective-permute-start | bytes 393224 | tf_op jit(solution)/shard_map/ppermute | solution.py:545
  4.7 6.6 %collective-permute-start.1 = (bf16[128,512]{1,0:T(8,128)(2,1)}, bf16[128,512]{1,0:T(8,128)(2,1)S(1)}, u32[]{:S(2)}, u32[]{:S(2)}) collective-permute-start(bf16[128,512]{1,0:T(8,128)(2,1)} %array_ref.1), channel_id=1, source_target_pairs={{8,16},{9,17},{10,18},{11,19},{12,20},{13,21},{14,22},{15,23},{16,... | collective-permute-start | bytes 393224 | tf_op jit(solution)/shard_map/ppermute | solution.py:545
  5.4 16.5 %copy-start.1 = (f32[32,128]{1,0:T(8,128)S(1)}, f32[32,128]{1,0:T(8,128)}, u32[]{:S(2)}) copy-start(f32[32,128]{1,0:T(8,128)} %taps_ref.1) | copy-start | bytes 49156
  12.3 13.0 %collective-permute-start.9 = (bf16[256,512]{1,0:T(8,128)(2,1)S(1)}, bf16[256,512]{1,0:T(8,128)(2,1)S(1)}, u32[]{:S(2)}, u32[]{:S(2)}) collective-permute-start(bf16[256,512]{1,0:T(8,128)(2,1)S(1)} %own_slice.2.refs_0_), channel_id=1, source_target_pairs={{0,6},{1,7},{2,4},{3,5},{4,2},{5,3},{6,0},{7,1},{8,14},{9,15},{10,... | collective-permute-start | bytes 786440 | tf_op jit(solution)/shard_map/ppermute | solution.py:531
  14.8 10.1 %collective-permute-start.2 = (bf16[128,512]{1,0:T(8,128)(2,1)S(1)}, bf16[128,512]{1,0:T(8,128)(2,1)S(1)}, u32[]{:S(2)}, u32[]{:S(2)}) collective-permute-start(bf16[128,512]{1,0:T(8,128)(2,1)S(1)} %copied.1.array_ref), channel_id=1, source_target_pairs={{0,8},{1,9},{2,10},{3,11},{4,12},{5,13},{6,14},{7,15},{8,24},{9,25... | collective-permute-start | bytes 393224 | tf_op jit(solution)/shard_map/ppermute | solution.py:545
  20.6 4.5 %collective-permute-start.3 = (bf16[128,512]{1,0:T(8,128)(2,1)S(1)}, bf16[128,512]{1,0:T(8,128)(2,1)S(1)}, u32[]{:S(2)}, u32[]{:S(2)}) collective-permute-start(bf16[128,512]{1,0:T(8,128)(2,1)S(1)} %copied.1.array_ref), channel_id=1, source_target_pairs={{8,16},{9,17},{10,18},{11,19},{12,20},{13,21},{14,22},{15,23},{16,... | collective-permute-start | bytes 393224 | tf_op jit(solution)/shard_map/ppermute | solution.py:545
  21.2 10.2 %collective-permute-start.7 = (bf16[256,512]{1,0:T(8,128)(2,1)S(1)}, bf16[256,512]{1,0:T(8,128)(2,1)S(1)}, u32[]{:S(2)}, u32[]{:S(2)}) collective-permute-start(bf16[256,512]{1,0:T(8,128)(2,1)S(1)} %own_slice.2.refs_0_), channel_id=1, source_target_pairs={{0,4},{1,5},{2,6},{3,7},{4,0},{5,1},{6,2},{7,3},{8,12},{9,13},{10,... | collective-permute-start | bytes 786440 | tf_op jit(solution)/shard_map/ppermute | solution.py:531
  21.3 10.1 %collective-permute-start.8 = (bf16[256,512]{1,0:T(8,128)(2,1)S(1)}, bf16[256,512]{1,0:T(8,128)(2,1)S(1)}, u32[]{:S(2)}, u32[]{:S(2)}) collective-permute-start(bf16[256,512]{1,0:T(8,128)(2,1)S(1)} %own_slice.2.refs_0_), channel_id=1, source_target_pairs={{0,2},{1,3},{2,0},{3,1},{4,6},{5,7},{6,4},{7,5},{8,10},{9,11},{10,... | collective-permute-start | bytes 786440 | tf_op jit(solution)/shard_map/ppermute | solution.py:531
  25.0 7.0 %collective-permute-start.10 = (bf16[256,512]{1,0:T(8,128)(2,1)S(1)}, bf16[256,512]{1,0:T(8,128)(2,1)S(1)}, u32[]{:S(2)}, u32[]{:S(2)}) collective-permute-start(bf16[256,512]{1,0:T(8,128)(2,1)S(1)} %own_slice.2.refs_0_), channel_id=1, source_target_pairs={{0,1},{1,0},{2,3},{3,2},{4,5},{5,4},{6,7},{7,6},{8,9},{9,8},{10,11... | collective-permute-start | bytes 786440 | tf_op jit(solution)/shard_map/ppermute | solution.py:531
  25.3 7.1 %collective-permute-start.13 = (bf16[256,512]{1,0:T(8,128)(2,1)S(1)}, bf16[256,512]{1,0:T(8,128)(2,1)S(1)}, u32[]{:S(2)}, u32[]{:S(2)}) collective-permute-start(bf16[256,512]{1,0:T(8,128)(2,1)S(1)} %relayed.2.refs_3_), channel_id=1, source_target_pairs={{0,1},{1,0},{2,3},{3,2},{4,5},{5,4},{6,7},{7,6},{8,9},{9,8},{10,11... | collective-permute-start | bytes 786440 | tf_op jit(solution)/shard_map/ppermute | solution.py:531
  31.4 4.0 %collective-permute-start.11 = (bf16[256,512]{1,0:T(8,128)(2,1)S(1)}, bf16[256,512]{1,0:T(8,128)(2,1)S(1)}, u32[]{:S(2)}, u32[]{:S(2)}) collective-permute-start(bf16[256,512]{1,0:T(8,128)(2,1)S(1)} %collective-permute-done.7.refs_1_), channel_id=1, source_target_pairs={{0,1},{1,0},{2,3},{3,2},{4,5},{5,4},{6,7},{7,6},{8,9},{9,8},{10,11... | collective-permute-start | bytes 786440 | tf_op jit(solution)/shard_map/ppermute | solution.py:531
  31.4 4.0 %collective-permute-start.12 = (bf16[256,512]{1,0:T(8,128)(2,1)S(1)}, bf16[256,512]{1,0:T(8,128)(2,1)S(1)}, u32[]{:S(2)}, u32[]{:S(2)}) collective-permute-start(bf16[256,512]{1,0:T(8,128)(2,1)S(1)} %collective-permute-done.8.refs_2_), channel_id=1, source_target_pairs={{0,1},{1,0},{2,3},{3,2},{4,5},{5,4},{6,7},{7,6},{8,9},{9,8},{10,11... | collective-permute-start | bytes 786440 | tf_op jit(solution)/shard_map/ppermute | solution.py:531
  31.9 9.2 %collective-permute-start.4 = (bf16[256,512]{1,0:T(8,128)(2,1)S(1)}, bf16[256,512]{1,0:T(8,128)(2,1)S(1)}, u32[]{:S(2)}, u32[]{:S(2)}) collective-permute-start(bf16[256,512]{1,0:T(8,128)(2,1)S(1)} %own_slice.3.refs_2_.refs_0_), channel_id=1, source_target_pairs={{0,4},{1,5},{2,6},{3,7},{4,0},{5,1},{6,2},{7,3},{8,12},{9,13},{10,... | collective-permute-start | bytes 786440 | tf_op jit(solution)/shard_map/ppermute | solution.py:531
  32.0 13.9 %collective-permute-start.5 = (bf16[256,512]{1,0:T(8,128)(2,1)S(1)}, bf16[256,512]{1,0:T(8,128)(2,1)S(1)}, u32[]{:S(2)}, u32[]{:S(2)}) collective-permute-start(bf16[256,512]{1,0:T(8,128)(2,1)S(1)} %own_slice.3.refs_2_.refs_0_), channel_id=1, source_target_pairs={{0,2},{1,3},{2,0},{3,1},{4,6},{5,7},{6,4},{7,5},{8,10},{9,11},{10,... | collective-permute-start | bytes 786440 | tf_op jit(solution)/shard_map/ppermute | solution.py:531
  32.4 13.4 %collective-permute-start.6 = (bf16[256,512]{1,0:T(8,128)(2,1)S(1)}, bf16[256,512]{1,0:T(8,128)(2,1)S(1)}, u32[]{:S(2)}, u32[]{:S(2)}) collective-permute-start(bf16[256,512]{1,0:T(8,128)(2,1)S(1)} %own_slice.3.refs_2_.refs_0_), channel_id=1, source_target_pairs={{0,6},{1,7},{2,4},{3,5},{4,2},{5,3},{6,0},{7,1},{8,14},{9,15},{10,... | collective-permute-start | bytes 786440 | tf_op jit(solution)/shard_map/ppermute | solution.py:531
  38.0 14.8 %collective-permute-start.20 = (bf16[2,512,256]{2,1,0:T(8,128)(2,1)S(1)}, bf16[2,512,256]{2,1,0:T(8,128)(2,1)S(1)}, u32[]{:S(2)}, u32[]{:S(2)}) collective-permute-start(bf16[2,512,256]{2,1,0:T(8,128)(2,1)S(1)} %get-tuple-element.39.refs_0_), channel_id=1, source_target_pairs={{0,16},{16,0},{1,17},{17,1},{2,18},{18,2},{3,19},{19,3},{4,20},{20... | collective-permute-start | bytes 1572872 | tf_op jit(solution)/shard_map/ppermute | solution.py:535
  45.9 1.5 %collective-permute-start.14 = (bf16[256,512]{1,0:T(8,128)(2,1)S(1)}, bf16[256,512]{1,0:T(8,128)(2,1)S(1)}, u32[]{:S(2)}, u32[]{:S(2)}) collective-permute-start(bf16[256,512]{1,0:T(8,128)(2,1)S(1)} %get-tuple-element.35.refs_0_), channel_id=1, source_target_pairs={{0,1},{1,0},{2,3},{3,2},{4,5},{5,4},{6,7},{7,6},{8,9},{9,8},{10,11... | collective-permute-start | bytes 786440 | tf_op jit(solution)/shard_map/ppermute | solution.py:531
  45.9 4.4 %collective-permute-start.15 = (bf16[256,512]{1,0:T(8,128)(2,1)S(1)}, bf16[256,512]{1,0:T(8,128)(2,1)S(1)}, u32[]{:S(2)}, u32[]{:S(2)}) collective-permute-start(bf16[256,512]{1,0:T(8,128)(2,1)S(1)} %get-tuple-element.36.refs_1_), channel_id=1, source_target_pairs={{0,1},{1,0},{2,3},{3,2},{4,5},{5,4},{6,7},{7,6},{8,9},{9,8},{10,11... | collective-permute-start | bytes 786440 | tf_op jit(solution)/shard_map/ppermute | solution.py:531
  46.4 3.9 %collective-permute-start.16 = (bf16[256,512]{1,0:T(8,128)(2,1)S(1)}, bf16[256,512]{1,0:T(8,128)(2,1)S(1)}, u32[]{:S(2)}, u32[]{:S(2)}) collective-permute-start(bf16[256,512]{1,0:T(8,128)(2,1)S(1)} %get-tuple-element.37.refs_2_), channel_id=1, source_target_pairs={{0,1},{1,0},{2,3},{3,2},{4,5},{5,4},{6,7},{7,6},{8,9},{9,8},{10,11... | collective-permute-start | bytes 786440 | tf_op jit(solution)/shard_map/ppermute | solution.py:531
  46.4 3.9 %collective-permute-start.17 = (bf16[256,512]{1,0:T(8,128)(2,1)S(1)}, bf16[256,512]{1,0:T(8,128)(2,1)S(1)}, u32[]{:S(2)}, u32[]{:S(2)}) collective-permute-start(bf16[256,512]{1,0:T(8,128)(2,1)S(1)} %get-tuple-element.38.refs_3_), channel_id=1, source_target_pairs={{0,1},{1,0},{2,3},{3,2},{4,5},{5,4},{6,7},{7,6},{8,9},{9,8},{10,11... | collective-permute-start | bytes 786440 | tf_op jit(solution)/shard_map/ppermute | solution.py:531
  47.4 10.0 %collective-permute-start.19 = (bf16[512,256]{1,0:T(8,128)(2,1)S(1)}, bf16[512,256]{1,0:T(8,128)(2,1)S(1)}, u32[]{:S(2)}, u32[]{:S(2)}) collective-permute-start(bf16[512,256]{1,0:T(8,128)(2,1)S(1)} %proj_queries.1.refs_4_.refs_2_), channel_id=1, source_target_pairs={{0,16},{16,0},{1,17},{17,1},{2,18},{18,2},{3,19},{19,3},{4,20},{20... | collective-permute-start | bytes 786440 | tf_op jit(solution)/shard_map/ppermute | solution.py:535
  51.6 10.9 %collective-permute-start.18 = (bf16[512,256]{1,0:T(8,128)(2,1)S(1)}, bf16[512,256]{1,0:T(8,128)(2,1)S(1)}, u32[]{:S(2)}, u32[]{:S(2)}) collective-permute-start(bf16[512,256]{1,0:T(8,128)(2,1)S(1)} %grad_z_partial.1.refs_0_), channel_id=1, source_target_pairs={{0,16},{16,0},{1,17},{17,1},{2,18},{18,2},{3,19},{19,3},{4,20},{20... | collective-permute-start | bytes 786440 | tf_op jit(solution)/shard_map/ppermute | solution.py:535
  64.4 3.0 %collective-permute-start.21 = (bf16[3,512,256]{2,1,0:T(8,128)(2,1)S(1)}, bf16[3,512,256]{2,1,0:T(8,128)(2,1)S(1)}, u32[]{:S(2)}, u32[]{:S(2)}) collective-permute-start(bf16[3,512,256]{2,1,0:T(8,128)(2,1)S(1)} %input_partial.4), channel_id=1, source_target_pairs={{0,1},{1,0},{2,3},{3,2},{4,5},{5,4},{6,7},{7,6},{8,9},{9,8},{10,11... | collective-permute-start | bytes 2359304 | tf_op jit(solution)/shard_map/ppermute | solution.py:531
  65.0 2.4 %collective-permute-start.22 = (bf16[1,512,256]{2,1,0:T(8,128)(2,1)S(1)}, bf16[1,512,256]{2,1,0:T(8,128)(2,1)S(1)}, u32[]{:S(2)}, u32[]{:S(2)}) collective-permute-start(bf16[1,512,256]{2,1,0:T(8,128)(2,1)S(1)} %input_partial.5), channel_id=1, source_target_pairs={{0,1},{1,0},{2,3},{3,2},{4,5},{5,4},{6,7},{7,6},{8,9},{9,8},{10,11... | collective-permute-start | bytes 786440 | tf_op jit(solution)/shard_map/ppermute | solution.py:531
  67.7 6.0 %collective-permute-start.26 = (bf16[512,128]{1,0:T(8,128)(2,1)S(1)}, bf16[512,128]{1,0:T(8,128)(2,1)S(1)}, u32[]{:S(2)}, u32[]{:S(2)}) collective-permute-start(bf16[512,128]{1,0:T(8,128)(2,1)S(1)} %get-tuple-element.49), channel_id=1, source_target_pairs={{0,4},{1,5},{2,6},{3,7},{4,0},{5,1},{6,2},{7,3},{8,12},{9,13},{10,... | collective-permute-start | bytes 393224 | tf_op jit(solution)/shard_map/ppermute | solution.py:531
  69.0 9.0 %collective-permute-start.27 = (bf16[512,128]{1,0:T(8,128)(2,1)S(1)}, bf16[512,128]{1,0:T(8,128)(2,1)S(1)}, u32[]{:S(2)}, u32[]{:S(2)}) collective-permute-start(bf16[512,128]{1,0:T(8,128)(2,1)S(1)} %get-tuple-element.50), channel_id=1, source_target_pairs={{0,2},{1,3},{2,0},{3,1},{4,6},{5,7},{6,4},{7,5},{8,10},{9,11},{10,... | collective-permute-start | bytes 393224 | tf_op jit(solution)/shard_map/ppermute | solution.py:531
  69.5 8.5 %collective-permute-start.28 = (bf16[512,128]{1,0:T(8,128)(2,1)S(1)}, bf16[512,128]{1,0:T(8,128)(2,1)S(1)}, u32[]{:S(2)}, u32[]{:S(2)}) collective-permute-start(bf16[512,128]{1,0:T(8,128)(2,1)S(1)} %get-tuple-element.51), channel_id=1, source_target_pairs={{0,6},{1,7},{2,4},{3,5},{4,2},{5,3},{6,0},{7,1},{8,14},{9,15},{10,... | collective-permute-start | bytes 393224 | tf_op jit(solution)/shard_map/ppermute | solution.py:531
  71.2 8.7 %collective-permute-start.23 = (bf16[512,128]{1,0:T(8,128)(2,1)S(1)}, bf16[512,128]{1,0:T(8,128)(2,1)S(1)}, u32[]{:S(2)}, u32[]{:S(2)}) collective-permute-start(bf16[512,128]{1,0:T(8,128)(2,1)S(1)} %get-tuple-element.45), channel_id=1, source_target_pairs={{0,4},{1,5},{2,6},{3,7},{4,0},{5,1},{6,2},{7,3},{8,12},{9,13},{10,... | collective-permute-start | bytes 393224 | tf_op jit(solution)/shard_map/ppermute | solution.py:531
  72.5 10.1 %collective-permute-start.24 = (bf16[512,128]{1,0:T(8,128)(2,1)S(1)}, bf16[512,128]{1,0:T(8,128)(2,1)S(1)}, u32[]{:S(2)}, u32[]{:S(2)}) collective-permute-start(bf16[512,128]{1,0:T(8,128)(2,1)S(1)} %get-tuple-element.46), channel_id=1, source_target_pairs={{0,2},{1,3},{2,0},{3,1},{4,6},{5,7},{6,4},{7,5},{8,10},{9,11},{10,... | collective-permute-start | bytes 393224 | tf_op jit(solution)/shard_map/ppermute | solution.py:531
  73.7 8.9 %collective-permute-start.25 = (bf16[512,128]{1,0:T(8,128)(2,1)S(1)}, bf16[512,128]{1,0:T(8,128)(2,1)S(1)}, u32[]{:S(2)}, u32[]{:S(2)}) collective-permute-start(bf16[512,128]{1,0:T(8,128)(2,1)S(1)} %get-tuple-element.47), channel_id=1, source_target_pairs={{0,6},{1,7},{2,4},{3,5},{4,2},{5,3},{6,0},{7,1},{8,14},{9,15},{10,... | collective-permute-start | bytes 393224 | tf_op jit(solution)/shard_map/ppermute | solution.py:531
  78.2 5.0 %collective-permute-start.29 = (bf16[512,128]{1,0:T(8,128)(2,1)S(1)}, bf16[512,128]{1,0:T(8,128)(2,1)S(1)}, u32[]{:S(2)}, u32[]{:S(2)}) collective-permute-start(bf16[512,128]{1,0:T(8,128)(2,1)S(1)} %total.1), channel_id=1, source_target_pairs={{0,16},{16,0},{1,17},{17,1},{2,18},{18,2},{3,19},{19,3},{4,20},{20... | collective-permute-start | bytes 393224 | tf_op jit(solution)/shard_map/ppermute | solution.py:535
  83.3 8.5 %collective-permute-start.30 = (bf16[512,128]{1,0:T(8,128)(2,1)S(1)}, bf16[512,128]{1,0:T(8,128)(2,1)S(1)}, u32[]{:S(2)}, u32[]{:S(2)}) collective-permute-start(bf16[512,128]{1,0:T(8,128)(2,1)S(1)} %get-tuple-element.53), channel_id=1, source_target_pairs={{0,8},{1,9},{2,10},{3,11},{4,12},{5,13},{6,14},{7,15},{8,0},{9,1},... | collective-permute-start | bytes 393224 | tf_op jit(solution)/shard_map/ppermute | solution.py:531
  (1 other events, 9.4 us)
